TPU v7x, 256 devices: a whole 4x4x8 slice. The times are simulated.
256 devices in a mesh: dp: 64 (over z, x, core), sub: 4 (over y).
Axes of the slice: x: 4, y: 4, z: 8, core: 2. Of those that a mesh axis runs over, the one named last changes fastest.
Arguments:
- embeddings: bfloat16 [256, 512, 1024], P('dp', 'sub'), may hold values from -6 to 6
- cluster_ids: int32 [256, 512], P('dp', 'sub'), may hold values from 0 to 15
- valid: int32 [256, 512], P('dp', 'sub'), may hold values 0 or 1
- pair_left: int32 [2048], P('dp'), may hold values from 0 to 255, as said below
- pair_right: int32 [2048], P('dp'), may hold values from 0 to 255, as said below
Outputs:
- best_match: float32 [256, 512], P('dp', 'sub')
Inputs may be any that keep to these rules, and one draw needn't show every extreme that they name: pair_left[p] is one of the 4 blocks of index p // 32 of dp, that is, it lies in [(p // 32) * 4, (p // 32 + 1) * 4). The 32 pairs listed for one index of dp name second blocks held by 32 different indices of dp, one pair for each of them and none for the other 32; a block is held by index pair_right // 4.
All inputs are finite; a program needn't handle non-finite values. No bound on the sum of `valid` on one device may be relied on, other than what follows from the above.
Results may differ from a plain program's by a relative error of at most 0.00037.
Values may be sent and summed in bfloat16 or wider, within the bound.
No kernel may reach another device: no remote copies, remote signals or barrier semaphores. Data moves between devices by JAX's collectives and lax.ppermute only.
A program may use at most 128 MiB of HBM per device.

v0:
```python
import jax
import jax.numpy as jnp
from jax import lax
from jax.experimental import pallas as pl
from jax.experimental.pallas import tpu as pltpu
from jax.sharding import Mesh, PartitionSpec as P

epsilon = 1e-06
ROWS = 128
BLOCKS = 4
META = 16
HALF1 = 2 * ROWS + META
HALF2 = 2 * ROWS
FULL = HALF1 + HALF2
SLOTS = 4
DEPTH = 5
VMEM_LIMIT = 12 * 1024 * 1024


def unit_kernel(emb_ref, meta_ref, full_ref, first_ref, second_ref):
    for block in range(BLOCKS):
        rows = emb_ref[block].astype(jnp.float32)
        scale = lax.rsqrt(jnp.sum(rows * rows, axis=-1, keepdims=True) + epsilon)
        unit = (rows * scale).astype(jnp.bfloat16)
        low = block * ROWS
        at = low + (META if block >= 2 else 0)
        full_ref[at : at + ROWS, :] = unit
        if block < 2:
            first_ref[low : low + ROWS, :] = unit
        else:
            second_ref[low - 2 * ROWS : low - ROWS, :] = unit
    full_ref[2 * ROWS : HALF1, :] = meta_ref[...]
    first_ref[2 * ROWS : HALF1, :] = meta_ref[...]


def choose(index, low, high, act):
    if high - low == 1:
        act(low)
        return
    mid = (low + high) // 2

    @pl.when(index < mid)
    def _():
        choose(index, low, mid, act)

    @pl.when(index >= mid)
    def _():
        choose(index, mid, high, act)


def pair_kernel(right_at, meta_at, table, place, left_ref, *rest):
    refs = rest[:-11]
    left_out, right_out, todo, left_buf, right_buf, left_meta, right_meta, left_tags, right_tags, sems, meta_sems = rest[-11:]
    for k in range(16):
        pltpu.make_async_copy(left_ref.at[pl.ds(k * FULL + 2 * ROWS, META), :], left_meta.at[k], meta_sems.at[0]).start()
        ref, row = meta_at[k]
        pltpu.make_async_copy(refs[ref].at[pl.ds(row, META), :], right_meta.at[k], meta_sems.at[1]).start()

    def note(s, n):
        todo[n] = s
        return n + jnp.where(table[s] > 0, 1, 0)

    count = lax.fori_loop(0, 64, note, 0)

    def parse(i):
        s = todo[i]
        code = table[s] - 1
        return s // 4, s % 4, code // 4, code % 4

    def start(i):
        slot = lax.rem(i, SLOTS)
        chunk, dx, a, b = parse(i)
        row = chunk * FULL + a * ROWS + jnp.where(a >= 2, META, 0)
        pltpu.make_async_copy(left_ref.at[pl.ds(pl.multiple_of(row, 16), ROWS), :], left_buf.at[slot], sems.at[slot, 4]).start()

        def fetch_right(leaf):
            for dy in range(4):
                ref, base = right_at[leaf // 4 * 4 + dy][leaf % 4]
                pltpu.make_async_copy(
                    refs[ref].at[pl.ds(base, ROWS), :], right_buf.at[slot, pl.ds(dy * ROWS, ROWS), :], sems.at[slot, dy]
                ).start()

        choose(dx * 4 + b, 0, 16, fetch_right)

    def finish(i):
        slot = lax.rem(i, SLOTS)
        pltpu.make_async_copy(left_buf.at[slot], left_buf.at[slot], sems.at[slot, 4]).wait()
        for dy in range(4):
            part = right_buf.at[slot, pl.ds(dy * ROWS, ROWS), :]
            pltpu.make_async_copy(part, part, sems.at[slot, dy]).wait()

    for i in range(SLOTS):

        @pl.when(i < count)
        def _(i=i):
            start(jnp.int32(i))

    left_out[...] = jnp.full(left_out.shape, -1.0, jnp.float32)
    right_out[...] = jnp.full(right_out.shape, -1.0, jnp.float32)
    pltpu.make_async_copy(left_meta, left_meta, meta_sems.at[0]).wait()
    pltpu.make_async_copy(right_meta, right_meta, meta_sems.at[1]).wait()
    for k in range(16):
        left_row = left_meta[k, 0:1, : 4 * ROWS].astype(jnp.float32)
        right_row = right_meta[k, 0:1, : 4 * ROWS].astype(jnp.float32)
        right_row = jnp.where(right_row < 0.0, -2.0, right_row)
        for block in range(4):
            left_tags[k * 4 + block : k * 4 + block + 1, :] = left_row[:, block * ROWS : (block + 1) * ROWS]
            right_tags[k * 4 + block : k * 4 + block + 1, :] = right_row[:, block * ROWS : (block + 1) * ROWS]

    row_ids = lax.broadcasted_iota(jnp.int32, (ROWS, ROWS), 0)
    col_ids = lax.broadcasted_iota(jnp.int32, (ROWS, ROWS), 1)
    my_z, my_x, my_c, my_y = place[0], place[1], place[2], place[3]

    def step(i, carry):
        slot = lax.rem(i, SLOTS)
        chunk, dx, a, b = parse(i)
        finish(i)
        scores = lax.dot_general(
            left_buf[slot], right_buf[slot], (((1,), (1,)), ((), ())), preferred_element_type=jnp.float32
        )
        tags = jnp.broadcast_to(left_tags[pl.ds(chunk * 4 + a, 1), :], (ROWS, ROWS)).T
        selfish = (chunk == my_z * 2 + my_c) & (dx == 0) & (a == b)
        best = None
        right_x = lax.rem(my_x + dx, 4)
        for dy in range(4):
            keep = tags == right_tags[pl.ds((dx * 4 + dy) * 4 + b, 1), :]
            if dy == 0:
                keep = keep & ((row_ids != col_ids) | jnp.logical_not(selfish))
            masked = jnp.where(keep, scores[:, dy * ROWS : (dy + 1) * ROWS], -1.0)
            best = masked if best is None else jnp.maximum(best, masked)
            row = (right_x * 4 + lax.rem(my_y + dy, 4)) * 4 + b
            right_out[pl.ds(row, 1), :] = jnp.maximum(right_out[pl.ds(row, 1), :], jnp.max(masked, axis=0, keepdims=True))
        row = chunk * 4 + a
        left_out[pl.ds(row, 1), :] = jnp.maximum(left_out[pl.ds(row, 1), :], jnp.max(best.T, axis=0, keepdims=True))

        @pl.when(i + SLOTS < count)
        def _():
            start(i + SLOTS)

        return carry

    lax.fori_loop(0, count, step, 0)


def pair_maxima(table, place, left_rows, operands, right_at, meta_at):
    def kernel(*refs):
        pair_kernel(right_at, meta_at, *refs)

    smem, vmem, hbm = (pl.BlockSpec(memory_space=s) for s in (pltpu.SMEM, pltpu.VMEM, pltpu.HBM))
    return pl.pallas_call(
        kernel,
        out_shape=(jax.ShapeDtypeStruct((64, ROWS), jnp.float32),) * 2,
        in_specs=[smem, smem] + [hbm] * (len(operands) + 1),
        out_specs=(vmem, vmem),
        scratch_shapes=[
            pltpu.SMEM((65,), jnp.int32),
            pltpu.VMEM((SLOTS, ROWS, 1024), jnp.bfloat16),
            pltpu.VMEM((SLOTS, 4 * ROWS, 1024), jnp.bfloat16),
            pltpu.VMEM((16, META, 1024), jnp.bfloat16),
            pltpu.VMEM((16, META, 1024), jnp.bfloat16),
            pltpu.VMEM((64, ROWS), jnp.float32),
            pltpu.VMEM((64, ROWS), jnp.float32),
            pltpu.SemaphoreType.DMA((SLOTS, 5)),
            pltpu.SemaphoreType.DMA((2,)),
        ],
        compiler_params=pltpu.CompilerParams(vmem_limit_bytes=VMEM_LIMIT),
        name="pair_maxima",
    )(table, place, *(pltpu.with_memory_space_constraint(v, pltpu.HBM) for v in (left_rows, *operands)))


class Carrier:
    def __init__(self):
        self.sent = []

    def __call__(self, value, axis, by):
        if len(self.sent) >= DEPTH:
            k = len(self.sent) - DEPTH
            value, self.sent[k][0] = lax.optimization_barrier((value, self.sent[k][0]))
        size = lax.axis_size(axis)
        cell = [lax.ppermute(value, axis, [((i + by) % size, i) for i in range(size)])]
        self.sent.append(cell)
        return cell


def gather_plane(h1, h2):
    send = Carrier()
    xp, xm, yp, ym = [], [], [], []
    order = ((xp, "x", 1), (xm, "x", -1), (yp, "y", 1), (ym, "y", -1))

    def send_all(values):
        for (into, axis, by), value in zip(order, values):
            into.append(send(value[0], axis, by))

    own1, own2 = [h1], [h2]
    send_all((own1, own2, own1, own2))
    send_all((own2, own1, own2, own1))
    x1, x3 = (xp[0], xp[1]), (xm[1], xm[0])
    y1, y3 = (yp[0], yp[1]), (ym[1], ym[0])
    send_all((x1[0], x3[1], y1[0], y3[1]))
    x2, y2 = (xp[2], xm[2]), (yp[2], ym[2])
    send_all((y1[1], y1[1], x1[0], x1[0]))
    send_all((y3[1], y3[1], x3[0], x3[0]))
    send_all((y2[1], y2[1], x2[0], x2[0]))
    send_all((xp[3], xm[4], yp[3], ym[4]))
    low, high = [xp[5][0][:ROWS]], [xm[5][0][ROWS:]]
    low_y, high_y = [yp[5][0][:ROWS]], [ym[5][0][ROWS:]]
    send_all((low, high, low_y, high_y))
    second = {(1, 1): xp[3], (3, 1): xm[3], (1, 3): xp[4], (3, 3): xm[4], (1, 2): xp[5], (3, 2): xm[5], (2, 1): xp[6], (2, 3): xm[6]}
    first = {(1, 1): yp[3], (1, 3): ym[3], (3, 1): yp[4], (3, 3): ym[4], (2, 1): yp[5], (2, 3): ym[5], (1, 2): yp[6], (3, 2): ym[6]}
    whole = {(0, 0): (own1, own2), (1, 0): x1, (3, 0): x3, (2, 0): x2, (0, 1): y1, (0, 3): y3, (0, 2): y2}
    for key in first:
        whole[key] = (first[key], second[key])
    parts = {}
    for key, (a, b) in whole.items():
        parts[key] = ((a[0], 0), (a[0], ROWS), (b[0], 0), (b[0], ROWS))
    parts[2, 2] = ((yp[7][0], 0), (ym[7][0], 0), (xp[7][0], 0), (xm[7][0], 0))
    metas = {key: (a[0], 2 * ROWS) for key, (a, _) in whole.items()}
    metas[2, 2] = (ym[7][0], ROWS)
    return parts, metas


def local(embeddings, cluster_ids, valid, pair_left, pair_right):
    my_z, my_x, my_c, my_y = (lax.axis_index(name) for name in ("z", "x", "c", "y"))
    labels = jnp.where(valid > 0, cluster_ids, -1).reshape(1, -1)
    meta = jnp.concatenate([labels, (pair_left % BLOCKS)[None], pair_right[None]], axis=1).astype(jnp.bfloat16)
    meta = jnp.pad(meta, ((0, META - 1), (0, 1024 - meta.shape[1])))
    full, h1, h2 = pl.pallas_call(
        unit_kernel,
        out_shape=[jax.ShapeDtypeStruct((n, 1024), jnp.bfloat16) for n in (FULL, HALF1, HALF2)],
        compiler_params=pltpu.CompilerParams(vmem_limit_bytes=VMEM_LIMIT),
        name="unit_rows",
    )(embeddings, meta)
    left_rows = lax.all_gather(full, ("z", "c"), axis=0, tiled=True)
    parts, metas = gather_plane(h1, h2)

    listed = left_rows.reshape(16, FULL, 1024)[:, 2 * ROWS, 512:576].astype(jnp.int32)
    a, b = listed[:, :32], listed[:, 32:]
    group = b // BLOCKS
    mine = (group // 8 == my_z) & (group % 2 == my_c)
    dx = ((group // 2) % 4 - my_x) % 4
    code = jnp.where(mine, 1 + a * BLOCKS + b % BLOCKS, 0)
    table = jnp.max(jnp.where(dx[:, :, None] == jnp.arange(4), code[:, :, None], 0), axis=1).reshape(64)
    place = jnp.stack([my_z, my_x, my_c, my_y]).astype(jnp.int32)

    operands, known, right_at, meta_at = [], {}, [], []

    def place_of(value):
        if id(value) not in known:
            known[id(value)] = len(operands)
            operands.append(value)
        return known[id(value)]

    for k in [(dx, dy) for dx in range(4) for dy in range(4)]:
        right_at.append([(place_of(value), base) for value, base in parts[k]])
        meta_at.append((place_of(metas[k][0]), metas[k][1]))
    left_best, right_best = pair_maxima(table, place, left_rows, operands, right_at, meta_at)
    from_left = lax.all_to_all(left_best.reshape(16, BLOCKS, ROWS), ("z", "c"), 0, 0, tiled=True)
    from_right = lax.all_to_all(right_best.reshape(16, BLOCKS, ROWS), ("x", "y"), 0, 0, tiled=True)
    return jnp.maximum(jnp.max(from_left, axis=0), jnp.max(from_right, axis=0))


def solution(mesh):
    wide = Mesh(mesh.devices.reshape(8, 4, 2, 4), ("z", "x", "c", "y"))
    dp = ("z", "x", "c")
    placed = (P(dp, "y", None), P(dp, "y"), P(dp, "y"), P(dp), P(dp))
    return jax.shard_map(local, mesh=wide, in_specs=placed, out_specs=P(dp, "y"), check_vma=False)
```

profile of v0, /device:TPU:1, one launch (start us, length us, event | category | flops | bytes accessed | tf_op | source)
XLA Modules:
  0.0 192.6 jit_solution(2400253792237678768)
XLA Ops:
  6.5 0.7 fusion.23
  7.2 0.7 fusion.25
  8.0 1.2 copy-done
  9.2 1.3 unit_rows.1
  10.6 3.4 %collective-permute-start.1 = (bf16[272,1024]{1,0:T(8,128)(2,1)S(1)}, bf16[272,1024]{1,0:T(8,128)(2,1)S(1)}, u32[]{:S(2)}, u32[]{:S(2)}) collective-permute-start(bf16[272,1024]{1,0:T(8,128)(2,1)S(1)} %get-tuple-element.77.refs_3_), channel_id=1, source_target_pairs={{8,0},{16,8},{24,16},{0,24},{9,1},{17,9},{25,17},{1,25},{10,2},{18... | collective-permute-start | bytes 1671176 | tf_op jit(solution)/shard_map/ppermute | solution.py:180
  14.0 2.7 %collective-permute-start = (bf16[272,1024]{1,0:T(8,128)(2,1)S(1)}, bf16[272,1024]{1,0:T(8,128)(2,1)S(1)}, u32[]{:S(2)}, u32[]{:S(2)}) collective-permute-start(bf16[272,1024]{1,0:T(8,128)(2,1)S(1)} %get-tuple-element.77.refs_3_), channel_id=1, source_target_pairs={{1,0},{2,1},{3,2},{0,3},{5,4},{6,5},{7,6},{4,7},{9,8},{10,9},{11,1... | collective-permute-start | bytes 1671176 | tf_op jit(solution)/shard_map/ppermute | solution.py:180
  16.7 8.6 %collective-permute-done.1.refs_11_ = bf16[272,1024]{1,0:T(8,128)(2,1)S(1)} collective-permute-done((bf16[272,1024]{1,0:T(8,128)(2,1)S(1)}, bf16[272,1024]{1,0:T(8,128)(2,1)S(1)}, u32[]{:S(2)}, u32[]{:S(2)}) %collective-permute-start.1) | collective-permute-done | bytes 557088 | tf_op jit(solution)/shard_map/ppermute | solution.py:180
  25.3 0.9 collective-permute-start.5
  26.2 2.5 %collective-permute-start.9 = (bf16[256,1024]{1,0:T(8,128)(2,1)S(1)}, bf16[256,1024]{1,0:T(8,128)(2,1)S(1)}, u32[]{:S(2)}, u32[]{:S(2)}) collective-permute-start(bf16[256,1024]{1,0:T(8,128)(2,1)S(1)} %get-tuple-element.70.refs_4_), channel_id=1, source_target_pairs={{8,0},{16,8},{24,16},{0,24},{9,1},{17,9},{25,17},{1,25},{10,2},{18... | collective-permute-start | bytes 1572872 | tf_op jit(solution)/shard_map/ppermute | solution.py:180
  28.7 2.7 %collective-permute-start.4 = (bf16[256,1024]{1,0:T(8,128)(2,1)S(1)}, bf16[256,1024]{1,0:T(8,128)(2,1)S(1)}, u32[]{:S(2)}, u32[]{:S(2)}) collective-permute-start(bf16[256,1024]{1,0:T(8,128)(2,1)S(1)} %get-tuple-element.70.refs_4_), channel_id=1, source_target_pairs={{1,0},{2,1},{3,2},{0,3},{5,4},{6,5},{7,6},{4,7},{9,8},{10,9},{11,1... | collective-permute-start | bytes 1572872 | tf_op jit(solution)/shard_map/ppermute | solution.py:180
  31.4 1.5 collective-permute-start.13
  32.9 5.5 %collective-permute-done.9.refs_12_ = bf16[256,1024]{1,0:T(8,128)(2,1)S(1)} collective-permute-done((bf16[256,1024]{1,0:T(8,128)(2,1)S(1)}, bf16[256,1024]{1,0:T(8,128)(2,1)S(1)}, u32[]{:S(2)}, u32[]{:S(2)}) %collective-permute-start.9) | collective-permute-done | bytes 524320 | tf_op jit(solution)/shard_map/ppermute | solution.py:180
  38.4 1.7 collective-permute-start.10
  40.1 1.4 collective-permute-start.8
  41.4 1.5 collective-permute-start.6
  43.0 6.8 %collective-permute-done.10.refs_20_ = bf16[256,1024]{1,0:T(8,128)(2,1)S(1)} collective-permute-done((bf16[256,1024]{1,0:T(8,128)(2,1)S(1)}, bf16[256,1024]{1,0:T(8,128)(2,1)S(1)}, u32[]{:S(2)}, u32[]{:S(2)}) %collective-permute-start.10) | collective-permute-done | bytes 524320 | tf_op jit(solution)/shard_map/ppermute | solution.py:180
  49.8 2.7 %collective-permute-start.11 = (bf16[272,1024]{1,0:T(8,128)(2,1)S(1)}, bf16[272,1024]{1,0:T(8,128)(2,1)}, u32[]{:S(2)}, u32[]{:S(2)}) collective-permute-start(bf16[272,1024]{1,0:T(8,128)(2,1)S(1)} %collective-permute-done.1.refs_11_), channel_id=1, source_target_pairs={{1,0},{2,1},{3,2},{0,3},{5,4},{6,5},{7,6},{4,7},{9,8},{10,9},{11,1... | collective-permute-start | bytes 1671176 | tf_op jit(solution)/shard_map/ppermute | solution.py:180
  52.5 2.7 %collective-permute-start.12 = (bf16[256,1024]{1,0:T(8,128)(2,1)S(1)}, bf16[256,1024]{1,0:T(8,128)(2,1)}, u32[]{:S(2)}, u32[]{:S(2)}) collective-permute-start(bf16[256,1024]{1,0:T(8,128)(2,1)S(1)} %collective-permute-done.4.refs_6_), channel_id=1, source_target_pairs={{8,0},{16,8},{24,16},{0,24},{9,1},{17,9},{25,17},{1,25},{10,2},{18... | collective-permute-start | bytes 1572872 | tf_op jit(solution)/shard_map/ppermute | solution.py:180
  55.2 7.0 %collective-permute-done.7.refs_8_ = bf16[256,1024]{1,0:T(8,128)(2,1)S(1)} collective-permute-done((bf16[256,1024]{1,0:T(8,128)(2,1)S(1)}, bf16[256,1024]{1,0:T(8,128)(2,1)S(1)}, u32[]{:S(2)}, u32[]{:S(2)}) %collective-permute-start.7) | collective-permute-done | bytes 524320 | tf_op jit(solution)/shard_map/ppermute | solution.py:180
  62.2 2.9 %collective-permute-start.17 = (bf16[256,1024]{1,0:T(8,128)(2,1)S(1)}, bf16[256,1024]{1,0:T(8,128)(2,1)S(1)}, u32[]{:S(2)}, u32[]{:S(2)}) collective-permute-start(bf16[256,1024]{1,0:T(8,128)(2,1)S(1)} %collective-permute-done.2.refs_10_), channel_id=1, source_target_pairs={{8,0},{16,8},{24,16},{0,24},{9,1},{17,9},{25,17},{1,25},{10,2},{18... | collective-permute-start | bytes 1572872 | tf_op jit(solution)/shard_map/ppermute | solution.py:180
  65.2 2.7 %collective-permute-start.15 = (bf16[272,1024]{1,0:T(8,128)(2,1)S(1)}, bf16[272,1024]{1,0:T(8,128)(2,1)S(1)}, u32[]{:S(2)}, u32[]{:S(2)}) collective-permute-start(bf16[272,1024]{1,0:T(8,128)(2,1)S(1)} %collective-permute-done.5.refs_29_), channel_id=1, source_target_pairs={{1,0},{2,1},{3,2},{0,3},{5,4},{6,5},{7,6},{4,7},{9,8},{10,9},{11,1... | collective-permute-start | bytes 1671176 | tf_op jit(solution)/shard_map/ppermute | solution.py:180
  68.0 8.8 %collective-permute-done.17.refs_18_ = bf16[256,1024]{1,0:T(8,128)(2,1)S(1)} collective-permute-done((bf16[256,1024]{1,0:T(8,128)(2,1)S(1)}, bf16[256,1024]{1,0:T(8,128)(2,1)S(1)}, u32[]{:S(2)}, u32[]{:S(2)}) %collective-permute-start.17) | collective-permute-done | bytes 524320 | tf_op jit(solution)/shard_map/ppermute | solution.py:180
  76.8 0.4 collective-permute-start.18
  77.2 3.2 %collective-permute-start.22 = (bf16[256,1024]{1,0:T(8,128)(2,1)S(1)}, bf16[256,1024]{1,0:T(8,128)(2,1)S(1)}, u32[]{:S(2)}, u32[]{:S(2)}) collective-permute-start(bf16[256,1024]{1,0:T(8,128)(2,1)S(1)} %collective-permute-done.7.refs_8_), channel_id=1, source_target_pairs={{8,0},{16,8},{24,16},{0,24},{9,1},{17,9},{25,17},{1,25},{10,2},{18... | collective-permute-start | bytes 1572872 | tf_op jit(solution)/shard_map/ppermute | solution.py:180
  80.4 1.4 collective-permute-start.24
  81.9 11.0 %collective-permute-done.18.refs_34_ = bf16[256,1024]{1,0:T(8,128)(2,1)S(1)} collective-permute-done((bf16[256,1024]{1,0:T(8,128)(2,1)S(1)}, bf16[256,1024]{1,0:T(8,128)(2,1)S(1)}, u32[]{:S(2)}, u32[]{:S(2)}) %collective-permute-start.18) | collective-permute-done | bytes 524320 | tf_op jit(solution)/shard_map/ppermute | solution.py:180
  92.9 1.3 collective-permute-start.19
  94.2 1.5 collective-permute-start.25
  96.0 0.7 slice.25
  96.8 6.1 %collective-permute-done.25.refs_22_ = bf16[256,1024]{1,0:T(8,128)(2,1)} collective-permute-done((bf16[256,1024]{1,0:T(8,128)(2,1)}, bf16[256,1024]{1,0:T(8,128)(2,1)}, u32[]{:S(2)}, u32[]{:S(2)}) %collective-permute-start.25) | collective-permute-done | bytes 524320 | tf_op jit(solution)/shard_map/ppermute | solution.py:180
  102.9 0.7 slice.26
  103.6 0.1 collective-permute-start.31
  103.7 0.7 slice.27
  104.4 2.7 %collective-permute-start.29 = (bf16[128,1024]{1,0:T(8,128)(2,1)}, bf16[128,1024]{1,0:T(8,128)(2,1)}, u32[]{:S(2)}, u32[]{:S(2)}) collective-permute-start(bf16[128,1024]{1,0:T(8,128)(2,1)} %slice.27), channel_id=1, source_target_pairs={{8,0},{16,8},{24,16},{0,24},{9,1},{17,9},{25,17},{1,25},{10,2},{18... | collective-permute-start | bytes 786440 | tf_op jit(solution)/shard_map/ppermute | solution.py:180
  107.1 0.7 slice.31
  107.8 0.7 collective-permute-start.28
  108.5 2.1 %collective-permute-start.27 = (bf16[128,1024]{1,0:T(8,128)(2,1)}, bf16[128,1024]{1,0:T(8,128)(2,1)}, u32[]{:S(2)}, u32[]{:S(2)}) collective-permute-start(bf16[128,1024]{1,0:T(8,128)(2,1)} %slice.26), channel_id=1, source_target_pairs={{1,0},{2,1},{3,2},{0,3},{5,4},{6,5},{7,6},{4,7},{9,8},{10,9},{11,1... | collective-permute-start | bytes 786440 | tf_op jit(solution)/shard_map/ppermute | solution.py:180
  110.6 2.3 %all-gather.2.cloned.1.call-done.refs_2_ = bf16[8448,1024]{1,0:T(8,128)(2,1)} async-done(((bf16[528,1024]{1,0:T(8,128)(2,1)}), bf16[8448,1024]{1,0:T(8,128)(2,1)}) %all-gather.2.cloned.1.call-update) | async-done | bytes 17301520 | tf_op jit(solution)/shard_map/all_gather | solution.py:233
  112.8 0.8 slice_convert_fusion
  113.6 0.1 add_select_fusion.3
  113.8 0.1 select_reduce_fusion
  114.2 2.4 %collective-permute-done.28.refs_24_ = bf16[144,1024]{1,0:T(8,128)(2,1)S(1)} collective-permute-done((bf16[144,1024]{1,0:T(8,128)(2,1)}, bf16[144,1024]{1,0:T(8,128)(2,1)S(1)}, u32[]{:S(2)}, u32[]{:S(2)}) %collective-permute-start.28) | collective-permute-done | bytes 294944 | tf_op jit(solution)/shard_map/ppermute | solution.py:180
  116.6 0.7 copy-done.22
  117.3 23.0 %pair_maxima.1 = (f32[64,128]{1,0:T(8,128)}, f32[64,128]{1,0:T(8,128)S(1)}) custom-call(s32[64]{0:T(128)S(1)} %reshape.73.refs_0_, s32[4]{0:T(128)S(1)} %pad_add_fusion.refs_1_, bf16[8448,1024]{1,0:T(8,128)(2,1)} %all-gather.2.cloned.1.call-done.refs_2_, bf16[272,1024]{1,0:T(8,128)(2,1)} %copy-done.1, bf16[256,1024]{1,0:T(8,128)(2,1)} %copy-done.2, ...), custom_call_target="tpu_custom_call" | custom-call | tf_op jit(solution)/shard_map/pair_maxima/pallas_call | solution.py:150
  140.3 13.1 %all_to_all.10 = f32[16,4,128]{2,1,0:T(4,128)S(1)} all-to-all(f32[16,4,128]{2,1,0:T(4,128)S(1)} %bitcast.18), channel_id=1, replica_groups=mesh['z'=8,'x'=4,'c'=2,'y'=4] {'x','y'}, dimensions={0} | all-to-all | bytes 65536 | tf_op jit(solution)/shard_map/all_to_all | solution.py:258
  153.4 24.4 %all-to-all-start = ((f32[16,4,128]{2,1,0:T(4,128)}), f32[16,4,128]{2,1,0:T(4,128)S(1)}, u32[]{:S(2)}, u32[]{:S(2)}) async-start(f32[16,4,128]{2,1,0:T(4,128)} %bitcast.8), calls=%async_computation | async-start | bytes 65536 | tf_op jit(solution)/shard_map/all_to_all | solution.py:257
  177.8 7.4 %all-to-all-done = f32[16,4,128]{2,1,0:T(4,128)S(1)} async-done(((f32[16,4,128]{2,1,0:T(4,128)}), f32[16,4,128]{2,1,0:T(4,128)S(1)}, u32[]{:S(2)}, u32[]{:S(2)}) %all-to-all-start) | async-done | bytes 32800 | tf_op jit(solution)/shard_map/all_to_all | solution.py:257
  185.2 0.6 max.3
  (88 shorter events, 1.0 us)
Async XLA Ops:
  6.5 106.3 %all-gather.2.cloned.1.call-start = ((), (), s32[]{:S(2)}) async-start(), calls=%async_computation.2 | async-start | bytes 18382848 | tf_op jit(solution)/shard_map/all_gather | solution.py:233
  10.6 106.0 %copy-start.1 = (bf16[272,1024]{1,0:T(8,128)(2,1)}, bf16[272,1024]{1,0:T(8,128)(2,1)S(1)}, u32[]{:S(2)}) copy-start(bf16[272,1024]{1,0:T(8,128)(2,1)S(1)} %get-tuple-element.77.refs_3_) | copy-start | bytes 1671172
  10.6 106.0 %copy-start.2 = (bf16[256,1024]{1,0:T(8,128)(2,1)}, bf16[256,1024]{1,0:T(8,128)(2,1)S(1)}, u32[]{:S(2)}) copy-start(bf16[256,1024]{1,0:T(8,128)(2,1)S(1)} %get-tuple-element.70.refs_4_) | copy-start | bytes 1572868
  10.6 14.7 %collective-permute-start.1 = (bf16[272,1024]{1,0:T(8,128)(2,1)S(1)}, bf16[272,1024]{1,0:T(8,128)(2,1)S(1)}, u32[]{:S(2)}, u32[]{:S(2)}) collective-permute-start(bf16[272,1024]{1,0:T(8,128)(2,1)S(1)} %get-tuple-element.77.refs_3_), channel_id=1, source_target_pairs={{8,0},{16,8},{24,16},{0,24},{9,1},{17,9},{25,17},{1,25},{10,2},{18... | collective-permute-start | bytes 1671176 | tf_op jit(solution)/shard_map/ppermute | solution.py:180
  14.0 14.7 %collective-permute-start.3 = (bf16[256,1024]{1,0:T(8,128)(2,1)S(1)}, bf16[256,1024]{1,0:T(8,128)(2,1)S(1)}, u32[]{:S(2)}, u32[]{:S(2)}) collective-permute-start(bf16[256,1024]{1,0:T(8,128)(2,1)S(1)} %get-tuple-element.70.refs_4_), channel_id=1, source_target_pairs={{24,0},{0,8},{8,16},{16,24},{25,1},{1,9},{9,17},{17,25},{26,2},{2,... | collective-permute-start | bytes 1572872 | tf_op jit(solution)/shard_map/ppermute | solution.py:180
  14.0 26.1 %collective-permute-start = (bf16[272,1024]{1,0:T(8,128)(2,1)S(1)}, bf16[272,1024]{1,0:T(8,128)(2,1)S(1)}, u32[]{:S(2)}, u32[]{:S(2)}) collective-permute-start(bf16[272,1024]{1,0:T(8,128)(2,1)S(1)} %get-tuple-element.77.refs_3_), channel_id=1, source_target_pairs={{1,0},{2,1},{3,2},{0,3},{5,4},{6,5},{7,6},{4,7},{9,8},{10,9},{11,1... | collective-permute-start | bytes 1671176 | tf_op jit(solution)/shard_map/ppermute | solution.py:180
  16.7 14.7 %collective-permute-start.2 = (bf16[256,1024]{1,0:T(8,128)(2,1)S(1)}, bf16[256,1024]{1,0:T(8,128)(2,1)S(1)}, u32[]{:S(2)}, u32[]{:S(2)}) collective-permute-start(bf16[256,1024]{1,0:T(8,128)(2,1)S(1)} %get-tuple-element.70.refs_4_), channel_id=1, source_target_pairs={{3,0},{0,1},{1,2},{2,3},{7,4},{4,5},{5,6},{6,7},{11,8},{8,9},{9,10... | collective-permute-start | bytes 1572872 | tf_op jit(solution)/shard_map/ppermute | solution.py:180
  25.3 70.5 %copy-start.7 = (bf16[272,1024]{1,0:T(8,128)(2,1)}, bf16[272,1024]{1,0:T(8,128)(2,1)S(1)}, u32[]{:S(2)}) copy-start(bf16[272,1024]{1,0:T(8,128)(2,1)S(1)} %collective-permute-done.1.refs_11_) | copy-start | bytes 1671172
  25.3 16.2 %collective-permute-start.5 = (bf16[272,1024]{1,0:T(8,128)(2,1)S(1)}, bf16[272,1024]{1,0:T(8,128)(2,1)S(1)}, u32[]{:S(2)}, u32[]{:S(2)}) collective-permute-start(bf16[272,1024]{1,0:T(8,128)(2,1)S(1)} %get-tuple-element.77.refs_3_), channel_id=1, source_target_pairs={{24,0},{0,8},{8,16},{16,24},{25,1},{1,9},{9,17},{17,25},{26,2},{2,... | collective-permute-start | bytes 1671176 | tf_op jit(solution)/shard_map/ppermute | solution.py:180
  26.2 12.2 %collective-permute-start.9 = (bf16[256,1024]{1,0:T(8,128)(2,1)S(1)}, bf16[256,1024]{1,0:T(8,128)(2,1)S(1)}, u32[]{:S(2)}, u32[]{:S(2)}) collective-permute-start(bf16[256,1024]{1,0:T(8,128)(2,1)S(1)} %get-tuple-element.70.refs_4_), channel_id=1, source_target_pairs={{8,0},{16,8},{24,16},{0,24},{9,1},{17,9},{25,17},{1,25},{10,2},{18... | collective-permute-start | bytes 1572872 | tf_op jit(solution)/shard_map/ppermute | solution.py:180
  28.7 36.4 %copy-start.15 = (bf16[256,1024]{1,0:T(8,128)(2,1)}, bf16[256,1024]{1,0:T(8,128)(2,1)S(1)}, u32[]{:S(2)}) copy-start(bf16[256,1024]{1,0:T(8,128)(2,1)S(1)} %collective-permute-done.3.refs_30_) | copy-start | bytes 1572868
  28.7 14.3 %collective-permute-start.4 = (bf16[256,1024]{1,0:T(8,128)(2,1)S(1)}, bf16[256,1024]{1,0:T(8,128)(2,1)S(1)}, u32[]{:S(2)}, u32[]{:S(2)}) collective-permute-start(bf16[256,1024]{1,0:T(8,128)(2,1)S(1)} %get-tuple-element.70.refs_4_), channel_id=1, source_target_pairs={{1,0},{2,1},{3,2},{0,3},{5,4},{6,5},{7,6},{4,7},{9,8},{10,9},{11,1... | collective-permute-start | bytes 1572872 | tf_op jit(solution)/shard_map/ppermute | solution.py:180
  31.4 64.4 %copy-start.16 = (bf16[256,1024]{1,0:T(8,128)(2,1)}, bf16[256,1024]{1,0:T(8,128)(2,1)S(1)}, u32[]{:S(2)}) copy-start(bf16[256,1024]{1,0:T(8,128)(2,1)S(1)} %collective-permute-done.2.refs_10_) | copy-start | bytes 1572868
  31.4 21.1 %collective-permute-start.13 = (bf16[272,1024]{1,0:T(8,128)(2,1)S(1)}, bf16[272,1024]{1,0:T(8,128)(2,1)}, u32[]{:S(2)}, u32[]{:S(2)}) collective-permute-start(bf16[272,1024]{1,0:T(8,128)(2,1)S(1)} %collective-permute-done.1.refs_11_), channel_id=1, source_target_pairs={{8,0},{16,8},{24,16},{0,24},{9,1},{17,9},{25,17},{1,25},{10,2},{18... | collective-permute-start | bytes 1671176 | tf_op jit(solution)/shard_map/ppermute | solution.py:180
  38.4 11.4 %collective-permute-start.10 = (bf16[256,1024]{1,0:T(8,128)(2,1)S(1)}, bf16[256,1024]{1,0:T(8,128)(2,1)S(1)}, u32[]{:S(2)}, u32[]{:S(2)}) collective-permute-start(bf16[256,1024]{1,0:T(8,128)(2,1)S(1)} %collective-permute-done.3.refs_30_), channel_id=1, source_target_pairs={{24,0},{0,8},{8,16},{16,24},{25,1},{1,9},{9,17},{17,25},{26,2},{2,... | collective-permute-start | bytes 1572872 | tf_op jit(solution)/shard_map/ppermute | solution.py:180
  40.1 55.8 %copy-start.8 = (bf16[272,1024]{1,0:T(8,128)(2,1)}, bf16[272,1024]{1,0:T(8,128)(2,1)S(1)}, u32[]{:S(2)}) copy-start(bf16[272,1024]{1,0:T(8,128)(2,1)S(1)} %collective-permute-done.refs_5_) | copy-start | bytes 1671172
  40.1 12.5 %collective-permute-start.8 = (bf16[272,1024]{1,0:T(8,128)(2,1)S(1)}, bf16[272,1024]{1,0:T(8,128)(2,1)S(1)}, u32[]{:S(2)}, u32[]{:S(2)}) collective-permute-start(bf16[272,1024]{1,0:T(8,128)(2,1)S(1)} %get-tuple-element.77.refs_3_), channel_id=1, source_target_pairs={{3,0},{0,1},{1,2},{2,3},{7,4},{4,5},{5,6},{6,7},{11,8},{8,9},{9,10... | collective-permute-start | bytes 1671176 | tf_op jit(solution)/shard_map/ppermute | solution.py:180
  41.4 54.4 %copy-start.9 = (bf16[272,1024]{1,0:T(8,128)(2,1)}, bf16[272,1024]{1,0:T(8,128)(2,1)S(1)}, u32[]{:S(2)}) copy-start(bf16[272,1024]{1,0:T(8,128)(2,1)S(1)} %collective-permute-done.5.refs_29_) | copy-start | bytes 1671172
  41.4 23.7 %collective-permute-start.6 = (bf16[272,1024]{1,0:T(8,128)(2,1)S(1)}, bf16[272,1024]{1,0:T(8,128)(2,1)S(1)}, u32[]{:S(2)}, u32[]{:S(2)}) collective-permute-start(bf16[272,1024]{1,0:T(8,128)(2,1)S(1)} %collective-permute-done.refs_5_), channel_id=1, source_target_pairs={{1,0},{2,1},{3,2},{0,3},{5,4},{6,5},{7,6},{4,7},{9,8},{10,9},{11,1... | collective-permute-start | bytes 1671176 | tf_op jit(solution)/shard_map/ppermute | solution.py:180
  43.0 52.9 %copy-start.18 = (bf16[256,1024]{1,0:T(8,128)(2,1)}, bf16[256,1024]{1,0:T(8,128)(2,1)S(1)}, u32[]{:S(2)}) copy-start(bf16[256,1024]{1,0:T(8,128)(2,1)S(1)} %collective-permute-done.4.refs_6_) | copy-start | bytes 1572868
  43.0 19.2 %collective-permute-start.7 = (bf16[256,1024]{1,0:T(8,128)(2,1)S(1)}, bf16[256,1024]{1,0:T(8,128)(2,1)S(1)}, u32[]{:S(2)}, u32[]{:S(2)}) collective-permute-start(bf16[256,1024]{1,0:T(8,128)(2,1)S(1)} %collective-permute-done.2.refs_10_), channel_id=1, source_target_pairs={{3,0},{0,1},{1,2},{2,3},{7,4},{4,5},{5,6},{6,7},{11,8},{8,9},{9,10... | collective-permute-start | bytes 1572872 | tf_op jit(solution)/shard_map/ppermute | solution.py:180
  49.8 18.1 %collective-permute-start.11 = (bf16[272,1024]{1,0:T(8,128)(2,1)S(1)}, bf16[272,1024]{1,0:T(8,128)(2,1)}, u32[]{:S(2)}, u32[]{:S(2)}) collective-permute-start(bf16[272,1024]{1,0:T(8,128)(2,1)S(1)} %collective-permute-done.1.refs_11_), channel_id=1, source_target_pairs={{1,0},{2,1},{3,2},{0,3},{5,4},{6,5},{7,6},{4,7},{9,8},{10,9},{11,1... | collective-permute-start | bytes 1671176 | tf_op jit(solution)/shard_map/ppermute | solution.py:180
  52.5 12.7 %collective-permute-start.14 = (bf16[256,1024]{1,0:T(8,128)(2,1)S(1)}, bf16[256,1024]{1,0:T(8,128)(2,1)}, u32[]{:S(2)}, u32[]{:S(2)}) collective-permute-start(bf16[256,1024]{1,0:T(8,128)(2,1)S(1)} %collective-permute-done.4.refs_6_), channel_id=1, source_target_pairs={{24,0},{0,8},{8,16},{16,24},{25,1},{1,9},{9,17},{17,25},{26,2},{2,... | collective-permute-start | bytes 1572872 | tf_op jit(solution)/shard_map/ppermute | solution.py:180
  52.5 43.4 %copy-start.10 = (bf16[272,1024]{1,0:T(8,128)(2,1)}, bf16[272,1024]{1,0:T(8,128)(2,1)S(1)}, u32[]{:S(2)}) copy-start(bf16[272,1024]{1,0:T(8,128)(2,1)S(1)} %collective-permute-done.8.refs_9_) | copy-start | bytes 1671172
  52.5 15.3 %collective-permute-start.12 = (bf16[256,1024]{1,0:T(8,128)(2,1)S(1)}, bf16[256,1024]{1,0:T(8,128)(2,1)}, u32[]{:S(2)}, u32[]{:S(2)}) collective-permute-start(bf16[256,1024]{1,0:T(8,128)(2,1)S(1)} %collective-permute-done.4.refs_6_), channel_id=1, source_target_pairs={{8,0},{16,8},{24,16},{0,24},{9,1},{17,9},{25,17},{1,25},{10,2},{18... | collective-permute-start | bytes 1572872 | tf_op jit(solution)/shard_map/ppermute | solution.py:180
  62.2 33.7 %copy-start.20 = (bf16[256,1024]{1,0:T(8,128)(2,1)}, bf16[256,1024]{1,0:T(8,128)(2,1)S(1)}, u32[]{:S(2)}) copy-start(bf16[256,1024]{1,0:T(8,128)(2,1)S(1)} %collective-permute-done.7.refs_8_) | copy-start | bytes 1572868
  62.2 14.6 %collective-permute-start.17 = (bf16[256,1024]{1,0:T(8,128)(2,1)S(1)}, bf16[256,1024]{1,0:T(8,128)(2,1)S(1)}, u32[]{:S(2)}, u32[]{:S(2)}) collective-permute-start(bf16[256,1024]{1,0:T(8,128)(2,1)S(1)} %collective-permute-done.2.refs_10_), channel_id=1, source_target_pairs={{8,0},{16,8},{24,16},{0,24},{9,1},{17,9},{25,17},{1,25},{10,2},{18... | collective-permute-start | bytes 1572872 | tf_op jit(solution)/shard_map/ppermute | solution.py:180
  65.1 30.8 %copy-start.11 = (bf16[272,1024]{1,0:T(8,128)(2,1)}, bf16[272,1024]{1,0:T(8,128)(2,1)S(1)}, u32[]{:S(2)}) copy-start(bf16[272,1024]{1,0:T(8,128)(2,1)S(1)} %collective-permute-done.6.refs_7_) | copy-start | bytes 1671172
  65.1 12.1 %collective-permute-start.21 = (bf16[272,1024]{1,0:T(8,128)(2,1)S(1)}, bf16[272,1024]{1,0:T(8,128)(2,1)S(1)}, u32[]{:S(2)}, u32[]{:S(2)}) collective-permute-start(bf16[272,1024]{1,0:T(8,128)(2,1)S(1)} %collective-permute-done.1.refs_11_), channel_id=1, source_target_pairs={{3,0},{0,1},{1,2},{2,3},{7,4},{4,5},{5,6},{6,7},{11,8},{8,9},{9,10... | collective-permute-start | bytes 1671176 | tf_op jit(solution)/shard_map/ppermute | solution.py:180
  65.2 16.6 %collective-permute-start.15 = (bf16[272,1024]{1,0:T(8,128)(2,1)S(1)}, bf16[272,1024]{1,0:T(8,128)(2,1)S(1)}, u32[]{:S(2)}, u32[]{:S(2)}) collective-permute-start(bf16[272,1024]{1,0:T(8,128)(2,1)S(1)} %collective-permute-done.5.refs_29_), channel_id=1, source_target_pairs={{1,0},{2,1},{3,2},{0,3},{5,4},{6,5},{7,6},{4,7},{9,8},{10,9},{11,1... | collective-permute-start | bytes 1671176 | tf_op jit(solution)/shard_map/ppermute | solution.py:180
  67.9 26.3 %collective-permute-start.23 = (bf16[272,1024]{1,0:T(8,128)(2,1)S(1)}, bf16[272,1024]{1,0:T(8,128)(2,1)S(1)}, u32[]{:S(2)}, u32[]{:S(2)}) collective-permute-start(bf16[272,1024]{1,0:T(8,128)(2,1)S(1)} %collective-permute-done.5.refs_29_), channel_id=1, source_target_pairs={{3,0},{0,1},{1,2},{2,3},{7,4},{4,5},{5,6},{6,7},{11,8},{8,9},{9,10... | collective-permute-start | bytes 1671176 | tf_op jit(solution)/shard_map/ppermute | solution.py:180
  67.9 12.5 %collective-permute-start.20 = (bf16[256,1024]{1,0:T(8,128)(2,1)S(1)}, bf16[256,1024]{1,0:T(8,128)(2,1)}, u32[]{:S(2)}, u32[]{:S(2)}) collective-permute-start(bf16[256,1024]{1,0:T(8,128)(2,1)S(1)} %collective-permute-done.2.refs_10_), channel_id=1, source_target_pairs={{24,0},{0,8},{8,16},{16,24},{25,1},{1,9},{9,17},{17,25},{26,2},{2,... | collective-permute-start | bytes 1572872 | tf_op jit(solution)/shard_map/ppermute | solution.py:180
  76.8 19.1 %copy-start.21 = (bf16[256,1024]{1,0:T(8,128)(2,1)}, bf16[256,1024]{1,0:T(8,128)(2,1)S(1)}, u32[]{:S(2)}) copy-start(bf16[256,1024]{1,0:T(8,128)(2,1)S(1)} %collective-permute-done.17.refs_18_) | copy-start | bytes 1572868
  76.8 16.1 %collective-permute-start.18 = (bf16[256,1024]{1,0:T(8,128)(2,1)S(1)}, bf16[256,1024]{1,0:T(8,128)(2,1)S(1)}, u32[]{:S(2)}, u32[]{:S(2)}) collective-permute-start(bf16[256,1024]{1,0:T(8,128)(2,1)S(1)} %collective-permute-done.7.refs_8_), channel_id=1, source_target_pairs={{24,0},{0,8},{8,16},{16,24},{25,1},{1,9},{9,17},{17,25},{26,2},{2,... | collective-permute-start | bytes 1572872 | tf_op jit(solution)/shard_map/ppermute | solution.py:180
  77.2 18.5 %collective-permute-start.22 = (bf16[256,1024]{1,0:T(8,128)(2,1)S(1)}, bf16[256,1024]{1,0:T(8,128)(2,1)S(1)}, u32[]{:S(2)}, u32[]{:S(2)}) collective-permute-start(bf16[256,1024]{1,0:T(8,128)(2,1)S(1)} %collective-permute-done.7.refs_8_), channel_id=1, source_target_pairs={{8,0},{16,8},{24,16},{0,24},{9,1},{17,9},{25,17},{1,25},{10,2},{18... | collective-permute-start | bytes 1572872 | tf_op jit(solution)/shard_map/ppermute | solution.py:180
  80.4 22.4 %collective-permute-start.24 = (bf16[272,1024]{1,0:T(8,128)(2,1)}, bf16[272,1024]{1,0:T(8,128)(2,1)S(1)}, u32[]{:S(2)}, u32[]{:S(2)}) collective-permute-start(bf16[272,1024]{1,0:T(8,128)(2,1)} %collective-permute-done.13.refs_19_), channel_id=1, source_target_pairs={{1,0},{2,1},{3,2},{0,3},{5,4},{6,5},{7,6},{4,7},{9,8},{10,9},{11,1... | collective-permute-start | bytes 1671176 | tf_op jit(solution)/shard_map/ppermute | solution.py:180
  81.8 22.6 %collective-permute-start.16 = (bf16[272,1024]{1,0:T(8,128)(2,1)}, bf16[272,1024]{1,0:T(8,128)(2,1)S(1)}, u32[]{:S(2)}, u32[]{:S(2)}) collective-permute-start(bf16[272,1024]{1,0:T(8,128)(2,1)} %collective-permute-done.13.refs_19_), channel_id=1, source_target_pairs={{3,0},{0,1},{1,2},{2,3},{7,4},{4,5},{5,6},{6,7},{11,8},{8,9},{9,10... | collective-permute-start | bytes 1671176 | tf_op jit(solution)/shard_map/ppermute | solution.py:180
  92.8 23.7 %copy-start.5 = (bf16[256,1024]{1,0:T(8,128)(2,1)}, bf16[256,1024]{1,0:T(8,128)(2,1)S(1)}, u32[]{:S(2)}) copy-start(bf16[256,1024]{1,0:T(8,128)(2,1)S(1)} %collective-permute-done.18.refs_34_) | copy-start | bytes 1572868
  92.9 15.0 %collective-permute-start.19 = (bf16[272,1024]{1,0:T(8,128)(2,1)}, bf16[272,1024]{1,0:T(8,128)(2,1)}, u32[]{:S(2)}, u32[]{:S(2)}) collective-permute-start(bf16[272,1024]{1,0:T(8,128)(2,1)} %collective-permute-done.11.refs_13_), channel_id=1, source_target_pairs={{1,0},{2,1},{3,2},{0,3},{5,4},{6,5},{7,6},{4,7},{9,8},{10,9},{11,1... | collective-permute-start | bytes 1671176 | tf_op jit(solution)/shard_map/ppermute | solution.py:180
  94.2 8.6 %collective-permute-start.25 = (bf16[256,1024]{1,0:T(8,128)(2,1)}, bf16[256,1024]{1,0:T(8,128)(2,1)}, u32[]{:S(2)}, u32[]{:S(2)}) collective-permute-start(bf16[256,1024]{1,0:T(8,128)(2,1)} %collective-permute-done.12.refs_14_), channel_id=1, source_target_pairs={{8,0},{16,8},{24,16},{0,24},{9,1},{17,9},{25,17},{1,25},{10,2},{18... | collective-permute-start | bytes 1572872 | tf_op jit(solution)/shard_map/ppermute | solution.py:180
  95.8 20.8 %copy-start.6 = (bf16[256,1024]{1,0:T(8,128)(2,1)}, bf16[256,1024]{1,0:T(8,128)(2,1)S(1)}, u32[]{:S(2)}) copy-start(bf16[256,1024]{1,0:T(8,128)(2,1)S(1)} %collective-permute-done.22.refs_16_) | copy-start | bytes 1572868
  95.8 12.7 %collective-permute-start.26 = (bf16[256,1024]{1,0:T(8,128)(2,1)}, bf16[256,1024]{1,0:T(8,128)(2,1)}, u32[]{:S(2)}, u32[]{:S(2)}) collective-permute-start(bf16[256,1024]{1,0:T(8,128)(2,1)} %collective-permute-done.20.refs_36_), channel_id=1, source_target_pairs={{24,0},{0,8},{8,16},{16,24},{25,1},{1,9},{9,17},{17,25},{26,2},{2,... | collective-permute-start | bytes 1572872 | tf_op jit(solution)/shard_map/ppermute | solution.py:180
  102.8 11.3 %collective-permute-start.30 = (bf16[128,1024]{1,0:T(8,128)(2,1)}, bf16[128,1024]{1,0:T(8,128)(2,1)}, u32[]{:S(2)}, u32[]{:S(2)}) collective-permute-start(bf16[128,1024]{1,0:T(8,128)(2,1)} %slice.25), channel_id=1, source_target_pairs={{24,0},{0,8},{8,16},{16,24},{25,1},{1,9},{9,17},{17,25},{26,2},{2,... | collective-permute-start | bytes 786440 | tf_op jit(solution)/shard_map/ppermute | solution.py:180
  103.6 10.6 %collective-permute-start.31 = (bf16[272,1024]{1,0:T(8,128)(2,1)}, bf16[272,1024]{1,0:T(8,128)(2,1)}, u32[]{:S(2)}, u32[]{:S(2)}) collective-permute-start(bf16[272,1024]{1,0:T(8,128)(2,1)} %copy-done.14), channel_id=1, source_target_pairs={{3,0},{0,1},{1,2},{2,3},{7,4},{4,5},{5,6},{6,7},{11,8},{8,9},{9,10... | collective-permute-start | bytes 1671176 | tf_op jit(solution)/shard_map/ppermute | solution.py:180
  104.4 9.7 %collective-permute-start.29 = (bf16[128,1024]{1,0:T(8,128)(2,1)}, bf16[128,1024]{1,0:T(8,128)(2,1)}, u32[]{:S(2)}, u32[]{:S(2)}) collective-permute-start(bf16[128,1024]{1,0:T(8,128)(2,1)} %slice.27), channel_id=1, source_target_pairs={{8,0},{16,8},{24,16},{0,24},{9,1},{17,9},{25,17},{1,25},{10,2},{18... | collective-permute-start | bytes 786440 | tf_op jit(solution)/shard_map/ppermute | solution.py:180
  107.8 8.7 %collective-permute-start.28 = (bf16[144,1024]{1,0:T(8,128)(2,1)}, bf16[144,1024]{1,0:T(8,128)(2,1)S(1)}, u32[]{:S(2)}, u32[]{:S(2)}) collective-permute-start(bf16[144,1024]{1,0:T(8,128)(2,1)} %slice.31), channel_id=1, source_target_pairs={{3,0},{0,1},{1,2},{2,3},{7,4},{4,5},{5,6},{6,7},{11,8},{8,9},{9,10... | collective-permute-start | bytes 884744 | tf_op jit(solution)/shard_map/ppermute | solution.py:180
  108.5 8.1 %collective-permute-start.27 = (bf16[128,1024]{1,0:T(8,128)(2,1)}, bf16[128,1024]{1,0:T(8,128)(2,1)}, u32[]{:S(2)}, u32[]{:S(2)}) collective-permute-start(bf16[128,1024]{1,0:T(8,128)(2,1)} %slice.26), channel_id=1, source_target_pairs={{1,0},{2,1},{3,2},{0,3},{5,4},{6,5},{7,6},{4,7},{9,8},{10,9},{11,1... | collective-permute-start | bytes 786440 | tf_op jit(solution)/shard_map/ppermute | solution.py:180
  153.4 31.8 %all-to-all-start = ((f32[16,4,128]{2,1,0:T(4,128)}), f32[16,4,128]{2,1,0:T(4,128)S(1)}, u32[]{:S(2)}, u32[]{:S(2)}) async-start(f32[16,4,128]{2,1,0:T(4,128)} %bitcast.8), calls=%async_computation | async-start | bytes 65536 | tf_op jit(solution)/shard_map/all_to_all | solution.py:257
  (9 other events, 79.5 us)
Sparse Core Ops, SparseCore 0:
  10.7 102.0 all-gather.1
where the time goes:
time: 191 us; the launch traced here: 193 us
  starting transfers between devices  67.4 us (35%)
  waiting for transfers between devices  65.8 us (34%)
  Pallas kernels  24.3 us (13%)
  between operations  13.7 us (7%)
  blocking collectives  13.1 us (7%)
  local copies, waits for them, and re-layouts  5.04 us (3%)
  other arithmetic  3.29 us (2%)
    ppermute x32, waiting for transfers between devices, __call__(): lax.ppermute(value, axis, [((i + by) % size, i) for i in range(size)])  56.1 us
    ppermute x32, starting transfers between devices, __call__(): lax.ppermute(value, axis, [((i + by) % size, i) for i in range(size)])  43 us
    all_to_all x1, starting transfers between devices, local(): lax.all_to_all(left_best.reshape(16, BLOCKS, ROWS), ('z', 'c'), 0, 0, til...  24.4 us
    pallas_call x1, Pallas kernels, pair_maxima(): pl.pallas_call(kernel, out_shape=(jax.ShapeDtypeStruct((64, ROWS), jnp.fl...  23 us
    all_to_all x1, blocking collectives, local(): lax.all_to_all(right_best.reshape(16, BLOCKS, ROWS), ('x', 'y'), 0, 0, ti...  13.1 us
    all_to_all x1, waiting for transfers between devices, local(): lax.all_to_all(left_best.reshape(16, BLOCKS, ROWS), ('z', 'c'), 0, 0, til...  7.36 us
  transfers between devices with their start and end apart: 34, of which 10 were waited for; matrix products, arithmetic and copies ran while one was open for 2% of the time, Pallas kernels for 0%

commit v1 on v0

v1 whole, which is shorter than its diff:
```python
import jax
import jax.numpy as jnp
from jax import lax
from jax.experimental import pallas as pl
from jax.experimental.pallas import tpu as pltpu
from jax.sharding import Mesh, PartitionSpec as P

epsilon = 1e-06
ROWS = 128
BLOCKS = 4
META = 16
HALF1 = 2 * ROWS + META
HALF2 = 2 * ROWS
FULL = HALF1 + HALF2
SLOTS = 8
DEPTH = 5
VMEM_LIMIT = 32 * 1024 * 1024


def unit_kernel(emb_ref, meta_ref, unit_ref, full_ref):
    for block in range(BLOCKS):
        rows = emb_ref[block].astype(jnp.float32)
        scale = lax.rsqrt(jnp.sum(rows * rows, axis=-1, keepdims=True) + epsilon)
        unit = (rows * scale).astype(jnp.bfloat16)
        unit_ref[block * ROWS : (block + 1) * ROWS, :] = unit
        at = block * ROWS + (META if block >= 2 else 0)
        full_ref[at : at + ROWS, :] = unit
    full_ref[2 * ROWS : HALF1, :] = meta_ref[...]


def pair_kernel(right_at, meta_at, todo, first, place, left_tags, left_ref, *rest):
    refs = rest[:-10]
    left_out, right_out, left_buf, right_buf, right_meta, tags_buf, best_buf, left_best, left_sems, right_sems = rest[-10:]

    def fetch_right(j):
        for dy in range(4):
            ref, base = right_at[j // 4 * 4 + dy][j % 4]
            pltpu.make_async_copy(
                refs[ref].at[pl.ds(base, ROWS), :], right_buf.at[j, pl.ds(dy * ROWS, ROWS), :], right_sems.at[j]
            ).start()

    for k in range(16):
        ref, row = meta_at[k]
        pltpu.make_async_copy(refs[ref].at[pl.ds(row, META), :], right_meta.at[k], right_sems.at[16]).start()
    for j in range(4):
        fetch_right(j)

    count = first[16]

    def each_left(i, act):
        slot = lax.rem(i, SLOTS)
        for h in range(2):
            unit = todo[2 * i + h]
            into = left_buf.at[slot, pl.ds(h * ROWS, ROWS), :]

            @pl.when(unit < 64)
            def _():
                row = pl.multiple_of(unit * ROWS, ROWS)
                act(pltpu.make_async_copy(left_ref.at[pl.ds(row, ROWS), :], into, left_sems.at[slot, h]))

    def fetch_left(i):
        each_left(i, lambda copy: copy.start())

    def early(i, carry):
        fetch_left(i)
        return carry

    lax.fori_loop(0, jnp.minimum(count, SLOTS), early, 0)
    for j in range(4, 16):
        fetch_right(j)
    left_best[...] = jnp.full(left_best.shape, -1.0, jnp.float32)
    pltpu.make_async_copy(right_meta, right_meta, right_sems.at[16]).wait()

    row_ids = lax.broadcasted_iota(jnp.int32, (ROWS, ROWS), 0)
    col_ids = lax.broadcasted_iota(jnp.int32, (ROWS, ROWS), 1)
    my_z, my_x, my_c, my_y = place[0], place[1], place[2], place[3]
    me = my_z * 2 + my_c

    for j in range(16):
        dx, b = j // 4, j % 4
        for dy in range(4):
            row = right_meta[dx * 4 + dy, 0:1, b * ROWS : (b + 1) * ROWS].astype(jnp.float32)
            row = jnp.where(row < 0.0, -2.0, row)
            tags_buf[dy * ROWS : (dy + 1) * ROWS, :] = jnp.broadcast_to(row, (ROWS, ROWS)).T
        best_buf[...] = jnp.full(best_buf.shape, -1.0, jnp.float32)
        pltpu.make_async_copy(right_buf.at[j], right_buf.at[j], right_sems.at[j]).wait()

        def step(i, carry):
            each_left(i, lambda copy: copy.wait())
            scores = lax.dot_general(
                right_buf[j], left_buf[lax.rem(i, SLOTS)], (((1,), (1,)), ((), ())), preferred_element_type=jnp.float32
            )
            for h in range(2):
                unit = todo[2 * i + h]
                tags = left_tags[pl.ds(unit, 1), :]
                top = None
                for dy in range(4):
                    part = slice(dy * ROWS, (dy + 1) * ROWS)
                    keep = tags_buf[part, :] == tags
                    if dx == 0 and dy == 0:
                        keep = keep & ((row_ids != col_ids) | (unit != me * 4 + b))
                    masked = jnp.where(keep, scores[part, h * ROWS : (h + 1) * ROWS], -1.0)
                    best_buf[part, :] = jnp.maximum(best_buf[part, :], masked)
                    top = masked if top is None else jnp.maximum(top, masked)
                top = jnp.max(top, axis=0, keepdims=True)
                left_best[pl.ds(unit, 1), :] = jnp.maximum(left_best[pl.ds(unit, 1), :], top)

            @pl.when(i + SLOTS < count)
            def _():
                fetch_left(i + SLOTS)

            return carry

        lax.fori_loop(first[j], first[j + 1], step, 0)
        right_x = lax.rem(my_x + dx, 4)
        for dy in range(4):
            row = (right_x * 4 + lax.rem(my_y + dy, 4)) * 4 + b
            right_out[pl.ds(row, 1), :] = jnp.max(best_buf[dy * ROWS : (dy + 1) * ROWS, :].T, axis=0, keepdims=True)
    left_out[...] = left_best[0:64, :]


def pair_maxima(todo, first, place, left_tags, left_rows, operands, right_at, meta_at):
    def kernel(*refs):
        pair_kernel(right_at, meta_at, *refs)

    smem, vmem, hbm = (pl.BlockSpec(memory_space=s) for s in (pltpu.SMEM, pltpu.VMEM, pltpu.HBM))
    return pl.pallas_call(
        kernel,
        out_shape=(jax.ShapeDtypeStruct((64, ROWS), jnp.float32),) * 2,
        in_specs=[smem, smem, smem, vmem] + [hbm] * (len(operands) + 1),
        out_specs=(vmem, vmem),
        scratch_shapes=[
            pltpu.VMEM((SLOTS, 2 * ROWS, 1024), jnp.bfloat16),
            pltpu.VMEM((16, 4 * ROWS, 1024), jnp.bfloat16),
            pltpu.VMEM((16, META, 1024), jnp.bfloat16),
            pltpu.VMEM((4 * ROWS, ROWS), jnp.float32),
            pltpu.VMEM((4 * ROWS, ROWS), jnp.float32),
            pltpu.VMEM((72, ROWS), jnp.float32),
            pltpu.SemaphoreType.DMA((SLOTS, 2)),
            pltpu.SemaphoreType.DMA((17,)),
        ],
        compiler_params=pltpu.CompilerParams(vmem_limit_bytes=VMEM_LIMIT),
        name="pair_maxima",
    )(todo, first, place, left_tags, *(pltpu.with_memory_space_constraint(v, pltpu.HBM) for v in (left_rows, *operands)))


class Carrier:
    def __init__(self):
        self.sent = []

    def __call__(self, value, axis, by):
        if len(self.sent) >= DEPTH:
            k = len(self.sent) - DEPTH
            value, self.sent[k][0] = lax.optimization_barrier((value, self.sent[k][0]))
        size = lax.axis_size(axis)
        cell = [lax.ppermute(value, axis, [((i + by) % size, i) for i in range(size)])]
        self.sent.append(cell)
        return cell


def gather_plane(own, extra):
    send = Carrier()
    xp, xm, yp, ym = ("x", 1), ("x", -1), ("y", 1), ("y", -1)
    whole = {(0, 0): [own]}
    whole[0, 1], whole[0, 3] = send(own, *yp), send(own, *ym)
    whole[1, 0], whole[3, 0] = send(own, *xp), send(own, *xm)
    whole[0, 1][0], extra = lax.optimization_barrier((whole[0, 1][0], extra))
    whole[1, 1] = send(whole[0, 1][0], *xp)
    whole[3, 3] = send(whole[0, 3][0], *xm)
    whole[3, 1] = send(whole[3, 0][0], *yp)
    whole[1, 3] = send(whole[1, 0][0], *ym)
    half = {}
    half["y", 0] = send(whole[0, 1][0][:HALF1], *yp)
    half["y", 1] = send(whole[0, 3][0][HALF1:], *ym)
    half["x", 0] = send(whole[1, 0][0][:HALF1], *xp)
    half["x", 1] = send(whole[3, 0][0][HALF1:], *xm)
    whole[1, 2] = send(whole[1, 1][0], *yp)
    whole[3, 2] = send(whole[3, 3][0], *ym)
    whole[2, 3] = send(whole[1, 3][0], *xp)
    whole[2, 1] = send(whole[3, 1][0], *xm)
    last = [
        send(whole[1, 2][0][:ROWS], *xp),
        send(whole[3, 2][0][ROWS:HALF1], *xm),
        send(whole[2, 3][0][HALF1 : HALF1 + ROWS], *ym),
        send(whole[2, 1][0][HALF1 + ROWS :], *yp),
    ]
    starts = (0, ROWS, HALF1, HALF1 + ROWS)
    parts = {key: [(v[0], at) for at in starts] for key, v in whole.items()}
    metas = {key: (v[0], 2 * ROWS) for key, v in whole.items()}
    for key, axis in (((2, 0), "x"), ((0, 2), "y")):
        h1, h2 = half[axis, 0][0], half[axis, 1][0]
        parts[key] = [(h1, 0), (h1, ROWS), (h2, 0), (h2, ROWS)]
        metas[key] = (h1, 2 * ROWS)
    parts[2, 2] = [(v[0], 0) for v in last]
    metas[2, 2] = (last[1][0], ROWS)
    return parts, metas, extra


def local(embeddings, cluster_ids, valid, pair_left, pair_right):
    my_z, my_x, my_c, my_y = (lax.axis_index(name) for name in ("z", "x", "c", "y"))
    place = jnp.stack([my_z, my_x, my_c, my_y]).astype(jnp.int32)
    labels = jnp.where(valid > 0, cluster_ids, -1).reshape(1, -1)
    lists = jnp.concatenate([labels, (pair_left % BLOCKS)[None], pair_right[None]], axis=1)
    meta = jnp.pad(lists.astype(jnp.bfloat16), ((0, META - 1), (0, 1024 - lists.shape[1])))
    unit, full = pl.pallas_call(
        unit_kernel,
        out_shape=[jax.ShapeDtypeStruct((n, 1024), jnp.bfloat16) for n in (4 * ROWS, FULL)],
        compiler_params=pltpu.CompilerParams(vmem_limit_bytes=VMEM_LIMIT),
        name="unit_rows",
    )(embeddings, meta)
    unit, lists = lax.optimization_barrier((unit, lists))
    left_rows = lax.all_gather(unit, ("z", "c"), axis=0, tiled=True)
    left_lists = lax.all_to_all(jnp.broadcast_to(lists, (16, lists.shape[1])), ("z", "c"), 0, 0, tiled=True)
    parts, metas, left_lists = gather_plane(full, left_lists)

    left_tags = left_lists[:, :512].astype(jnp.float32).reshape(64, ROWS)
    a, b = left_lists[:, 512:544], left_lists[:, 544:]
    group = b // BLOCKS
    mine = (group // 8 == my_z) & (group % 2 == my_c)
    dx = ((group // 2) % 4 - my_x) % 4
    unit_of = (jnp.arange(16)[:, None] * BLOCKS + a)[:, :, None]
    block = jnp.where(mine, dx * BLOCKS + b % BLOCKS, -1)
    unit_of = jnp.max(jnp.where(block[:, :, None] == jnp.arange(16), unit_of + 1, 0), axis=1).T.reshape(256)
    listed = (unit_of > 0).reshape(16, 16)
    order = jnp.arange(16)
    rank = jnp.sum(listed[:, None, :] & (order[None, None, :] < order[None, :, None]), axis=2)
    steps = (jnp.sum(listed, axis=1) + 1) // 2
    first = jnp.sum(jnp.where(order[None, :] < jnp.arange(17)[:, None], steps[None, :], 0), axis=1)
    at = jnp.where(listed, 2 * first[:16, None] + rank, -1).reshape(256)
    todo = jnp.max(jnp.where(at == jnp.arange(80)[:, None], unit_of, 0), axis=1)
    todo = jnp.where(todo > 0, todo - 1, 64)
    left_tags = jnp.pad(left_tags, ((0, 8), (0, 0)), constant_values=-3.0)

    operands, known, right_at, meta_at = [], {}, [], []

    def place_of(value):
        if id(value) not in known:
            known[id(value)] = len(operands)
            operands.append(value)
        return known[id(value)]

    for k in [(dx, dy) for dx in range(4) for dy in range(4)]:
        right_at.append([(place_of(value), base) for value, base in parts[k]])
        meta_at.append((place_of(metas[k][0]), metas[k][1]))
    left_best, right_best = pair_maxima(todo, first, place, left_tags, left_rows, operands, right_at, meta_at)
    from_left = lax.all_to_all(left_best.reshape(16, BLOCKS, ROWS), ("z", "c"), 0, 0, tiled=True)
    from_right = lax.all_to_all(right_best.reshape(16, BLOCKS, ROWS), ("x", "y"), 0, 0, tiled=True)
    return jnp.maximum(jnp.max(from_left, axis=0), jnp.max(from_right, axis=0))


def solution(mesh):
    wide = Mesh(mesh.devices.reshape(8, 4, 2, 4), ("z", "x", "c", "y"))
    dp = ("z", "x", "c")
    placed = (P(dp, "y", None), P(dp, "y"), P(dp, "y"), P(dp), P(dp))
    return jax.shard_map(local, mesh=wide, in_specs=placed, out_specs=P(dp, "y"), check_vma=False)
```

time: 191 us -> 191 us (level)
  starting transfers between devices: 67.4 us -> 41.8 us
  blocking collectives: 13.1 us -> 30.2 us
  waiting for transfers between devices: 65.8 us -> 73.2 us
  Pallas kernels: 24.3 us -> 16.9 us
  local copies, waits for them, and re-layouts: 5.04 us -> 11.4 us
    ppermute x32 -> x20, starting transfers between devices: 43 us -> 22.9 us  [__call__(): lax.ppermute(value, axis, [((i + by) % size, i) for i in range(size)])]
    all_to_all x0 -> x1, blocking collectives: none -> 17.1 us  [local(): lax.all_to_all(jnp.broadcast_to(lists, (16, lists.shape[1])), ('z', 'c'),...]
    ppermute x32 -> x20, waiting for transfers between devices: 56.1 us -> 65.8 us  [__call__(): lax.ppermute(value, axis, [((i + by) % size, i) for i in range(size)])]
    pallas_call x1, Pallas kernels: 23 us -> 15.5 us  [pair_maxima(): pl.pallas_call(kernel, out_shape=(jax.ShapeDtypeStruct((64, ROWS), jnp.fl...]
    slice x4 -> x8, local copies, waits for them, and re-layouts: 2.9 us -> 9.69 us  [the longest x1 1.92 us: gather_plane(): half['x', 1] = send(whole[3, 0][0][HALF1:], *xm)]
    all_to_all x1, starting transfers between devices: 24.4 us -> 18.8 us  [local(): lax.all_to_all(left_best.reshape(16, BLOCKS, ROWS), ('z', 'c'), 0, 0, til...]
    all_gather x1, waiting for transfers between devices: 2.29 us -> 0.01 us  [local(): left_rows = lax.all_gather(unit, ('z', 'c'), axis=0, tiled=True)]
  transfers between devices with their start and end apart: 34 -> 22, of which waited for: 10 -> 9; matrix products, arithmetic and copies ran while one was open for 2% -> 6% of each run, Pallas kernels for 0% -> 0%
where the time goes in v1:
time: 191 us
  waiting for transfers between devices  73.2 us (38%)
  starting transfers between devices  41.8 us (22%)
  blocking collectives  30.2 us (16%)
  Pallas kernels  16.9 us (9%)
  between operations  13.6 us (7%)
  local copies, waits for them, and re-layouts  11.4 us (6%)
  other arithmetic  3.88 us (2%)
    ppermute x20, waiting for transfers between devices, __call__(): lax.ppermute(value, axis, [((i + by) % size, i) for i in range(size)])  65.8 us
    ppermute x20, starting transfers between devices, __call__(): lax.ppermute(value, axis, [((i + by) % size, i) for i in range(size)])  22.9 us
    all_to_all x1, starting transfers between devices, local(): lax.all_to_all(left_best.reshape(16, BLOCKS, ROWS), ('z', 'c'), 0, 0, til...  18.8 us
    all_to_all x1, blocking collectives, local(): lax.all_to_all(jnp.broadcast_to(lists, (16, lists.shape[1])), ('z', 'c'),...  17.1 us
    pallas_call x1, Pallas kernels, pair_maxima(): pl.pallas_call(kernel, out_shape=(jax.ShapeDtypeStruct((64, ROWS), jnp.fl...  15.5 us
    all_to_all x1, blocking collectives, local(): lax.all_to_all(right_best.reshape(16, BLOCKS, ROWS), ('x', 'y'), 0, 0, ti...  13.1 us
    all_to_all x1, waiting for transfers between devices, local(): lax.all_to_all(left_best.reshape(16, BLOCKS, ROWS), ('z', 'c'), 0, 0, til...  7.36 us
  transfers between devices with their start and end apart: 22, of which 9 were waited for; matrix products, arithmetic and copies ran while one was open for 6% of the time, Pallas kernels for 0%

profile of v1, /device:TPU:1, one launch (start us, length us, event | category | flops | bytes accessed | tf_op | source)
XLA Modules:
  0.0 190.9 jit_solution(935339293956592111)
XLA Ops:
  6.5 0.7 fusion.13
  7.2 0.7 compare_select_fusion.3
  7.9 0.7 fusion.15
  8.7 1.2 copy-done.1
  9.9 1.3 unit_rows.1
  11.2 3.6 %collective-permute-start = (bf16[528,1024]{1,0:T(8,128)(2,1)S(1)}, bf16[528,1024]{1,0:T(8,128)(2,1)S(1)}, u32[]{:S(2)}, u32[]{:S(2)}) collective-permute-start(bf16[528,1024]{1,0:T(8,128)(2,1)S(1)} %get-tuple-element.43.refs_5_), channel_id=1, source_target_pairs={{1,0},{2,1},{3,2},{0,3},{5,4},{6,5},{7,6},{4,7},{9,8},{10,9},{11,1... | collective-permute-start | bytes 3244040 | tf_op jit(solution)/shard_map/ppermute | solution.py:156
  14.9 2.5 %collective-permute-start.2 = (bf16[528,1024]{1,0:T(8,128)(2,1)S(1)}, bf16[528,1024]{1,0:T(8,128)(2,1)S(1)}, u32[]{:S(2)}, u32[]{:S(2)}) collective-permute-start(bf16[528,1024]{1,0:T(8,128)(2,1)S(1)} %get-tuple-element.43.refs_5_), channel_id=1, source_target_pairs={{8,0},{16,8},{24,16},{0,24},{9,1},{17,9},{25,17},{1,25},{10,2},{18... | collective-permute-start | bytes 3244040 | tf_op jit(solution)/shard_map/ppermute | solution.py:156
  17.4 17.1 %all_to_all.19 = s32[16,1,576]{2,1,0:T(1,128)S(1)} all-to-all(s32[16,1,576]{2,1,0:T(1,128)S(1)} %broadcast_in_dim.65), channel_id=1, replica_groups=mesh['z'=8,'x'=4,'c'=2,'y'=4] {'z','c'}, dimensions={0} | all-to-all | bytes 73728 | tf_op jit(solution)/shard_map/all_to_all | solution.py:213
  34.5 2.9 %collective-permute-done.refs_6_ = bf16[528,1024]{1,0:T(8,128)(2,1)S(1)} collective-permute-done((bf16[528,1024]{1,0:T(8,128)(2,1)S(1)}, bf16[528,1024]{1,0:T(8,128)(2,1)S(1)}, u32[]{:S(2)}, u32[]{:S(2)}) %collective-permute-start) | collective-permute-done | bytes 1081376 | tf_op jit(solution)/shard_map/ppermute | solution.py:156
  37.4 3.2 %collective-permute-done.1.refs_9_ = bf16[528,1024]{1,0:T(8,128)(2,1)} collective-permute-done((bf16[528,1024]{1,0:T(8,128)(2,1)S(1)}, bf16[528,1024]{1,0:T(8,128)(2,1)}, u32[]{:S(2)}, u32[]{:S(2)}) %collective-permute-start.1) | collective-permute-done | bytes 1081376 | tf_op jit(solution)/shard_map/ppermute | solution.py:156
  40.6 1.2 collective-permute-start.3
  41.8 1.5 collective-permute-start.6
  43.3 2.7 %collective-permute-start.11 = (bf16[528,1024]{1,0:T(8,128)(2,1)}, bf16[528,1024]{1,0:T(8,128)(2,1)}, u32[]{:S(2)}, u32[]{:S(2)}) collective-permute-start(bf16[528,1024]{1,0:T(8,128)(2,1)} %collective-permute-done.4.refs_22_), channel_id=1, source_target_pairs={{1,0},{2,1},{3,2},{0,3},{5,4},{6,5},{7,6},{4,7},{9,8},{10,9},{11,1... | collective-permute-start | bytes 3244040 | tf_op jit(solution)/shard_map/ppermute | solution.py:156
  46.0 0.1 pad_add_fusion.1.refs_2_
  46.1 0.8 slice.40
  46.9 0.9 slice.41
  47.8 1.9 slice.42
  49.7 15.9 %collective-permute-done.3.refs_25_ = bf16[528,1024]{1,0:T(8,128)(2,1)} collective-permute-done((bf16[528,1024]{1,0:T(8,128)(2,1)}, bf16[528,1024]{1,0:T(8,128)(2,1)}, u32[]{:S(2)}, u32[]{:S(2)}) %collective-permute-start.3) | collective-permute-done | bytes 1081376 | tf_op jit(solution)/shard_map/ppermute | solution.py:156
  65.6 0.7 collective-permute-start.8
  66.3 1.5 collective-permute-start.12
  67.8 0.1 fusion.8
  67.9 0.3 select_reduce_fusion
  68.3 0.1 reshape.115
  68.4 0.1 copy.7
  68.5 1.9 %slice.44 = bf16[256,1024]{1,0:T(8,128)(2,1)} slice(bf16[528,1024]{1,0:T(8,128)(2,1)} %collective-permute-done.4.refs_22_), slice={[272:528], [0:1024]} | slice | bytes 1048576 | tf_op jit(solution)/shard_map/slice | solution.py:176
  70.5 8.1 %collective-permute-done.5.refs_7_ = bf16[272,1024]{1,0:T(8,128)(2,1)S(1)} collective-permute-done((bf16[272,1024]{1,0:T(8,128)(2,1)}, bf16[272,1024]{1,0:T(8,128)(2,1)S(1)}, u32[]{:S(2)}, u32[]{:S(2)}) %collective-permute-start.5) | collective-permute-done | bytes 557088 | tf_op jit(solution)/shard_map/ppermute | solution.py:156
  78.6 2.7 %collective-permute-start.10 = (bf16[528,1024]{1,0:T(8,128)(2,1)}, bf16[528,1024]{1,0:T(8,128)(2,1)S(1)}, u32[]{:S(2)}, u32[]{:S(2)}) collective-permute-start(bf16[528,1024]{1,0:T(8,128)(2,1)} %collective-permute-done.6.refs_11_), channel_id=1, source_target_pairs={{1,0},{2,1},{3,2},{0,3},{5,4},{6,5},{7,6},{4,7},{9,8},{10,9},{11,1... | collective-permute-start | bytes 3244040 | tf_op jit(solution)/shard_map/ppermute | solution.py:156
  81.3 2.2 %collective-permute-start.17 = (bf16[528,1024]{1,0:T(8,128)(2,1)}, bf16[528,1024]{1,0:T(8,128)(2,1)}, u32[]{:S(2)}, u32[]{:S(2)}) collective-permute-start(bf16[528,1024]{1,0:T(8,128)(2,1)} %collective-permute-done.7.refs_13_), channel_id=1, source_target_pairs={{8,0},{16,8},{24,16},{0,24},{9,1},{17,9},{25,17},{1,25},{10,2},{18... | collective-permute-start | bytes 3244040 | tf_op jit(solution)/shard_map/ppermute | solution.py:156
  83.5 0.1 select_reduce_fusion.2.refs_1_
  83.6 0.3 collective-permute-start.13
  83.8 0.3 convert_reduce_fusion
  84.3 0.1 copy.9
  84.3 0.1 eq.54
  84.4 16.9 %collective-permute-done.9.refs_24_ = bf16[528,1024]{1,0:T(8,128)(2,1)S(1)} collective-permute-done((bf16[528,1024]{1,0:T(8,128)(2,1)}, bf16[528,1024]{1,0:T(8,128)(2,1)S(1)}, u32[]{:S(2)}, u32[]{:S(2)}) %collective-permute-start.9) | collective-permute-done | bytes 1081376 | tf_op jit(solution)/shard_map/ppermute | solution.py:156
  101.4 0.8 slice.49
  102.2 15.3 %collective-permute-done.13.refs_15_ = bf16[256,1024]{1,0:T(8,128)(2,1)} collective-permute-done((bf16[256,1024]{1,0:T(8,128)(2,1)}, bf16[256,1024]{1,0:T(8,128)(2,1)}, u32[]{:S(2)}, u32[]{:S(2)}) %collective-permute-start.13) | collective-permute-done | bytes 524320 | tf_op jit(solution)/shard_map/ppermute | solution.py:156
  117.5 1.5 collective-permute-start.16
  119.0 1.7 slice.50
  120.6 1.7 slice.51
  122.3 2.7 %collective-permute-start.19 = (bf16[128,1024]{1,0:T(8,128)(2,1)}, bf16[128,1024]{1,0:T(8,128)(2,1)}, u32[]{:S(2)}, u32[]{:S(2)}) collective-permute-start(bf16[128,1024]{1,0:T(8,128)(2,1)} %slice.51), channel_id=1, source_target_pairs={{1,0},{2,1},{3,2},{0,3},{5,4},{6,5},{7,6},{4,7},{9,8},{10,9},{11,1... | collective-permute-start | bytes 786440 | tf_op jit(solution)/shard_map/ppermute | solution.py:156
  125.0 0.1 select_reduce_fusion.1
  125.1 2.2 %collective-permute-done.18.refs_19_ = bf16[128,1024]{1,0:T(8,128)(2,1)} collective-permute-done((bf16[128,1024]{1,0:T(8,128)(2,1)}, bf16[128,1024]{1,0:T(8,128)(2,1)}, u32[]{:S(2)}, u32[]{:S(2)}) %collective-permute-start.18) | collective-permute-done | bytes 262176 | tf_op jit(solution)/shard_map/ppermute | solution.py:156
  127.4 1.2 collective-permute-done.19.refs_20_
  128.6 15.5 %pair_maxima.1 = (f32[64,128]{1,0:T(8,128)}, f32[64,128]{1,0:T(8,128)S(1)}) custom-call(s32[80]{0:T(128)S(1)} %compare_select_fusion.2.refs_0_, s32[17]{0:T(128)S(1)} %select_reduce_fusion.2.refs_1_, s32[4]{0:T(128)S(1)} %pad_add_fusion.1.refs_2_, f32[72,128]{1,0:T(8,128)S(1)} %pad.9.refs_3_, bf16[8192,1024]{1,0:T(8,128)(2,1)} %all-gather.2.cloned.1.call-done.refs_4_, ...), custom_call_target="tpu_custom_call" | custom-call | tf_op jit(solution)/shard_map/pair_maxima/pallas_call | solution.py:127
  144.2 13.1 %all_to_all.20 = f32[16,4,128]{2,1,0:T(4,128)S(1)} all-to-all(f32[16,4,128]{2,1,0:T(4,128)S(1)} %bitcast.16), channel_id=1, replica_groups=mesh['z'=8,'x'=4,'c'=2,'y'=4] {'x','y'}, dimensions={0} | all-to-all | bytes 65536 | tf_op jit(solution)/shard_map/all_to_all | solution.py:247
  157.3 18.8 %all-to-all-start.1 = ((f32[16,4,128]{2,1,0:T(4,128)}), f32[16,4,128]{2,1,0:T(4,128)S(1)}, u32[]{:S(2)}, u32[]{:S(2)}) async-start(f32[16,4,128]{2,1,0:T(4,128)} %bitcast.8), calls=%async_computation.1 | async-start | bytes 65536 | tf_op jit(solution)/shard_map/all_to_all | solution.py:246
  176.1 7.4 %all-to-all-done.1 = f32[16,4,128]{2,1,0:T(4,128)S(1)} async-done(((f32[16,4,128]{2,1,0:T(4,128)}), f32[16,4,128]{2,1,0:T(4,128)S(1)}, u32[]{:S(2)}, u32[]{:S(2)}) %all-to-all-start.1) | async-done | bytes 32800 | tf_op jit(solution)/shard_map/all_to_all | solution.py:246
  183.5 0.6 max.3
  (57 shorter events, 0.4 us)
Async XLA Ops:
  6.5 122.1 %all-gather.2.cloned.1.call-start = ((), (), s32[]{:S(2)}) async-start(), calls=%async_computation.3 | async-start | bytes 17825792 | tf_op jit(solution)/shard_map/all_gather | solution.py:212
  8.6 1.2 copy-start.1
  11.2 35.7 %copy-start = (bf16[528,1024]{1,0:T(8,128)(2,1)}, bf16[528,1024]{1,0:T(8,128)(2,1)S(1)}, u32[]{:S(2)}) copy-start(bf16[528,1024]{1,0:T(8,128)(2,1)S(1)} %get-tuple-element.43.refs_5_) | copy-start | bytes 3244036
  11.2 26.2 %collective-permute-start = (bf16[528,1024]{1,0:T(8,128)(2,1)S(1)}, bf16[528,1024]{1,0:T(8,128)(2,1)S(1)}, u32[]{:S(2)}, u32[]{:S(2)}) collective-permute-start(bf16[528,1024]{1,0:T(8,128)(2,1)S(1)} %get-tuple-element.43.refs_5_), channel_id=1, source_target_pairs={{1,0},{2,1},{3,2},{0,3},{5,4},{6,5},{7,6},{4,7},{9,8},{10,9},{11,1... | collective-permute-start | bytes 3244040 | tf_op jit(solution)/shard_map/ppermute | solution.py:156
  14.9 25.7 %collective-permute-start.1 = (bf16[528,1024]{1,0:T(8,128)(2,1)S(1)}, bf16[528,1024]{1,0:T(8,128)(2,1)}, u32[]{:S(2)}, u32[]{:S(2)}) collective-permute-start(bf16[528,1024]{1,0:T(8,128)(2,1)S(1)} %get-tuple-element.43.refs_5_), channel_id=1, source_target_pairs={{3,0},{0,1},{1,2},{2,3},{7,4},{4,5},{5,6},{6,7},{11,8},{8,9},{9,10... | collective-permute-start | bytes 3244040 | tf_op jit(solution)/shard_map/ppermute | solution.py:156
  14.9 28.4 %collective-permute-start.2 = (bf16[528,1024]{1,0:T(8,128)(2,1)S(1)}, bf16[528,1024]{1,0:T(8,128)(2,1)S(1)}, u32[]{:S(2)}, u32[]{:S(2)}) collective-permute-start(bf16[528,1024]{1,0:T(8,128)(2,1)S(1)} %get-tuple-element.43.refs_5_), channel_id=1, source_target_pairs={{8,0},{16,8},{24,16},{0,24},{9,1},{17,9},{25,17},{1,25},{10,2},{18... | collective-permute-start | bytes 3244040 | tf_op jit(solution)/shard_map/ppermute | solution.py:156
  17.4 25.9 %collective-permute-start.4 = (bf16[528,1024]{1,0:T(8,128)(2,1)S(1)}, bf16[528,1024]{1,0:T(8,128)(2,1)}, u32[]{:S(2)}, u32[]{:S(2)}) collective-permute-start(bf16[528,1024]{1,0:T(8,128)(2,1)S(1)} %get-tuple-element.43.refs_5_), channel_id=1, source_target_pairs={{24,0},{0,8},{8,16},{16,24},{25,1},{1,9},{9,17},{17,25},{26,2},{2,... | collective-permute-start | bytes 3244040 | tf_op jit(solution)/shard_map/ppermute | solution.py:156
  37.4 10.4 %copy-start.2 = (bf16[528,1024]{1,0:T(8,128)(2,1)}, bf16[528,1024]{1,0:T(8,128)(2,1)S(1)}, u32[]{:S(2)}) copy-start(bf16[528,1024]{1,0:T(8,128)(2,1)S(1)} %collective-permute-done.refs_6_) | copy-start | bytes 3244036
  40.6 25.0 %collective-permute-start.3 = (bf16[528,1024]{1,0:T(8,128)(2,1)}, bf16[528,1024]{1,0:T(8,128)(2,1)}, u32[]{:S(2)}, u32[]{:S(2)}) collective-permute-start(bf16[528,1024]{1,0:T(8,128)(2,1)} %collective-permute-done.1.refs_9_), channel_id=1, source_target_pairs={{24,0},{0,8},{8,16},{16,24},{25,1},{1,9},{9,17},{17,25},{26,2},{2,... | collective-permute-start | bytes 3244040 | tf_op jit(solution)/shard_map/ppermute | solution.py:156
  41.8 23.8 %collective-permute-start.6 = (bf16[528,1024]{1,0:T(8,128)(2,1)S(1)}, bf16[528,1024]{1,0:T(8,128)(2,1)}, u32[]{:S(2)}, u32[]{:S(2)}) collective-permute-start(bf16[528,1024]{1,0:T(8,128)(2,1)S(1)} %collective-permute-done.refs_6_), channel_id=1, source_target_pairs={{8,0},{16,8},{24,16},{0,24},{9,1},{17,9},{25,17},{1,25},{10,2},{18... | collective-permute-start | bytes 3244040 | tf_op jit(solution)/shard_map/ppermute | solution.py:156
  43.3 4.5 %copy-start.3 = (bf16[528,1024]{1,0:T(8,128)(2,1)}, bf16[528,1024]{1,0:T(8,128)(2,1)S(1)}, u32[]{:S(2)}) copy-start(bf16[528,1024]{1,0:T(8,128)(2,1)S(1)} %collective-permute-done.2.refs_10_) | copy-start | bytes 3244036
  43.3 35.3 %collective-permute-start.7 = (bf16[528,1024]{1,0:T(8,128)(2,1)S(1)}, bf16[528,1024]{1,0:T(8,128)(2,1)}, u32[]{:S(2)}, u32[]{:S(2)}) collective-permute-start(bf16[528,1024]{1,0:T(8,128)(2,1)S(1)} %collective-permute-done.2.refs_10_), channel_id=1, source_target_pairs={{3,0},{0,1},{1,2},{2,3},{7,4},{4,5},{5,6},{6,7},{11,8},{8,9},{9,10... | collective-permute-start | bytes 3244040 | tf_op jit(solution)/shard_map/ppermute | solution.py:156
  43.3 37.9 %collective-permute-start.11 = (bf16[528,1024]{1,0:T(8,128)(2,1)}, bf16[528,1024]{1,0:T(8,128)(2,1)}, u32[]{:S(2)}, u32[]{:S(2)}) collective-permute-start(bf16[528,1024]{1,0:T(8,128)(2,1)} %collective-permute-done.4.refs_22_), channel_id=1, source_target_pairs={{1,0},{2,1},{3,2},{0,3},{5,4},{6,5},{7,6},{4,7},{9,8},{10,9},{11,1... | collective-permute-start | bytes 3244040 | tf_op jit(solution)/shard_map/ppermute | solution.py:156
  47.8 30.8 %collective-permute-start.5 = (bf16[272,1024]{1,0:T(8,128)(2,1)}, bf16[272,1024]{1,0:T(8,128)(2,1)S(1)}, u32[]{:S(2)}, u32[]{:S(2)}) collective-permute-start(bf16[272,1024]{1,0:T(8,128)(2,1)} %slice.41), channel_id=1, source_target_pairs={{1,0},{2,1},{3,2},{0,3},{5,4},{6,5},{7,6},{4,7},{9,8},{10,9},{11,1... | collective-permute-start | bytes 1671176 | tf_op jit(solution)/shard_map/ppermute | solution.py:156
  65.6 15.6 %collective-permute-start.8 = (bf16[256,1024]{1,0:T(8,128)(2,1)}, bf16[256,1024]{1,0:T(8,128)(2,1)}, u32[]{:S(2)}, u32[]{:S(2)}) collective-permute-start(bf16[256,1024]{1,0:T(8,128)(2,1)} %slice.42), channel_id=1, source_target_pairs={{3,0},{0,1},{1,2},{2,3},{7,4},{4,5},{5,6},{6,7},{11,8},{8,9},{9,10... | collective-permute-start | bytes 1572872 | tf_op jit(solution)/shard_map/ppermute | solution.py:156
  66.3 17.1 %collective-permute-start.12 = (bf16[272,1024]{1,0:T(8,128)(2,1)}, bf16[272,1024]{1,0:T(8,128)(2,1)}, u32[]{:S(2)}, u32[]{:S(2)}) collective-permute-start(bf16[272,1024]{1,0:T(8,128)(2,1)} %slice.40), channel_id=1, source_target_pairs={{8,0},{16,8},{24,16},{0,24},{9,1},{17,9},{25,17},{1,25},{10,2},{18... | collective-permute-start | bytes 1671176 | tf_op jit(solution)/shard_map/ppermute | solution.py:156
  78.6 50.0 %copy-start.6 = (bf16[272,1024]{1,0:T(8,128)(2,1)}, bf16[272,1024]{1,0:T(8,128)(2,1)S(1)}, u32[]{:S(2)}) copy-start(bf16[272,1024]{1,0:T(8,128)(2,1)S(1)} %collective-permute-done.5.refs_7_) | copy-start | bytes 1671172
  78.6 22.8 %collective-permute-start.9 = (bf16[528,1024]{1,0:T(8,128)(2,1)}, bf16[528,1024]{1,0:T(8,128)(2,1)S(1)}, u32[]{:S(2)}, u32[]{:S(2)}) collective-permute-start(bf16[528,1024]{1,0:T(8,128)(2,1)} %collective-permute-done.3.refs_25_), channel_id=1, source_target_pairs={{3,0},{0,1},{1,2},{2,3},{7,4},{4,5},{5,6},{6,7},{11,8},{8,9},{9,10... | collective-permute-start | bytes 3244040 | tf_op jit(solution)/shard_map/ppermute | solution.py:156
  78.6 22.8 %collective-permute-start.10 = (bf16[528,1024]{1,0:T(8,128)(2,1)}, bf16[528,1024]{1,0:T(8,128)(2,1)S(1)}, u32[]{:S(2)}, u32[]{:S(2)}) collective-permute-start(bf16[528,1024]{1,0:T(8,128)(2,1)} %collective-permute-done.6.refs_11_), channel_id=1, source_target_pairs={{1,0},{2,1},{3,2},{0,3},{5,4},{6,5},{7,6},{4,7},{9,8},{10,9},{11,1... | collective-permute-start | bytes 3244040 | tf_op jit(solution)/shard_map/ppermute | solution.py:156
  81.3 37.7 %collective-permute-start.17 = (bf16[528,1024]{1,0:T(8,128)(2,1)}, bf16[528,1024]{1,0:T(8,128)(2,1)}, u32[]{:S(2)}, u32[]{:S(2)}) collective-permute-start(bf16[528,1024]{1,0:T(8,128)(2,1)} %collective-permute-done.7.refs_13_), channel_id=1, source_target_pairs={{8,0},{16,8},{24,16},{0,24},{9,1},{17,9},{25,17},{1,25},{10,2},{18... | collective-permute-start | bytes 3244040 | tf_op jit(solution)/shard_map/ppermute | solution.py:156
  83.5 37.2 %collective-permute-start.14 = (bf16[528,1024]{1,0:T(8,128)(2,1)}, bf16[528,1024]{1,0:T(8,128)(2,1)}, u32[]{:S(2)}, u32[]{:S(2)}) collective-permute-start(bf16[528,1024]{1,0:T(8,128)(2,1)} %collective-permute-done.11.refs_23_), channel_id=1, source_target_pairs={{24,0},{0,8},{8,16},{16,24},{25,1},{1,9},{9,17},{17,25},{26,2},{2,... | collective-permute-start | bytes 3244040 | tf_op jit(solution)/shard_map/ppermute | solution.py:156
  83.6 33.9 %collective-permute-start.13 = (bf16[256,1024]{1,0:T(8,128)(2,1)}, bf16[256,1024]{1,0:T(8,128)(2,1)}, u32[]{:S(2)}, u32[]{:S(2)}) collective-permute-start(bf16[256,1024]{1,0:T(8,128)(2,1)} %slice.44), channel_id=1, source_target_pairs={{24,0},{0,8},{8,16},{16,24},{25,1},{1,9},{9,17},{17,25},{26,2},{2,... | collective-permute-start | bytes 1572872 | tf_op jit(solution)/shard_map/ppermute | solution.py:156
  101.4 20.9 %copy-start.4 = (bf16[528,1024]{1,0:T(8,128)(2,1)}, bf16[528,1024]{1,0:T(8,128)(2,1)S(1)}, u32[]{:S(2)}) copy-start(bf16[528,1024]{1,0:T(8,128)(2,1)S(1)} %collective-permute-done.9.refs_24_) | copy-start | bytes 3244036
  101.4 27.2 %copy-start.5 = (bf16[528,1024]{1,0:T(8,128)(2,1)}, bf16[528,1024]{1,0:T(8,128)(2,1)S(1)}, u32[]{:S(2)}) copy-start(bf16[528,1024]{1,0:T(8,128)(2,1)S(1)} %collective-permute-done.10.refs_12_) | copy-start | bytes 3244036
  117.5 7.6 %collective-permute-start.15 = (bf16[128,1024]{1,0:T(8,128)(2,1)}, bf16[128,1024]{1,0:T(8,128)(2,1)}, u32[]{:S(2)}, u32[]{:S(2)}) collective-permute-start(bf16[128,1024]{1,0:T(8,128)(2,1)} %slice.49), channel_id=1, source_target_pairs={{8,0},{16,8},{24,16},{0,24},{9,1},{17,9},{25,17},{1,25},{10,2},{18... | collective-permute-start | bytes 786440 | tf_op jit(solution)/shard_map/ppermute | solution.py:156
  117.5 7.6 %collective-permute-start.16 = (bf16[144,1024]{1,0:T(8,128)(2,1)S(1)}, bf16[144,1024]{1,0:T(8,128)(2,1)S(1)}, u32[]{:S(2)}, u32[]{:S(2)}) collective-permute-start(bf16[144,1024]{1,0:T(8,128)(2,1)S(1)} %slice.48), channel_id=1, source_target_pairs={{24,0},{0,8},{8,16},{16,24},{25,1},{1,9},{9,17},{17,25},{26,2},{2,... | collective-permute-start | bytes 884744 | tf_op jit(solution)/shard_map/ppermute | solution.py:156
  120.6 6.7 %collective-permute-start.18 = (bf16[128,1024]{1,0:T(8,128)(2,1)}, bf16[128,1024]{1,0:T(8,128)(2,1)}, u32[]{:S(2)}, u32[]{:S(2)}) collective-permute-start(bf16[128,1024]{1,0:T(8,128)(2,1)} %slice.50), channel_id=1, source_target_pairs={{3,0},{0,1},{1,2},{2,3},{7,4},{4,5},{5,6},{6,7},{11,8},{8,9},{9,10... | collective-permute-start | bytes 786440 | tf_op jit(solution)/shard_map/ppermute | solution.py:156
  122.3 6.3 %collective-permute-start.19 = (bf16[128,1024]{1,0:T(8,128)(2,1)}, bf16[128,1024]{1,0:T(8,128)(2,1)}, u32[]{:S(2)}, u32[]{:S(2)}) collective-permute-start(bf16[128,1024]{1,0:T(8,128)(2,1)} %slice.51), channel_id=1, source_target_pairs={{1,0},{2,1},{3,2},{0,3},{5,4},{6,5},{7,6},{4,7},{9,8},{10,9},{11,1... | collective-permute-start | bytes 786440 | tf_op jit(solution)/shard_map/ppermute | solution.py:156
  125.1 3.5 %copy-start.7 = (bf16[144,1024]{1,0:T(8,128)(2,1)}, bf16[144,1024]{1,0:T(8,128)(2,1)S(1)}, u32[]{:S(2)}) copy-start(bf16[144,1024]{1,0:T(8,128)(2,1)S(1)} %collective-permute-done.16.refs_18_) | copy-start | bytes 884740
  157.3 26.2 %all-to-all-start.1 = ((f32[16,4,128]{2,1,0:T(4,128)}), f32[16,4,128]{2,1,0:T(4,128)S(1)}, u32[]{:S(2)}, u32[]{:S(2)}) async-start(f32[16,4,128]{2,1,0:T(4,128)} %bitcast.8), calls=%async_computation.1 | async-start | bytes 65536 | tf_op jit(solution)/shard_map/all_to_all | solution.py:246
Sparse Core Ops, SparseCore 0:
  11.4 100.5 all-gather.1

commit v2 on v1

--- a/solution.py
+++ b/solution.py
@@ -17,20 +17,23 @@
 VMEM_LIMIT = 32 * 1024 * 1024
 
 
-def unit_kernel(emb_ref, meta_ref, unit_ref, full_ref):
+def unit_kernel(emb_ref, unit_ref):
     for block in range(BLOCKS):
         rows = emb_ref[block].astype(jnp.float32)
         scale = lax.rsqrt(jnp.sum(rows * rows, axis=-1, keepdims=True) + epsilon)
-        unit = (rows * scale).astype(jnp.bfloat16)
-        unit_ref[block * ROWS : (block + 1) * ROWS, :] = unit
-        at = block * ROWS + (META if block >= 2 else 0)
-        full_ref[at : at + ROWS, :] = unit
+        unit_ref[block * ROWS : (block + 1) * ROWS, :] = (rows * scale).astype(jnp.bfloat16)
+
+
+def message_kernel(unit_ref, meta_ref, full_ref):
+    full_ref[: 2 * ROWS, :] = unit_ref[: 2 * ROWS, :]
     full_ref[2 * ROWS : HALF1, :] = meta_ref[...]
+    full_ref[HALF1:, :] = unit_ref[2 * ROWS :, :]
 
 
 def pair_kernel(right_at, meta_at, todo, first, place, left_tags, left_ref, *rest):
-    refs = rest[:-10]
-    left_out, right_out, left_buf, right_buf, right_meta, tags_buf, best_buf, left_best, left_sems, right_sems = rest[-10:]
+    refs = rest[:-13]
+    left_out, *right_out = rest[-13:-8]
+    left_buf, right_buf, right_meta, tags_buf, best_buf, left_best, left_sems, right_sems = rest[-8:]
 
     def fetch_right(j):
         for dy in range(4):
@@ -73,8 +76,7 @@
 
     row_ids = lax.broadcasted_iota(jnp.int32, (ROWS, ROWS), 0)
     col_ids = lax.broadcasted_iota(jnp.int32, (ROWS, ROWS), 1)
-    my_z, my_x, my_c, my_y = place[0], place[1], place[2], place[3]
-    me = my_z * 2 + my_c
+    me = place[0]
 
     for j in range(16):
         dx, b = j // 4, j % 4
@@ -112,10 +114,8 @@
             return carry
 
         lax.fori_loop(first[j], first[j + 1], step, 0)
-        right_x = lax.rem(my_x + dx, 4)
         for dy in range(4):
-            row = (right_x * 4 + lax.rem(my_y + dy, 4)) * 4 + b
-            right_out[pl.ds(row, 1), :] = jnp.max(best_buf[dy * ROWS : (dy + 1) * ROWS, :].T, axis=0, keepdims=True)
+            right_out[dy][j : j + 1, :] = jnp.max(best_buf[dy * ROWS : (dy + 1) * ROWS, :].T, axis=0, keepdims=True)
     left_out[...] = left_best[0:64, :]
 
 
@@ -126,9 +126,9 @@
     smem, vmem, hbm = (pl.BlockSpec(memory_space=s) for s in (pltpu.SMEM, pltpu.VMEM, pltpu.HBM))
     return pl.pallas_call(
         kernel,
-        out_shape=(jax.ShapeDtypeStruct((64, ROWS), jnp.float32),) * 2,
+        out_shape=[jax.ShapeDtypeStruct((n, ROWS), jnp.float32) for n in (64, 16, 16, 16, 16)],
         in_specs=[smem, smem, smem, vmem] + [hbm] * (len(operands) + 1),
-        out_specs=(vmem, vmem),
+        out_specs=[vmem] * 5,
         scratch_shapes=[
             pltpu.VMEM((SLOTS, 2 * ROWS, 1024), jnp.bfloat16),
             pltpu.VMEM((16, 4 * ROWS, 1024), jnp.bfloat16),
@@ -144,17 +144,20 @@
     )(todo, first, place, left_tags, *(pltpu.with_memory_space_constraint(v, pltpu.HBM) for v in (left_rows, *operands)))
 
 
+def shift(value, axis, by):
+    size = lax.axis_size(axis)
+    return lax.ppermute(value, axis, [((i + by) % size, i) for i in range(size)])
+
+
 class Carrier:
     def __init__(self):
-        self.sent = []
+        self.last = {}
 
     def __call__(self, value, axis, by):
-        if len(self.sent) >= DEPTH:
-            k = len(self.sent) - DEPTH
-            value, self.sent[k][0] = lax.optimization_barrier((value, self.sent[k][0]))
-        size = lax.axis_size(axis)
-        cell = [lax.ppermute(value, axis, [((i + by) % size, i) for i in range(size)])]
-        self.sent.append(cell)
+        if (axis, by) in self.last:
+            before = self.last[axis, by]
+            value, before[0] = lax.optimization_barrier((value, before[0]))
+        self.last[axis, by] = cell = [shift(value, axis, by)]
         return cell
 
 
@@ -169,15 +172,15 @@
     whole[3, 3] = send(whole[0, 3][0], *xm)
     whole[3, 1] = send(whole[3, 0][0], *yp)
     whole[1, 3] = send(whole[1, 0][0], *ym)
+    whole[1, 2] = send(whole[1, 1][0], *yp)
+    whole[3, 2] = send(whole[3, 3][0], *ym)
+    whole[2, 3] = send(whole[1, 3][0], *xp)
+    whole[2, 1] = send(whole[3, 1][0], *xm)
     half = {}
     half["y", 0] = send(whole[0, 1][0][:HALF1], *yp)
     half["y", 1] = send(whole[0, 3][0][HALF1:], *ym)
     half["x", 0] = send(whole[1, 0][0][:HALF1], *xp)
     half["x", 1] = send(whole[3, 0][0][HALF1:], *xm)
-    whole[1, 2] = send(whole[1, 1][0], *yp)
-    whole[3, 2] = send(whole[3, 3][0], *ym)
-    whole[2, 3] = send(whole[1, 3][0], *xp)
-    whole[2, 1] = send(whole[3, 1][0], *xm)
     last = [
         send(whole[1, 2][0][:ROWS], *xp),
         send(whole[3, 2][0][ROWS:HALF1], *xm),
@@ -197,19 +200,21 @@
 
 
 def local(embeddings, cluster_ids, valid, pair_left, pair_right):
-    my_z, my_x, my_c, my_y = (lax.axis_index(name) for name in ("z", "x", "c", "y"))
-    place = jnp.stack([my_z, my_x, my_c, my_y]).astype(jnp.int32)
+    my_z, my_x, my_c = (lax.axis_index(name) for name in ("z", "x", "c"))
+    place = (my_z * 2 + my_c).astype(jnp.int32).reshape(1)
+    limit = pltpu.CompilerParams(vmem_limit_bytes=VMEM_LIMIT)
+    unit = pl.pallas_call(
+        unit_kernel, out_shape=jax.ShapeDtypeStruct((4 * ROWS, 1024), jnp.bfloat16), compiler_params=limit, name="unit_rows"
+    )(embeddings)
+    unit, cluster_ids, pair_left = lax.optimization_barrier((unit, cluster_ids, pair_left))
+    left_rows = lax.all_gather(unit, ("z", "c"), axis=0, tiled=True)
     labels = jnp.where(valid > 0, cluster_ids, -1).reshape(1, -1)
     lists = jnp.concatenate([labels, (pair_left % BLOCKS)[None], pair_right[None]], axis=1)
     meta = jnp.pad(lists.astype(jnp.bfloat16), ((0, META - 1), (0, 1024 - lists.shape[1])))
-    unit, full = pl.pallas_call(
-        unit_kernel,
-        out_shape=[jax.ShapeDtypeStruct((n, 1024), jnp.bfloat16) for n in (4 * ROWS, FULL)],
-        compiler_params=pltpu.CompilerParams(vmem_limit_bytes=VMEM_LIMIT),
-        name="unit_rows",
-    )(embeddings, meta)
-    unit, lists = lax.optimization_barrier((unit, lists))
-    left_rows = lax.all_gather(unit, ("z", "c"), axis=0, tiled=True)
+    full = pl.pallas_call(
+        message_kernel, out_shape=jax.ShapeDtypeStruct((FULL, 1024), jnp.bfloat16), compiler_params=limit, name="message_rows"
+    )(unit, meta)
+    full, lists = lax.optimization_barrier((full, lists))
     left_lists = lax.all_to_all(jnp.broadcast_to(lists, (16, lists.shape[1])), ("z", "c"), 0, 0, tiled=True)
     parts, metas, left_lists = gather_plane(full, left_lists)
 
@@ -242,10 +247,15 @@
     for k in [(dx, dy) for dx in range(4) for dy in range(4)]:
         right_at.append([(place_of(value), base) for value, base in parts[k]])
         meta_at.append((place_of(metas[k][0]), metas[k][1]))
-    left_best, right_best = pair_maxima(todo, first, place, left_tags, left_rows, operands, right_at, meta_at)
+    left_best, *right_best = pair_maxima(todo, first, place, left_tags, left_rows, operands, right_at, meta_at)
     from_left = lax.all_to_all(left_best.reshape(16, BLOCKS, ROWS), ("z", "c"), 0, 0, tiled=True)
-    from_right = lax.all_to_all(right_best.reshape(16, BLOCKS, ROWS), ("x", "y"), 0, 0, tiled=True)
-    return jnp.maximum(jnp.max(from_left, axis=0), jnp.max(from_right, axis=0))
+    own = right_best[0]
+    for came in [shift(right_best[dy], "y", -dy) for dy in (1, 2, 3)]:
+        own = jnp.maximum(own, came)
+    best = own[:BLOCKS]
+    for came in [shift(own[dx * BLOCKS : (dx + 1) * BLOCKS], "x", -dx) for dx in (1, 2, 3)]:
+        best = jnp.maximum(best, came)
+    return jnp.maximum(jnp.max(from_left, axis=0), best)
 
 
 def solution(mesh):

time: 191 us -> 173 us (0.906)
  waiting for transfers between devices: 73.2 us -> 56.3 us
  blocking collectives: 30.2 us -> 17.7 us
  starting transfers between devices: 41.8 us -> 47 us
  Pallas kernels: 16.9 us -> 21.7 us
  local copies, waits for them, and re-layouts: 11.4 us -> 14 us
  other arithmetic: 3.88 us -> 1.79 us
    ppermute x20 -> x26, waiting for transfers between devices: 65.8 us -> 50.7 us  [shift(): lax.ppermute(value, axis, [((i + by) % size, i) for i in range(size)])]
    all_to_all x1 -> x0, blocking collectives: 13.1 us -> none  [local(): lax.all_to_all(right_best.reshape(16, BLOCKS, ROWS), ('x', 'y'), 0, 0, ti...]
    pallas_call x2 -> x3, Pallas kernels: 16.9 us -> 21.7 us  [the longest x1 19.2 us: pair_maxima(): pl.pallas_call(kernel, out_shape=[jax.ShapeDtypeStruct((n, ROWS), jnp.flo...]
    ppermute x20 -> x26, starting transfers between devices: 22.9 us -> 27.5 us  [shift(): lax.ppermute(value, axis, [((i + by) % size, i) for i in range(size)])]
  transfers between devices with their start and end apart: 22 -> 28, of which waited for: 9 -> 13; matrix products, arithmetic and copies ran while one was open for 6% -> 8% of each run, Pallas kernels for 0% -> 1%
where the time goes in v2:
time: 173 us; the launch traced here: 172 us
  waiting for transfers between devices  56.3 us (33%)
  starting transfers between devices  47 us (27%)
  Pallas kernels  21.7 us (13%)
  blocking collectives  17.7 us (10%)
  local copies, waits for them, and re-layouts  14 us (8%)
  between operations  13.7 us (8%)
  other arithmetic  1.79 us (1%)
    ppermute x26, waiting for transfers between devices, shift(): lax.ppermute(value, axis, [((i + by) % size, i) for i in range(size)])  50.7 us
    ppermute x26, starting transfers between devices, shift(): lax.ppermute(value, axis, [((i + by) % size, i) for i in range(size)])  27.5 us
    all_to_all x1, starting transfers between devices, local(): lax.all_to_all(left_best.reshape(16, BLOCKS, ROWS), ('z', 'c'), 0, 0, til...  19.5 us
    pallas_call x1, Pallas kernels, pair_maxima(): pl.pallas_call(kernel, out_shape=[jax.ShapeDtypeStruct((n, ROWS), jnp.flo...  19.2 us
    all_to_all x1, blocking collectives, local(): lax.all_to_all(jnp.broadcast_to(lists, (16, lists.shape[1])), ('z', 'c'),...  17.7 us
    all_to_all x1, waiting for transfers between devices, local(): lax.all_to_all(left_best.reshape(16, BLOCKS, ROWS), ('z', 'c'), 0, 0, til...  5.54 us
  transfers between devices with their start and end apart: 28, of which 13 were waited for; matrix products, arithmetic and copies ran while one was open for 8% of the time, Pallas kernels for 1%

profile of v2, /device:TPU:1, one launch (start us, length us, event | category | flops | bytes accessed | tf_op | source)
XLA Modules:
  0.0 172.3 jit_solution(9975831950504527955)
XLA Ops:
  6.5 1.2 copy-done.1
  7.8 1.3 unit_rows.1.unit_ref
  9.2 1.3 message_rows.1.refs_5_
  10.5 3.6 %collective-permute-start = (bf16[528,1024]{1,0:T(8,128)(2,1)S(1)}, bf16[528,1024]{1,0:T(8,128)(2,1)S(1)}, u32[]{:S(2)}, u32[]{:S(2)}) collective-permute-start(bf16[528,1024]{1,0:T(8,128)(2,1)S(1)} %message_rows.1.refs_5_), channel_id=1, source_target_pairs={{1,0},{2,1},{3,2},{0,3},{5,4},{6,5},{7,6},{4,7},{9,8},{10,9},{11,1... | collective-permute-start | bytes 3244040 | tf_op jit(solution)/shard_map/ppermute | solution.py:149
  14.2 1.2 collective-permute-start.2
  15.4 1.5 collective-permute-start.3
  16.9 17.7 %all_to_all.14 = s32[16,1,576]{2,1,0:T(1,128)S(1)} all-to-all(s32[16,1,576]{2,1,0:T(1,128)S(1)} %broadcast_in_dim.65), channel_id=1, replica_groups=mesh['z'=8,'x'=4,'c'=2,'y'=4] {'z','c'}, dimensions={0} | all-to-all | bytes 73728 | tf_op jit(solution)/shard_map/all_to_all | solution.py:218
  34.6 2.1 %collective-permute-done.refs_6_ = bf16[528,1024]{1,0:T(8,128)(2,1)S(1)} collective-permute-done((bf16[528,1024]{1,0:T(8,128)(2,1)S(1)}, bf16[528,1024]{1,0:T(8,128)(2,1)S(1)}, u32[]{:S(2)}, u32[]{:S(2)}) %collective-permute-start) | collective-permute-done | bytes 1081376 | tf_op jit(solution)/shard_map/ppermute | solution.py:149
  36.7 3.2 %collective-permute-done.1.refs_9_ = bf16[528,1024]{1,0:T(8,128)(2,1)} collective-permute-done((bf16[528,1024]{1,0:T(8,128)(2,1)S(1)}, bf16[528,1024]{1,0:T(8,128)(2,1)}, u32[]{:S(2)}, u32[]{:S(2)}) %collective-permute-start.1) | collective-permute-done | bytes 1081376 | tf_op jit(solution)/shard_map/ppermute | solution.py:149
  39.9 2.6 %collective-permute-start.4 = (bf16[528,1024]{1,0:T(8,128)(2,1)S(1)}, bf16[528,1024]{1,0:T(8,128)(2,1)}, u32[]{:S(2)}, u32[]{:S(2)}) collective-permute-start(bf16[528,1024]{1,0:T(8,128)(2,1)S(1)} %collective-permute-done.refs_6_), channel_id=1, source_target_pairs={{8,0},{16,8},{24,16},{0,24},{9,1},{17,9},{25,17},{1,25},{10,2},{18... | collective-permute-start | bytes 3244040 | tf_op jit(solution)/shard_map/ppermute | solution.py:149
  42.5 2.2 %collective-permute-start.5 = (bf16[528,1024]{1,0:T(8,128)(2,1)}, bf16[528,1024]{1,0:T(8,128)(2,1)}, u32[]{:S(2)}, u32[]{:S(2)}) collective-permute-start(bf16[528,1024]{1,0:T(8,128)(2,1)} %collective-permute-done.2.refs_22_), channel_id=1, source_target_pairs={{1,0},{2,1},{3,2},{0,3},{5,4},{6,5},{7,6},{4,7},{9,8},{10,9},{11,1... | collective-permute-start | bytes 3244040 | tf_op jit(solution)/shard_map/ppermute | solution.py:149
  44.7 1.9 %slice.52 = bf16[256,1024]{1,0:T(8,128)(2,1)} slice(bf16[528,1024]{1,0:T(8,128)(2,1)} %collective-permute-done.2.refs_22_), slice={[272:528], [0:1024]} | slice | bytes 1048576 | tf_op jit(solution)/shard_map/slice | solution.py:183
  46.6 0.9 slice.55
  47.5 16.3 %collective-permute-done.4.refs_11_ = bf16[528,1024]{1,0:T(8,128)(2,1)} collective-permute-done((bf16[528,1024]{1,0:T(8,128)(2,1)S(1)}, bf16[528,1024]{1,0:T(8,128)(2,1)}, u32[]{:S(2)}, u32[]{:S(2)}) %collective-permute-start.4) | collective-permute-done | bytes 1081376 | tf_op jit(solution)/shard_map/ppermute | solution.py:149
  63.8 2.2 %collective-permute-done.5.refs_23_ = bf16[528,1024]{1,0:T(8,128)(2,1)} collective-permute-done((bf16[528,1024]{1,0:T(8,128)(2,1)}, bf16[528,1024]{1,0:T(8,128)(2,1)}, u32[]{:S(2)}, u32[]{:S(2)}) %collective-permute-start.5) | collective-permute-done | bytes 1081376 | tf_op jit(solution)/shard_map/ppermute | solution.py:149
  66.0 2.7 %collective-permute-done.6.refs_25_ = bf16[528,1024]{1,0:T(8,128)(2,1)} collective-permute-done((bf16[528,1024]{1,0:T(8,128)(2,1)}, bf16[528,1024]{1,0:T(8,128)(2,1)}, u32[]{:S(2)}, u32[]{:S(2)}) %collective-permute-start.6) | collective-permute-done | bytes 1081376 | tf_op jit(solution)/shard_map/ppermute | solution.py:149
  68.7 0.3 collective-permute-start.8
  69.0 2.7 %collective-permute-start.11 = (bf16[528,1024]{1,0:T(8,128)(2,1)}, bf16[528,1024]{1,0:T(8,128)(2,1)}, u32[]{:S(2)}, u32[]{:S(2)}) collective-permute-start(bf16[528,1024]{1,0:T(8,128)(2,1)} %collective-permute-done.10.refs_13_), channel_id=1, source_target_pairs={{8,0},{16,8},{24,16},{0,24},{9,1},{17,9},{25,17},{1,25},{10,2},{18... | collective-permute-start | bytes 3244040 | tf_op jit(solution)/shard_map/ppermute | solution.py:149
  71.6 1.2 collective-permute-start.12
  72.9 0.3 select_reduce_fusion
  73.5 0.9 slice.54
  74.4 1.9 %slice.57 = bf16[256,1024]{1,0:T(8,128)(2,1)} slice(bf16[528,1024]{1,0:T(8,128)(2,1)} %collective-permute-done.1.refs_9_), slice={[272:528], [0:1024]} | slice | bytes 1048576 | tf_op jit(solution)/shard_map/slice | solution.py:181
  76.4 15.3 %collective-permute-done.7.refs_16_ = bf16[528,1024]{1,0:T(8,128)(2,1)} collective-permute-done((bf16[528,1024]{1,0:T(8,128)(2,1)}, bf16[528,1024]{1,0:T(8,128)(2,1)}, u32[]{:S(2)}, u32[]{:S(2)}) %collective-permute-start.7) | collective-permute-done | bytes 1081376 | tf_op jit(solution)/shard_map/ppermute | solution.py:149
  91.7 0.6 collective-permute-start.9
  92.3 1.8 %collective-permute-done.12.refs_24_ = bf16[528,1024]{1,0:T(8,128)(2,1)} collective-permute-done((bf16[528,1024]{1,0:T(8,128)(2,1)}, bf16[528,1024]{1,0:T(8,128)(2,1)}, u32[]{:S(2)}, u32[]{:S(2)}) %collective-permute-start.12) | collective-permute-done | bytes 1081376 | tf_op jit(solution)/shard_map/ppermute | solution.py:149
  94.2 1.2 collective-permute-start.14
  95.3 0.3 collective-permute-start.15
  95.6 0.3 convert_reduce_fusion
  96.2 1.7 slice.53
  97.9 1.7 slice.56
  99.5 1.7 %slice.58 = bf16[128,1024]{1,0:T(8,128)(2,1)} slice(bf16[528,1024]{1,0:T(8,128)(2,1)} %collective-permute-done.8.refs_12_), slice={[0:128], [0:1024]} | slice | bytes 524288 | tf_op jit(solution)/shard_map/slice | solution.py:185
  101.3 1.0 slice.59
  102.3 2.4 %collective-permute-done.13.refs_8_ = bf16[256,1024]{1,0:T(8,128)(2,1)S(1)} collective-permute-done((bf16[256,1024]{1,0:T(8,128)(2,1)}, bf16[256,1024]{1,0:T(8,128)(2,1)S(1)}, u32[]{:S(2)}, u32[]{:S(2)}) %collective-permute-start.13) | collective-permute-done | bytes 524320 | tf_op jit(solution)/shard_map/ppermute | solution.py:149
  104.7 0.5 collective-permute-done.15.refs_15_
  105.2 0.2 collective-permute-start.18
  105.4 2.8 %collective-permute-start.16 = (bf16[128,1024]{1,0:T(8,128)(2,1)}, bf16[128,1024]{1,0:T(8,128)(2,1)S(1)}, u32[]{:S(2)}, u32[]{:S(2)}) collective-permute-start(bf16[128,1024]{1,0:T(8,128)(2,1)} %slice.58), channel_id=1, source_target_pairs={{8,0},{16,8},{24,16},{0,24},{9,1},{17,9},{25,17},{1,25},{10,2},{18... | collective-permute-start | bytes 786440 | tf_op jit(solution)/shard_map/ppermute | solution.py:149
  108.1 2.5 %collective-permute-start.19 = (bf16[128,1024]{1,0:T(8,128)(2,1)}, bf16[128,1024]{1,0:T(8,128)(2,1)S(1)}, u32[]{:S(2)}, u32[]{:S(2)}) collective-permute-start(bf16[128,1024]{1,0:T(8,128)(2,1)} %slice.53), channel_id=1, source_target_pairs={{1,0},{2,1},{3,2},{0,3},{5,4},{6,5},{7,6},{4,7},{9,8},{10,9},{11,1... | collective-permute-start | bytes 786440 | tf_op jit(solution)/shard_map/ppermute | solution.py:149
  110.8 2.4 %collective-permute-done.18.refs_19_ = bf16[128,1024]{1,0:T(8,128)(2,1)S(1)} collective-permute-done((bf16[128,1024]{1,0:T(8,128)(2,1)}, bf16[128,1024]{1,0:T(8,128)(2,1)S(1)}, u32[]{:S(2)}, u32[]{:S(2)}) %collective-permute-start.18) | collective-permute-done | bytes 262176 | tf_op jit(solution)/shard_map/ppermute | solution.py:149
  113.2 0.6 collective-permute-done.16.refs_17_
  113.7 1.2 collective-permute-done.17.refs_18_
  115.0 0.6 copy-done.7
  115.7 19.2 %pair_maxima.1 = (f32[64,128]{1,0:T(8,128)}, f32[16,128]{1,0:T(8,128)S(1)}, f32[16,128]{1,0:T(8,128)S(1)}, f32[16,128]{1,0:T(8,128)S(1)}, f32[16,128]{1,0:T(8,128)S(1)}) custom-call(s32[80]{0:T(128)S(1)} %compare_select_fusion.2.refs_0_, s32[17]{0:T(128)S(1)} %select_reduce_fusion.2.refs_1_, s32[1]{0:T(128)} %bitcast.4.refs_2_, f32[72,128]{1,0:T(8,128)S(1)} %pad.9.refs_3_, ...), custom_call_target="tpu_custom_call" | custom-call | tf_op jit(solution)/shard_map/pair_maxima/pallas_call | solution.py:127
  134.9 2.4 %collective-permute-start.22 = (f32[16,128]{1,0:T(8,128)S(1)}, f32[16,128]{1,0:T(8,128)S(1)}, u32[]{:S(2)}, u32[]{:S(2)}) collective-permute-start(f32[16,128]{1,0:T(8,128)S(1)} %get-tuple-element.92), channel_id=1, source_target_pairs={{1,0},{2,1},{3,2},{0,3},{5,4},{6,5},{7,6},{4,7},{9,8},{10,9},{11,1... | collective-permute-start | bytes 24584 | tf_op jit(solution)/shard_map/ppermute | solution.py:149
  137.3 0.7 collective-permute-start.20
  137.9 19.5 %all-to-all-start.1 = ((f32[16,4,128]{2,1,0:T(4,128)}), f32[16,4,128]{2,1,0:T(4,128)S(1)}, u32[]{:S(2)}, u32[]{:S(2)}) async-start(f32[16,4,128]{2,1,0:T(4,128)} %bitcast.5), calls=%async_computation.1 | async-start | bytes 65536 | tf_op jit(solution)/shard_map/all_to_all | solution.py:251
  157.6 1.7 collective-permute-start.24
  159.3 5.5 %all-to-all-done.1 = f32[16,4,128]{2,1,0:T(4,128)S(1)} async-done(((f32[16,4,128]{2,1,0:T(4,128)}), f32[16,4,128]{2,1,0:T(4,128)S(1)}, u32[]{:S(2)}, u32[]{:S(2)}) %all-to-all-start.1) | async-done | bytes 32800 | tf_op jit(solution)/shard_map/all_to_all | solution.py:251
  164.9 0.6 fusion.15
  (83 shorter events, 1.3 us)
Async XLA Ops:
  6.5 108.4 %all-gather.2.cloned.1.call-start = ((), (), s32[]{:S(2)}) async-start(), calls=%async_computation.2 | async-start | bytes 17825792 | tf_op jit(solution)/shard_map/all_gather | solution.py:210
  6.5 1.2 copy-start.1
  7.8 1.3 copy-start.14
  7.8 1.3 copy-start.11
  7.8 1.4 copy-start.12
  7.8 1.4 copy-start.13
  10.5 36.9 %copy-start = (bf16[528,1024]{1,0:T(8,128)(2,1)}, bf16[528,1024]{1,0:T(8,128)(2,1)S(1)}, u32[]{:S(2)}) copy-start(bf16[528,1024]{1,0:T(8,128)(2,1)S(1)} %message_rows.1.refs_5_) | copy-start | bytes 3244036
  10.5 26.2 %collective-permute-start = (bf16[528,1024]{1,0:T(8,128)(2,1)S(1)}, bf16[528,1024]{1,0:T(8,128)(2,1)S(1)}, u32[]{:S(2)}, u32[]{:S(2)}) collective-permute-start(bf16[528,1024]{1,0:T(8,128)(2,1)S(1)} %message_rows.1.refs_5_), channel_id=1, source_target_pairs={{1,0},{2,1},{3,2},{0,3},{5,4},{6,5},{7,6},{4,7},{9,8},{10,9},{11,1... | collective-permute-start | bytes 3244040 | tf_op jit(solution)/shard_map/ppermute | solution.py:149
  14.2 25.7 %collective-permute-start.1 = (bf16[528,1024]{1,0:T(8,128)(2,1)S(1)}, bf16[528,1024]{1,0:T(8,128)(2,1)}, u32[]{:S(2)}, u32[]{:S(2)}) collective-permute-start(bf16[528,1024]{1,0:T(8,128)(2,1)S(1)} %message_rows.1.refs_5_), channel_id=1, source_target_pairs={{3,0},{0,1},{1,2},{2,3},{7,4},{4,5},{5,6},{6,7},{11,8},{8,9},{9,10... | collective-permute-start | bytes 3244040 | tf_op jit(solution)/shard_map/ppermute | solution.py:149
  14.2 25.7 %collective-permute-start.2 = (bf16[528,1024]{1,0:T(8,128)(2,1)S(1)}, bf16[528,1024]{1,0:T(8,128)(2,1)}, u32[]{:S(2)}, u32[]{:S(2)}) collective-permute-start(bf16[528,1024]{1,0:T(8,128)(2,1)S(1)} %message_rows.1.refs_5_), channel_id=1, source_target_pairs={{24,0},{0,8},{8,16},{16,24},{25,1},{1,9},{9,17},{17,25},{26,2},{2,... | collective-permute-start | bytes 3244040 | tf_op jit(solution)/shard_map/ppermute | solution.py:149
  15.4 24.5 %collective-permute-start.3 = (bf16[528,1024]{1,0:T(8,128)(2,1)S(1)}, bf16[528,1024]{1,0:T(8,128)(2,1)S(1)}, u32[]{:S(2)}, u32[]{:S(2)}) collective-permute-start(bf16[528,1024]{1,0:T(8,128)(2,1)S(1)} %message_rows.1.refs_5_), channel_id=1, source_target_pairs={{8,0},{16,8},{24,16},{0,24},{9,1},{17,9},{25,17},{1,25},{10,2},{18... | collective-permute-start | bytes 3244040 | tf_op jit(solution)/shard_map/ppermute | solution.py:149
  36.7 36.8 %copy-start.2 = (bf16[528,1024]{1,0:T(8,128)(2,1)}, bf16[528,1024]{1,0:T(8,128)(2,1)S(1)}, u32[]{:S(2)}) copy-start(bf16[528,1024]{1,0:T(8,128)(2,1)S(1)} %collective-permute-done.refs_6_) | copy-start | bytes 3244036
  39.9 62.3 %copy-start.3 = (bf16[528,1024]{1,0:T(8,128)(2,1)}, bf16[528,1024]{1,0:T(8,128)(2,1)S(1)}, u32[]{:S(2)}) copy-start(bf16[528,1024]{1,0:T(8,128)(2,1)S(1)} %collective-permute-done.3.refs_10_) | copy-start | bytes 3244036
  39.9 23.8 %collective-permute-start.4 = (bf16[528,1024]{1,0:T(8,128)(2,1)S(1)}, bf16[528,1024]{1,0:T(8,128)(2,1)}, u32[]{:S(2)}, u32[]{:S(2)}) collective-permute-start(bf16[528,1024]{1,0:T(8,128)(2,1)S(1)} %collective-permute-done.refs_6_), channel_id=1, source_target_pairs={{8,0},{16,8},{24,16},{0,24},{9,1},{17,9},{25,17},{1,25},{10,2},{18... | collective-permute-start | bytes 3244040 | tf_op jit(solution)/shard_map/ppermute | solution.py:149
  42.5 23.5 %collective-permute-start.5 = (bf16[528,1024]{1,0:T(8,128)(2,1)}, bf16[528,1024]{1,0:T(8,128)(2,1)}, u32[]{:S(2)}, u32[]{:S(2)}) collective-permute-start(bf16[528,1024]{1,0:T(8,128)(2,1)} %collective-permute-done.2.refs_22_), channel_id=1, source_target_pairs={{1,0},{2,1},{3,2},{0,3},{5,4},{6,5},{7,6},{4,7},{9,8},{10,9},{11,1... | collective-permute-start | bytes 3244040 | tf_op jit(solution)/shard_map/ppermute | solution.py:149
  44.7 24.0 %collective-permute-start.6 = (bf16[528,1024]{1,0:T(8,128)(2,1)}, bf16[528,1024]{1,0:T(8,128)(2,1)}, u32[]{:S(2)}, u32[]{:S(2)}) collective-permute-start(bf16[528,1024]{1,0:T(8,128)(2,1)} %collective-permute-done.1.refs_9_), channel_id=1, source_target_pairs={{24,0},{0,8},{8,16},{16,24},{25,1},{1,9},{9,17},{17,25},{26,2},{2,... | collective-permute-start | bytes 3244040 | tf_op jit(solution)/shard_map/ppermute | solution.py:149
  44.7 24.3 %collective-permute-start.10 = (bf16[528,1024]{1,0:T(8,128)(2,1)S(1)}, bf16[528,1024]{1,0:T(8,128)(2,1)}, u32[]{:S(2)}, u32[]{:S(2)}) collective-permute-start(bf16[528,1024]{1,0:T(8,128)(2,1)S(1)} %collective-permute-done.3.refs_10_), channel_id=1, source_target_pairs={{3,0},{0,1},{1,2},{2,3},{7,4},{4,5},{5,6},{6,7},{11,8},{8,9},{9,10... | collective-permute-start | bytes 3244040 | tf_op jit(solution)/shard_map/ppermute | solution.py:149
  68.7 23.1 %collective-permute-start.7 = (bf16[528,1024]{1,0:T(8,128)(2,1)}, bf16[528,1024]{1,0:T(8,128)(2,1)}, u32[]{:S(2)}, u32[]{:S(2)}) collective-permute-start(bf16[528,1024]{1,0:T(8,128)(2,1)} %collective-permute-done.5.refs_23_), channel_id=1, source_target_pairs={{24,0},{0,8},{8,16},{16,24},{25,1},{1,9},{9,17},{17,25},{26,2},{2,... | collective-permute-start | bytes 3244040 | tf_op jit(solution)/shard_map/ppermute | solution.py:149
  68.7 23.1 %collective-permute-start.8 = (bf16[528,1024]{1,0:T(8,128)(2,1)}, bf16[528,1024]{1,0:T(8,128)(2,1)}, u32[]{:S(2)}, u32[]{:S(2)}) collective-permute-start(bf16[528,1024]{1,0:T(8,128)(2,1)} %collective-permute-done.4.refs_11_), channel_id=1, source_target_pairs={{1,0},{2,1},{3,2},{0,3},{5,4},{6,5},{7,6},{4,7},{9,8},{10,9},{11,1... | collective-permute-start | bytes 3244040 | tf_op jit(solution)/shard_map/ppermute | solution.py:149
  69.0 23.3 %collective-permute-start.11 = (bf16[528,1024]{1,0:T(8,128)(2,1)}, bf16[528,1024]{1,0:T(8,128)(2,1)}, u32[]{:S(2)}, u32[]{:S(2)}) collective-permute-start(bf16[528,1024]{1,0:T(8,128)(2,1)} %collective-permute-done.10.refs_13_), channel_id=1, source_target_pairs={{8,0},{16,8},{24,16},{0,24},{9,1},{17,9},{25,17},{1,25},{10,2},{18... | collective-permute-start | bytes 3244040 | tf_op jit(solution)/shard_map/ppermute | solution.py:149
  71.6 22.5 %collective-permute-start.12 = (bf16[528,1024]{1,0:T(8,128)(2,1)}, bf16[528,1024]{1,0:T(8,128)(2,1)}, u32[]{:S(2)}, u32[]{:S(2)}) collective-permute-start(bf16[528,1024]{1,0:T(8,128)(2,1)} %collective-permute-done.6.refs_25_), channel_id=1, source_target_pairs={{3,0},{0,1},{1,2},{2,3},{7,4},{4,5},{5,6},{6,7},{11,8},{8,9},{9,10... | collective-permute-start | bytes 3244040 | tf_op jit(solution)/shard_map/ppermute | solution.py:149
  91.7 13.6 %collective-permute-start.9 = (bf16[272,1024]{1,0:T(8,128)(2,1)}, bf16[272,1024]{1,0:T(8,128)(2,1)S(1)}, u32[]{:S(2)}, u32[]{:S(2)}) collective-permute-start(bf16[272,1024]{1,0:T(8,128)(2,1)} %slice.54), channel_id=1, source_target_pairs={{1,0},{2,1},{3,2},{0,3},{5,4},{6,5},{7,6},{4,7},{9,8},{10,9},{11,1... | collective-permute-start | bytes 1671176 | tf_op jit(solution)/shard_map/ppermute | solution.py:149
  94.1 10.5 %collective-permute-start.13 = (bf16[256,1024]{1,0:T(8,128)(2,1)}, bf16[256,1024]{1,0:T(8,128)(2,1)S(1)}, u32[]{:S(2)}, u32[]{:S(2)}) collective-permute-start(bf16[256,1024]{1,0:T(8,128)(2,1)} %slice.57), channel_id=1, source_target_pairs={{3,0},{0,1},{1,2},{2,3},{7,4},{4,5},{5,6},{6,7},{11,8},{8,9},{9,10... | collective-permute-start | bytes 1572872 | tf_op jit(solution)/shard_map/ppermute | solution.py:149
  94.2 11.2 %collective-permute-start.14 = (bf16[272,1024]{1,0:T(8,128)(2,1)}, bf16[272,1024]{1,0:T(8,128)(2,1)S(1)}, u32[]{:S(2)}, u32[]{:S(2)}) collective-permute-start(bf16[272,1024]{1,0:T(8,128)(2,1)} %slice.55), channel_id=1, source_target_pairs={{8,0},{16,8},{24,16},{0,24},{9,1},{17,9},{25,17},{1,25},{10,2},{18... | collective-permute-start | bytes 1671176 | tf_op jit(solution)/shard_map/ppermute | solution.py:149
  95.3 9.9 %collective-permute-start.15 = (bf16[256,1024]{1,0:T(8,128)(2,1)}, bf16[256,1024]{1,0:T(8,128)(2,1)}, u32[]{:S(2)}, u32[]{:S(2)}) collective-permute-start(bf16[256,1024]{1,0:T(8,128)(2,1)} %slice.52), channel_id=1, source_target_pairs={{24,0},{0,8},{8,16},{16,24},{25,1},{1,9},{9,17},{17,25},{26,2},{2,... | collective-permute-start | bytes 1572872 | tf_op jit(solution)/shard_map/ppermute | solution.py:149
  104.7 10.3 %copy-start.6 = (bf16[256,1024]{1,0:T(8,128)(2,1)}, bf16[256,1024]{1,0:T(8,128)(2,1)S(1)}, u32[]{:S(2)}) copy-start(bf16[256,1024]{1,0:T(8,128)(2,1)S(1)} %collective-permute-done.13.refs_8_) | copy-start | bytes 1572868
  105.2 9.7 %collective-permute-start.17 = (bf16[144,1024]{1,0:T(8,128)(2,1)S(1)}, bf16[144,1024]{1,0:T(8,128)(2,1)S(1)}, u32[]{:S(2)}, u32[]{:S(2)}) collective-permute-start(bf16[144,1024]{1,0:T(8,128)(2,1)S(1)} %slice.59), channel_id=1, source_target_pairs={{24,0},{0,8},{8,16},{16,24},{25,1},{1,9},{9,17},{17,25},{26,2},{2,... | collective-permute-start | bytes 884744 | tf_op jit(solution)/shard_map/ppermute | solution.py:149
  105.2 8.0 %collective-permute-start.18 = (bf16[128,1024]{1,0:T(8,128)(2,1)}, bf16[128,1024]{1,0:T(8,128)(2,1)S(1)}, u32[]{:S(2)}, u32[]{:S(2)}) collective-permute-start(bf16[128,1024]{1,0:T(8,128)(2,1)} %slice.56), channel_id=1, source_target_pairs={{3,0},{0,1},{1,2},{2,3},{7,4},{4,5},{5,6},{6,7},{11,8},{8,9},{9,10... | collective-permute-start | bytes 786440 | tf_op jit(solution)/shard_map/ppermute | solution.py:149
  105.4 9.6 %copy-start.4 = (bf16[272,1024]{1,0:T(8,128)(2,1)}, bf16[272,1024]{1,0:T(8,128)(2,1)S(1)}, u32[]{:S(2)}) copy-start(bf16[272,1024]{1,0:T(8,128)(2,1)S(1)} %collective-permute-done.9.refs_7_) | copy-start | bytes 1671172
  105.4 9.6 %copy-start.5 = (bf16[272,1024]{1,0:T(8,128)(2,1)}, bf16[272,1024]{1,0:T(8,128)(2,1)S(1)}, u32[]{:S(2)}) copy-start(bf16[272,1024]{1,0:T(8,128)(2,1)S(1)} %collective-permute-done.14.refs_14_) | copy-start | bytes 1671172
  105.4 8.4 %collective-permute-start.16 = (bf16[128,1024]{1,0:T(8,128)(2,1)}, bf16[128,1024]{1,0:T(8,128)(2,1)S(1)}, u32[]{:S(2)}, u32[]{:S(2)}) collective-permute-start(bf16[128,1024]{1,0:T(8,128)(2,1)} %slice.58), channel_id=1, source_target_pairs={{8,0},{16,8},{24,16},{0,24},{9,1},{17,9},{25,17},{1,25},{10,2},{18... | collective-permute-start | bytes 786440 | tf_op jit(solution)/shard_map/ppermute | solution.py:149
  108.1 6.8 %collective-permute-start.19 = (bf16[128,1024]{1,0:T(8,128)(2,1)}, bf16[128,1024]{1,0:T(8,128)(2,1)S(1)}, u32[]{:S(2)}, u32[]{:S(2)}) collective-permute-start(bf16[128,1024]{1,0:T(8,128)(2,1)} %slice.53), channel_id=1, source_target_pairs={{1,0},{2,1},{3,2},{0,3},{5,4},{6,5},{7,6},{4,7},{9,8},{10,9},{11,1... | collective-permute-start | bytes 786440 | tf_op jit(solution)/shard_map/ppermute | solution.py:149
  113.2 1.8 %copy-start.8 = (bf16[128,1024]{1,0:T(8,128)(2,1)}, bf16[128,1024]{1,0:T(8,128)(2,1)S(1)}, u32[]{:S(2)}) copy-start(bf16[128,1024]{1,0:T(8,128)(2,1)S(1)} %collective-permute-done.18.refs_19_) | copy-start | bytes 786436
  113.7 1.3 copy-start.9
  114.9 0.7 copy-start.7
  114.9 0.8 copy-start.10
  134.9 22.5 %collective-permute-start.22 = (f32[16,128]{1,0:T(8,128)S(1)}, f32[16,128]{1,0:T(8,128)S(1)}, u32[]{:S(2)}, u32[]{:S(2)}) collective-permute-start(f32[16,128]{1,0:T(8,128)S(1)} %get-tuple-element.92), channel_id=1, source_target_pairs={{1,0},{2,1},{3,2},{0,3},{5,4},{6,5},{7,6},{4,7},{9,8},{10,9},{11,1... | collective-permute-start | bytes 24584 | tf_op jit(solution)/shard_map/ppermute | solution.py:149
  137.3 20.2 %collective-permute-start.21 = (f32[16,128]{1,0:T(8,128)S(1)}, f32[16,128]{1,0:T(8,128)S(1)}, u32[]{:S(2)}, u32[]{:S(2)}) collective-permute-start(f32[16,128]{1,0:T(8,128)S(1)} %get-tuple-element.91), channel_id=1, source_target_pairs={{2,0},{3,1},{0,2},{1,3},{6,4},{7,5},{4,6},{5,7},{10,8},{11,9},{8,1... | collective-permute-start | bytes 24584 | tf_op jit(solution)/shard_map/ppermute | solution.py:149
  137.3 20.2 %collective-permute-start.20 = (f32[16,128]{1,0:T(8,128)S(1)}, f32[16,128]{1,0:T(8,128)S(1)}, u32[]{:S(2)}, u32[]{:S(2)}) collective-permute-start(f32[16,128]{1,0:T(8,128)S(1)} %get-tuple-element.90), channel_id=1, source_target_pairs={{3,0},{0,1},{1,2},{2,3},{7,4},{4,5},{5,6},{6,7},{11,8},{8,9},{9,10... | collective-permute-start | bytes 24584 | tf_op jit(solution)/shard_map/ppermute | solution.py:149
  137.9 26.9 %all-to-all-start.1 = ((f32[16,4,128]{2,1,0:T(4,128)}), f32[16,4,128]{2,1,0:T(4,128)S(1)}, u32[]{:S(2)}, u32[]{:S(2)}) async-start(f32[16,4,128]{2,1,0:T(4,128)} %bitcast.5), calls=%async_computation.1 | async-start | bytes 65536 | tf_op jit(solution)/shard_map/all_to_all | solution.py:251
  157.5 7.4 %collective-permute-start.25 = (f32[4,128]{1,0:T(4,128)S(1)}, f32[4,128]{1,0:T(4,128)S(1)}, u32[]{:S(2)}, u32[]{:S(2)}) collective-permute-start(f32[4,128]{1,0:T(4,128)S(1)} %get-tuple-element.100), channel_id=1, source_target_pairs={{8,0},{16,8},{24,16},{0,24},{9,1},{17,9},{25,17},{1,25},{10,2},{18... | collective-permute-start | bytes 6152 | tf_op jit(solution)/shard_map/ppermute | solution.py:149
  157.6 7.3 %collective-permute-start.24 = (f32[4,128]{1,0:T(4,128)S(1)}, f32[4,128]{1,0:T(4,128)S(1)}, u32[]{:S(2)}, u32[]{:S(2)}) collective-permute-start(f32[4,128]{1,0:T(4,128)S(1)} %get-tuple-element.101), channel_id=1, source_target_pairs={{16,0},{24,8},{0,16},{8,24},{17,1},{25,9},{1,17},{9,25},{18,2},{26... | collective-permute-start | bytes 6152 | tf_op jit(solution)/shard_map/ppermute | solution.py:149
  159.3 5.6 %collective-permute-start.23 = (f32[4,128]{1,0:T(4,128)S(1)}, f32[4,128]{1,0:T(4,128)S(1)}, u32[]{:S(2)}, u32[]{:S(2)}) collective-permute-start(f32[4,128]{1,0:T(4,128)S(1)} %get-tuple-element.99), channel_id=1, source_target_pairs={{24,0},{0,8},{8,16},{16,24},{25,1},{1,9},{9,17},{17,25},{26,2},{2,... | collective-permute-start | bytes 6152 | tf_op jit(solution)/shard_map/ppermute | solution.py:149
Sparse Core Ops, SparseCore 0:
  9.2 100.5 all-gather.1

commit v3 on v2

v3 whole, which is shorter than its diff:
```python
import jax
import jax.numpy as jnp
from jax import lax
from jax.experimental import pallas as pl
from jax.experimental.pallas import tpu as pltpu
from jax.sharding import Mesh, PartitionSpec as P

epsilon = 1e-06
ROWS = 128
BLOCKS = 4
META = 16
HALF1 = 2 * ROWS + META
HALF2 = 2 * ROWS
FULL = HALF1 + HALF2
SLOTS = 8
DEPTH = 5
VMEM_LIMIT = 32 * 1024 * 1024


def unit_kernel(emb_ref, unit_ref):
    for block in range(BLOCKS):
        rows = emb_ref[block].astype(jnp.float32)
        scale = lax.rsqrt(jnp.sum(rows * rows, axis=-1, keepdims=True) + epsilon)
        unit_ref[block * ROWS : (block + 1) * ROWS, :] = (rows * scale).astype(jnp.bfloat16)


def message_kernel(unit_ref, meta_ref, full_ref):
    full_ref[: 2 * ROWS, :] = unit_ref[: 2 * ROWS, :]
    full_ref[2 * ROWS : HALF1, :] = meta_ref[...]
    full_ref[HALF1:, :] = unit_ref[2 * ROWS :, :]


def pair_kernel(right_at, meta_at, todo, block_of, used, place, left_tags, left_ref, *rest):
    refs = rest[:-15]
    left_out, *right_out = rest[-15:-10]
    left_buf, tags_buf, right_buf, right_meta, right_tags, even, odd, left_best, right_best, sems = rest[-10:]
    left_sems, right_sems = sems.at[0], sems.at[1]

    def each_right(j, act):
        for dy in range(4):
            ref, base = right_at[j // 4 * 4 + dy][j % 4]
            act(refs[ref].at[pl.ds(base, ROWS), :], right_buf.at[j, pl.ds(dy * ROWS, ROWS), :])

    def fetch_right(j):
        @pl.when(used[j] > 0)
        def _():
            each_right(j, lambda source, into: pltpu.make_async_copy(source, into, right_sems.at[j]).start())

    def each_left(i, act):
        slot = lax.rem(i, SLOTS)
        for h in range(2):
            unit = todo[2 * i + h]
            part = pl.ds(h * ROWS, ROWS)
            act(pltpu.make_async_copy(left_tags.at[unit], tags_buf.at[slot, part, :], left_sems.at[2 * SLOTS + slot * 2 + h]))

            @pl.when(unit < 64)
            def _():
                row = pl.multiple_of(unit * ROWS, ROWS)
                act(pltpu.make_async_copy(left_ref.at[pl.ds(row, ROWS), :], left_buf.at[slot, part, :], left_sems.at[slot * 2 + h]))

    count = used[16]
    for k in range(16):
        ref, row = meta_at[k]
        pltpu.make_async_copy(refs[ref].at[pl.ds(row, META), :], right_meta.at[k], right_sems.at[16]).start()
    for j in range(2):
        fetch_right(j)
    for i in range(SLOTS):

        @pl.when(i < count + 2)
        def _(i=i):
            each_left(jnp.int32(i), lambda copy: copy.start())

    for j in range(2, 16):
        fetch_right(j)
    left_best[...] = jnp.full(left_best.shape, -1.0, jnp.float32)
    right_best[...] = jnp.full(right_best.shape, -1.0, jnp.float32)
    pltpu.make_async_copy(right_meta, right_meta, right_sems.at[16]).wait()
    for k in range(16):
        row = right_meta[k, 0:1, : 4 * ROWS].astype(jnp.float32)
        row = jnp.where(row < 0.0, -2.0, row)
        for b in range(4):
            j = k // 4 * 4 + b
            right_tags[j : j + 1, k % 4 * ROWS : (k % 4 + 1) * ROWS] = row[:, b * ROWS : (b + 1) * ROWS]

    off_diagonal = lax.broadcasted_iota(jnp.int32, (ROWS, ROWS), 0) != lax.broadcasted_iota(jnp.int32, (ROWS, ROWS), 1)
    me = place[0]

    def arrive(i):
        each_left(i, lambda copy: copy.wait())
        j = block_of[i]
        before = block_of[jnp.maximum(i - 1, 0)]

        @pl.when((i < used[17]) & ((i == 0) | (j != before)))
        def _():
            pltpu.make_async_copy(right_buf.at[j], right_buf.at[j], right_sems.at[j]).wait()

    def multiply(i, into):
        into[...] = lax.dot_general(
            left_buf[lax.rem(i, SLOTS)], right_buf[block_of[i]], (((1,), (1,)), ((), ())), preferred_element_type=jnp.float32
        )

    def maxima(i, scores):
        slot, j = lax.rem(i, SLOTS), block_of[i]
        right_row = right_tags[pl.ds(j, 1), :]
        tops = [None] * 4
        for h in range(2):
            unit = todo[2 * i + h]
            tags = tags_buf[slot, h * ROWS : (h + 1) * ROWS, :]
            same = (j < 4) & (unit == me * 4 + j)
            best = None
            for dy in range(4):
                cols = slice(dy * ROWS, (dy + 1) * ROWS)
                keep = tags == right_row[:, cols]
                if dy == 0:
                    keep = keep & (off_diagonal | jnp.logical_not(same))
                masked = jnp.where(keep, scores[h * ROWS : (h + 1) * ROWS, cols], -1.0)
                best = masked if best is None else jnp.maximum(best, masked)
                top = jnp.max(masked, axis=0, keepdims=True)
                tops[dy] = top if tops[dy] is None else jnp.maximum(tops[dy], top)
            best = jnp.max(best.T, axis=0, keepdims=True)
            left_best[pl.ds(unit, 1), :] = jnp.maximum(left_best[pl.ds(unit, 1), :], best)
        right_best[pl.ds(j, 1), :] = jnp.maximum(right_best[pl.ds(j, 1), :], jnp.concatenate(tops, axis=1))

    def refill(i):
        @pl.when(i + SLOTS < count + 2)
        def _():
            each_left(i + SLOTS, lambda copy: copy.start())

    arrive(jnp.int32(0))
    multiply(jnp.int32(0), even)

    def two(q, carry):
        i = 2 * q
        arrive(i + 1)
        multiply(i + 1, odd)
        maxima(i, even)
        refill(i)
        arrive(i + 2)
        multiply(i + 2, even)
        maxima(i + 1, odd)
        refill(i + 1)
        return carry

    lax.fori_loop(0, count // 2, two, 0)
    each_left(count + 1, lambda copy: copy.wait())
    left_out[...] = left_best[0:64, :]
    for dy in range(4):
        right_out[dy][...] = right_best[:, dy * ROWS : (dy + 1) * ROWS]


def pair_maxima(todo, block_of, used, place, left_tags, left_rows, operands, right_at, meta_at):
    def kernel(*refs):
        pair_kernel(right_at, meta_at, *refs)

    smem, vmem, hbm = (pl.BlockSpec(memory_space=s) for s in (pltpu.SMEM, pltpu.VMEM, pltpu.HBM))
    return pl.pallas_call(
        kernel,
        out_shape=[jax.ShapeDtypeStruct((n, ROWS), jnp.float32) for n in (64, 16, 16, 16, 16)],
        in_specs=[smem] * 4 + [hbm] * (len(operands) + 2),
        out_specs=[vmem] * 5,
        scratch_shapes=[
            pltpu.VMEM((SLOTS, 2 * ROWS, 1024), jnp.bfloat16),
            pltpu.VMEM((SLOTS, 2 * ROWS, ROWS), jnp.float32),
            pltpu.VMEM((16, 4 * ROWS, 1024), jnp.bfloat16),
            pltpu.VMEM((16, META, 1024), jnp.bfloat16),
            pltpu.VMEM((16, 4 * ROWS), jnp.float32),
            pltpu.VMEM((2 * ROWS, 4 * ROWS), jnp.float32),
            pltpu.VMEM((2 * ROWS, 4 * ROWS), jnp.float32),
            pltpu.VMEM((72, ROWS), jnp.float32),
            pltpu.VMEM((16, 4 * ROWS), jnp.float32),
            pltpu.SemaphoreType.DMA((2, 4 * SLOTS)),
        ],
        compiler_params=pltpu.CompilerParams(vmem_limit_bytes=VMEM_LIMIT),
        name="pair_maxima",
    )(todo, block_of, used, place, *(pltpu.with_memory_space_constraint(v, pltpu.HBM) for v in (left_tags, left_rows, *operands)))


def shift(value, axis, by):
    size = lax.axis_size(axis)
    return lax.ppermute(value, axis, [((i + by) % size, i) for i in range(size)])


class Carrier:
    def __init__(self):
        self.last = {}

    def __call__(self, value, axis, by):
        if (axis, by) in self.last:
            before = self.last[axis, by]
            value, before[0] = lax.optimization_barrier((value, before[0]))
        self.last[axis, by] = cell = [shift(value, axis, by)]
        return cell


def gather_plane(own, extra):
    send = Carrier()
    xp, xm, yp, ym = ("x", 1), ("x", -1), ("y", 1), ("y", -1)
    whole = {(0, 0): [own]}
    whole[0, 1], whole[0, 3] = send(own, *yp), send(own, *ym)
    whole[1, 0], whole[3, 0] = send(own, *xp), send(own, *xm)
    whole[0, 1][0], extra = lax.optimization_barrier((whole[0, 1][0], extra))
    half = {}
    whole[1, 1], half["y", 0] = send(whole[0, 1][0], *xp), send(whole[0, 1][0][:HALF1], *yp)
    whole[3, 3], half["y", 1] = send(whole[0, 3][0], *xm), send(whole[0, 3][0][HALF1:], *ym)
    whole[3, 1], whole[1, 3] = send(whole[3, 0][0], *yp), send(whole[1, 0][0], *ym)
    half["x", 0], half["x", 1] = send(whole[1, 0][0][:HALF1], *xp), send(whole[3, 0][0][HALF1:], *xm)
    whole[1, 2], whole[3, 2] = send(whole[1, 1][0], *yp), send(whole[3, 3][0], *ym)
    whole[2, 3], whole[2, 1] = send(whole[1, 3][0], *xp), send(whole[3, 1][0], *xm)
    last = [
        send(whole[1, 2][0][:ROWS], *xp),
        send(whole[3, 2][0][ROWS:HALF1], *xm),
        send(whole[2, 3][0][HALF1 : HALF1 + ROWS], *ym),
        send(whole[2, 1][0][HALF1 + ROWS :], *yp),
    ]
    starts = (0, ROWS, HALF1, HALF1 + ROWS)
    parts = {key: [(v[0], at) for at in starts] for key, v in whole.items()}
    metas = {key: (v[0], 2 * ROWS) for key, v in whole.items()}
    for key, axis in (((2, 0), "x"), ((0, 2), "y")):
        h1, h2 = half[axis, 0][0], half[axis, 1][0]
        parts[key] = [(h1, 0), (h1, ROWS), (h2, 0), (h2, ROWS)]
        metas[key] = (h1, 2 * ROWS)
    parts[2, 2] = [(v[0], 0) for v in last]
    metas[2, 2] = (last[1][0], ROWS)
    return parts, metas, extra


def local(embeddings, cluster_ids, valid, pair_left, pair_right):
    my_z, my_x, my_c = (lax.axis_index(name) for name in ("z", "x", "c"))
    place = (my_z * 2 + my_c).astype(jnp.int32).reshape(1)
    limit = pltpu.CompilerParams(vmem_limit_bytes=VMEM_LIMIT)
    unit = pl.pallas_call(
        unit_kernel, out_shape=jax.ShapeDtypeStruct((4 * ROWS, 1024), jnp.bfloat16), compiler_params=limit, name="unit_rows"
    )(embeddings)
    unit, cluster_ids, pair_left = lax.optimization_barrier((unit, cluster_ids, pair_left))
    left_rows = lax.all_gather(unit, ("z", "c"), axis=0, tiled=True)
    labels = jnp.where(valid > 0, cluster_ids, -1).reshape(1, -1)
    lists = jnp.concatenate([labels, (pair_left % BLOCKS)[None], pair_right[None]], axis=1)
    meta = jnp.pad(lists.astype(jnp.bfloat16), ((0, META - 1), (0, 1024 - lists.shape[1])))
    full = pl.pallas_call(
        message_kernel, out_shape=jax.ShapeDtypeStruct((FULL, 1024), jnp.bfloat16), compiler_params=limit, name="message_rows"
    )(unit, meta)
    full, lists = lax.optimization_barrier((full, lists))
    left_lists = lax.all_to_all(jnp.broadcast_to(lists, (16, lists.shape[1])), ("z", "c"), 0, 0, tiled=True)
    parts, metas, left_lists = gather_plane(full, left_lists)

    left_tags = left_lists[:, :512].astype(jnp.float32).reshape(64, ROWS)
    a, b = left_lists[:, 512:544], left_lists[:, 544:]
    group = b // BLOCKS
    mine = (group // 8 == my_z) & (group % 2 == my_c)
    dx = ((group // 2) % 4 - my_x) % 4
    unit_of = (jnp.arange(16)[:, None] * BLOCKS + a)[:, :, None]
    block = jnp.where(mine, dx * BLOCKS + b % BLOCKS, -1)
    unit_of = jnp.max(jnp.where(block[:, :, None] == jnp.arange(16), unit_of + 1, 0), axis=1).T.reshape(256)
    listed = (unit_of > 0).reshape(16, 16)
    order = jnp.arange(16)
    rank = jnp.sum(listed[:, None, :] & (order[None, None, :] < order[None, :, None]), axis=2)
    steps = (jnp.sum(listed, axis=1) + 1) // 2
    first = jnp.sum(jnp.where(order[None, :] < jnp.arange(17)[:, None], steps[None, :], 0), axis=1)
    at = jnp.where(listed, 2 * first[:16, None] + rank, -1).reshape(256)
    todo = jnp.max(jnp.where(at == jnp.arange(88)[:, None], unit_of, 0), axis=1)
    todo = jnp.where(todo > 0, todo - 1, 64)
    block_of = jnp.minimum(jnp.sum(first[None, 1:] <= jnp.arange(44)[:, None], axis=1), 15)
    used = jnp.concatenate([steps, (first[16:] + 1) // 2 * 2, first[16:]])
    left_tags = jnp.pad(left_tags, ((0, 1), (0, 0)), constant_values=-3.0)
    left_tags = jnp.broadcast_to(left_tags[:, :, None], (65, ROWS, ROWS))

    operands, known, right_at, meta_at = [], {}, [], []

    def place_of(value):
        if id(value) not in known:
            known[id(value)] = len(operands)
            operands.append(value)
        return known[id(value)]

    for k in [(dx, dy) for dx in range(4) for dy in range(4)]:
        right_at.append([(place_of(value), base) for value, base in parts[k]])
        meta_at.append((place_of(metas[k][0]), metas[k][1]))
    left_best, *right_best = pair_maxima(todo, block_of, used, place, left_tags, left_rows, operands, right_at, meta_at)
    from_left = lax.all_to_all(left_best.reshape(16, BLOCKS, ROWS), ("z", "c"), 0, 0, tiled=True)
    own = right_best[0]
    for came in [shift(right_best[dy], "y", -dy) for dy in (1, 2, 3)]:
        own = jnp.maximum(own, came)
    best = own[:BLOCKS]
    for came in [shift(own[dx * BLOCKS : (dx + 1) * BLOCKS], "x", -dx) for dx in (1, 2, 3)]:
        best = jnp.maximum(best, came)
    return jnp.maximum(jnp.max(from_left, axis=0), best)


def solution(mesh):
    wide = Mesh(mesh.devices.reshape(8, 4, 2, 4), ("z", "x", "c", "y"))
    dp = ("z", "x", "c")
    placed = (P(dp, "y", None), P(dp, "y"), P(dp, "y"), P(dp), P(dp))
    return jax.shard_map(local, mesh=wide, in_specs=placed, out_specs=P(dp, "y"), check_vma=False)
```

time: 173 us -> 174 us (level)
  starting transfers between devices: 47 us -> 52.2 us
  waiting for transfers between devices: 56.3 us -> 51.3 us
  Pallas kernels: 21.7 us -> 19.3 us
    ppermute x26, starting transfers between devices: 27.5 us -> 34.8 us  [shift(): lax.ppermute(value, axis, [((i + by) % size, i) for i in range(size)])]
    ppermute x26, waiting for transfers between devices: 50.7 us -> 46.7 us  [shift(): lax.ppermute(value, axis, [((i + by) % size, i) for i in range(size)])]
    broadcast_in_dim x0 -> x1, local copies, waits for them, and re-layouts: none -> 2.65 us  [local(): left_tags = jnp.broadcast_to(left_tags[:, :, None], (65, ROWS, ROWS))]
    pallas_call x1, Pallas kernels: 19.2 us -> 16.7 us  [pair_maxima(): pl.pallas_call(kernel, out_shape=[jax.ShapeDtypeStruct((n, ROWS), jnp.flo...]
    all_to_all x1, starting transfers between devices: 19.5 us -> 17.4 us  [local(): lax.all_to_all(left_best.reshape(16, BLOCKS, ROWS), ('z', 'c'), 0, 0, til...]
    slice x4 -> x5, local copies, waits for them, and re-layouts: 5.51 us -> 6.09 us  [the longest x1 1.89 us: gather_plane(): whole[3, 0][0][HALF1:]]
  transfers between devices with their start and end apart: 28 -> 28, of which waited for: 13 -> 8; matrix products, arithmetic and copies ran while one was open for 8% -> 8% of each run, Pallas kernels for 1% -> 1%
where the time goes in v3:
time: 174 us
  starting transfers between devices  52.2 us (30%)
  waiting for transfers between devices  51.3 us (29%)
  Pallas kernels  19.3 us (11%)
  blocking collectives  17.9 us (10%)
  local copies, waits for them, and re-layouts  15.3 us (9%)
  between operations  14.4 us (8%)
  other arithmetic  3.27 us (2%)
    ppermute x26, waiting for transfers between devices, shift(): lax.ppermute(value, axis, [((i + by) % size, i) for i in range(size)])  46.7 us
    ppermute x26, starting transfers between devices, shift(): lax.ppermute(value, axis, [((i + by) % size, i) for i in range(size)])  34.8 us
    all_to_all x1, blocking collectives, local(): lax.all_to_all(jnp.broadcast_to(lists, (16, lists.shape[1])), ('z', 'c'),...  17.9 us
    all_to_all x1, starting transfers between devices, local(): lax.all_to_all(left_best.reshape(16, BLOCKS, ROWS), ('z', 'c'), 0, 0, til...  17.4 us
    pallas_call x1, Pallas kernels, pair_maxima(): pl.pallas_call(kernel, out_shape=[jax.ShapeDtypeStruct((n, ROWS), jnp.flo...  16.7 us
    all_to_all x1, waiting for transfers between devices, local(): lax.all_to_all(left_best.reshape(16, BLOCKS, ROWS), ('z', 'c'), 0, 0, til...  4.56 us
  transfers between devices with their start and end apart: 28, of which 8 were waited for; matrix products, arithmetic and copies ran while one was open for 8% of the time, Pallas kernels for 1%

profile of v3, /device:TPU:1, one launch (start us, length us, event | category | flops | bytes accessed | tf_op | source)
XLA Modules:
  0.0 173.7 jit_solution(16878990006125835024)
XLA Ops:
  6.5 1.2 copy-done.1
  7.8 1.3 unit_rows.1.unit_ref
  9.3 1.3 message_rows.1.refs_6_
  10.6 2.1 %collective-permute-start.2 = (bf16[528,1024]{1,0:T(8,128)(2,1)S(1)}, bf16[528,1024]{1,0:T(8,128)(2,1)}, u32[]{:S(2)}, u32[]{:S(2)}) collective-permute-start(bf16[528,1024]{1,0:T(8,128)(2,1)S(1)} %message_rows.1.refs_6_), channel_id=1, source_target_pairs={{24,0},{0,8},{8,16},{16,24},{25,1},{1,9},{9,17},{17,25},{26,2},{2,... | collective-permute-start | bytes 3244040 | tf_op jit(solution)/shard_map/ppermute | solution.py:180
  12.7 1.3 collective-permute-start.1
  14.0 1.4 collective-permute-start
  15.4 1.5 collective-permute-start.4
  16.9 17.9 %all_to_all.14 = s32[16,1,576]{2,1,0:T(1,128)S(1)} all-to-all(s32[16,1,576]{2,1,0:T(1,128)S(1)} %broadcast_in_dim.73), channel_id=1, replica_groups=mesh['z'=8,'x'=4,'c'=2,'y'=4] {'z','c'}, dimensions={0} | all-to-all | bytes 73728 | tf_op jit(solution)/shard_map/all_to_all | solution.py:243
  34.9 0.5 collective-permute-done.2.refs_23_
  35.4 2.8 %collective-permute-done.1.refs_10_ = bf16[528,1024]{1,0:T(8,128)(2,1)} collective-permute-done((bf16[528,1024]{1,0:T(8,128)(2,1)S(1)}, bf16[528,1024]{1,0:T(8,128)(2,1)}, u32[]{:S(2)}, u32[]{:S(2)}) %collective-permute-start.1) | collective-permute-done | bytes 1081376 | tf_op jit(solution)/shard_map/ppermute | solution.py:180
  38.2 1.6 collective-permute-start.7
  39.8 1.2 collective-permute-start.6
  41.0 0.9 slice.61
  41.8 2.5 %collective-permute-start.3 = (bf16[272,1024]{1,0:T(8,128)(2,1)}, bf16[272,1024]{1,0:T(8,128)(2,1)}, u32[]{:S(2)}, u32[]{:S(2)}) collective-permute-start(bf16[272,1024]{1,0:T(8,128)(2,1)} %slice.61), channel_id=1, source_target_pairs={{1,0},{2,1},{3,2},{0,3},{5,4},{6,5},{7,6},{4,7},{9,8},{10,9},{11,1... | collective-permute-start | bytes 1671176 | tf_op jit(solution)/shard_map/ppermute | solution.py:180
  44.4 1.9 %slice.73 = bf16[256,1024]{1,0:T(8,128)(2,1)} slice(bf16[528,1024]{1,0:T(8,128)(2,1)} %collective-permute-done.1.refs_10_), slice={[272:528], [0:1024]} | slice | bytes 1048576 | tf_op jit(solution)/shard_map/slice | solution.py:204
  46.3 12.0 %collective-permute-done.5.refs_9_ = bf16[256,1024]{1,0:T(8,128)(2,1)} collective-permute-done((bf16[256,1024]{1,0:T(8,128)(2,1)}, bf16[256,1024]{1,0:T(8,128)(2,1)}, u32[]{:S(2)}, u32[]{:S(2)}) %collective-permute-start.5) | collective-permute-done | bytes 524320 | tf_op jit(solution)/shard_map/ppermute | solution.py:180
  58.3 2.7 %collective-permute-start.10 = (bf16[528,1024]{1,0:T(8,128)(2,1)}, bf16[528,1024]{1,0:T(8,128)(2,1)}, u32[]{:S(2)}, u32[]{:S(2)}) collective-permute-start(bf16[528,1024]{1,0:T(8,128)(2,1)} %collective-permute-done.2.refs_23_), channel_id=1, source_target_pairs={{1,0},{2,1},{3,2},{0,3},{5,4},{6,5},{7,6},{4,7},{9,8},{10,9},{11,1... | collective-permute-start | bytes 3244040 | tf_op jit(solution)/shard_map/ppermute | solution.py:180
  61.0 1.9 %slice.64 = bf16[256,1024]{1,0:T(8,128)(2,1)} slice(bf16[528,1024]{1,0:T(8,128)(2,1)} %collective-permute-done.2.refs_23_), slice={[272:528], [0:1024]} | slice | bytes 1048576 | tf_op jit(solution)/shard_map/slice | solution.py:206
  62.9 0.9 slice.63
  63.9 0.3 select_reduce_fusion
  64.3 2.7 %collective-permute-start.14 = (bf16[272,1024]{1,0:T(8,128)(2,1)}, bf16[272,1024]{1,0:T(8,128)(2,1)}, u32[]{:S(2)}, u32[]{:S(2)}) collective-permute-start(bf16[272,1024]{1,0:T(8,128)(2,1)} %slice.63), channel_id=1, source_target_pairs={{8,0},{16,8},{24,16},{0,24},{9,1},{17,9},{25,17},{1,25},{10,2},{18... | collective-permute-start | bytes 1671176 | tf_op jit(solution)/shard_map/ppermute | solution.py:180
  67.1 0.6 slice.59
  68.5 0.4 convert_reduce_fusion
  68.9 12.3 %collective-permute-done.8.refs_14_ = bf16[528,1024]{1,0:T(8,128)(2,1)} collective-permute-done((bf16[528,1024]{1,0:T(8,128)(2,1)S(1)}, bf16[528,1024]{1,0:T(8,128)(2,1)}, u32[]{:S(2)}, u32[]{:S(2)}) %collective-permute-start.8) | collective-permute-done | bytes 1081376 | tf_op jit(solution)/shard_map/ppermute | solution.py:180
  81.2 1.2 collective-permute-start.15
  82.4 0.5 collective-permute-start.12
  82.9 2.7 %collective-permute-start.13 = (bf16[528,1024]{1,0:T(8,128)(2,1)}, bf16[528,1024]{1,0:T(8,128)(2,1)}, u32[]{:S(2)}, u32[]{:S(2)}) collective-permute-start(bf16[528,1024]{1,0:T(8,128)(2,1)} %collective-permute-done.6.refs_12_), channel_id=1, source_target_pairs={{1,0},{2,1},{3,2},{0,3},{5,4},{6,5},{7,6},{4,7},{9,8},{10,9},{11,1... | collective-permute-start | bytes 3244040 | tf_op jit(solution)/shard_map/ppermute | solution.py:180
  86.2 0.6 slice_convert_fusion
  86.8 16.7 %collective-permute-done.9.refs_25_ = bf16[528,1024]{1,0:T(8,128)(2,1)S(1)} collective-permute-done((bf16[528,1024]{1,0:T(8,128)(2,1)}, bf16[528,1024]{1,0:T(8,128)(2,1)S(1)}, u32[]{:S(2)}, u32[]{:S(2)}) %collective-permute-start.9) | collective-permute-done | bytes 1081376 | tf_op jit(solution)/shard_map/ppermute | solution.py:180
  103.5 0.8 slice.74
  104.3 0.3 collective-permute-done.12.refs_17_
  104.6 0.8 slice.66
  105.5 1.7 slice.75
  107.2 0.8 slice.68
  107.9 2.5 %collective-permute-start.16 = (bf16[128,1024]{1,0:T(8,128)(2,1)}, bf16[128,1024]{1,0:T(8,128)(2,1)S(1)}, u32[]{:S(2)}, u32[]{:S(2)}) collective-permute-start(bf16[128,1024]{1,0:T(8,128)(2,1)} %slice.75), channel_id=1, source_target_pairs={{8,0},{16,8},{24,16},{0,24},{9,1},{17,9},{25,17},{1,25},{10,2},{18... | collective-permute-start | bytes 786440 | tf_op jit(solution)/shard_map/ppermute | solution.py:180
  110.5 2.7 %collective-permute-start.19 = (bf16[128,1024]{1,0:T(8,128)(2,1)}, bf16[128,1024]{1,0:T(8,128)(2,1)S(1)}, u32[]{:S(2)}, u32[]{:S(2)}) collective-permute-start(bf16[128,1024]{1,0:T(8,128)(2,1)} %slice.66), channel_id=1, source_target_pairs={{1,0},{2,1},{3,2},{0,3},{5,4},{6,5},{7,6},{4,7},{9,8},{10,9},{11,1... | collective-permute-start | bytes 786440 | tf_op jit(solution)/shard_map/ppermute | solution.py:180
  113.1 0.7 pad_add_fusion.1.refs_2_
  113.8 0.8 reshape.123
  114.7 2.1 %collective-permute-done.19.refs_21_ = bf16[128,1024]{1,0:T(8,128)(2,1)S(1)} collective-permute-done((bf16[128,1024]{1,0:T(8,128)(2,1)}, bf16[128,1024]{1,0:T(8,128)(2,1)S(1)}, u32[]{:S(2)}, u32[]{:S(2)}) %collective-permute-start.19) | collective-permute-done | bytes 262176 | tf_op jit(solution)/shard_map/ppermute | solution.py:180
  116.8 2.7 %broadcast_in_dim.82.refs_4_ = f32[65,128,128]{2,1,0:T(8,128)} broadcast(f32[65,128]{1,0:T(8,128)S(1)} %pad.9), dimensions={0,1} | broadcast | bytes 4293120 | tf_op jit(solution)/shard_map/broadcast_in_dim | solution.py:265
  119.4 16.7 %pair_maxima.1 = (f32[64,128]{1,0:T(8,128)}, f32[16,128]{1,0:T(8,128)S(1)}, f32[16,128]{1,0:T(8,128)S(1)}, f32[16,128]{1,0:T(8,128)S(1)}, f32[16,128]{1,0:T(8,128)S(1)}) custom-call(s32[88]{0:T(128)S(1)} %compare_select_fusion.2.refs_0_, s32[44]{0:T(128)S(1)} %broadcast_minimum_fusion.refs_1_, s32[18]{0:T(128)S(1)} %pad_add_fusion.1.refs_2_, ...), custom_call_target="tpu_custom_call" | custom-call | tf_op jit(solution)/shard_map/pair_maxima/pallas_call | solution.py:156
  136.2 1.3 collective-permute-start.20
  137.4 3.4 %collective-permute-start.21 = (f32[16,128]{1,0:T(8,128)S(1)}, f32[16,128]{1,0:T(8,128)S(1)}, u32[]{:S(2)}, u32[]{:S(2)}) collective-permute-start(f32[16,128]{1,0:T(8,128)S(1)} %get-tuple-element.91), channel_id=1, source_target_pairs={{2,0},{3,1},{0,2},{1,3},{6,4},{7,5},{4,6},{5,7},{10,8},{11,9},{8,1... | collective-permute-start | bytes 24584 | tf_op jit(solution)/shard_map/ppermute | solution.py:180
  140.8 0.6 collective-permute-start.22
  141.4 17.4 %all-to-all-start.1 = ((f32[16,4,128]{2,1,0:T(4,128)}), f32[16,4,128]{2,1,0:T(4,128)S(1)}, u32[]{:S(2)}, u32[]{:S(2)}) async-start(f32[16,4,128]{2,1,0:T(4,128)} %bitcast.5), calls=%async_computation.1 | async-start | bytes 65536 | tf_op jit(solution)/shard_map/all_to_all | solution.py:279
  159.0 2.7 %collective-permute-start.25 = (f32[4,128]{1,0:T(4,128)S(1)}, f32[4,128]{1,0:T(4,128)S(1)}, u32[]{:S(2)}, u32[]{:S(2)}) collective-permute-start(f32[4,128]{1,0:T(4,128)S(1)} %get-tuple-element.100), channel_id=1, source_target_pairs={{8,0},{16,8},{24,16},{0,24},{9,1},{17,9},{25,17},{1,25},{10,2},{18... | collective-permute-start | bytes 6152 | tf_op jit(solution)/shard_map/ppermute | solution.py:180
  161.7 4.6 %all-to-all-done.1 = f32[16,4,128]{2,1,0:T(4,128)S(1)} async-done(((f32[16,4,128]{2,1,0:T(4,128)}), f32[16,4,128]{2,1,0:T(4,128)S(1)}, u32[]{:S(2)}, u32[]{:S(2)}) %all-to-all-start.1) | async-done | bytes 32800 | tf_op jit(solution)/shard_map/all_to_all | solution.py:279
  166.3 0.6 fusion.15
  (90 shorter events, 1.7 us)
Async XLA Ops:
  6.5 110.2 %all-gather.2.cloned.1.call-start = ((), (), s32[]{:S(2)}) async-start(), calls=%async_computation.2 | async-start | bytes 17825792 | tf_op jit(solution)/shard_map/all_gather | solution.py:235
  6.5 1.2 copy-start.1
  7.8 1.4 copy-start.15
  7.8 1.4 copy-start.10
  7.8 1.4 copy-start.11
  7.8 1.4 copy-start.12
  10.6 35.7 %copy-start = (bf16[528,1024]{1,0:T(8,128)(2,1)}, bf16[528,1024]{1,0:T(8,128)(2,1)S(1)}, u32[]{:S(2)}) copy-start(bf16[528,1024]{1,0:T(8,128)(2,1)S(1)} %message_rows.1.refs_6_) | copy-start | bytes 3244036
  10.6 24.8 %collective-permute-start.2 = (bf16[528,1024]{1,0:T(8,128)(2,1)S(1)}, bf16[528,1024]{1,0:T(8,128)(2,1)}, u32[]{:S(2)}, u32[]{:S(2)}) collective-permute-start(bf16[528,1024]{1,0:T(8,128)(2,1)S(1)} %message_rows.1.refs_6_), channel_id=1, source_target_pairs={{24,0},{0,8},{8,16},{16,24},{25,1},{1,9},{9,17},{17,25},{26,2},{2,... | collective-permute-start | bytes 3244040 | tf_op jit(solution)/shard_map/ppermute | solution.py:180
  12.7 25.5 %collective-permute-start.1 = (bf16[528,1024]{1,0:T(8,128)(2,1)S(1)}, bf16[528,1024]{1,0:T(8,128)(2,1)}, u32[]{:S(2)}, u32[]{:S(2)}) collective-permute-start(bf16[528,1024]{1,0:T(8,128)(2,1)S(1)} %message_rows.1.refs_6_), channel_id=1, source_target_pairs={{3,0},{0,1},{1,2},{2,3},{7,4},{4,5},{5,6},{6,7},{11,8},{8,9},{9,10... | collective-permute-start | bytes 3244040 | tf_op jit(solution)/shard_map/ppermute | solution.py:180
  14.0 25.8 %collective-permute-start = (bf16[528,1024]{1,0:T(8,128)(2,1)S(1)}, bf16[528,1024]{1,0:T(8,128)(2,1)S(1)}, u32[]{:S(2)}, u32[]{:S(2)}) collective-permute-start(bf16[528,1024]{1,0:T(8,128)(2,1)S(1)} %message_rows.1.refs_6_), channel_id=1, source_target_pairs={{1,0},{2,1},{3,2},{0,3},{5,4},{6,5},{7,6},{4,7},{9,8},{10,9},{11,1... | collective-permute-start | bytes 3244040 | tf_op jit(solution)/shard_map/ppermute | solution.py:180
  15.4 24.3 %collective-permute-start.4 = (bf16[528,1024]{1,0:T(8,128)(2,1)S(1)}, bf16[528,1024]{1,0:T(8,128)(2,1)S(1)}, u32[]{:S(2)}, u32[]{:S(2)}) collective-permute-start(bf16[528,1024]{1,0:T(8,128)(2,1)S(1)} %message_rows.1.refs_6_), channel_id=1, source_target_pairs={{8,0},{16,8},{24,16},{0,24},{9,1},{17,9},{25,17},{1,25},{10,2},{18... | collective-permute-start | bytes 3244040 | tf_op jit(solution)/shard_map/ppermute | solution.py:180
  38.2 26.0 %collective-permute-start.7 = (bf16[528,1024]{1,0:T(8,128)(2,1)}, bf16[528,1024]{1,0:T(8,128)(2,1)}, u32[]{:S(2)}, u32[]{:S(2)}) collective-permute-start(bf16[528,1024]{1,0:T(8,128)(2,1)} %collective-permute-done.1.refs_10_), channel_id=1, source_target_pairs={{24,0},{0,8},{8,16},{16,24},{25,1},{1,9},{9,17},{17,25},{26,2},{2,... | collective-permute-start | bytes 3244040 | tf_op jit(solution)/shard_map/ppermute | solution.py:180
  39.8 6.5 %copy-start.2 = (bf16[528,1024]{1,0:T(8,128)(2,1)}, bf16[528,1024]{1,0:T(8,128)(2,1)S(1)}, u32[]{:S(2)}) copy-start(bf16[528,1024]{1,0:T(8,128)(2,1)S(1)} %collective-permute-done.refs_7_) | copy-start | bytes 3244036
  39.8 23.1 %copy-start.3 = (bf16[528,1024]{1,0:T(8,128)(2,1)}, bf16[528,1024]{1,0:T(8,128)(2,1)S(1)}, u32[]{:S(2)}) copy-start(bf16[528,1024]{1,0:T(8,128)(2,1)S(1)} %collective-permute-done.4.refs_11_) | copy-start | bytes 3244036
  39.8 24.5 %collective-permute-start.6 = (bf16[528,1024]{1,0:T(8,128)(2,1)S(1)}, bf16[528,1024]{1,0:T(8,128)(2,1)}, u32[]{:S(2)}, u32[]{:S(2)}) collective-permute-start(bf16[528,1024]{1,0:T(8,128)(2,1)S(1)} %collective-permute-done.refs_7_), channel_id=1, source_target_pairs={{8,0},{16,8},{24,16},{0,24},{9,1},{17,9},{25,17},{1,25},{10,2},{18... | collective-permute-start | bytes 3244040 | tf_op jit(solution)/shard_map/ppermute | solution.py:180
  41.8 16.5 %collective-permute-start.3 = (bf16[272,1024]{1,0:T(8,128)(2,1)}, bf16[272,1024]{1,0:T(8,128)(2,1)}, u32[]{:S(2)}, u32[]{:S(2)}) collective-permute-start(bf16[272,1024]{1,0:T(8,128)(2,1)} %slice.61), channel_id=1, source_target_pairs={{1,0},{2,1},{3,2},{0,3},{5,4},{6,5},{7,6},{4,7},{9,8},{10,9},{11,1... | collective-permute-start | bytes 1671176 | tf_op jit(solution)/shard_map/ppermute | solution.py:180
  46.3 12.0 %collective-permute-start.5 = (bf16[256,1024]{1,0:T(8,128)(2,1)}, bf16[256,1024]{1,0:T(8,128)(2,1)}, u32[]{:S(2)}, u32[]{:S(2)}) collective-permute-start(bf16[256,1024]{1,0:T(8,128)(2,1)} %slice.73), channel_id=1, source_target_pairs={{3,0},{0,1},{1,2},{2,3},{7,4},{4,5},{5,6},{6,7},{11,8},{8,9},{9,10... | collective-permute-start | bytes 1572872 | tf_op jit(solution)/shard_map/ppermute | solution.py:180
  58.3 22.9 %collective-permute-start.8 = (bf16[528,1024]{1,0:T(8,128)(2,1)S(1)}, bf16[528,1024]{1,0:T(8,128)(2,1)}, u32[]{:S(2)}, u32[]{:S(2)}) collective-permute-start(bf16[528,1024]{1,0:T(8,128)(2,1)S(1)} %collective-permute-done.4.refs_11_), channel_id=1, source_target_pairs={{3,0},{0,1},{1,2},{2,3},{7,4},{4,5},{5,6},{6,7},{11,8},{8,9},{9,10... | collective-permute-start | bytes 3244040 | tf_op jit(solution)/shard_map/ppermute | solution.py:180
  58.3 22.9 %collective-permute-start.10 = (bf16[528,1024]{1,0:T(8,128)(2,1)}, bf16[528,1024]{1,0:T(8,128)(2,1)}, u32[]{:S(2)}, u32[]{:S(2)}) collective-permute-start(bf16[528,1024]{1,0:T(8,128)(2,1)} %collective-permute-done.2.refs_23_), channel_id=1, source_target_pairs={{1,0},{2,1},{3,2},{0,3},{5,4},{6,5},{7,6},{4,7},{9,8},{10,9},{11,1... | collective-permute-start | bytes 3244040 | tf_op jit(solution)/shard_map/ppermute | solution.py:180
  64.2 16.9 %collective-permute-start.11 = (bf16[256,1024]{1,0:T(8,128)(2,1)}, bf16[256,1024]{1,0:T(8,128)(2,1)}, u32[]{:S(2)}, u32[]{:S(2)}) collective-permute-start(bf16[256,1024]{1,0:T(8,128)(2,1)} %slice.64), channel_id=1, source_target_pairs={{24,0},{0,8},{8,16},{16,24},{25,1},{1,9},{9,17},{17,25},{26,2},{2,... | collective-permute-start | bytes 1572872 | tf_op jit(solution)/shard_map/ppermute | solution.py:180
  64.3 16.8 %collective-permute-start.14 = (bf16[272,1024]{1,0:T(8,128)(2,1)}, bf16[272,1024]{1,0:T(8,128)(2,1)}, u32[]{:S(2)}, u32[]{:S(2)}) collective-permute-start(bf16[272,1024]{1,0:T(8,128)(2,1)} %slice.63), channel_id=1, source_target_pairs={{8,0},{16,8},{24,16},{0,24},{9,1},{17,9},{25,17},{1,25},{10,2},{18... | collective-permute-start | bytes 1671176 | tf_op jit(solution)/shard_map/ppermute | solution.py:180
  67.0 1.3 copy-start.13
  81.2 22.3 %collective-permute-start.9 = (bf16[528,1024]{1,0:T(8,128)(2,1)}, bf16[528,1024]{1,0:T(8,128)(2,1)S(1)}, u32[]{:S(2)}, u32[]{:S(2)}) collective-permute-start(bf16[528,1024]{1,0:T(8,128)(2,1)} %collective-permute-done.7.refs_26_), channel_id=1, source_target_pairs={{3,0},{0,1},{1,2},{2,3},{7,4},{4,5},{5,6},{6,7},{11,8},{8,9},{9,10... | collective-permute-start | bytes 3244040 | tf_op jit(solution)/shard_map/ppermute | solution.py:180
  81.2 26.0 %collective-permute-start.15 = (bf16[528,1024]{1,0:T(8,128)(2,1)}, bf16[528,1024]{1,0:T(8,128)(2,1)S(1)}, u32[]{:S(2)}, u32[]{:S(2)}) collective-permute-start(bf16[528,1024]{1,0:T(8,128)(2,1)} %collective-permute-done.8.refs_14_), channel_id=1, source_target_pairs={{8,0},{16,8},{24,16},{0,24},{9,1},{17,9},{25,17},{1,25},{10,2},{18... | collective-permute-start | bytes 3244040 | tf_op jit(solution)/shard_map/ppermute | solution.py:180
  82.4 22.1 %collective-permute-start.12 = (bf16[528,1024]{1,0:T(8,128)(2,1)}, bf16[528,1024]{1,0:T(8,128)(2,1)S(1)}, u32[]{:S(2)}, u32[]{:S(2)}) collective-permute-start(bf16[528,1024]{1,0:T(8,128)(2,1)} %collective-permute-done.10.refs_24_), channel_id=1, source_target_pairs={{24,0},{0,8},{8,16},{16,24},{25,1},{1,9},{9,17},{17,25},{26,2},{2,... | collective-permute-start | bytes 3244040 | tf_op jit(solution)/shard_map/ppermute | solution.py:180
  82.9 22.6 %collective-permute-start.13 = (bf16[528,1024]{1,0:T(8,128)(2,1)}, bf16[528,1024]{1,0:T(8,128)(2,1)}, u32[]{:S(2)}, u32[]{:S(2)}) collective-permute-start(bf16[528,1024]{1,0:T(8,128)(2,1)} %collective-permute-done.6.refs_12_), channel_id=1, source_target_pairs={{1,0},{2,1},{3,2},{0,3},{5,4},{6,5},{7,6},{4,7},{9,8},{10,9},{11,1... | collective-permute-start | bytes 3244040 | tf_op jit(solution)/shard_map/ppermute | solution.py:180
  86.8 26.3 %copy-start.14 = (s32[16]{0:T(128)S(1)}, s32[16]{0:T(128)}, u32[]{:S(2)}) copy-start(s32[16]{0:T(128)} %copy-done.13) | copy-start | bytes 196
  103.5 4.4 %copy-start.4 = (bf16[528,1024]{1,0:T(8,128)(2,1)}, bf16[528,1024]{1,0:T(8,128)(2,1)S(1)}, u32[]{:S(2)}) copy-start(bf16[528,1024]{1,0:T(8,128)(2,1)S(1)} %collective-permute-done.9.refs_25_) | copy-start | bytes 3244036
  104.6 14.9 %copy-start.6 = (bf16[528,1024]{1,0:T(8,128)(2,1)}, bf16[528,1024]{1,0:T(8,128)(2,1)S(1)}, u32[]{:S(2)}) copy-start(bf16[528,1024]{1,0:T(8,128)(2,1)S(1)} %collective-permute-done.12.refs_17_) | copy-start | bytes 3244036
  105.3 11.4 %collective-permute-start.17 = (bf16[144,1024]{1,0:T(8,128)(2,1)}, bf16[144,1024]{1,0:T(8,128)(2,1)}, u32[]{:S(2)}, u32[]{:S(2)}) collective-permute-start(bf16[144,1024]{1,0:T(8,128)(2,1)} %slice.74), channel_id=1, source_target_pairs={{24,0},{0,8},{8,16},{16,24},{25,1},{1,9},{9,17},{17,25},{26,2},{2,... | collective-permute-start | bytes 884744 | tf_op jit(solution)/shard_map/ppermute | solution.py:180
  107.2 12.2 %copy-start.5 = (bf16[528,1024]{1,0:T(8,128)(2,1)}, bf16[528,1024]{1,0:T(8,128)(2,1)S(1)}, u32[]{:S(2)}) copy-start(bf16[528,1024]{1,0:T(8,128)(2,1)S(1)} %collective-permute-done.15.refs_22_) | copy-start | bytes 3244036
  107.9 6.7 %collective-permute-start.18 = (bf16[128,1024]{1,0:T(8,128)(2,1)}, bf16[128,1024]{1,0:T(8,128)(2,1)S(1)}, u32[]{:S(2)}, u32[]{:S(2)}) collective-permute-start(bf16[128,1024]{1,0:T(8,128)(2,1)} %slice.68), channel_id=1, source_target_pairs={{3,0},{0,1},{1,2},{2,3},{7,4},{4,5},{5,6},{6,7},{11,8},{8,9},{9,10... | collective-permute-start | bytes 786440 | tf_op jit(solution)/shard_map/ppermute | solution.py:180
  107.9 6.7 %collective-permute-start.16 = (bf16[128,1024]{1,0:T(8,128)(2,1)}, bf16[128,1024]{1,0:T(8,128)(2,1)S(1)}, u32[]{:S(2)}, u32[]{:S(2)}) collective-permute-start(bf16[128,1024]{1,0:T(8,128)(2,1)} %slice.75), channel_id=1, source_target_pairs={{8,0},{16,8},{24,16},{0,24},{9,1},{17,9},{25,17},{1,25},{10,2},{18... | collective-permute-start | bytes 786440 | tf_op jit(solution)/shard_map/ppermute | solution.py:180
  110.5 6.3 %collective-permute-start.19 = (bf16[128,1024]{1,0:T(8,128)(2,1)}, bf16[128,1024]{1,0:T(8,128)(2,1)S(1)}, u32[]{:S(2)}, u32[]{:S(2)}) collective-permute-start(bf16[128,1024]{1,0:T(8,128)(2,1)} %slice.66), channel_id=1, source_target_pairs={{1,0},{2,1},{3,2},{0,3},{5,4},{6,5},{7,6},{4,7},{9,8},{10,9},{11,1... | collective-permute-start | bytes 786440 | tf_op jit(solution)/shard_map/ppermute | solution.py:180
  114.6 4.8 %copy-start.7 = (bf16[128,1024]{1,0:T(8,128)(2,1)}, bf16[128,1024]{1,0:T(8,128)(2,1)S(1)}, u32[]{:S(2)}) copy-start(bf16[128,1024]{1,0:T(8,128)(2,1)S(1)} %collective-permute-done.18.refs_20_) | copy-start | bytes 786436
  114.7 4.8 %copy-start.8 = (bf16[128,1024]{1,0:T(8,128)(2,1)}, bf16[128,1024]{1,0:T(8,128)(2,1)S(1)}, u32[]{:S(2)}) copy-start(bf16[128,1024]{1,0:T(8,128)(2,1)S(1)} %collective-permute-done.16.refs_18_) | copy-start | bytes 786436
  116.8 2.7 %copy-start.9 = (bf16[128,1024]{1,0:T(8,128)(2,1)}, bf16[128,1024]{1,0:T(8,128)(2,1)S(1)}, u32[]{:S(2)}) copy-start(bf16[128,1024]{1,0:T(8,128)(2,1)S(1)} %collective-permute-done.19.refs_21_) | copy-start | bytes 786436
  136.2 22.7 %collective-permute-start.20 = (f32[16,128]{1,0:T(8,128)S(1)}, f32[16,128]{1,0:T(8,128)S(1)}, u32[]{:S(2)}, u32[]{:S(2)}) collective-permute-start(f32[16,128]{1,0:T(8,128)S(1)} %get-tuple-element.90), channel_id=1, source_target_pairs={{3,0},{0,1},{1,2},{2,3},{7,4},{4,5},{5,6},{6,7},{11,8},{8,9},{9,10... | collective-permute-start | bytes 24584 | tf_op jit(solution)/shard_map/ppermute | solution.py:180
  137.4 21.4 %collective-permute-start.21 = (f32[16,128]{1,0:T(8,128)S(1)}, f32[16,128]{1,0:T(8,128)S(1)}, u32[]{:S(2)}, u32[]{:S(2)}) collective-permute-start(f32[16,128]{1,0:T(8,128)S(1)} %get-tuple-element.91), channel_id=1, source_target_pairs={{2,0},{3,1},{0,2},{1,3},{6,4},{7,5},{4,6},{5,7},{10,8},{11,9},{8,1... | collective-permute-start | bytes 24584 | tf_op jit(solution)/shard_map/ppermute | solution.py:180
  140.8 18.0 %collective-permute-start.22 = (f32[16,128]{1,0:T(8,128)S(1)}, f32[16,128]{1,0:T(8,128)S(1)}, u32[]{:S(2)}, u32[]{:S(2)}) collective-permute-start(f32[16,128]{1,0:T(8,128)S(1)} %get-tuple-element.92), channel_id=1, source_target_pairs={{1,0},{2,1},{3,2},{0,3},{5,4},{6,5},{7,6},{4,7},{9,8},{10,9},{11,1... | collective-permute-start | bytes 24584 | tf_op jit(solution)/shard_map/ppermute | solution.py:180
  141.4 24.8 %all-to-all-start.1 = ((f32[16,4,128]{2,1,0:T(4,128)}), f32[16,4,128]{2,1,0:T(4,128)S(1)}, u32[]{:S(2)}, u32[]{:S(2)}) async-start(f32[16,4,128]{2,1,0:T(4,128)} %bitcast.5), calls=%async_computation.1 | async-start | bytes 65536 | tf_op jit(solution)/shard_map/all_to_all | solution.py:279
  158.9 7.4 %collective-permute-start.23 = (f32[4,128]{1,0:T(4,128)S(1)}, f32[4,128]{1,0:T(4,128)S(1)}, u32[]{:S(2)}, u32[]{:S(2)}) collective-permute-start(f32[4,128]{1,0:T(4,128)S(1)} %get-tuple-element.99), channel_id=1, source_target_pairs={{24,0},{0,8},{8,16},{16,24},{25,1},{1,9},{9,17},{17,25},{26,2},{2,... | collective-permute-start | bytes 6152 | tf_op jit(solution)/shard_map/ppermute | solution.py:180
  159.0 7.3 %collective-permute-start.25 = (f32[4,128]{1,0:T(4,128)S(1)}, f32[4,128]{1,0:T(4,128)S(1)}, u32[]{:S(2)}, u32[]{:S(2)}) collective-permute-start(f32[4,128]{1,0:T(4,128)S(1)} %get-tuple-element.100), channel_id=1, source_target_pairs={{8,0},{16,8},{24,16},{0,24},{9,1},{17,9},{25,17},{1,25},{10,2},{18... | collective-permute-start | bytes 6152 | tf_op jit(solution)/shard_map/ppermute | solution.py:180
  161.7 4.6 %collective-permute-start.24 = (f32[4,128]{1,0:T(4,128)S(1)}, f32[4,128]{1,0:T(4,128)S(1)}, u32[]{:S(2)}, u32[]{:S(2)}) collective-permute-start(f32[4,128]{1,0:T(4,128)S(1)} %get-tuple-element.101), channel_id=1, source_target_pairs={{16,0},{24,8},{0,16},{8,24},{17,1},{25,9},{1,17},{9,25},{18,2},{26... | collective-permute-start | bytes 6152 | tf_op jit(solution)/shard_map/ppermute | solution.py:180
Sparse Core Ops, SparseCore 0:
  9.2 100.5 all-gather.1

commit v4 on v3

--- a/solution.py
+++ b/solution.py
@@ -192,20 +192,21 @@
         return cell
 
 
-def gather_plane(own, extra):
+def gather_plane(own, extra, make_beside):
     send = Carrier()
     xp, xm, yp, ym = ("x", 1), ("x", -1), ("y", 1), ("y", -1)
     whole = {(0, 0): [own]}
     whole[0, 1], whole[0, 3] = send(own, *yp), send(own, *ym)
     whole[1, 0], whole[3, 0] = send(own, *xp), send(own, *xm)
     whole[0, 1][0], extra = lax.optimization_barrier((whole[0, 1][0], extra))
-    half = {}
-    whole[1, 1], half["y", 0] = send(whole[0, 1][0], *xp), send(whole[0, 1][0][:HALF1], *yp)
-    whole[3, 3], half["y", 1] = send(whole[0, 3][0], *xm), send(whole[0, 3][0][HALF1:], *ym)
+    whole[1, 1], whole[3, 3] = send(whole[0, 1][0], *xp), send(whole[0, 3][0], *xm)
     whole[3, 1], whole[1, 3] = send(whole[3, 0][0], *yp), send(whole[1, 0][0], *ym)
-    half["x", 0], half["x", 1] = send(whole[1, 0][0][:HALF1], *xp), send(whole[3, 0][0][HALF1:], *xm)
+    cut = [whole[1, 0][0][:HALF1], whole[3, 0][0][HALF1:], whole[0, 1][0][:HALF1], whole[0, 3][0][HALF1:]]
+    cut, whole[1, 1][0], beside = lax.optimization_barrier((cut, whole[1, 1][0], make_beside(extra)))
+    half = {("x", 0): send(cut[0], *xp), ("x", 1): send(cut[1], *xm)}
     whole[1, 2], whole[3, 2] = send(whole[1, 1][0], *yp), send(whole[3, 3][0], *ym)
     whole[2, 3], whole[2, 1] = send(whole[1, 3][0], *xp), send(whole[3, 1][0], *xm)
+    half["y", 0], half["y", 1] = send(cut[2], *yp), send(cut[3], *ym)
     last = [
         send(whole[1, 2][0][:ROWS], *xp),
         send(whole[3, 2][0][ROWS:HALF1], *xm),
@@ -221,28 +222,12 @@
         metas[key] = (h1, 2 * ROWS)
     parts[2, 2] = [(v[0], 0) for v in last]
     metas[2, 2] = (last[1][0], ROWS)
-    return parts, metas, extra
-
-
-def local(embeddings, cluster_ids, valid, pair_left, pair_right):
+    return parts, metas, beside
+
+
+def pair_lists(left_lists):
     my_z, my_x, my_c = (lax.axis_index(name) for name in ("z", "x", "c"))
     place = (my_z * 2 + my_c).astype(jnp.int32).reshape(1)
-    limit = pltpu.CompilerParams(vmem_limit_bytes=VMEM_LIMIT)
-    unit = pl.pallas_call(
-        unit_kernel, out_shape=jax.ShapeDtypeStruct((4 * ROWS, 1024), jnp.bfloat16), compiler_params=limit, name="unit_rows"
-    )(embeddings)
-    unit, cluster_ids, pair_left = lax.optimization_barrier((unit, cluster_ids, pair_left))
-    left_rows = lax.all_gather(unit, ("z", "c"), axis=0, tiled=True)
-    labels = jnp.where(valid > 0, cluster_ids, -1).reshape(1, -1)
-    lists = jnp.concatenate([labels, (pair_left % BLOCKS)[None], pair_right[None]], axis=1)
-    meta = jnp.pad(lists.astype(jnp.bfloat16), ((0, META - 1), (0, 1024 - lists.shape[1])))
-    full = pl.pallas_call(
-        message_kernel, out_shape=jax.ShapeDtypeStruct((FULL, 1024), jnp.bfloat16), compiler_params=limit, name="message_rows"
-    )(unit, meta)
-    full, lists = lax.optimization_barrier((full, lists))
-    left_lists = lax.all_to_all(jnp.broadcast_to(lists, (16, lists.shape[1])), ("z", "c"), 0, 0, tiled=True)
-    parts, metas, left_lists = gather_plane(full, left_lists)
-
     left_tags = left_lists[:, :512].astype(jnp.float32).reshape(64, ROWS)
     a, b = left_lists[:, 512:544], left_lists[:, 544:]
     group = b // BLOCKS
@@ -263,6 +248,25 @@
     used = jnp.concatenate([steps, (first[16:] + 1) // 2 * 2, first[16:]])
     left_tags = jnp.pad(left_tags, ((0, 1), (0, 0)), constant_values=-3.0)
     left_tags = jnp.broadcast_to(left_tags[:, :, None], (65, ROWS, ROWS))
+    return todo, block_of, used, place, left_tags
+
+
+def local(embeddings, cluster_ids, valid, pair_left, pair_right):
+    limit = pltpu.CompilerParams(vmem_limit_bytes=VMEM_LIMIT)
+    unit = pl.pallas_call(
+        unit_kernel, out_shape=jax.ShapeDtypeStruct((4 * ROWS, 1024), jnp.bfloat16), compiler_params=limit, name="unit_rows"
+    )(embeddings)
+    unit, cluster_ids, pair_left = lax.optimization_barrier((unit, cluster_ids, pair_left))
+    left_rows = lax.all_gather(unit, ("z", "c"), axis=0, tiled=True)
+    labels = jnp.where(valid > 0, cluster_ids, -1).reshape(1, -1)
+    lists = jnp.concatenate([labels, (pair_left % BLOCKS)[None], pair_right[None]], axis=1)
+    meta = jnp.pad(lists.astype(jnp.bfloat16), ((0, META - 1), (0, 1024 - lists.shape[1])))
+    full = pl.pallas_call(
+        message_kernel, out_shape=jax.ShapeDtypeStruct((FULL, 1024), jnp.bfloat16), compiler_params=limit, name="message_rows"
+    )(unit, meta)
+    full, lists = lax.optimization_barrier((full, lists))
+    left_lists = lax.all_to_all(jnp.broadcast_to(lists, (16, lists.shape[1])), ("z", "c"), 0, 0, tiled=True)
+    parts, metas, beside = gather_plane(full, left_lists, pair_lists)
 
     operands, known, right_at, meta_at = [], {}, [], []
 
@@ -275,7 +279,7 @@
     for k in [(dx, dy) for dx in range(4) for dy in range(4)]:
         right_at.append([(place_of(value), base) for value, base in parts[k]])
         meta_at.append((place_of(metas[k][0]), metas[k][1]))
-    left_best, *right_best = pair_maxima(todo, block_of, used, place, left_tags, left_rows, operands, right_at, meta_at)
+    left_best, *right_best = pair_maxima(*beside, left_rows, operands, right_at, meta_at)
     from_left = lax.all_to_all(left_best.reshape(16, BLOCKS, ROWS), ("z", "c"), 0, 0, tiled=True)
     own = right_best[0]
     for came in [shift(right_best[dy], "y", -dy) for dy in (1, 2, 3)]:

time: 174 us -> 169 us (0.971)
  blocking collectives: 17.9 us -> 0 us
  starting transfers between devices: 52.2 us -> 65 us
  waiting for transfers between devices: 51.3 us -> 56.9 us
  local copies, waits for them, and re-layouts: 15.3 us -> 11.6 us
  Pallas kernels: 19.3 us -> 16.3 us
    all_to_all x1 -> x0, blocking collectives: 17.9 us -> none  [local(): lax.all_to_all(jnp.broadcast_to(lists, (16, lists.shape[1])), ('z', 'c'),...]
    all_to_all x0 -> x1, starting transfers between devices: none -> 10.2 us  [local(): lax.all_to_all(jnp.broadcast_to(lists, (16, lists.shape[1])), ('z', 'c'),...]
    all_to_all x0 -> x1, waiting for transfers between devices: none -> 7.9 us  [local(): lax.all_to_all(jnp.broadcast_to(lists, (16, lists.shape[1])), ('z', 'c'),...]
    pallas_call x1, Pallas kernels: 16.7 us -> 13.7 us  [pair_maxima(): pl.pallas_call(kernel, out_shape=[jax.ShapeDtypeStruct((n, ROWS), jnp.flo...]
    all_to_all x1, starting transfers between devices: 17.4 us -> 20.3 us  [local(): lax.all_to_all(left_best.reshape(16, BLOCKS, ROWS), ('z', 'c'), 0, 0, til...]
    ppermute x26, waiting for transfers between devices: 46.7 us -> 44.5 us  [shift(): lax.ppermute(value, axis, [((i + by) % size, i) for i in range(size)])]
    unnamed x33 -> x41, local copies, waits for them, and re-layouts: 1.29 us -> 3.36 us
  transfers between devices with their start and end apart: 28 -> 29, of which waited for: 8 -> 9; matrix products, arithmetic and copies ran while one was open for 8% -> 6% of each run, Pallas kernels for 1% -> 1%
where the time goes in v4:
time: 169 us; the launch traced here: 167 us
  starting transfers between devices  65 us (38%)
  waiting for transfers between devices  56.9 us (34%)
  Pallas kernels  16.3 us (10%)
  between operations  14.4 us (9%)
  local copies, waits for them, and re-layouts  11.6 us (7%)
  other arithmetic  2.68 us (2%)
    ppermute x26, waiting for transfers between devices, shift(): lax.ppermute(value, axis, [((i + by) % size, i) for i in range(size)])  44.5 us
    ppermute x26, starting transfers between devices, shift(): lax.ppermute(value, axis, [((i + by) % size, i) for i in range(size)])  34.5 us
    all_to_all x1, starting transfers between devices, local(): lax.all_to_all(left_best.reshape(16, BLOCKS, ROWS), ('z', 'c'), 0, 0, til...  20.3 us
    pallas_call x1, Pallas kernels, pair_maxima(): pl.pallas_call(kernel, out_shape=[jax.ShapeDtypeStruct((n, ROWS), jnp.flo...  13.7 us
    all_to_all x1, starting transfers between devices, local(): lax.all_to_all(jnp.broadcast_to(lists, (16, lists.shape[1])), ('z', 'c'),...  10.2 us
    all_to_all x1, waiting for transfers between devices, local(): lax.all_to_all(jnp.broadcast_to(lists, (16, lists.shape[1])), ('z', 'c'),...  7.9 us
    all_to_all x1, waiting for transfers between devices, local(): lax.all_to_all(left_best.reshape(16, BLOCKS, ROWS), ('z', 'c'), 0, 0, til...  4.48 us
  transfers between devices with their start and end apart: 29, of which 9 were waited for; matrix products, arithmetic and copies ran while one was open for 6% of the time, Pallas kernels for 1%

profile of v4, /device:TPU:1, one launch (start us, length us, event | category | flops | bytes accessed | tf_op | source)
XLA Modules:
  0.0 167.0 jit_solution(9205172073020530928)
XLA Ops:
  6.5 1.2 copy-done.1
  7.8 1.3 unit_rows.1.unit_ref
  9.3 1.3 message_rows.1.refs_6_
  10.6 2.1 %collective-permute-start.3 = (bf16[528,1024]{1,0:T(8,128)(2,1)S(1)}, bf16[528,1024]{1,0:T(8,128)(2,1)}, u32[]{:S(2)}, u32[]{:S(2)}) collective-permute-start(bf16[528,1024]{1,0:T(8,128)(2,1)S(1)} %message_rows.1.refs_6_), channel_id=1, source_target_pairs={{24,0},{0,8},{8,16},{16,24},{25,1},{1,9},{9,17},{17,25},{26,2},{2,... | collective-permute-start | bytes 3244040 | tf_op jit(solution)/shard_map/ppermute | solution.py:180
  12.7 1.3 collective-permute-start.2
  14.0 1.4 collective-permute-start
  15.4 1.5 collective-permute-start.1
  16.9 0.6 broadcast_in_dim.73
  17.5 10.2 %all-to-all-start = ((s32[16,1,576]{2,1,0:T(1,128)}), s32[16,1,576]{2,1,0:T(1,128)S(1)}, u32[]{:S(2)}, u32[]{:S(2)}) async-start(s32[16,1,576]{2,1,0:T(1,128)} %broadcast_in_dim.73), calls=%async_computation | async-start | bytes 81920 | tf_op jit(solution)/shard_map/all_to_all | solution.py:268
  27.8 7.9 %all-to-all-done = s32[16,1,576]{2,1,0:T(1,128)S(1)} async-done(((s32[16,1,576]{2,1,0:T(1,128)}), s32[16,1,576]{2,1,0:T(1,128)S(1)}, u32[]{:S(2)}, u32[]{:S(2)}) %all-to-all-start) | async-done | bytes 36896 | tf_op jit(solution)/shard_map/all_to_all | solution.py:268
  35.7 2.5 %collective-permute-done.2.refs_10_ = bf16[528,1024]{1,0:T(8,128)(2,1)} collective-permute-done((bf16[528,1024]{1,0:T(8,128)(2,1)S(1)}, bf16[528,1024]{1,0:T(8,128)(2,1)}, u32[]{:S(2)}, u32[]{:S(2)}) %collective-permute-start.2) | collective-permute-done | bytes 1081376 | tf_op jit(solution)/shard_map/ppermute | solution.py:180
  38.2 1.6 collective-permute-start.5
  39.8 0.1 fusion.8
  39.9 0.3 select_reduce_fusion
  40.4 2.1 %collective-permute-start.4 = (bf16[528,1024]{1,0:T(8,128)(2,1)S(1)}, bf16[528,1024]{1,0:T(8,128)(2,1)}, u32[]{:S(2)}, u32[]{:S(2)}) collective-permute-start(bf16[528,1024]{1,0:T(8,128)(2,1)S(1)} %collective-permute-done.refs_7_), channel_id=1, source_target_pairs={{8,0},{16,8},{24,16},{0,24},{9,1},{17,9},{25,17},{1,25},{10,2},{18... | collective-permute-start | bytes 3244040 | tf_op jit(solution)/shard_map/ppermute | solution.py:180
  42.5 1.7 %collective-permute-start.8 = (bf16[528,1024]{1,0:T(8,128)(2,1)}, bf16[528,1024]{1,0:T(8,128)(2,1)}, u32[]{:S(2)}, u32[]{:S(2)}) collective-permute-start(bf16[528,1024]{1,0:T(8,128)(2,1)} %collective-permute-done.3.refs_23_), channel_id=1, source_target_pairs={{1,0},{2,1},{3,2},{0,3},{5,4},{6,5},{7,6},{4,7},{9,8},{10,9},{11,1... | collective-permute-start | bytes 3244040 | tf_op jit(solution)/shard_map/ppermute | solution.py:180
  44.4 0.3 convert_reduce_fusion
  44.7 1.9 %slice.56 = bf16[256,1024]{1,0:T(8,128)(2,1)} slice(bf16[528,1024]{1,0:T(8,128)(2,1)} %collective-permute-done.3.refs_23_), slice={[272:528], [0:1024]} | slice | bytes 1048576 | tf_op jit(solution)/shard_map/slice | solution.py:204
  46.6 0.6 slice.63
  47.8 0.8 slice.55
  49.1 1.1 slice.58
  50.3 0.7 pad_add_fusion.1.refs_2_
  51.2 12.4 %collective-permute-done.4.refs_12_ = bf16[528,1024]{1,0:T(8,128)(2,1)} collective-permute-done((bf16[528,1024]{1,0:T(8,128)(2,1)S(1)}, bf16[528,1024]{1,0:T(8,128)(2,1)}, u32[]{:S(2)}, u32[]{:S(2)}) %collective-permute-start.4) | collective-permute-done | bytes 1081376 | tf_op jit(solution)/shard_map/ppermute | solution.py:180
  63.6 2.6 %broadcast_in_dim.82.refs_4_ = f32[65,128,128]{2,1,0:T(8,128)} broadcast(f32[65,128]{1,0:T(8,128)S(1)} %pad.9), dimensions={0,1} | broadcast | bytes 4293120 | tf_op jit(solution)/shard_map/broadcast_in_dim | solution.py:250
  66.3 2.5 %collective-permute-start.11 = (bf16[528,1024]{1,0:T(8,128)(2,1)}, bf16[528,1024]{1,0:T(8,128)(2,1)S(1)}, u32[]{:S(2)}, u32[]{:S(2)}) collective-permute-start(bf16[528,1024]{1,0:T(8,128)(2,1)} %collective-permute-done.4.refs_12_), channel_id=1, source_target_pairs={{1,0},{2,1},{3,2},{0,3},{5,4},{6,5},{7,6},{4,7},{9,8},{10,9},{11,1... | collective-permute-start | bytes 3244040 | tf_op jit(solution)/shard_map/ppermute | solution.py:180
  68.8 1.0 collective-permute-start.13
  69.8 0.4 collective-permute-start.9
  70.3 0.6 collective-permute-start.7
  70.9 8.5 %collective-permute-done.9.refs_16_ = bf16[256,1024]{1,0:T(8,128)(2,1)} collective-permute-done((bf16[256,1024]{1,0:T(8,128)(2,1)S(1)}, bf16[256,1024]{1,0:T(8,128)(2,1)}, u32[]{:S(2)}, u32[]{:S(2)}) %collective-permute-start.9) | collective-permute-done | bytes 524320 | tf_op jit(solution)/shard_map/ppermute | solution.py:180
  79.5 2.7 %collective-permute-start.14 = (bf16[528,1024]{1,0:T(8,128)(2,1)}, bf16[528,1024]{1,0:T(8,128)(2,1)S(1)}, u32[]{:S(2)}, u32[]{:S(2)}) collective-permute-start(bf16[528,1024]{1,0:T(8,128)(2,1)} %collective-permute-done.6.refs_14_), channel_id=1, source_target_pairs={{8,0},{16,8},{24,16},{0,24},{9,1},{17,9},{25,17},{1,25},{10,2},{18... | collective-permute-start | bytes 3244040 | tf_op jit(solution)/shard_map/ppermute | solution.py:180
  82.1 6.8 %collective-permute-done.11.refs_13_ = bf16[528,1024]{1,0:T(8,128)(2,1)S(1)} collective-permute-done((bf16[528,1024]{1,0:T(8,128)(2,1)}, bf16[528,1024]{1,0:T(8,128)(2,1)S(1)}, u32[]{:S(2)}, u32[]{:S(2)}) %collective-permute-start.11) | collective-permute-done | bytes 1081376 | tf_op jit(solution)/shard_map/ppermute | solution.py:180
  89.0 3.4 %collective-permute-start.12 = (bf16[272,1024]{1,0:T(8,128)(2,1)S(1)}, bf16[272,1024]{1,0:T(8,128)(2,1)S(1)}, u32[]{:S(2)}, u32[]{:S(2)}) collective-permute-start(bf16[272,1024]{1,0:T(8,128)(2,1)S(1)} %slice.57), channel_id=1, source_target_pairs={{1,0},{2,1},{3,2},{0,3},{5,4},{6,5},{7,6},{4,7},{9,8},{10,9},{11,1... | collective-permute-start | bytes 1671176 | tf_op jit(solution)/shard_map/ppermute | solution.py:180
  92.4 0.2 collective-permute-start.15
  92.6 9.2 %collective-permute-done.10.refs_17_ = bf16[528,1024]{1,0:T(8,128)(2,1)S(1)} collective-permute-done((bf16[528,1024]{1,0:T(8,128)(2,1)}, bf16[528,1024]{1,0:T(8,128)(2,1)S(1)}, u32[]{:S(2)}, u32[]{:S(2)}) %collective-permute-start.10) | collective-permute-done | bytes 1081376 | tf_op jit(solution)/shard_map/ppermute | solution.py:180
  101.9 3.6 %collective-permute-start.19 = (bf16[128,1024]{1,0:T(8,128)(2,1)S(1)}, bf16[128,1024]{1,0:T(8,128)(2,1)S(1)}, u32[]{:S(2)}, u32[]{:S(2)}) collective-permute-start(bf16[128,1024]{1,0:T(8,128)(2,1)S(1)} %slice.66), channel_id=1, source_target_pairs={{1,0},{2,1},{3,2},{0,3},{5,4},{6,5},{7,6},{4,7},{9,8},{10,9},{11,1... | collective-permute-start | bytes 786440 | tf_op jit(solution)/shard_map/ppermute | solution.py:180
  105.5 2.8 %collective-permute-start.16 = (bf16[128,1024]{1,0:T(8,128)(2,1)S(1)}, bf16[128,1024]{1,0:T(8,128)(2,1)S(1)}, u32[]{:S(2)}, u32[]{:S(2)}) collective-permute-start(bf16[128,1024]{1,0:T(8,128)(2,1)S(1)} %slice.67), channel_id=1, source_target_pairs={{8,0},{16,8},{24,16},{0,24},{9,1},{17,9},{25,17},{1,25},{10,2},{18... | collective-permute-start | bytes 786440 | tf_op jit(solution)/shard_map/ppermute | solution.py:180
  108.3 0.7 copy-done.11
  109.0 2.5 %collective-permute-done.16.refs_18_ = bf16[128,1024]{1,0:T(8,128)(2,1)S(1)} collective-permute-done((bf16[128,1024]{1,0:T(8,128)(2,1)S(1)}, bf16[128,1024]{1,0:T(8,128)(2,1)S(1)}, u32[]{:S(2)}, u32[]{:S(2)}) %collective-permute-start.16) | collective-permute-done | bytes 262176 | tf_op jit(solution)/shard_map/ppermute | solution.py:180
  111.5 0.7 copy-done.14
  112.2 2.5 %collective-permute-done.18.refs_20_ = bf16[128,1024]{1,0:T(8,128)(2,1)S(1)} collective-permute-done((bf16[128,1024]{1,0:T(8,128)(2,1)S(1)}, bf16[128,1024]{1,0:T(8,128)(2,1)S(1)}, u32[]{:S(2)}, u32[]{:S(2)}) %collective-permute-start.18) | collective-permute-done | bytes 262176 | tf_op jit(solution)/shard_map/ppermute | solution.py:180
  114.8 0.7 copy-done.15
  115.5 13.7 %pair_maxima.1 = (f32[64,128]{1,0:T(8,128)}, f32[16,128]{1,0:T(8,128)S(1)}, f32[16,128]{1,0:T(8,128)S(1)}, f32[16,128]{1,0:T(8,128)S(1)}, f32[16,128]{1,0:T(8,128)S(1)}) custom-call(s32[88]{0:T(128)S(1)} %compare_select_fusion.2.refs_0_, s32[44]{0:T(128)S(1)} %broadcast_minimum_fusion.refs_1_, s32[18]{0:T(128)S(1)} %pad_add_fusion.1.refs_2_, ...), custom_call_target="tpu_custom_call" | custom-call | tf_op jit(solution)/shard_map/pair_maxima/pallas_call | solution.py:156
  129.3 0.7 collective-permute-start.21
  130.0 1.9 %collective-permute-start.22 = (f32[16,128]{1,0:T(8,128)S(1)}, f32[16,128]{1,0:T(8,128)S(1)}, u32[]{:S(2)}, u32[]{:S(2)}) collective-permute-start(f32[16,128]{1,0:T(8,128)S(1)} %get-tuple-element.112), channel_id=1, source_target_pairs={{1,0},{2,1},{3,2},{0,3},{5,4},{6,5},{7,6},{4,7},{9,8},{10,9},{11,1... | collective-permute-start | bytes 24584 | tf_op jit(solution)/shard_map/ppermute | solution.py:180
  131.9 20.3 %all-to-all-start.1 = ((f32[16,4,128]{2,1,0:T(4,128)}), f32[16,4,128]{2,1,0:T(4,128)S(1)}, u32[]{:S(2)}, u32[]{:S(2)}) async-start(f32[16,4,128]{2,1,0:T(4,128)} %bitcast.5), calls=%async_computation.1 | async-start | bytes 65536 | tf_op jit(solution)/shard_map/all_to_all | solution.py:283
  152.4 2.7 %collective-permute-start.25 = (f32[4,128]{1,0:T(4,128)S(1)}, f32[4,128]{1,0:T(4,128)S(1)}, u32[]{:S(2)}, u32[]{:S(2)}) collective-permute-start(f32[4,128]{1,0:T(4,128)S(1)} %get-tuple-element.120), channel_id=1, source_target_pairs={{8,0},{16,8},{24,16},{0,24},{9,1},{17,9},{25,17},{1,25},{10,2},{18... | collective-permute-start | bytes 6152 | tf_op jit(solution)/shard_map/ppermute | solution.py:180
  155.1 4.5 %all-to-all-done.1 = f32[16,4,128]{2,1,0:T(4,128)S(1)} async-done(((f32[16,4,128]{2,1,0:T(4,128)}), f32[16,4,128]{2,1,0:T(4,128)S(1)}, u32[]{:S(2)}, u32[]{:S(2)}) %all-to-all-start.1) | async-done | bytes 32800 | tf_op jit(solution)/shard_map/all_to_all | solution.py:283
  159.6 0.6 fusion.15
  (99 shorter events, 1.6 us)
Async XLA Ops:
  6.5 108.2 %all-gather.2.cloned.1.call-start = ((), (), s32[]{:S(2)}) async-start(), calls=%async_computation.2 | async-start | bytes 17825792 | tf_op jit(solution)/shard_map/all_gather | solution.py:260
  6.5 1.2 copy-start.1
  7.8 1.3 copy-start.19
  7.8 1.4 copy-start.16
  7.8 1.4 copy-start.17
  7.8 1.4 copy-start.18
  10.6 38.1 %copy-start = (bf16[528,1024]{1,0:T(8,128)(2,1)}, bf16[528,1024]{1,0:T(8,128)(2,1)S(1)}, u32[]{:S(2)}) copy-start(bf16[528,1024]{1,0:T(8,128)(2,1)S(1)} %message_rows.1.refs_6_) | copy-start | bytes 3244036
  10.6 25.1 %collective-permute-start.3 = (bf16[528,1024]{1,0:T(8,128)(2,1)S(1)}, bf16[528,1024]{1,0:T(8,128)(2,1)}, u32[]{:S(2)}, u32[]{:S(2)}) collective-permute-start(bf16[528,1024]{1,0:T(8,128)(2,1)S(1)} %message_rows.1.refs_6_), channel_id=1, source_target_pairs={{24,0},{0,8},{8,16},{16,24},{25,1},{1,9},{9,17},{17,25},{26,2},{2,... | collective-permute-start | bytes 3244040 | tf_op jit(solution)/shard_map/ppermute | solution.py:180
  12.7 25.5 %collective-permute-start.2 = (bf16[528,1024]{1,0:T(8,128)(2,1)S(1)}, bf16[528,1024]{1,0:T(8,128)(2,1)}, u32[]{:S(2)}, u32[]{:S(2)}) collective-permute-start(bf16[528,1024]{1,0:T(8,128)(2,1)S(1)} %message_rows.1.refs_6_), channel_id=1, source_target_pairs={{3,0},{0,1},{1,2},{2,3},{7,4},{4,5},{5,6},{6,7},{11,8},{8,9},{9,10... | collective-permute-start | bytes 3244040 | tf_op jit(solution)/shard_map/ppermute | solution.py:180
  14.0 25.8 %collective-permute-start = (bf16[528,1024]{1,0:T(8,128)(2,1)S(1)}, bf16[528,1024]{1,0:T(8,128)(2,1)S(1)}, u32[]{:S(2)}, u32[]{:S(2)}) collective-permute-start(bf16[528,1024]{1,0:T(8,128)(2,1)S(1)} %message_rows.1.refs_6_), channel_id=1, source_target_pairs={{1,0},{2,1},{3,2},{0,3},{5,4},{6,5},{7,6},{4,7},{9,8},{10,9},{11,1... | collective-permute-start | bytes 3244040 | tf_op jit(solution)/shard_map/ppermute | solution.py:180
  15.4 24.3 %collective-permute-start.1 = (bf16[528,1024]{1,0:T(8,128)(2,1)S(1)}, bf16[528,1024]{1,0:T(8,128)(2,1)S(1)}, u32[]{:S(2)}, u32[]{:S(2)}) collective-permute-start(bf16[528,1024]{1,0:T(8,128)(2,1)S(1)} %message_rows.1.refs_6_), channel_id=1, source_target_pairs={{8,0},{16,8},{24,16},{0,24},{9,1},{17,9},{25,17},{1,25},{10,2},{18... | collective-permute-start | bytes 3244040 | tf_op jit(solution)/shard_map/ppermute | solution.py:180
  17.5 18.1 %all-to-all-start = ((s32[16,1,576]{2,1,0:T(1,128)}), s32[16,1,576]{2,1,0:T(1,128)S(1)}, u32[]{:S(2)}, u32[]{:S(2)}) async-start(s32[16,1,576]{2,1,0:T(1,128)} %broadcast_in_dim.73), calls=%async_computation | async-start | bytes 81920 | tf_op jit(solution)/shard_map/all_to_all | solution.py:268
  38.2 31.6 %collective-permute-start.5 = (bf16[528,1024]{1,0:T(8,128)(2,1)}, bf16[528,1024]{1,0:T(8,128)(2,1)}, u32[]{:S(2)}, u32[]{:S(2)}) collective-permute-start(bf16[528,1024]{1,0:T(8,128)(2,1)} %collective-permute-done.2.refs_10_), channel_id=1, source_target_pairs={{24,0},{0,8},{8,16},{16,24},{25,1},{1,9},{9,17},{17,25},{26,2},{2,... | collective-permute-start | bytes 3244040 | tf_op jit(solution)/shard_map/ppermute | solution.py:180
  39.8 10.4 %copy-start.2 = (bf16[528,1024]{1,0:T(8,128)(2,1)}, bf16[528,1024]{1,0:T(8,128)(2,1)S(1)}, u32[]{:S(2)}) copy-start(bf16[528,1024]{1,0:T(8,128)(2,1)S(1)} %collective-permute-done.refs_7_) | copy-start | bytes 3244036
  39.8 26.5 %copy-start.3 = (bf16[528,1024]{1,0:T(8,128)(2,1)}, bf16[528,1024]{1,0:T(8,128)(2,1)S(1)}, u32[]{:S(2)}) copy-start(bf16[528,1024]{1,0:T(8,128)(2,1)S(1)} %collective-permute-done.1.refs_11_) | copy-start | bytes 3244036
  40.4 29.9 %collective-permute-start.6 = (bf16[528,1024]{1,0:T(8,128)(2,1)S(1)}, bf16[528,1024]{1,0:T(8,128)(2,1)}, u32[]{:S(2)}, u32[]{:S(2)}) collective-permute-start(bf16[528,1024]{1,0:T(8,128)(2,1)S(1)} %collective-permute-done.1.refs_11_), channel_id=1, source_target_pairs={{3,0},{0,1},{1,2},{2,3},{7,4},{4,5},{5,6},{6,7},{11,8},{8,9},{9,10... | collective-permute-start | bytes 3244040 | tf_op jit(solution)/shard_map/ppermute | solution.py:180
  40.4 23.2 %collective-permute-start.4 = (bf16[528,1024]{1,0:T(8,128)(2,1)S(1)}, bf16[528,1024]{1,0:T(8,128)(2,1)}, u32[]{:S(2)}, u32[]{:S(2)}) collective-permute-start(bf16[528,1024]{1,0:T(8,128)(2,1)S(1)} %collective-permute-done.refs_7_), channel_id=1, source_target_pairs={{8,0},{16,8},{24,16},{0,24},{9,1},{17,9},{25,17},{1,25},{10,2},{18... | collective-permute-start | bytes 3244040 | tf_op jit(solution)/shard_map/ppermute | solution.py:180
  42.5 23.8 %collective-permute-start.8 = (bf16[528,1024]{1,0:T(8,128)(2,1)}, bf16[528,1024]{1,0:T(8,128)(2,1)}, u32[]{:S(2)}, u32[]{:S(2)}) collective-permute-start(bf16[528,1024]{1,0:T(8,128)(2,1)} %collective-permute-done.3.refs_23_), channel_id=1, source_target_pairs={{1,0},{2,1},{3,2},{0,3},{5,4},{6,5},{7,6},{4,7},{9,8},{10,9},{11,1... | collective-permute-start | bytes 3244040 | tf_op jit(solution)/shard_map/ppermute | solution.py:180
  63.6 5.2 %copy-start.10 = (bf16[272,1024]{1,0:T(8,128)(2,1)S(1)}, bf16[272,1024]{1,0:T(8,128)(2,1)}, u32[]{:S(2)}) copy-start(bf16[272,1024]{1,0:T(8,128)(2,1)} %slice.55) | copy-start | bytes 1671172
  63.6 6.2 %copy-start.12 = (bf16[256,1024]{1,0:T(8,128)(2,1)S(1)}, bf16[256,1024]{1,0:T(8,128)(2,1)}, u32[]{:S(2)}) copy-start(bf16[256,1024]{1,0:T(8,128)(2,1)} %slice.56) | copy-start | bytes 1572868
  66.3 22.7 %collective-permute-start.11 = (bf16[528,1024]{1,0:T(8,128)(2,1)}, bf16[528,1024]{1,0:T(8,128)(2,1)S(1)}, u32[]{:S(2)}, u32[]{:S(2)}) collective-permute-start(bf16[528,1024]{1,0:T(8,128)(2,1)} %collective-permute-done.4.refs_12_), channel_id=1, source_target_pairs={{1,0},{2,1},{3,2},{0,3},{5,4},{6,5},{7,6},{4,7},{9,8},{10,9},{11,1... | collective-permute-start | bytes 3244040 | tf_op jit(solution)/shard_map/ppermute | solution.py:180
  68.8 10.7 %collective-permute-start.13 = (bf16[272,1024]{1,0:T(8,128)(2,1)S(1)}, bf16[272,1024]{1,0:T(8,128)(2,1)S(1)}, u32[]{:S(2)}, u32[]{:S(2)}) collective-permute-start(bf16[272,1024]{1,0:T(8,128)(2,1)S(1)} %copy-done.10), channel_id=1, source_target_pairs={{8,0},{16,8},{24,16},{0,24},{9,1},{17,9},{25,17},{1,25},{10,2},{18... | collective-permute-start | bytes 1671176 | tf_op jit(solution)/shard_map/ppermute | solution.py:180
  69.8 9.6 %collective-permute-start.9 = (bf16[256,1024]{1,0:T(8,128)(2,1)S(1)}, bf16[256,1024]{1,0:T(8,128)(2,1)}, u32[]{:S(2)}, u32[]{:S(2)}) collective-permute-start(bf16[256,1024]{1,0:T(8,128)(2,1)S(1)} %copy-done.12), channel_id=1, source_target_pairs={{24,0},{0,8},{8,16},{16,24},{25,1},{1,9},{9,17},{17,25},{26,2},{2,... | collective-permute-start | bytes 1572872 | tf_op jit(solution)/shard_map/ppermute | solution.py:180
  70.3 22.1 %collective-permute-start.7 = (bf16[528,1024]{1,0:T(8,128)(2,1)}, bf16[528,1024]{1,0:T(8,128)(2,1)S(1)}, u32[]{:S(2)}, u32[]{:S(2)}) collective-permute-start(bf16[528,1024]{1,0:T(8,128)(2,1)} %collective-permute-done.5.refs_26_), channel_id=1, source_target_pairs={{3,0},{0,1},{1,2},{2,3},{7,4},{4,5},{5,6},{6,7},{11,8},{8,9},{9,10... | collective-permute-start | bytes 3244040 | tf_op jit(solution)/shard_map/ppermute | solution.py:180
  79.5 22.3 %collective-permute-start.10 = (bf16[528,1024]{1,0:T(8,128)(2,1)}, bf16[528,1024]{1,0:T(8,128)(2,1)S(1)}, u32[]{:S(2)}, u32[]{:S(2)}) collective-permute-start(bf16[528,1024]{1,0:T(8,128)(2,1)} %collective-permute-done.8.refs_24_), channel_id=1, source_target_pairs={{24,0},{0,8},{8,16},{16,24},{25,1},{1,9},{9,17},{17,25},{26,2},{2,... | collective-permute-start | bytes 3244040 | tf_op jit(solution)/shard_map/ppermute | solution.py:180
  79.5 12.9 %copy-start.8 = (bf16[272,1024]{1,0:T(8,128)(2,1)}, bf16[272,1024]{1,0:T(8,128)(2,1)S(1)}, u32[]{:S(2)}) copy-start(bf16[272,1024]{1,0:T(8,128)(2,1)S(1)} %collective-permute-done.13.refs_15_) | copy-start | bytes 1671172
  79.5 26.0 %collective-permute-start.14 = (bf16[528,1024]{1,0:T(8,128)(2,1)}, bf16[528,1024]{1,0:T(8,128)(2,1)S(1)}, u32[]{:S(2)}, u32[]{:S(2)}) collective-permute-start(bf16[528,1024]{1,0:T(8,128)(2,1)} %collective-permute-done.6.refs_14_), channel_id=1, source_target_pairs={{8,0},{16,8},{24,16},{0,24},{9,1},{17,9},{25,17},{1,25},{10,2},{18... | collective-permute-start | bytes 3244040 | tf_op jit(solution)/shard_map/ppermute | solution.py:180
  89.0 19.3 %copy-start.5 = (bf16[528,1024]{1,0:T(8,128)(2,1)}, bf16[528,1024]{1,0:T(8,128)(2,1)S(1)}, u32[]{:S(2)}) copy-start(bf16[528,1024]{1,0:T(8,128)(2,1)S(1)} %collective-permute-done.11.refs_13_) | copy-start | bytes 3244036
  89.0 12.9 %collective-permute-start.12 = (bf16[272,1024]{1,0:T(8,128)(2,1)S(1)}, bf16[272,1024]{1,0:T(8,128)(2,1)S(1)}, u32[]{:S(2)}, u32[]{:S(2)}) collective-permute-start(bf16[272,1024]{1,0:T(8,128)(2,1)S(1)} %slice.57), channel_id=1, source_target_pairs={{1,0},{2,1},{3,2},{0,3},{5,4},{6,5},{7,6},{4,7},{9,8},{10,9},{11,1... | collective-permute-start | bytes 1671176 | tf_op jit(solution)/shard_map/ppermute | solution.py:180
  92.4 13.1 %copy-start.4 = (bf16[528,1024]{1,0:T(8,128)(2,1)}, bf16[528,1024]{1,0:T(8,128)(2,1)S(1)}, u32[]{:S(2)}) copy-start(bf16[528,1024]{1,0:T(8,128)(2,1)S(1)} %collective-permute-done.7.refs_25_) | copy-start | bytes 3244036
  92.4 15.8 %collective-permute-start.15 = (bf16[256,1024]{1,0:T(8,128)(2,1)S(1)}, bf16[256,1024]{1,0:T(8,128)(2,1)S(1)}, u32[]{:S(2)}, u32[]{:S(2)}) collective-permute-start(bf16[256,1024]{1,0:T(8,128)(2,1)S(1)} %slice.58), channel_id=1, source_target_pairs={{3,0},{0,1},{1,2},{2,3},{7,4},{4,5},{5,6},{6,7},{11,8},{8,9},{9,10... | collective-permute-start | bytes 1572872 | tf_op jit(solution)/shard_map/ppermute | solution.py:180
  101.8 13.0 %copy-start.6 = (bf16[528,1024]{1,0:T(8,128)(2,1)}, bf16[528,1024]{1,0:T(8,128)(2,1)S(1)}, u32[]{:S(2)}) copy-start(bf16[528,1024]{1,0:T(8,128)(2,1)S(1)} %collective-permute-done.10.refs_17_) | copy-start | bytes 3244036
  101.8 9.8 %collective-permute-start.17 = (bf16[144,1024]{1,0:T(8,128)(2,1)S(1)}, bf16[144,1024]{1,0:T(8,128)(2,1)}, u32[]{:S(2)}, u32[]{:S(2)}) collective-permute-start(bf16[144,1024]{1,0:T(8,128)(2,1)S(1)} %slice.65), channel_id=1, source_target_pairs={{24,0},{0,8},{8,16},{16,24},{25,1},{1,9},{9,17},{17,25},{26,2},{2,... | collective-permute-start | bytes 884744 | tf_op jit(solution)/shard_map/ppermute | solution.py:180
  101.8 6.4 %copy-start.9 = (bf16[272,1024]{1,0:T(8,128)(2,1)}, bf16[272,1024]{1,0:T(8,128)(2,1)S(1)}, u32[]{:S(2)}) copy-start(bf16[272,1024]{1,0:T(8,128)(2,1)S(1)} %collective-permute-done.12.refs_8_) | copy-start | bytes 1671172
  101.9 7.2 %collective-permute-start.19 = (bf16[128,1024]{1,0:T(8,128)(2,1)S(1)}, bf16[128,1024]{1,0:T(8,128)(2,1)S(1)}, u32[]{:S(2)}, u32[]{:S(2)}) collective-permute-start(bf16[128,1024]{1,0:T(8,128)(2,1)S(1)} %slice.66), channel_id=1, source_target_pairs={{1,0},{2,1},{3,2},{0,3},{5,4},{6,5},{7,6},{4,7},{9,8},{10,9},{11,1... | collective-permute-start | bytes 786440 | tf_op jit(solution)/shard_map/ppermute | solution.py:180
  105.4 9.3 %copy-start.7 = (bf16[528,1024]{1,0:T(8,128)(2,1)}, bf16[528,1024]{1,0:T(8,128)(2,1)S(1)}, u32[]{:S(2)}) copy-start(bf16[528,1024]{1,0:T(8,128)(2,1)S(1)} %collective-permute-done.14.refs_22_) | copy-start | bytes 3244036
  105.5 6.1 %collective-permute-start.16 = (bf16[128,1024]{1,0:T(8,128)(2,1)S(1)}, bf16[128,1024]{1,0:T(8,128)(2,1)S(1)}, u32[]{:S(2)}, u32[]{:S(2)}) collective-permute-start(bf16[128,1024]{1,0:T(8,128)(2,1)S(1)} %slice.67), channel_id=1, source_target_pairs={{8,0},{16,8},{24,16},{0,24},{9,1},{17,9},{25,17},{1,25},{10,2},{18... | collective-permute-start | bytes 786440 | tf_op jit(solution)/shard_map/ppermute | solution.py:180
  108.2 0.8 copy-start.11
  108.2 6.5 %collective-permute-start.18 = (bf16[128,1024]{1,0:T(8,128)(2,1)S(1)}, bf16[128,1024]{1,0:T(8,128)(2,1)S(1)}, u32[]{:S(2)}, u32[]{:S(2)}) collective-permute-start(bf16[128,1024]{1,0:T(8,128)(2,1)S(1)} %slice.68), channel_id=1, source_target_pairs={{3,0},{0,1},{1,2},{2,3},{7,4},{4,5},{5,6},{6,7},{11,8},{8,9},{9,10... | collective-permute-start | bytes 786440 | tf_op jit(solution)/shard_map/ppermute | solution.py:180
  109.0 5.7 %copy-start.13 = (bf16[128,1024]{1,0:T(8,128)(2,1)}, bf16[128,1024]{1,0:T(8,128)(2,1)S(1)}, u32[]{:S(2)}) copy-start(bf16[128,1024]{1,0:T(8,128)(2,1)S(1)} %collective-permute-done.19.refs_21_) | copy-start | bytes 786436
  111.5 0.7 copy-start.14
  129.2 23.0 %collective-permute-start.20 = (f32[16,128]{1,0:T(8,128)S(1)}, f32[16,128]{1,0:T(8,128)S(1)}, u32[]{:S(2)}, u32[]{:S(2)}) collective-permute-start(f32[16,128]{1,0:T(8,128)S(1)} %get-tuple-element.110), channel_id=1, source_target_pairs={{3,0},{0,1},{1,2},{2,3},{7,4},{4,5},{5,6},{6,7},{11,8},{8,9},{9,10... | collective-permute-start | bytes 24584 | tf_op jit(solution)/shard_map/ppermute | solution.py:180
  129.3 22.9 %collective-permute-start.21 = (f32[16,128]{1,0:T(8,128)S(1)}, f32[16,128]{1,0:T(8,128)S(1)}, u32[]{:S(2)}, u32[]{:S(2)}) collective-permute-start(f32[16,128]{1,0:T(8,128)S(1)} %get-tuple-element.111), channel_id=1, source_target_pairs={{2,0},{3,1},{0,2},{1,3},{6,4},{7,5},{4,6},{5,7},{10,8},{11,9},{8,1... | collective-permute-start | bytes 24584 | tf_op jit(solution)/shard_map/ppermute | solution.py:180
  130.0 22.2 %collective-permute-start.22 = (f32[16,128]{1,0:T(8,128)S(1)}, f32[16,128]{1,0:T(8,128)S(1)}, u32[]{:S(2)}, u32[]{:S(2)}) collective-permute-start(f32[16,128]{1,0:T(8,128)S(1)} %get-tuple-element.112), channel_id=1, source_target_pairs={{1,0},{2,1},{3,2},{0,3},{5,4},{6,5},{7,6},{4,7},{9,8},{10,9},{11,1... | collective-permute-start | bytes 24584 | tf_op jit(solution)/shard_map/ppermute | solution.py:180
  131.9 27.6 %all-to-all-start.1 = ((f32[16,4,128]{2,1,0:T(4,128)}), f32[16,4,128]{2,1,0:T(4,128)S(1)}, u32[]{:S(2)}, u32[]{:S(2)}) async-start(f32[16,4,128]{2,1,0:T(4,128)} %bitcast.5), calls=%async_computation.1 | async-start | bytes 65536 | tf_op jit(solution)/shard_map/all_to_all | solution.py:283
  152.3 7.3 %collective-permute-start.23 = (f32[4,128]{1,0:T(4,128)S(1)}, f32[4,128]{1,0:T(4,128)S(1)}, u32[]{:S(2)}, u32[]{:S(2)}) collective-permute-start(f32[4,128]{1,0:T(4,128)S(1)} %get-tuple-element.119), channel_id=1, source_target_pairs={{24,0},{0,8},{8,16},{16,24},{25,1},{1,9},{9,17},{17,25},{26,2},{2,... | collective-permute-start | bytes 6152 | tf_op jit(solution)/shard_map/ppermute | solution.py:180
  152.4 7.2 %collective-permute-start.25 = (f32[4,128]{1,0:T(4,128)S(1)}, f32[4,128]{1,0:T(4,128)S(1)}, u32[]{:S(2)}, u32[]{:S(2)}) collective-permute-start(f32[4,128]{1,0:T(4,128)S(1)} %get-tuple-element.120), channel_id=1, source_target_pairs={{8,0},{16,8},{24,16},{0,24},{9,1},{17,9},{25,17},{1,25},{10,2},{18... | collective-permute-start | bytes 6152 | tf_op jit(solution)/shard_map/ppermute | solution.py:180
  155.0 4.5 %collective-permute-start.24 = (f32[4,128]{1,0:T(4,128)S(1)}, f32[4,128]{1,0:T(4,128)S(1)}, u32[]{:S(2)}, u32[]{:S(2)}) collective-permute-start(f32[4,128]{1,0:T(4,128)S(1)} %get-tuple-element.121), channel_id=1, source_target_pairs={{16,0},{24,8},{0,16},{8,24},{17,1},{25,9},{1,17},{9,25},{18,2},{26... | collective-permute-start | bytes 6152 | tf_op jit(solution)/shard_map/ppermute | solution.py:180
  (1 other events, 0.7 us)
Sparse Core Ops, SparseCore 0:
  9.2 100.5 all-gather.1

commit v5 on v4

--- a/solution.py
+++ b/solution.py
@@ -31,9 +31,9 @@
 
 
 def pair_kernel(right_at, meta_at, todo, block_of, used, place, left_tags, left_ref, *rest):
-    refs = rest[:-15]
-    left_out, *right_out = rest[-15:-10]
-    left_buf, tags_buf, right_buf, right_meta, right_tags, even, odd, left_best, right_best, sems = rest[-10:]
+    refs = rest[:-14]
+    left_out, *right_out = rest[-14:-9]
+    left_buf, right_buf, right_meta, right_tags, even, odd, left_best, right_best, sems = rest[-9:]
     left_sems, right_sems = sems.at[0], sems.at[1]
 
     def each_right(j, act):
@@ -51,7 +51,6 @@
         for h in range(2):
             unit = todo[2 * i + h]
             part = pl.ds(h * ROWS, ROWS)
-            act(pltpu.make_async_copy(left_tags.at[unit], tags_buf.at[slot, part, :], left_sems.at[2 * SLOTS + slot * 2 + h]))
 
             @pl.when(unit < 64)
             def _():
@@ -100,12 +99,12 @@
         )
 
     def maxima(i, scores):
-        slot, j = lax.rem(i, SLOTS), block_of[i]
+        j = block_of[i]
         right_row = right_tags[pl.ds(j, 1), :]
         tops = [None] * 4
         for h in range(2):
             unit = todo[2 * i + h]
-            tags = tags_buf[slot, h * ROWS : (h + 1) * ROWS, :]
+            tags = jnp.broadcast_to(left_tags[pl.ds(unit, 1), :], (ROWS, ROWS)).T
             same = (j < 4) & (unit == me * 4 + j)
             best = None
             for dy in range(4):
@@ -156,11 +155,10 @@
     return pl.pallas_call(
         kernel,
         out_shape=[jax.ShapeDtypeStruct((n, ROWS), jnp.float32) for n in (64, 16, 16, 16, 16)],
-        in_specs=[smem] * 4 + [hbm] * (len(operands) + 2),
+        in_specs=[smem] * 4 + [vmem] + [hbm] * (len(operands) + 1),
         out_specs=[vmem] * 5,
         scratch_shapes=[
             pltpu.VMEM((SLOTS, 2 * ROWS, 1024), jnp.bfloat16),
-            pltpu.VMEM((SLOTS, 2 * ROWS, ROWS), jnp.float32),
             pltpu.VMEM((16, 4 * ROWS, 1024), jnp.bfloat16),
             pltpu.VMEM((16, META, 1024), jnp.bfloat16),
             pltpu.VMEM((16, 4 * ROWS), jnp.float32),
@@ -168,11 +166,11 @@
             pltpu.VMEM((2 * ROWS, 4 * ROWS), jnp.float32),
             pltpu.VMEM((72, ROWS), jnp.float32),
             pltpu.VMEM((16, 4 * ROWS), jnp.float32),
-            pltpu.SemaphoreType.DMA((2, 4 * SLOTS)),
+            pltpu.SemaphoreType.DMA((2, 2 * SLOTS + 1)),
         ],
         compiler_params=pltpu.CompilerParams(vmem_limit_bytes=VMEM_LIMIT),
         name="pair_maxima",
-    )(todo, block_of, used, place, *(pltpu.with_memory_space_constraint(v, pltpu.HBM) for v in (left_tags, left_rows, *operands)))
+    )(todo, block_of, used, place, left_tags, *(pltpu.with_memory_space_constraint(v, pltpu.HBM) for v in (left_rows, *operands)))
 
 
 def shift(value, axis, by):
@@ -180,48 +178,55 @@
     return lax.ppermute(value, axis, [((i + by) % size, i) for i in range(size)])
 
 
-class Carrier:
-    def __init__(self):
-        self.last = {}
-
-    def __call__(self, value, axis, by):
-        if (axis, by) in self.last:
-            before = self.last[axis, by]
-            value, before[0] = lax.optimization_barrier((value, before[0]))
-        self.last[axis, by] = cell = [shift(value, axis, by)]
-        return cell
+LINKS = {"x-": ("x", -1), "y-": ("y", -1), "x+": ("x", 1), "y+": ("y", 1)}
+CARRIED = {"c": {"x+": "y+", "x-": "y-", "y+": "x-", "y-": "x+"}, "d": {"y+": "x+", "y-": "x-", "x+": "y-", "x-": "y+"}}
+QUARTERS = {"x+": ("dy+", 0), "x-": ("dy-", ROWS), "y-": ("dx+", HALF1), "y+": ("dx-", HALF1 + ROWS)}
+STEPS = (
+    ("cx-", "cy-", "cx+", "cy+", "=", "dy-", "dy+", "bx-", "bx+"),
+    ("dx-", "dx+", "by-", "by+", "ey-", "ey+", "ex-", "ex+"),
+)
+AFTER = {"bx": "cx", "dx": "bx", "ex": "dx", "dy": "cy", "by": "dy"}
 
 
 def gather_plane(own, extra, make_beside):
-    send = Carrier()
-    xp, xm, yp, ym = ("x", 1), ("x", -1), ("y", 1), ("y", -1)
+    cells, cut = {}, {}
+
+    def send(name, value):
+        before = AFTER.get(name[:2])
+        if before:
+            other = cells[before + name[2]]
+            value, other[0] = lax.optimization_barrier((value, other[0]))
+        cells[name] = [shift(value, *LINKS[name[1:]])]
+
+    for link in LINKS:
+        send("a" + link, own)
+    for step in STEPS[0] + STEPS[1]:
+        kind, link = step[0], step[1:]
+        if kind == "=":
+            extra, cells["ay+"][0] = lax.optimization_barrier((extra, cells["ay+"][0]))
+            for other in LINKS:
+                cut[other] = cells["a" + other][0][:HALF1] if other[1] == "+" else cells["a" + other][0][HALF1:]
+            cut, cells["cx+"][0], beside = lax.optimization_barrier((cut, cells["cx+"][0], make_beside(extra)))
+        elif kind in CARRIED:
+            send(step, cells[{"c": "a", "d": "c"}[kind] + CARRIED[kind][link]][0])
+        elif kind == "b":
+            send(step, cut[link])
+        else:
+            name, at = QUARTERS[link]
+            send(step, cells[name][0][at : HALF1 if link == "x-" else at + ROWS])
     whole = {(0, 0): [own]}
-    whole[0, 1], whole[0, 3] = send(own, *yp), send(own, *ym)
-    whole[1, 0], whole[3, 0] = send(own, *xp), send(own, *xm)
-    whole[0, 1][0], extra = lax.optimization_barrier((whole[0, 1][0], extra))
-    whole[1, 1], whole[3, 3] = send(whole[0, 1][0], *xp), send(whole[0, 3][0], *xm)
-    whole[3, 1], whole[1, 3] = send(whole[3, 0][0], *yp), send(whole[1, 0][0], *ym)
-    cut = [whole[1, 0][0][:HALF1], whole[3, 0][0][HALF1:], whole[0, 1][0][:HALF1], whole[0, 3][0][HALF1:]]
-    cut, whole[1, 1][0], beside = lax.optimization_barrier((cut, whole[1, 1][0], make_beside(extra)))
-    half = {("x", 0): send(cut[0], *xp), ("x", 1): send(cut[1], *xm)}
-    whole[1, 2], whole[3, 2] = send(whole[1, 1][0], *yp), send(whole[3, 3][0], *ym)
-    whole[2, 3], whole[2, 1] = send(whole[1, 3][0], *xp), send(whole[3, 1][0], *xm)
-    half["y", 0], half["y", 1] = send(cut[2], *yp), send(cut[3], *ym)
-    last = [
-        send(whole[1, 2][0][:ROWS], *xp),
-        send(whole[3, 2][0][ROWS:HALF1], *xm),
-        send(whole[2, 3][0][HALF1 : HALF1 + ROWS], *ym),
-        send(whole[2, 1][0][HALF1 + ROWS :], *yp),
-    ]
+    names = ("ax+", "ax-", "ay+", "ay-", "cx+", "cx-", "cy+", "cy-", "dy+", "dy-", "dx+", "dx-")
+    spots = [(1, 0), (3, 0), (0, 1), (0, 3), (1, 1), (3, 3), (3, 1), (1, 3), (1, 2), (3, 2), (2, 3), (2, 1)]
+    whole.update((spot, cells[name]) for spot, name in zip(spots, names))
     starts = (0, ROWS, HALF1, HALF1 + ROWS)
     parts = {key: [(v[0], at) for at in starts] for key, v in whole.items()}
     metas = {key: (v[0], 2 * ROWS) for key, v in whole.items()}
     for key, axis in (((2, 0), "x"), ((0, 2), "y")):
-        h1, h2 = half[axis, 0][0], half[axis, 1][0]
+        h1, h2 = cells["b" + axis + "+"][0], cells["b" + axis + "-"][0]
         parts[key] = [(h1, 0), (h1, ROWS), (h2, 0), (h2, ROWS)]
         metas[key] = (h1, 2 * ROWS)
-    parts[2, 2] = [(v[0], 0) for v in last]
-    metas[2, 2] = (last[1][0], ROWS)
+    parts[2, 2] = [(cells[name][0], 0) for name in ("ex+", "ex-", "ey-", "ey+")]
+    metas[2, 2] = (cells["ex-"][0], ROWS)
     return parts, metas, beside
 
 
@@ -246,8 +251,7 @@
     todo = jnp.where(todo > 0, todo - 1, 64)
     block_of = jnp.minimum(jnp.sum(first[None, 1:] <= jnp.arange(44)[:, None], axis=1), 15)
     used = jnp.concatenate([steps, (first[16:] + 1) // 2 * 2, first[16:]])
-    left_tags = jnp.pad(left_tags, ((0, 1), (0, 0)), constant_values=-3.0)
-    left_tags = jnp.broadcast_to(left_tags[:, :, None], (65, ROWS, ROWS))
+    left_tags = jnp.pad(left_tags, ((0, 8), (0, 0)), constant_values=-3.0)
     return todo, block_of, used, place, left_tags
 
 

time: 169 us -> 162 us (0.959); the launches traced: 167 us -> 163 us
  starting transfers between devices: 65 us -> 62.1 us
  local copies, waits for them, and re-layouts: 11.6 us -> 9.07 us
  waiting for transfers between devices: 56.9 us -> 58.7 us
    broadcast_in_dim x1 -> x0, local copies, waits for them, and re-layouts: 2.63 us -> none  [pair_lists(): left_tags = jnp.broadcast_to(left_tags[:, :, None], (65, ROWS, ROWS))]
    unnamed x41 -> x43, local copies, waits for them, and re-layouts: 3.36 us -> 4.2 us
  transfers between devices with their start and end apart: 29 -> 29, of which waited for: 9 -> 13; matrix products, arithmetic and copies ran while one was open for 6% -> 4% of each run, Pallas kernels for 1% -> 1%
where the time goes in v5:
time: 162 us; the launch traced here: 163 us
  starting transfers between devices  62.1 us (38%)
  waiting for transfers between devices  58.7 us (36%)
  Pallas kernels  15.6 us (10%)
  between operations  14.5 us (9%)
  local copies, waits for them, and re-layouts  9.07 us (6%)
  other arithmetic  2.67 us (2%)
    ppermute x26, waiting for transfers between devices, shift(): lax.ppermute(value, axis, [((i + by) % size, i) for i in range(size)])  45 us
    ppermute x26, starting transfers between devices, shift(): lax.ppermute(value, axis, [((i + by) % size, i) for i in range(size)])  33.4 us
    all_to_all x1, starting transfers between devices, local(): lax.all_to_all(left_best.reshape(16, BLOCKS, ROWS), ('z', 'c'), 0, 0, til...  19 us
    pallas_call x1, Pallas kernels, pair_maxima(): pl.pallas_call(kernel, out_shape=[jax.ShapeDtypeStruct((n, ROWS), jnp.flo...  13 us
    all_to_all x1, starting transfers between devices, local(): lax.all_to_all(jnp.broadcast_to(lists, (16, lists.shape[1])), ('z', 'c'),...  9.71 us
    all_to_all x1, waiting for transfers between devices, local(): lax.all_to_all(jnp.broadcast_to(lists, (16, lists.shape[1])), ('z', 'c'),...  7.9 us
    all_to_all x1, waiting for transfers between devices, local(): lax.all_to_all(left_best.reshape(16, BLOCKS, ROWS), ('z', 'c'), 0, 0, til...  5.77 us
    unnamed x43, local copies, waits for them, and re-layouts  4.2 us
  transfers between devices with their start and end apart: 29, of which 13 were waited for; matrix products, arithmetic and copies ran while one was open for 4% of the time, Pallas kernels for 1%

profile of v5, /device:TPU:1, one launch (start us, length us, event | category | flops | bytes accessed | tf_op | source)
XLA Modules:
  0.0 162.6 jit_solution(1438415732145827503)
XLA Ops:
  6.5 1.2 copy-done.1
  7.8 1.3 unit_rows.1.unit_ref
  9.3 1.3 message_rows.1.refs_6_
  10.6 3.6 %collective-permute-start.2 = (bf16[528,1024]{1,0:T(8,128)(2,1)S(1)}, bf16[528,1024]{1,0:T(8,128)(2,1)S(1)}, u32[]{:S(2)}, u32[]{:S(2)}) collective-permute-start(bf16[528,1024]{1,0:T(8,128)(2,1)S(1)} %message_rows.1.refs_6_), channel_id=1, source_target_pairs={{1,0},{2,1},{3,2},{0,3},{5,4},{6,5},{7,6},{4,7},{9,8},{10,9},{11,1... | collective-permute-start | bytes 3244040 | tf_op jit(solution)/shard_map/ppermute | solution.py:178
  14.2 2.5 %collective-permute-start = (bf16[528,1024]{1,0:T(8,128)(2,1)S(1)}, bf16[528,1024]{1,0:T(8,128)(2,1)S(1)}, u32[]{:S(2)}, u32[]{:S(2)}) collective-permute-start(bf16[528,1024]{1,0:T(8,128)(2,1)S(1)} %message_rows.1.refs_6_), channel_id=1, source_target_pairs={{8,0},{16,8},{24,16},{0,24},{9,1},{17,9},{25,17},{1,25},{10,2},{18... | collective-permute-start | bytes 3244040 | tf_op jit(solution)/shard_map/ppermute | solution.py:178
  16.7 0.6 broadcast_in_dim.67
  17.3 9.7 %all-to-all-start = ((s32[16,1,576]{2,1,0:T(1,128)}), s32[16,1,576]{2,1,0:T(1,128)S(1)}, u32[]{:S(2)}, u32[]{:S(2)}) async-start(s32[16,1,576]{2,1,0:T(1,128)} %broadcast_in_dim.67), calls=%async_computation | async-start | bytes 81920 | tf_op jit(solution)/shard_map/all_to_all | solution.py:272
  27.1 7.9 %all-to-all-done = s32[16,1,576]{2,1,0:T(1,128)S(1)} async-done(((s32[16,1,576]{2,1,0:T(1,128)}), s32[16,1,576]{2,1,0:T(1,128)S(1)}, u32[]{:S(2)}, u32[]{:S(2)}) %all-to-all-start) | async-done | bytes 36896 | tf_op jit(solution)/shard_map/all_to_all | solution.py:272
  35.0 1.8 %collective-permute-done.2.refs_7_ = bf16[528,1024]{1,0:T(8,128)(2,1)S(1)} collective-permute-done((bf16[528,1024]{1,0:T(8,128)(2,1)S(1)}, bf16[528,1024]{1,0:T(8,128)(2,1)S(1)}, u32[]{:S(2)}, u32[]{:S(2)}) %collective-permute-start.2) | collective-permute-done | bytes 1081376 | tf_op jit(solution)/shard_map/ppermute | solution.py:178
  36.9 0.3 select_reduce_fusion
  37.3 2.5 %collective-permute-start.4 = (bf16[528,1024]{1,0:T(8,128)(2,1)S(1)}, bf16[528,1024]{1,0:T(8,128)(2,1)}, u32[]{:S(2)}, u32[]{:S(2)}) collective-permute-start(bf16[528,1024]{1,0:T(8,128)(2,1)S(1)} %collective-permute-done.2.refs_7_), channel_id=1, source_target_pairs={{8,0},{16,8},{24,16},{0,24},{9,1},{17,9},{25,17},{1,25},{10,2},{18... | collective-permute-start | bytes 3244040 | tf_op jit(solution)/shard_map/ppermute | solution.py:178
  39.8 0.1 collective-permute-done.3.refs_10_
  39.9 1.2 collective-permute-start.8
  41.3 0.3 convert_reduce_fusion
  41.8 0.4 collective-permute-done.1.refs_23_
  42.1 2.4 %collective-permute-start.5 = (bf16[528,1024]{1,0:T(8,128)(2,1)}, bf16[528,1024]{1,0:T(8,128)(2,1)}, u32[]{:S(2)}, u32[]{:S(2)}) collective-permute-start(bf16[528,1024]{1,0:T(8,128)(2,1)} %collective-permute-done.1.refs_23_), channel_id=1, source_target_pairs={{1,0},{2,1},{3,2},{0,3},{5,4},{6,5},{7,6},{4,7},{9,8},{10,9},{11,1... | collective-permute-start | bytes 3244040 | tf_op jit(solution)/shard_map/ppermute | solution.py:178
  44.5 0.6 slice.63
  45.8 0.8 slice.57
  47.0 1.1 slice.74
  48.2 1.1 slice.75
  49.3 0.7 pad_add_fusion.1.refs_2_
  50.1 0.1 select_reduce_fusion.1
  50.2 11.3 %collective-permute-done.4.refs_12_ = bf16[528,1024]{1,0:T(8,128)(2,1)} collective-permute-done((bf16[528,1024]{1,0:T(8,128)(2,1)S(1)}, bf16[528,1024]{1,0:T(8,128)(2,1)}, u32[]{:S(2)}, u32[]{:S(2)}) %collective-permute-start.4) | collective-permute-done | bytes 1081376 | tf_op jit(solution)/shard_map/ppermute | solution.py:178
  61.5 3.5 %collective-permute-start.12 = (bf16[272,1024]{1,0:T(8,128)(2,1)S(1)}, bf16[272,1024]{1,0:T(8,128)(2,1)S(1)}, u32[]{:S(2)}, u32[]{:S(2)}) collective-permute-start(bf16[272,1024]{1,0:T(8,128)(2,1)S(1)} %slice.73), channel_id=1, source_target_pairs={{8,0},{16,8},{24,16},{0,24},{9,1},{17,9},{25,17},{1,25},{10,2},{18... | collective-permute-start | bytes 1671176 | tf_op jit(solution)/shard_map/ppermute | solution.py:178
  65.1 0.6 collective-permute-done.9.refs_14_
  65.7 0.3 collective-permute-start.10
  66.0 3.0 %collective-permute-start.6 = (bf16[528,1024]{1,0:T(8,128)(2,1)}, bf16[528,1024]{1,0:T(8,128)(2,1)S(1)}, u32[]{:S(2)}, u32[]{:S(2)}) collective-permute-start(bf16[528,1024]{1,0:T(8,128)(2,1)} %collective-permute-done.4.refs_12_), channel_id=1, source_target_pairs={{1,0},{2,1},{3,2},{0,3},{5,4},{6,5},{7,6},{4,7},{9,8},{10,9},{11,1... | collective-permute-start | bytes 3244040 | tf_op jit(solution)/shard_map/ppermute | solution.py:178
  69.0 8.2 %collective-permute-done.13.refs_16_ = bf16[256,1024]{1,0:T(8,128)(2,1)S(1)} collective-permute-done((bf16[256,1024]{1,0:T(8,128)(2,1)S(1)}, bf16[256,1024]{1,0:T(8,128)(2,1)S(1)}, u32[]{:S(2)}, u32[]{:S(2)}) %collective-permute-start.13) | collective-permute-done | bytes 524320 | tf_op jit(solution)/shard_map/ppermute | solution.py:178
  77.1 0.8 copy-done.11
  77.9 2.1 %collective-permute-start.15 = (bf16[528,1024]{1,0:T(8,128)(2,1)}, bf16[528,1024]{1,0:T(8,128)(2,1)S(1)}, u32[]{:S(2)}, u32[]{:S(2)}) collective-permute-start(bf16[528,1024]{1,0:T(8,128)(2,1)} %collective-permute-done.9.refs_14_), channel_id=1, source_target_pairs={{8,0},{16,8},{24,16},{0,24},{9,1},{17,9},{25,17},{1,25},{10,2},{18... | collective-permute-start | bytes 3244040 | tf_op jit(solution)/shard_map/ppermute | solution.py:178
  80.1 10.0 %collective-permute-done.10.refs_25_ = bf16[528,1024]{1,0:T(8,128)(2,1)S(1)} collective-permute-done((bf16[528,1024]{1,0:T(8,128)(2,1)}, bf16[528,1024]{1,0:T(8,128)(2,1)S(1)}, u32[]{:S(2)}, u32[]{:S(2)}) %collective-permute-start.10) | collective-permute-done | bytes 1081376 | tf_op jit(solution)/shard_map/ppermute | solution.py:178
  90.1 2.7 %collective-permute-start.7 = (bf16[272,1024]{1,0:T(8,128)(2,1)S(1)}, bf16[272,1024]{1,0:T(8,128)(2,1)S(1)}, u32[]{:S(2)}, u32[]{:S(2)}) collective-permute-start(bf16[272,1024]{1,0:T(8,128)(2,1)S(1)} %copy-done.8), channel_id=1, source_target_pairs={{1,0},{2,1},{3,2},{0,3},{5,4},{6,5},{7,6},{4,7},{9,8},{10,9},{11,1... | collective-permute-start | bytes 1671176 | tf_op jit(solution)/shard_map/ppermute | solution.py:178
  92.8 7.7 %collective-permute-done.14.refs_17_ = bf16[528,1024]{1,0:T(8,128)(2,1)S(1)} collective-permute-done((bf16[528,1024]{1,0:T(8,128)(2,1)}, bf16[528,1024]{1,0:T(8,128)(2,1)S(1)}, u32[]{:S(2)}, u32[]{:S(2)}) %collective-permute-start.14) | collective-permute-done | bytes 1081376 | tf_op jit(solution)/shard_map/ppermute | solution.py:178
  100.6 3.6 %collective-permute-start.19 = (bf16[128,1024]{1,0:T(8,128)(2,1)S(1)}, bf16[128,1024]{1,0:T(8,128)(2,1)S(1)}, u32[]{:S(2)}, u32[]{:S(2)}) collective-permute-start(bf16[128,1024]{1,0:T(8,128)(2,1)S(1)} %slice.77), channel_id=1, source_target_pairs={{1,0},{2,1},{3,2},{0,3},{5,4},{6,5},{7,6},{4,7},{9,8},{10,9},{11,1... | collective-permute-start | bytes 786440 | tf_op jit(solution)/shard_map/ppermute | solution.py:178
  104.2 2.7 %collective-permute-start.16 = (bf16[128,1024]{1,0:T(8,128)(2,1)S(1)}, bf16[128,1024]{1,0:T(8,128)(2,1)S(1)}, u32[]{:S(2)}, u32[]{:S(2)}) collective-permute-start(bf16[128,1024]{1,0:T(8,128)(2,1)S(1)} %slice.66), channel_id=1, source_target_pairs={{8,0},{16,8},{24,16},{0,24},{9,1},{17,9},{25,17},{1,25},{10,2},{18... | collective-permute-start | bytes 786440 | tf_op jit(solution)/shard_map/ppermute | solution.py:178
  107.1 1.0 collective-permute-done.19.refs_21_
  108.1 2.1 %collective-permute-done.16.refs_18_ = bf16[128,1024]{1,0:T(8,128)(2,1)S(1)} collective-permute-done((bf16[128,1024]{1,0:T(8,128)(2,1)S(1)}, bf16[128,1024]{1,0:T(8,128)(2,1)S(1)}, u32[]{:S(2)}, u32[]{:S(2)}) %collective-permute-start.16) | collective-permute-done | bytes 262176 | tf_op jit(solution)/shard_map/ppermute | solution.py:178
  110.2 0.7 copy-done.15
  110.9 0.7 copy-done.13
  111.6 1.8 %collective-permute-done.18.refs_20_ = bf16[128,1024]{1,0:T(8,128)(2,1)S(1)} collective-permute-done((bf16[128,1024]{1,0:T(8,128)(2,1)S(1)}, bf16[128,1024]{1,0:T(8,128)(2,1)S(1)}, u32[]{:S(2)}, u32[]{:S(2)}) %collective-permute-start.18) | collective-permute-done | bytes 262176 | tf_op jit(solution)/shard_map/ppermute | solution.py:178
  113.5 0.7 copy-done.16
  114.2 13.0 %pair_maxima.1 = (f32[64,128]{1,0:T(8,128)}, f32[16,128]{1,0:T(8,128)S(1)}, f32[16,128]{1,0:T(8,128)S(1)}, f32[16,128]{1,0:T(8,128)S(1)}, f32[16,128]{1,0:T(8,128)S(1)}) custom-call(s32[88]{0:T(128)S(1)} %compare_select_fusion.2.refs_0_, s32[44]{0:T(128)S(1)} %broadcast_minimum_fusion.refs_1_, s32[18]{0:T(128)S(1)} %pad_add_fusion.1.refs_2_, ...), custom_call_target="tpu_custom_call" | custom-call | tf_op jit(solution)/shard_map/pair_maxima/pallas_call | solution.py:155
  127.3 0.9 collective-permute-start.21
  128.2 0.6 collective-permute-start.20
  128.7 19.0 %all-to-all-start.1 = ((f32[16,4,128]{2,1,0:T(4,128)}), f32[16,4,128]{2,1,0:T(4,128)S(1)}, u32[]{:S(2)}, u32[]{:S(2)}) async-start(f32[16,4,128]{2,1,0:T(4,128)} %bitcast.5), calls=%async_computation.1 | async-start | bytes 65536 | tf_op jit(solution)/shard_map/all_to_all | solution.py:287
  148.0 1.4 collective-permute-start.23
  149.4 5.8 %all-to-all-done.1 = f32[16,4,128]{2,1,0:T(4,128)S(1)} async-done(((f32[16,4,128]{2,1,0:T(4,128)}), f32[16,4,128]{2,1,0:T(4,128)S(1)}, u32[]{:S(2)}, u32[]{:S(2)}) %all-to-all-start.1) | async-done | bytes 32800 | tf_op jit(solution)/shard_map/all_to_all | solution.py:287
  155.2 0.6 fusion.15
  (100 shorter events, 1.6 us)
Async XLA Ops:
  6.5 106.9 %all-gather.2.cloned.1.call-start = ((), (), s32[]{:S(2)}) async-start(), calls=%async_computation.2 | async-start | bytes 17825792 | tf_op jit(solution)/shard_map/all_gather | solution.py:264
  6.5 1.2 copy-start.1
  7.8 1.3 copy-start.20
  7.8 1.4 copy-start.17
  7.8 1.4 copy-start.18
  7.8 1.4 copy-start.19
  10.6 36.4 %copy-start = (bf16[528,1024]{1,0:T(8,128)(2,1)}, bf16[528,1024]{1,0:T(8,128)(2,1)S(1)}, u32[]{:S(2)}) copy-start(bf16[528,1024]{1,0:T(8,128)(2,1)S(1)} %message_rows.1.refs_6_) | copy-start | bytes 3244036
  10.6 26.2 %collective-permute-start.2 = (bf16[528,1024]{1,0:T(8,128)(2,1)S(1)}, bf16[528,1024]{1,0:T(8,128)(2,1)S(1)}, u32[]{:S(2)}, u32[]{:S(2)}) collective-permute-start(bf16[528,1024]{1,0:T(8,128)(2,1)S(1)} %message_rows.1.refs_6_), channel_id=1, source_target_pairs={{1,0},{2,1},{3,2},{0,3},{5,4},{6,5},{7,6},{4,7},{9,8},{10,9},{11,1... | collective-permute-start | bytes 3244040 | tf_op jit(solution)/shard_map/ppermute | solution.py:178
  14.2 25.7 %collective-permute-start.3 = (bf16[528,1024]{1,0:T(8,128)(2,1)S(1)}, bf16[528,1024]{1,0:T(8,128)(2,1)}, u32[]{:S(2)}, u32[]{:S(2)}) collective-permute-start(bf16[528,1024]{1,0:T(8,128)(2,1)S(1)} %message_rows.1.refs_6_), channel_id=1, source_target_pairs={{3,0},{0,1},{1,2},{2,3},{7,4},{4,5},{5,6},{6,7},{11,8},{8,9},{9,10... | collective-permute-start | bytes 3244040 | tf_op jit(solution)/shard_map/ppermute | solution.py:178
  14.2 26.9 %collective-permute-start = (bf16[528,1024]{1,0:T(8,128)(2,1)S(1)}, bf16[528,1024]{1,0:T(8,128)(2,1)S(1)}, u32[]{:S(2)}, u32[]{:S(2)}) collective-permute-start(bf16[528,1024]{1,0:T(8,128)(2,1)S(1)} %message_rows.1.refs_6_), channel_id=1, source_target_pairs={{8,0},{16,8},{24,16},{0,24},{9,1},{17,9},{25,17},{1,25},{10,2},{18... | collective-permute-start | bytes 3244040 | tf_op jit(solution)/shard_map/ppermute | solution.py:178
  16.7 25.4 %collective-permute-start.1 = (bf16[528,1024]{1,0:T(8,128)(2,1)S(1)}, bf16[528,1024]{1,0:T(8,128)(2,1)}, u32[]{:S(2)}, u32[]{:S(2)}) collective-permute-start(bf16[528,1024]{1,0:T(8,128)(2,1)S(1)} %message_rows.1.refs_6_), channel_id=1, source_target_pairs={{24,0},{0,8},{8,16},{16,24},{25,1},{1,9},{9,17},{17,25},{26,2},{2,... | collective-permute-start | bytes 3244040 | tf_op jit(solution)/shard_map/ppermute | solution.py:178
  17.3 17.6 %all-to-all-start = ((s32[16,1,576]{2,1,0:T(1,128)}), s32[16,1,576]{2,1,0:T(1,128)S(1)}, u32[]{:S(2)}, u32[]{:S(2)}) async-start(s32[16,1,576]{2,1,0:T(1,128)} %broadcast_in_dim.67), calls=%async_computation | async-start | bytes 81920 | tf_op jit(solution)/shard_map/all_to_all | solution.py:272
  36.7 10.3 %copy-start.2 = (bf16[528,1024]{1,0:T(8,128)(2,1)}, bf16[528,1024]{1,0:T(8,128)(2,1)S(1)}, u32[]{:S(2)}) copy-start(bf16[528,1024]{1,0:T(8,128)(2,1)S(1)} %collective-permute-done.2.refs_7_) | copy-start | bytes 3244036
  37.3 24.2 %collective-permute-start.4 = (bf16[528,1024]{1,0:T(8,128)(2,1)S(1)}, bf16[528,1024]{1,0:T(8,128)(2,1)}, u32[]{:S(2)}, u32[]{:S(2)}) collective-permute-start(bf16[528,1024]{1,0:T(8,128)(2,1)S(1)} %collective-permute-done.2.refs_7_), channel_id=1, source_target_pairs={{8,0},{16,8},{24,16},{0,24},{9,1},{17,9},{25,17},{1,25},{10,2},{18... | collective-permute-start | bytes 3244040 | tf_op jit(solution)/shard_map/ppermute | solution.py:178
  39.9 25.1 %collective-permute-start.8 = (bf16[528,1024]{1,0:T(8,128)(2,1)}, bf16[528,1024]{1,0:T(8,128)(2,1)}, u32[]{:S(2)}, u32[]{:S(2)}) collective-permute-start(bf16[528,1024]{1,0:T(8,128)(2,1)} %collective-permute-done.3.refs_10_), channel_id=1, source_target_pairs={{24,0},{0,8},{8,16},{16,24},{25,1},{1,9},{9,17},{17,25},{26,2},{2,... | collective-permute-start | bytes 3244040 | tf_op jit(solution)/shard_map/ppermute | solution.py:178
  41.2 65.7 %copy-start.3 = (bf16[528,1024]{1,0:T(8,128)(2,1)}, bf16[528,1024]{1,0:T(8,128)(2,1)S(1)}, u32[]{:S(2)}) copy-start(bf16[528,1024]{1,0:T(8,128)(2,1)S(1)} %collective-permute-done.refs_11_) | copy-start | bytes 3244036
  41.2 24.5 %collective-permute-start.9 = (bf16[528,1024]{1,0:T(8,128)(2,1)S(1)}, bf16[528,1024]{1,0:T(8,128)(2,1)}, u32[]{:S(2)}, u32[]{:S(2)}) collective-permute-start(bf16[528,1024]{1,0:T(8,128)(2,1)S(1)} %collective-permute-done.refs_11_), channel_id=1, source_target_pairs={{3,0},{0,1},{1,2},{2,3},{7,4},{4,5},{5,6},{6,7},{11,8},{8,9},{9,10... | collective-permute-start | bytes 3244040 | tf_op jit(solution)/shard_map/ppermute | solution.py:178
  42.1 23.9 %collective-permute-start.5 = (bf16[528,1024]{1,0:T(8,128)(2,1)}, bf16[528,1024]{1,0:T(8,128)(2,1)}, u32[]{:S(2)}, u32[]{:S(2)}) collective-permute-start(bf16[528,1024]{1,0:T(8,128)(2,1)} %collective-permute-done.1.refs_23_), channel_id=1, source_target_pairs={{1,0},{2,1},{3,2},{0,3},{5,4},{6,5},{7,6},{4,7},{9,8},{10,9},{11,1... | collective-permute-start | bytes 3244040 | tf_op jit(solution)/shard_map/ppermute | solution.py:178
  47.0 43.0 %copy-start.8 = (bf16[272,1024]{1,0:T(8,128)(2,1)S(1)}, bf16[272,1024]{1,0:T(8,128)(2,1)}, u32[]{:S(2)}) copy-start(bf16[272,1024]{1,0:T(8,128)(2,1)} %slice.57) | copy-start | bytes 1671172
  61.5 16.4 %collective-permute-start.12 = (bf16[272,1024]{1,0:T(8,128)(2,1)S(1)}, bf16[272,1024]{1,0:T(8,128)(2,1)S(1)}, u32[]{:S(2)}, u32[]{:S(2)}) collective-permute-start(bf16[272,1024]{1,0:T(8,128)(2,1)S(1)} %slice.73), channel_id=1, source_target_pairs={{8,0},{16,8},{24,16},{0,24},{9,1},{17,9},{25,17},{1,25},{10,2},{18... | collective-permute-start | bytes 1671176 | tf_op jit(solution)/shard_map/ppermute | solution.py:178
  65.1 12.1 %collective-permute-start.13 = (bf16[256,1024]{1,0:T(8,128)(2,1)S(1)}, bf16[256,1024]{1,0:T(8,128)(2,1)S(1)}, u32[]{:S(2)}, u32[]{:S(2)}) collective-permute-start(bf16[256,1024]{1,0:T(8,128)(2,1)S(1)} %slice.74), channel_id=1, source_target_pairs={{24,0},{0,8},{8,16},{16,24},{25,1},{1,9},{9,17},{17,25},{26,2},{2,... | collective-permute-start | bytes 1572872 | tf_op jit(solution)/shard_map/ppermute | solution.py:178
  65.7 24.4 %collective-permute-start.10 = (bf16[528,1024]{1,0:T(8,128)(2,1)}, bf16[528,1024]{1,0:T(8,128)(2,1)S(1)}, u32[]{:S(2)}, u32[]{:S(2)}) collective-permute-start(bf16[528,1024]{1,0:T(8,128)(2,1)} %collective-permute-done.8.refs_26_), channel_id=1, source_target_pairs={{3,0},{0,1},{1,2},{2,3},{7,4},{4,5},{5,6},{6,7},{11,8},{8,9},{9,10... | collective-permute-start | bytes 3244040 | tf_op jit(solution)/shard_map/ppermute | solution.py:178
  66.0 24.1 %collective-permute-start.6 = (bf16[528,1024]{1,0:T(8,128)(2,1)}, bf16[528,1024]{1,0:T(8,128)(2,1)S(1)}, u32[]{:S(2)}, u32[]{:S(2)}) collective-permute-start(bf16[528,1024]{1,0:T(8,128)(2,1)} %collective-permute-done.4.refs_12_), channel_id=1, source_target_pairs={{1,0},{2,1},{3,2},{0,3},{5,4},{6,5},{7,6},{4,7},{9,8},{10,9},{11,1... | collective-permute-start | bytes 3244040 | tf_op jit(solution)/shard_map/ppermute | solution.py:178
  77.1 0.8 copy-start.11
  77.1 23.4 %collective-permute-start.14 = (bf16[528,1024]{1,0:T(8,128)(2,1)}, bf16[528,1024]{1,0:T(8,128)(2,1)S(1)}, u32[]{:S(2)}, u32[]{:S(2)}) collective-permute-start(bf16[528,1024]{1,0:T(8,128)(2,1)} %collective-permute-done.5.refs_24_), channel_id=1, source_target_pairs={{24,0},{0,8},{8,16},{16,24},{25,1},{1,9},{9,17},{17,25},{26,2},{2,... | collective-permute-start | bytes 3244040 | tf_op jit(solution)/shard_map/ppermute | solution.py:178
  77.9 29.0 %copy-start.9 = (bf16[272,1024]{1,0:T(8,128)(2,1)}, bf16[272,1024]{1,0:T(8,128)(2,1)S(1)}, u32[]{:S(2)}) copy-start(bf16[272,1024]{1,0:T(8,128)(2,1)S(1)} %collective-permute-done.12.refs_15_) | copy-start | bytes 1671172
  77.9 26.3 %collective-permute-start.15 = (bf16[528,1024]{1,0:T(8,128)(2,1)}, bf16[528,1024]{1,0:T(8,128)(2,1)S(1)}, u32[]{:S(2)}, u32[]{:S(2)}) collective-permute-start(bf16[528,1024]{1,0:T(8,128)(2,1)} %collective-permute-done.9.refs_14_), channel_id=1, source_target_pairs={{8,0},{16,8},{24,16},{0,24},{9,1},{17,9},{25,17},{1,25},{10,2},{18... | collective-permute-start | bytes 3244040 | tf_op jit(solution)/shard_map/ppermute | solution.py:178
  90.0 16.9 %copy-start.4 = (bf16[528,1024]{1,0:T(8,128)(2,1)}, bf16[528,1024]{1,0:T(8,128)(2,1)S(1)}, u32[]{:S(2)}) copy-start(bf16[528,1024]{1,0:T(8,128)(2,1)S(1)} %collective-permute-done.10.refs_25_) | copy-start | bytes 3244036
  90.1 16.9 %collective-permute-start.11 = (bf16[256,1024]{1,0:T(8,128)(2,1)S(1)}, bf16[256,1024]{1,0:T(8,128)(2,1)S(1)}, u32[]{:S(2)}, u32[]{:S(2)}) collective-permute-start(bf16[256,1024]{1,0:T(8,128)(2,1)S(1)} %slice.75), channel_id=1, source_target_pairs={{3,0},{0,1},{1,2},{2,3},{7,4},{4,5},{5,6},{6,7},{11,8},{8,9},{9,10... | collective-permute-start | bytes 1572872 | tf_op jit(solution)/shard_map/ppermute | solution.py:178
  90.1 16.9 %copy-start.5 = (bf16[528,1024]{1,0:T(8,128)(2,1)}, bf16[528,1024]{1,0:T(8,128)(2,1)S(1)}, u32[]{:S(2)}) copy-start(bf16[528,1024]{1,0:T(8,128)(2,1)S(1)} %collective-permute-done.6.refs_13_) | copy-start | bytes 3244036
  90.1 17.0 %collective-permute-start.7 = (bf16[272,1024]{1,0:T(8,128)(2,1)S(1)}, bf16[272,1024]{1,0:T(8,128)(2,1)S(1)}, u32[]{:S(2)}, u32[]{:S(2)}) collective-permute-start(bf16[272,1024]{1,0:T(8,128)(2,1)S(1)} %copy-done.8), channel_id=1, source_target_pairs={{1,0},{2,1},{3,2},{0,3},{5,4},{6,5},{7,6},{4,7},{9,8},{10,9},{11,1... | collective-permute-start | bytes 1671176 | tf_op jit(solution)/shard_map/ppermute | solution.py:178
  100.5 6.5 %copy-start.6 = (bf16[528,1024]{1,0:T(8,128)(2,1)}, bf16[528,1024]{1,0:T(8,128)(2,1)S(1)}, u32[]{:S(2)}) copy-start(bf16[528,1024]{1,0:T(8,128)(2,1)S(1)} %collective-permute-done.14.refs_17_) | copy-start | bytes 3244036
  100.5 9.7 %collective-permute-start.17 = (bf16[144,1024]{1,0:T(8,128)(2,1)S(1)}, bf16[144,1024]{1,0:T(8,128)(2,1)S(1)}, u32[]{:S(2)}, u32[]{:S(2)}) collective-permute-start(bf16[144,1024]{1,0:T(8,128)(2,1)S(1)} %slice.65), channel_id=1, source_target_pairs={{24,0},{0,8},{8,16},{16,24},{25,1},{1,9},{9,17},{17,25},{26,2},{2,... | collective-permute-start | bytes 884744 | tf_op jit(solution)/shard_map/ppermute | solution.py:178
  100.6 7.5 %collective-permute-start.19 = (bf16[128,1024]{1,0:T(8,128)(2,1)S(1)}, bf16[128,1024]{1,0:T(8,128)(2,1)S(1)}, u32[]{:S(2)}, u32[]{:S(2)}) collective-permute-start(bf16[128,1024]{1,0:T(8,128)(2,1)S(1)} %slice.77), channel_id=1, source_target_pairs={{1,0},{2,1},{3,2},{0,3},{5,4},{6,5},{7,6},{4,7},{9,8},{10,9},{11,1... | collective-permute-start | bytes 786440 | tf_op jit(solution)/shard_map/ppermute | solution.py:178
  104.2 2.9 %copy-start.7 = (bf16[528,1024]{1,0:T(8,128)(2,1)}, bf16[528,1024]{1,0:T(8,128)(2,1)S(1)}, u32[]{:S(2)}) copy-start(bf16[528,1024]{1,0:T(8,128)(2,1)S(1)} %collective-permute-done.15.refs_22_) | copy-start | bytes 3244036
  104.2 6.0 %collective-permute-start.16 = (bf16[128,1024]{1,0:T(8,128)(2,1)S(1)}, bf16[128,1024]{1,0:T(8,128)(2,1)S(1)}, u32[]{:S(2)}, u32[]{:S(2)}) collective-permute-start(bf16[128,1024]{1,0:T(8,128)(2,1)S(1)} %slice.66), channel_id=1, source_target_pairs={{8,0},{16,8},{24,16},{0,24},{9,1},{17,9},{25,17},{1,25},{10,2},{18... | collective-permute-start | bytes 786440 | tf_op jit(solution)/shard_map/ppermute | solution.py:178
  106.9 3.2 %copy-start.12 = (bf16[256,1024]{1,0:T(8,128)(2,1)}, bf16[256,1024]{1,0:T(8,128)(2,1)S(1)}, u32[]{:S(2)}) copy-start(bf16[256,1024]{1,0:T(8,128)(2,1)S(1)} %collective-permute-done.11.refs_9_) | copy-start | bytes 1572868
  106.9 6.5 %collective-permute-start.18 = (bf16[128,1024]{1,0:T(8,128)(2,1)S(1)}, bf16[128,1024]{1,0:T(8,128)(2,1)S(1)}, u32[]{:S(2)}, u32[]{:S(2)}) collective-permute-start(bf16[128,1024]{1,0:T(8,128)(2,1)S(1)} %slice.76), channel_id=1, source_target_pairs={{3,0},{0,1},{1,2},{2,3},{7,4},{4,5},{5,6},{6,7},{11,8},{8,9},{9,10... | collective-permute-start | bytes 786440 | tf_op jit(solution)/shard_map/ppermute | solution.py:178
  107.1 1.0 copy-start.10
  108.1 5.4 %copy-start.14 = (bf16[128,1024]{1,0:T(8,128)(2,1)}, bf16[128,1024]{1,0:T(8,128)(2,1)S(1)}, u32[]{:S(2)}) copy-start(bf16[128,1024]{1,0:T(8,128)(2,1)S(1)} %collective-permute-done.19.refs_21_) | copy-start | bytes 786436
  110.9 0.7 copy-start.13
  127.2 20.6 %collective-permute-start.22 = (f32[16,128]{1,0:T(8,128)S(1)}, f32[16,128]{1,0:T(8,128)S(1)}, u32[]{:S(2)}, u32[]{:S(2)}) collective-permute-start(f32[16,128]{1,0:T(8,128)S(1)} %get-tuple-element.88), channel_id=1, source_target_pairs={{1,0},{2,1},{3,2},{0,3},{5,4},{6,5},{7,6},{4,7},{9,8},{10,9},{11,1... | collective-permute-start | bytes 24584 | tf_op jit(solution)/shard_map/ppermute | solution.py:178
  127.3 20.5 %collective-permute-start.21 = (f32[16,128]{1,0:T(8,128)S(1)}, f32[16,128]{1,0:T(8,128)S(1)}, u32[]{:S(2)}, u32[]{:S(2)}) collective-permute-start(f32[16,128]{1,0:T(8,128)S(1)} %get-tuple-element.87), channel_id=1, source_target_pairs={{2,0},{3,1},{0,2},{1,3},{6,4},{7,5},{4,6},{5,7},{10,8},{11,9},{8,1... | collective-permute-start | bytes 24584 | tf_op jit(solution)/shard_map/ppermute | solution.py:178
  128.2 19.6 %collective-permute-start.20 = (f32[16,128]{1,0:T(8,128)S(1)}, f32[16,128]{1,0:T(8,128)S(1)}, u32[]{:S(2)}, u32[]{:S(2)}) collective-permute-start(f32[16,128]{1,0:T(8,128)S(1)} %get-tuple-element.86), channel_id=1, source_target_pairs={{3,0},{0,1},{1,2},{2,3},{7,4},{4,5},{5,6},{6,7},{11,8},{8,9},{9,10... | collective-permute-start | bytes 24584 | tf_op jit(solution)/shard_map/ppermute | solution.py:178
  128.7 26.4 %all-to-all-start.1 = ((f32[16,4,128]{2,1,0:T(4,128)}), f32[16,4,128]{2,1,0:T(4,128)S(1)}, u32[]{:S(2)}, u32[]{:S(2)}) async-start(f32[16,4,128]{2,1,0:T(4,128)} %bitcast.5), calls=%async_computation.1 | async-start | bytes 65536 | tf_op jit(solution)/shard_map/all_to_all | solution.py:287
  147.8 7.4 %collective-permute-start.25 = (f32[4,128]{1,0:T(4,128)S(1)}, f32[4,128]{1,0:T(4,128)S(1)}, u32[]{:S(2)}, u32[]{:S(2)}) collective-permute-start(f32[4,128]{1,0:T(4,128)S(1)} %get-tuple-element.96), channel_id=1, source_target_pairs={{8,0},{16,8},{24,16},{0,24},{9,1},{17,9},{25,17},{1,25},{10,2},{18... | collective-permute-start | bytes 6152 | tf_op jit(solution)/shard_map/ppermute | solution.py:178
  147.9 7.3 %collective-permute-start.24 = (f32[4,128]{1,0:T(4,128)S(1)}, f32[4,128]{1,0:T(4,128)S(1)}, u32[]{:S(2)}, u32[]{:S(2)}) collective-permute-start(f32[4,128]{1,0:T(4,128)S(1)} %get-tuple-element.97), channel_id=1, source_target_pairs={{16,0},{24,8},{0,16},{8,24},{17,1},{25,9},{1,17},{9,25},{18,2},{26... | collective-permute-start | bytes 6152 | tf_op jit(solution)/shard_map/ppermute | solution.py:178
  148.0 7.2 %collective-permute-start.23 = (f32[4,128]{1,0:T(4,128)S(1)}, f32[4,128]{1,0:T(4,128)S(1)}, u32[]{:S(2)}, u32[]{:S(2)}) collective-permute-start(f32[4,128]{1,0:T(4,128)S(1)} %get-tuple-element.95), channel_id=1, source_target_pairs={{24,0},{0,8},{8,16},{16,24},{25,1},{1,9},{9,17},{17,25},{26,2},{2,... | collective-permute-start | bytes 6152 | tf_op jit(solution)/shard_map/ppermute | solution.py:178
  (2 other events, 1.4 us)
Sparse Core Ops, SparseCore 0:
  9.2 100.5 all-gather.1

commit v6 on v5

--- a/solution.py
+++ b/solution.py
@@ -15,30 +15,36 @@
 SLOTS = 8
 DEPTH = 5
 VMEM_LIMIT = 32 * 1024 * 1024
-
-
-def unit_kernel(emb_ref, unit_ref):
+COLUMNS = ((0, 1, 3), (2,))
+
+
+def unit_kernel(ids_ref, valid_ref, emb_ref, unit_ref, full_ref, rows_buf, sems):
+    copies = [pltpu.make_async_copy(emb_ref.at[block], rows_buf.at[block], sems.at[block]) for block in range(BLOCKS)]
+    for copy in copies:
+        copy.start()
+    labels = jnp.where(valid_ref[...] > 0, ids_ref[...], -1).astype(jnp.float32).astype(jnp.bfloat16)
+    full_ref[2 * ROWS : HALF1, :] = jnp.zeros((META, 1024), jnp.bfloat16)
     for block in range(BLOCKS):
-        rows = emb_ref[block].astype(jnp.float32)
+        full_ref[2 * ROWS : 2 * ROWS + 1, block * ROWS : (block + 1) * ROWS] = labels[block : block + 1, :]
+        copies[block].wait()
+        rows = rows_buf[block].astype(jnp.float32)
         scale = lax.rsqrt(jnp.sum(rows * rows, axis=-1, keepdims=True) + epsilon)
-        unit_ref[block * ROWS : (block + 1) * ROWS, :] = (rows * scale).astype(jnp.bfloat16)
-
-
-def message_kernel(unit_ref, meta_ref, full_ref):
-    full_ref[: 2 * ROWS, :] = unit_ref[: 2 * ROWS, :]
-    full_ref[2 * ROWS : HALF1, :] = meta_ref[...]
-    full_ref[HALF1:, :] = unit_ref[2 * ROWS :, :]
-
-
-def pair_kernel(right_at, meta_at, todo, block_of, used, place, left_tags, left_ref, *rest):
-    refs = rest[:-14]
+        unit = (rows * scale).astype(jnp.bfloat16)
+        unit_ref[block * ROWS : (block + 1) * ROWS, :] = unit
+        at = block * ROWS + (META if block >= 2 else 0)
+        full_ref[at : at + ROWS, :] = unit
+
+
+def pair_kernel(columns, right_at, meta_at, todo, block_of, used, place, left_tags, *rest):
+    blocks = 4 * len(columns)
+    before, left_ref, refs = rest[:5], rest[5], rest[6:-14]
     left_out, *right_out = rest[-14:-9]
     left_buf, right_buf, right_meta, right_tags, even, odd, left_best, right_best, sems = rest[-9:]
     left_sems, right_sems = sems.at[0], sems.at[1]
 
     def each_right(j, act):
         for dy in range(4):
-            ref, base = right_at[j // 4 * 4 + dy][j % 4]
+            ref, base = right_at[columns[j // 4] * 4 + dy][j % 4]
             act(refs[ref].at[pl.ds(base, ROWS), :], right_buf.at[j, pl.ds(dy * ROWS, ROWS), :])
 
     def fetch_right(j):
@@ -57,10 +63,10 @@
                 row = pl.multiple_of(unit * ROWS, ROWS)
                 act(pltpu.make_async_copy(left_ref.at[pl.ds(row, ROWS), :], left_buf.at[slot, part, :], left_sems.at[slot * 2 + h]))
 
-    count = used[16]
-    for k in range(16):
-        ref, row = meta_at[k]
-        pltpu.make_async_copy(refs[ref].at[pl.ds(row, META), :], right_meta.at[k], right_sems.at[16]).start()
+    count = used[blocks]
+    for k in range(blocks):
+        ref, row = meta_at[columns[k // 4] * 4 + k % 4]
+        pltpu.make_async_copy(refs[ref].at[pl.ds(row, META), :], right_meta.at[k], right_sems.at[blocks]).start()
     for j in range(2):
         fetch_right(j)
     for i in range(SLOTS):
@@ -69,12 +75,13 @@
         def _(i=i):
             each_left(jnp.int32(i), lambda copy: copy.start())
 
-    for j in range(2, 16):
+    for j in range(2, blocks):
         fetch_right(j)
-    left_best[...] = jnp.full(left_best.shape, -1.0, jnp.float32)
+    left_best[0:64, :] = before[0][...]
+    left_best[64:72, :] = jnp.full((8, ROWS), -1.0, jnp.float32)
     right_best[...] = jnp.full(right_best.shape, -1.0, jnp.float32)
-    pltpu.make_async_copy(right_meta, right_meta, right_sems.at[16]).wait()
-    for k in range(16):
+    pltpu.make_async_copy(right_meta, right_meta, right_sems.at[blocks]).wait()
+    for k in range(blocks):
         row = right_meta[k, 0:1, : 4 * ROWS].astype(jnp.float32)
         row = jnp.where(row < 0.0, -2.0, row)
         for b in range(4):
@@ -89,7 +96,7 @@
         j = block_of[i]
         before = block_of[jnp.maximum(i - 1, 0)]
 
-        @pl.when((i < used[17]) & ((i == 0) | (j != before)))
+        @pl.when((i < used[blocks + 1]) & ((i == 0) | (j != before)))
         def _():
             pltpu.make_async_copy(right_buf.at[j], right_buf.at[j], right_sems.at[j]).wait()
 
@@ -105,12 +112,12 @@
         for h in range(2):
             unit = todo[2 * i + h]
             tags = jnp.broadcast_to(left_tags[pl.ds(unit, 1), :], (ROWS, ROWS)).T
-            same = (j < 4) & (unit == me * 4 + j)
+            same = (j < 4) & (unit == me * 4 + j) if columns[0] == 0 else False
             best = None
             for dy in range(4):
                 cols = slice(dy * ROWS, (dy + 1) * ROWS)
                 keep = tags == right_row[:, cols]
-                if dy == 0:
+                if dy == 0 and columns[0] == 0:
                     keep = keep & (off_diagonal | jnp.logical_not(same))
                 masked = jnp.where(keep, scores[h * ROWS : (h + 1) * ROWS, cols], -1.0)
                 best = masked if best is None else jnp.maximum(best, masked)
@@ -144,33 +151,50 @@
     each_left(count + 1, lambda copy: copy.wait())
     left_out[...] = left_best[0:64, :]
     for dy in range(4):
-        right_out[dy][...] = right_best[:, dy * ROWS : (dy + 1) * ROWS]
-
-
-def pair_maxima(todo, block_of, used, place, left_tags, left_rows, operands, right_at, meta_at):
+        right_out[dy][...] = before[1 + dy][...]
+        for k, dx in enumerate(columns):
+            right_out[dy][dx * 4 : dx * 4 + 4, :] = right_best[k * 4 : k * 4 + 4, dy * ROWS : (dy + 1) * ROWS]
+
+
+def pair_maxima(columns, steps, place, left_tags, before, left_rows, parts, metas):
+    operands, known = [], {}
+
+    def place_of(value):
+        if id(value) not in known:
+            known[id(value)] = len(operands)
+            operands.append(value)
+        return known[id(value)]
+
+    right_at, meta_at = {}, {}
+    for dx in columns:
+        for dy in range(4):
+            right_at[dx * 4 + dy] = [(place_of(value), base) for value, base in parts[dx, dy]]
+            meta_at[dx * 4 + dy] = (place_of(metas[dx, dy][0]), metas[dx, dy][1])
+
     def kernel(*refs):
-        pair_kernel(right_at, meta_at, *refs)
-
+        pair_kernel(columns, right_at, meta_at, *refs)
+
+    blocks = 4 * len(columns)
     smem, vmem, hbm = (pl.BlockSpec(memory_space=s) for s in (pltpu.SMEM, pltpu.VMEM, pltpu.HBM))
     return pl.pallas_call(
         kernel,
         out_shape=[jax.ShapeDtypeStruct((n, ROWS), jnp.float32) for n in (64, 16, 16, 16, 16)],
-        in_specs=[smem] * 4 + [vmem] + [hbm] * (len(operands) + 1),
+        in_specs=[smem] * 4 + [vmem] * 6 + [hbm] * (len(operands) + 1),
         out_specs=[vmem] * 5,
         scratch_shapes=[
             pltpu.VMEM((SLOTS, 2 * ROWS, 1024), jnp.bfloat16),
-            pltpu.VMEM((16, 4 * ROWS, 1024), jnp.bfloat16),
-            pltpu.VMEM((16, META, 1024), jnp.bfloat16),
-            pltpu.VMEM((16, 4 * ROWS), jnp.float32),
+            pltpu.VMEM((blocks, 4 * ROWS, 1024), jnp.bfloat16),
+            pltpu.VMEM((blocks, META, 1024), jnp.bfloat16),
+            pltpu.VMEM((blocks, 4 * ROWS), jnp.float32),
             pltpu.VMEM((2 * ROWS, 4 * ROWS), jnp.float32),
             pltpu.VMEM((2 * ROWS, 4 * ROWS), jnp.float32),
             pltpu.VMEM((72, ROWS), jnp.float32),
-            pltpu.VMEM((16, 4 * ROWS), jnp.float32),
+            pltpu.VMEM((blocks, 4 * ROWS), jnp.float32),
             pltpu.SemaphoreType.DMA((2, 2 * SLOTS + 1)),
         ],
         compiler_params=pltpu.CompilerParams(vmem_limit_bytes=VMEM_LIMIT),
         name="pair_maxima",
-    )(todo, block_of, used, place, left_tags, *(pltpu.with_memory_space_constraint(v, pltpu.HBM) for v in (left_rows, *operands)))
+    )(*steps, place, left_tags, *before, *(pltpu.with_memory_space_constraint(v, pltpu.HBM) for v in (left_rows, *operands)))
 
 
 def shift(value, axis, by):
@@ -240,50 +264,49 @@
     dx = ((group // 2) % 4 - my_x) % 4
     unit_of = (jnp.arange(16)[:, None] * BLOCKS + a)[:, :, None]
     block = jnp.where(mine, dx * BLOCKS + b % BLOCKS, -1)
-    unit_of = jnp.max(jnp.where(block[:, :, None] == jnp.arange(16), unit_of + 1, 0), axis=1).T.reshape(256)
-    listed = (unit_of > 0).reshape(16, 16)
+    unit_of = jnp.max(jnp.where(block[:, :, None] == jnp.arange(16), unit_of + 1, 0), axis=1).T
+    left_tags = jnp.pad(left_tags, ((0, 8), (0, 0)), constant_values=-3.0)
+    return [step_lists(columns, unit_of) for columns in COLUMNS], place, left_tags
+
+
+def step_lists(columns, unit_of):
+    blocks = 4 * len(columns)
+    unit_of = jnp.concatenate([unit_of[4 * dx : 4 * dx + 4] for dx in columns])
+    listed = unit_of > 0
     order = jnp.arange(16)
     rank = jnp.sum(listed[:, None, :] & (order[None, None, :] < order[None, :, None]), axis=2)
     steps = (jnp.sum(listed, axis=1) + 1) // 2
-    first = jnp.sum(jnp.where(order[None, :] < jnp.arange(17)[:, None], steps[None, :], 0), axis=1)
-    at = jnp.where(listed, 2 * first[:16, None] + rank, -1).reshape(256)
-    todo = jnp.max(jnp.where(at == jnp.arange(88)[:, None], unit_of, 0), axis=1)
+    first = jnp.sum(jnp.where(order[None, :blocks] < jnp.arange(blocks + 1)[:, None], steps[None, :], 0), axis=1)
+    at = jnp.where(listed, 2 * first[:blocks, None] + rank, -1).reshape(-1)
+    most = 10 * len(columns) + 4
+    todo = jnp.max(jnp.where(at == jnp.arange(2 * most)[:, None], unit_of.reshape(-1), 0), axis=1)
     todo = jnp.where(todo > 0, todo - 1, 64)
-    block_of = jnp.minimum(jnp.sum(first[None, 1:] <= jnp.arange(44)[:, None], axis=1), 15)
-    used = jnp.concatenate([steps, (first[16:] + 1) // 2 * 2, first[16:]])
-    left_tags = jnp.pad(left_tags, ((0, 8), (0, 0)), constant_values=-3.0)
-    return todo, block_of, used, place, left_tags
+    block_of = jnp.minimum(jnp.sum(first[None, 1:] <= jnp.arange(most)[:, None], axis=1), blocks - 1)
+    used = jnp.concatenate([steps, (first[blocks:] + 1) // 2 * 2, first[blocks:]])
+    return todo, block_of, used
 
 
 def local(embeddings, cluster_ids, valid, pair_left, pair_right):
-    limit = pltpu.CompilerParams(vmem_limit_bytes=VMEM_LIMIT)
-    unit = pl.pallas_call(
-        unit_kernel, out_shape=jax.ShapeDtypeStruct((4 * ROWS, 1024), jnp.bfloat16), compiler_params=limit, name="unit_rows"
-    )(embeddings)
-    unit, cluster_ids, pair_left = lax.optimization_barrier((unit, cluster_ids, pair_left))
+    vmem, hbm = (pl.BlockSpec(memory_space=s) for s in (pltpu.VMEM, pltpu.HBM))
+    unit, full = pl.pallas_call(
+        unit_kernel,
+        out_shape=[jax.ShapeDtypeStruct((n, 1024), jnp.bfloat16) for n in (4 * ROWS, FULL)],
+        in_specs=[vmem, vmem, hbm],
+        out_specs=[vmem, vmem],
+        scratch_shapes=[pltpu.VMEM(embeddings.shape, jnp.bfloat16), pltpu.SemaphoreType.DMA((BLOCKS,))],
+        compiler_params=pltpu.CompilerParams(vmem_limit_bytes=VMEM_LIMIT),
+        name="unit_rows",
+    )(cluster_ids, valid, pltpu.with_memory_space_constraint(embeddings, pltpu.HBM))
+    full, cluster_ids, pair_left = lax.optimization_barrier((full, cluster_ids, pair_left))
     left_rows = lax.all_gather(unit, ("z", "c"), axis=0, tiled=True)
     labels = jnp.where(valid > 0, cluster_ids, -1).reshape(1, -1)
     lists = jnp.concatenate([labels, (pair_left % BLOCKS)[None], pair_right[None]], axis=1)
-    meta = jnp.pad(lists.astype(jnp.bfloat16), ((0, META - 1), (0, 1024 - lists.shape[1])))
-    full = pl.pallas_call(
-        message_kernel, out_shape=jax.ShapeDtypeStruct((FULL, 1024), jnp.bfloat16), compiler_params=limit, name="message_rows"
-    )(unit, meta)
-    full, lists = lax.optimization_barrier((full, lists))
     left_lists = lax.all_to_all(jnp.broadcast_to(lists, (16, lists.shape[1])), ("z", "c"), 0, 0, tiled=True)
-    parts, metas, beside = gather_plane(full, left_lists, pair_lists)
-
-    operands, known, right_at, meta_at = [], {}, [], []
-
-    def place_of(value):
-        if id(value) not in known:
-            known[id(value)] = len(operands)
-            operands.append(value)
-        return known[id(value)]
-
-    for k in [(dx, dy) for dx in range(4) for dy in range(4)]:
-        right_at.append([(place_of(value), base) for value, base in parts[k]])
-        meta_at.append((place_of(metas[k][0]), metas[k][1]))
-    left_best, *right_best = pair_maxima(*beside, left_rows, operands, right_at, meta_at)
+    parts, metas, (steps, place, left_tags) = gather_plane(full, left_lists, pair_lists)
+    found = [jnp.full((n, ROWS), -1.0, jnp.float32) for n in (64, 16, 16, 16, 16)]
+    for columns, some in zip(COLUMNS, steps):
+        found = pair_maxima(columns, some, place, left_tags, found, left_rows, parts, metas)
+    left_best, *right_best = found
     from_left = lax.all_to_all(left_best.reshape(16, BLOCKS, ROWS), ("z", "c"), 0, 0, tiled=True)
     own = right_best[0]
     for came in [shift(right_best[dy], "y", -dy) for dy in (1, 2, 3)]:

time: 162 us -> 163 us (level); the launches traced: 163 us -> 162 us
  waiting for transfers between devices: 58.7 us -> 53 us
  Pallas kernels: 15.6 us -> 18.8 us
  starting transfers between devices: 62.1 us -> 59 us
  local copies, waits for them, and re-layouts: 9.07 us -> 11.7 us
    ppermute x26, waiting for transfers between devices: 45 us -> 39.8 us  [shift(): lax.ppermute(value, axis, [((i + by) % size, i) for i in range(size)])]
    all_to_all x1, starting transfers between devices: 19 us -> 14.7 us  [local(): lax.all_to_all(left_best.reshape(16, BLOCKS, ROWS), ('z', 'c'), 0, 0, til...]
    pallas_call x1 -> x2, Pallas kernels: 13 us -> 16.2 us  [pair_maxima(): pl.pallas_call(kernel, out_shape=[jax.ShapeDtypeStruct((n, ROWS), jnp.flo...]
    slice x4, local copies, waits for them, and re-layouts: 0.07 us -> 2.25 us  [gather_plane(): send(step, cells[name][0][at:HALF1 if link == 'x-' else at + ROWS])]
    unnamed x43 -> x41, local copies, waits for them, and re-layouts: 4.2 us -> 3.66 us
  transfers between devices with their start and end apart: 29 -> 29, of which waited for: 13 -> 9; matrix products, arithmetic and copies ran while one was open for 4% -> 7% of each run, Pallas kernels for 1% -> 6%
where the time goes in v6:
time: 163 us; the launch traced here: 162 us
  starting transfers between devices  59 us (36%)
  waiting for transfers between devices  53 us (33%)
  Pallas kernels  18.8 us (12%)
  between operations  15.2 us (9%)
  local copies, waits for them, and re-layouts  11.7 us (7%)
  other arithmetic  4.12 us (3%)
    ppermute x26, waiting for transfers between devices, shift(): lax.ppermute(value, axis, [((i + by) % size, i) for i in range(size)])  39.8 us
    ppermute x26, starting transfers between devices, shift(): lax.ppermute(value, axis, [((i + by) % size, i) for i in range(size)])  34.5 us
    pallas_call x2, Pallas kernels, pair_maxima(): pl.pallas_call(kernel, out_shape=[jax.ShapeDtypeStruct((n, ROWS), jnp.flo...  16.2 us
    all_to_all x1, starting transfers between devices, local(): lax.all_to_all(left_best.reshape(16, BLOCKS, ROWS), ('z', 'c'), 0, 0, til...  14.7 us
    all_to_all x1, starting transfers between devices, local(): lax.all_to_all(jnp.broadcast_to(lists, (16, lists.shape[1])), ('z', 'c'),...  9.71 us
    all_to_all x1, waiting for transfers between devices, local(): lax.all_to_all(jnp.broadcast_to(lists, (16, lists.shape[1])), ('z', 'c'),...  7.87 us
    all_to_all x1, waiting for transfers between devices, local(): lax.all_to_all(left_best.reshape(16, BLOCKS, ROWS), ('z', 'c'), 0, 0, til...  5.28 us
    unnamed x41, local copies, waits for them, and re-layouts  3.66 us
  transfers between devices with their start and end apart: 29, of which 9 were waited for; matrix products, arithmetic and copies ran while one was open for 7% of the time, Pallas kernels for 6%

profile of v6, /device:TPU:1, one launch (start us, length us, event | category | flops | bytes accessed | tf_op | source)
XLA Modules:
  0.0 161.7 jit_solution(8537641435226962421)
XLA Ops:
  6.5 0.7 copy-done.1
  7.2 0.7 copy-done.3
  7.9 2.6 %unit_rows.1 = (bf16[512,1024]{1,0:T(8,128)(2,1)}, bf16[528,1024]{1,0:T(8,128)(2,1)S(1)}) custom-call(s32[4,128]{1,0:T(4,128)S(1)} %copy-done.1, s32[4,128]{1,0:T(4,128)S(1)} %copy-done.3, bf16[4,128,1024]{2,1,0:T(8,128)(2,1)} %emb_ref.1), custom_call_target="tpu_custom_call" | custom-call | tf_op jit(solution)/shard_map/unit_rows/pallas_call | solution.py:291
  10.5 3.6 %collective-permute-start.2 = (bf16[528,1024]{1,0:T(8,128)(2,1)S(1)}, bf16[528,1024]{1,0:T(8,128)(2,1)S(1)}, u32[]{:S(2)}, u32[]{:S(2)}) collective-permute-start(bf16[528,1024]{1,0:T(8,128)(2,1)S(1)} %get-tuple-element.56.refs_11_), channel_id=1, source_target_pairs={{1,0},{2,1},{3,2},{0,3},{5,4},{6,5},{7,6},{4,7},{9,8},{10,9},{11,1... | collective-permute-start | bytes 3244040 | tf_op jit(solution)/shard_map/ppermute | solution.py:202
  14.2 2.5 %collective-permute-start = (bf16[528,1024]{1,0:T(8,128)(2,1)S(1)}, bf16[528,1024]{1,0:T(8,128)(2,1)S(1)}, u32[]{:S(2)}, u32[]{:S(2)}) collective-permute-start(bf16[528,1024]{1,0:T(8,128)(2,1)S(1)} %get-tuple-element.56.refs_11_), channel_id=1, source_target_pairs={{8,0},{16,8},{24,16},{0,24},{9,1},{17,9},{25,17},{1,25},{10,2},{18... | collective-permute-start | bytes 3244040 | tf_op jit(solution)/shard_map/ppermute | solution.py:202
  16.8 0.6 broadcast_in_dim.115
  17.4 9.7 %all-to-all-start = ((s32[16,1,576]{2,1,0:T(1,128)}), s32[16,1,576]{2,1,0:T(1,128)S(1)}, u32[]{:S(2)}, u32[]{:S(2)}) async-start(s32[16,1,576]{2,1,0:T(1,128)} %broadcast_in_dim.115), calls=%async_computation | async-start | bytes 81920 | tf_op jit(solution)/shard_map/all_to_all | solution.py:304
  27.2 7.9 %all-to-all-done = s32[16,1,576]{2,1,0:T(1,128)S(1)} async-done(((s32[16,1,576]{2,1,0:T(1,128)}), s32[16,1,576]{2,1,0:T(1,128)S(1)}, u32[]{:S(2)}, u32[]{:S(2)}) %all-to-all-start) | async-done | bytes 36896 | tf_op jit(solution)/shard_map/all_to_all | solution.py:304
  35.0 1.6 %collective-permute-done.2.refs_12_ = bf16[528,1024]{1,0:T(8,128)(2,1)S(1)} collective-permute-done((bf16[528,1024]{1,0:T(8,128)(2,1)S(1)}, bf16[528,1024]{1,0:T(8,128)(2,1)S(1)}, u32[]{:S(2)}, u32[]{:S(2)}) %collective-permute-start.2) | collective-permute-done | bytes 1081376 | tf_op jit(solution)/shard_map/ppermute | solution.py:202
  39.1 2.5 %collective-permute-start.4 = (bf16[528,1024]{1,0:T(8,128)(2,1)S(1)}, bf16[528,1024]{1,0:T(8,128)(2,1)}, u32[]{:S(2)}, u32[]{:S(2)}) collective-permute-start(bf16[528,1024]{1,0:T(8,128)(2,1)S(1)} %collective-permute-done.2.refs_12_), channel_id=1, source_target_pairs={{8,0},{16,8},{24,16},{0,24},{9,1},{17,9},{25,17},{1,25},{10,2},{18... | collective-permute-start | bytes 3244040 | tf_op jit(solution)/shard_map/ppermute | solution.py:202
  41.6 0.5 collective-permute-done.3.refs_15_
  42.1 0.5 collective-permute-start.9
  42.8 0.6 slice.98
  44.1 2.7 %collective-permute-start.5 = (bf16[528,1024]{1,0:T(8,128)(2,1)}, bf16[528,1024]{1,0:T(8,128)(2,1)}, u32[]{:S(2)}, u32[]{:S(2)}) collective-permute-start(bf16[528,1024]{1,0:T(8,128)(2,1)} %collective-permute-done.1.refs_20_), channel_id=1, source_target_pairs={{1,0},{2,1},{3,2},{0,3},{5,4},{6,5},{7,6},{4,7},{9,8},{10,9},{11,1... | collective-permute-start | bytes 3244040 | tf_op jit(solution)/shard_map/ppermute | solution.py:202
  46.9 0.7 pad_add_fusion.2.refs_2_
  47.7 0.6 slice.93
  48.9 0.9 slice.84
  49.8 1.1 slice.109
  51.0 1.1 slice.110
  52.2 0.7 pad_add_fusion.1
  52.9 10.3 %collective-permute-done.4.refs_17_ = bf16[528,1024]{1,0:T(8,128)(2,1)} collective-permute-done((bf16[528,1024]{1,0:T(8,128)(2,1)S(1)}, bf16[528,1024]{1,0:T(8,128)(2,1)}, u32[]{:S(2)}, u32[]{:S(2)}) %collective-permute-start.4) | collective-permute-done | bytes 1081376 | tf_op jit(solution)/shard_map/ppermute | solution.py:202
  63.2 3.6 %collective-permute-done.8.refs_23_ = bf16[528,1024]{1,0:T(8,128)(2,1)} collective-permute-done((bf16[528,1024]{1,0:T(8,128)(2,1)}, bf16[528,1024]{1,0:T(8,128)(2,1)}, u32[]{:S(2)}, u32[]{:S(2)}) %collective-permute-start.8) | collective-permute-done | bytes 1081376 | tf_op jit(solution)/shard_map/ppermute | solution.py:202
  66.8 0.9 collective-permute-start.12
  67.7 0.6 collective-permute-start.13
  68.3 0.8 collective-permute-start.10
  69.1 2.7 %collective-permute-start.6 = (bf16[528,1024]{1,0:T(8,128)(2,1)}, bf16[528,1024]{1,0:T(8,128)(2,1)S(1)}, u32[]{:S(2)}, u32[]{:S(2)}) collective-permute-start(bf16[528,1024]{1,0:T(8,128)(2,1)} %collective-permute-done.4.refs_17_), channel_id=1, source_target_pairs={{1,0},{2,1},{3,2},{0,3},{5,4},{6,5},{7,6},{4,7},{9,8},{10,9},{11,1... | collective-permute-start | bytes 3244040 | tf_op jit(solution)/shard_map/ppermute | solution.py:202
  71.8 6.9 %collective-permute-done.13.refs_12_ = bf16[256,1024]{1,0:T(8,128)(2,1)S(1)} collective-permute-done((bf16[256,1024]{1,0:T(8,128)(2,1)S(1)}, bf16[256,1024]{1,0:T(8,128)(2,1)S(1)}, u32[]{:S(2)}, u32[]{:S(2)}) %collective-permute-start.13) | collective-permute-done | bytes 524320 | tf_op jit(solution)/shard_map/ppermute | solution.py:202
  78.7 2.7 %collective-permute-start.15 = (bf16[528,1024]{1,0:T(8,128)(2,1)}, bf16[528,1024]{1,0:T(8,128)(2,1)S(1)}, u32[]{:S(2)}, u32[]{:S(2)}) collective-permute-start(bf16[528,1024]{1,0:T(8,128)(2,1)} %collective-permute-done.9.refs_19_), channel_id=1, source_target_pairs={{8,0},{16,8},{24,16},{0,24},{9,1},{17,9},{25,17},{1,25},{10,2},{18... | collective-permute-start | bytes 3244040 | tf_op jit(solution)/shard_map/ppermute | solution.py:202
  81.4 11.6 %collective-permute-done.10.refs_22_ = bf16[528,1024]{1,0:T(8,128)(2,1)S(1)} collective-permute-done((bf16[528,1024]{1,0:T(8,128)(2,1)}, bf16[528,1024]{1,0:T(8,128)(2,1)S(1)}, u32[]{:S(2)}, u32[]{:S(2)}) %collective-permute-start.10) | collective-permute-done | bytes 1081376 | tf_op jit(solution)/shard_map/ppermute | solution.py:202
  93.1 2.7 %collective-permute-start.7 = (bf16[272,1024]{1,0:T(8,128)(2,1)S(1)}, bf16[272,1024]{1,0:T(8,128)(2,1)S(1)}, u32[]{:S(2)}, u32[]{:S(2)}) collective-permute-start(bf16[272,1024]{1,0:T(8,128)(2,1)S(1)} %copy-done.13), channel_id=1, source_target_pairs={{1,0},{2,1},{3,2},{0,3},{5,4},{6,5},{7,6},{4,7},{9,8},{10,9},{11,1... | collective-permute-start | bytes 1671176 | tf_op jit(solution)/shard_map/ppermute | solution.py:202
  95.9 5.2 %collective-permute-done.14.refs_13_ = bf16[528,1024]{1,0:T(8,128)(2,1)S(1)} collective-permute-done((bf16[528,1024]{1,0:T(8,128)(2,1)}, bf16[528,1024]{1,0:T(8,128)(2,1)S(1)}, u32[]{:S(2)}, u32[]{:S(2)}) %collective-permute-start.14) | collective-permute-done | bytes 1081376 | tf_op jit(solution)/shard_map/ppermute | solution.py:202
  101.1 0.8 slice.101
  101.9 0.7 slice.115
  102.7 4.7 %collective-permute-start.19 = (bf16[128,1024]{1,0:T(8,128)(2,1)}, bf16[128,1024]{1,0:T(8,128)(2,1)}, u32[]{:S(2)}, u32[]{:S(2)}) collective-permute-start(bf16[128,1024]{1,0:T(8,128)(2,1)} %slice.115), channel_id=1, source_target_pairs={{1,0},{2,1},{3,2},{0,3},{5,4},{6,5},{7,6},{4,7},{9,8},{10,9},{11,1... | collective-permute-start | bytes 786440 | tf_op jit(solution)/shard_map/ppermute | solution.py:202
  107.4 2.6 %collective-permute-start.16 = (bf16[128,1024]{1,0:T(8,128)(2,1)}, bf16[128,1024]{1,0:T(8,128)(2,1)}, u32[]{:S(2)}, u32[]{:S(2)}) collective-permute-start(bf16[128,1024]{1,0:T(8,128)(2,1)} %slice.101), channel_id=1, source_target_pairs={{8,0},{16,8},{24,16},{0,24},{9,1},{17,9},{25,17},{1,25},{10,2},{18... | collective-permute-start | bytes 786440 | tf_op jit(solution)/shard_map/ppermute | solution.py:202
  110.0 0.7 slice.114
  110.8 0.7 copy-done.14
  111.5 0.8 copy-done.11
  112.3 9.9 %pair_maxima.2 = (f32[64,128]{1,0:T(8,128)S(1)}, f32[16,128]{1,0:T(8,128)S(1)}, f32[16,128]{1,0:T(8,128)S(1)}, f32[16,128]{1,0:T(8,128)S(1)}, f32[16,128]{1,0:T(8,128)S(1)}) custom-call(s32[68]{0:T(128)S(1)} %compare_select_fusion.3.refs_0_, s32[34]{0:T(128)S(1)} %broadcast_minimum_fusion.1.refs_1_, s32[14]{0:T(128)S(1)} %get-tuple-element.68.refs_2_, ...), custom_call_target="tpu_custom_call" | custom-call | tf_op jit(solution)/shard_map/pair_maxima/pallas_call | solution.py:179
  122.3 0.7 copy-done.16
  123.1 6.3 %pair_maxima.3 = (f32[64,128]{1,0:T(8,128)}, f32[16,128]{1,0:T(8,128)S(1)}, f32[16,128]{1,0:T(8,128)S(1)}, f32[16,128]{1,0:T(8,128)S(1)}, f32[16,128]{1,0:T(8,128)S(1)}) custom-call(s32[28]{0:T(128)S(1)} %compare_select_fusion.2.refs_0_, s32[14]{0:T(128)S(1)} %get-tuple-element.62.refs_1_, s32[6]{0:T(128)S(1)} %pad_add_fusion.2.refs_2_, s32[1]{0:T(128)} %bitcast.4.refs_3_, ...), custom_call_target="tpu_custom_call" | custom-call | tf_op jit(solution)/shard_map/pair_maxima/pallas_call | solution.py:179
  129.4 2.0 %collective-permute-start.22 = (f32[16,128]{1,0:T(8,128)S(1)}, f32[16,128]{1,0:T(8,128)S(1)}, u32[]{:S(2)}, u32[]{:S(2)}) collective-permute-start(f32[16,128]{1,0:T(8,128)S(1)} %get-tuple-element.104), channel_id=1, source_target_pairs={{1,0},{2,1},{3,2},{0,3},{5,4},{6,5},{7,6},{4,7},{9,8},{10,9},{11,1... | collective-permute-start | bytes 24584 | tf_op jit(solution)/shard_map/ppermute | solution.py:202
  131.4 0.7 collective-permute-start.20
  132.1 14.7 %all-to-all-start.1 = ((f32[16,4,128]{2,1,0:T(4,128)}), f32[16,4,128]{2,1,0:T(4,128)S(1)}, u32[]{:S(2)}, u32[]{:S(2)}) async-start(f32[16,4,128]{2,1,0:T(4,128)} %bitcast.5), calls=%async_computation.1 | async-start | bytes 65536 | tf_op jit(solution)/shard_map/all_to_all | solution.py:310
  146.9 0.7 collective-permute-start.25
  147.6 1.4 collective-permute-start.24
  149.0 5.3 %all-to-all-done.1 = f32[16,4,128]{2,1,0:T(4,128)S(1)} async-done(((f32[16,4,128]{2,1,0:T(4,128)}), f32[16,4,128]{2,1,0:T(4,128)S(1)}, u32[]{:S(2)}, u32[]{:S(2)}) %all-to-all-start.1) | async-done | bytes 32800 | tf_op jit(solution)/shard_map/all_to_all | solution.py:310
  154.3 0.6 fusion.15
  (116 shorter events, 3.4 us)
Async XLA Ops:
  6.5 105.0 %all-gather.2.cloned.1.call-start = ((), (), s32[]{:S(2)}) async-start(), calls=%async_computation.2 | async-start | bytes 17825792 | tf_op jit(solution)/shard_map/all_gather | solution.py:301
  7.2 0.7 copy-start.3
  7.9 8.8 %copy-start.19 = (s32[32]{0:T(128)S(1)}, s32[32]{0:T(128)}, u32[]{:S(2)}) copy-start(s32[32]{0:T(128)} %param.8) | copy-start | bytes 388
  7.9 8.8 %copy-start.2 = (s32[4,128]{1,0:T(4,128)S(1)}, s32[4,128]{1,0:T(4,128)}, u32[]{:S(2)}) copy-start(s32[4,128]{1,0:T(4,128)} %ids_ref.1) | copy-start | bytes 6148
  7.9 8.8 %copy-start.4 = (s32[4,128]{1,0:T(4,128)S(1)}, s32[4,128]{1,0:T(4,128)}, u32[]{:S(2)}) copy-start(s32[4,128]{1,0:T(4,128)} %valid_ref.1) | copy-start | bytes 6148
  7.9 8.8 %copy-start.18 = (s32[32]{0:T(128)S(1)}, s32[32]{0:T(128)}, u32[]{:S(2)}) copy-start(s32[32]{0:T(128)} %param.9) | copy-start | bytes 388
  10.5 39.3 %copy-start = (bf16[528,1024]{1,0:T(8,128)(2,1)}, bf16[528,1024]{1,0:T(8,128)(2,1)S(1)}, u32[]{:S(2)}) copy-start(bf16[528,1024]{1,0:T(8,128)(2,1)S(1)} %get-tuple-element.56.refs_11_) | copy-start | bytes 3244036
  10.5 26.2 %collective-permute-start.2 = (bf16[528,1024]{1,0:T(8,128)(2,1)S(1)}, bf16[528,1024]{1,0:T(8,128)(2,1)S(1)}, u32[]{:S(2)}, u32[]{:S(2)}) collective-permute-start(bf16[528,1024]{1,0:T(8,128)(2,1)S(1)} %get-tuple-element.56.refs_11_), channel_id=1, source_target_pairs={{1,0},{2,1},{3,2},{0,3},{5,4},{6,5},{7,6},{4,7},{9,8},{10,9},{11,1... | collective-permute-start | bytes 3244040 | tf_op jit(solution)/shard_map/ppermute | solution.py:202
  14.2 27.9 %collective-permute-start = (bf16[528,1024]{1,0:T(8,128)(2,1)S(1)}, bf16[528,1024]{1,0:T(8,128)(2,1)S(1)}, u32[]{:S(2)}, u32[]{:S(2)}) collective-permute-start(bf16[528,1024]{1,0:T(8,128)(2,1)S(1)} %get-tuple-element.56.refs_11_), channel_id=1, source_target_pairs={{8,0},{16,8},{24,16},{0,24},{9,1},{17,9},{25,17},{1,25},{10,2},{18... | collective-permute-start | bytes 3244040 | tf_op jit(solution)/shard_map/ppermute | solution.py:202
  16.6 27.5 %collective-permute-start.1 = (bf16[528,1024]{1,0:T(8,128)(2,1)S(1)}, bf16[528,1024]{1,0:T(8,128)(2,1)}, u32[]{:S(2)}, u32[]{:S(2)}) collective-permute-start(bf16[528,1024]{1,0:T(8,128)(2,1)S(1)} %get-tuple-element.56.refs_11_), channel_id=1, source_target_pairs={{24,0},{0,8},{8,16},{16,24},{25,1},{1,9},{9,17},{17,25},{26,2},{2,... | collective-permute-start | bytes 3244040 | tf_op jit(solution)/shard_map/ppermute | solution.py:202
  16.6 25.4 %collective-permute-start.3 = (bf16[528,1024]{1,0:T(8,128)(2,1)S(1)}, bf16[528,1024]{1,0:T(8,128)(2,1)}, u32[]{:S(2)}, u32[]{:S(2)}) collective-permute-start(bf16[528,1024]{1,0:T(8,128)(2,1)S(1)} %get-tuple-element.56.refs_11_), channel_id=1, source_target_pairs={{3,0},{0,1},{1,2},{2,3},{7,4},{4,5},{5,6},{6,7},{11,8},{8,9},{9,10... | collective-permute-start | bytes 3244040 | tf_op jit(solution)/shard_map/ppermute | solution.py:202
  17.4 17.6 %all-to-all-start = ((s32[16,1,576]{2,1,0:T(1,128)}), s32[16,1,576]{2,1,0:T(1,128)S(1)}, u32[]{:S(2)}, u32[]{:S(2)}) async-start(s32[16,1,576]{2,1,0:T(1,128)} %broadcast_in_dim.115), calls=%async_computation | async-start | bytes 81920 | tf_op jit(solution)/shard_map/all_to_all | solution.py:304
  36.7 13.1 %copy-start.5 = (bf16[528,1024]{1,0:T(8,128)(2,1)}, bf16[528,1024]{1,0:T(8,128)(2,1)S(1)}, u32[]{:S(2)}) copy-start(bf16[528,1024]{1,0:T(8,128)(2,1)S(1)} %collective-permute-done.2.refs_12_) | copy-start | bytes 3244036
  39.1 24.1 %collective-permute-start.4 = (bf16[528,1024]{1,0:T(8,128)(2,1)S(1)}, bf16[528,1024]{1,0:T(8,128)(2,1)}, u32[]{:S(2)}, u32[]{:S(2)}) collective-permute-start(bf16[528,1024]{1,0:T(8,128)(2,1)S(1)} %collective-permute-done.2.refs_12_), channel_id=1, source_target_pairs={{8,0},{16,8},{24,16},{0,24},{9,1},{17,9},{25,17},{1,25},{10,2},{18... | collective-permute-start | bytes 3244040 | tf_op jit(solution)/shard_map/ppermute | solution.py:202
  42.1 24.7 %collective-permute-start.8 = (bf16[528,1024]{1,0:T(8,128)(2,1)}, bf16[528,1024]{1,0:T(8,128)(2,1)}, u32[]{:S(2)}, u32[]{:S(2)}) collective-permute-start(bf16[528,1024]{1,0:T(8,128)(2,1)} %collective-permute-done.3.refs_15_), channel_id=1, source_target_pairs={{24,0},{0,8},{8,16},{16,24},{25,1},{1,9},{9,17},{17,25},{26,2},{2,... | collective-permute-start | bytes 3244040 | tf_op jit(solution)/shard_map/ppermute | solution.py:202
  42.1 7.7 %copy-start.6 = (bf16[528,1024]{1,0:T(8,128)(2,1)}, bf16[528,1024]{1,0:T(8,128)(2,1)S(1)}, u32[]{:S(2)}) copy-start(bf16[528,1024]{1,0:T(8,128)(2,1)S(1)} %collective-permute-done.refs_16_) | copy-start | bytes 3244036
  42.1 26.2 %collective-permute-start.9 = (bf16[528,1024]{1,0:T(8,128)(2,1)S(1)}, bf16[528,1024]{1,0:T(8,128)(2,1)}, u32[]{:S(2)}, u32[]{:S(2)}) collective-permute-start(bf16[528,1024]{1,0:T(8,128)(2,1)S(1)} %collective-permute-done.refs_16_), channel_id=1, source_target_pairs={{3,0},{0,1},{1,2},{2,3},{7,4},{4,5},{5,6},{6,7},{11,8},{8,9},{9,10... | collective-permute-start | bytes 3244040 | tf_op jit(solution)/shard_map/ppermute | solution.py:202
  44.1 25.0 %collective-permute-start.5 = (bf16[528,1024]{1,0:T(8,128)(2,1)}, bf16[528,1024]{1,0:T(8,128)(2,1)}, u32[]{:S(2)}, u32[]{:S(2)}) collective-permute-start(bf16[528,1024]{1,0:T(8,128)(2,1)} %collective-permute-done.1.refs_20_), channel_id=1, source_target_pairs={{1,0},{2,1},{3,2},{0,3},{5,4},{6,5},{7,6},{4,7},{9,8},{10,9},{11,1... | collective-permute-start | bytes 3244040 | tf_op jit(solution)/shard_map/ppermute | solution.py:202
  49.8 43.2 %copy-start.13 = (bf16[272,1024]{1,0:T(8,128)(2,1)S(1)}, bf16[272,1024]{1,0:T(8,128)(2,1)}, u32[]{:S(2)}) copy-start(bf16[272,1024]{1,0:T(8,128)(2,1)} %slice.84) | copy-start | bytes 1671172
  66.8 11.9 %collective-permute-start.12 = (bf16[272,1024]{1,0:T(8,128)(2,1)S(1)}, bf16[272,1024]{1,0:T(8,128)(2,1)S(1)}, u32[]{:S(2)}, u32[]{:S(2)}) collective-permute-start(bf16[272,1024]{1,0:T(8,128)(2,1)S(1)} %slice.108), channel_id=1, source_target_pairs={{8,0},{16,8},{24,16},{0,24},{9,1},{17,9},{25,17},{1,25},{10,2},{18... | collective-permute-start | bytes 1671176 | tf_op jit(solution)/shard_map/ppermute | solution.py:202
  67.7 11.0 %collective-permute-start.13 = (bf16[256,1024]{1,0:T(8,128)(2,1)S(1)}, bf16[256,1024]{1,0:T(8,128)(2,1)S(1)}, u32[]{:S(2)}, u32[]{:S(2)}) collective-permute-start(bf16[256,1024]{1,0:T(8,128)(2,1)S(1)} %slice.109), channel_id=1, source_target_pairs={{24,0},{0,8},{8,16},{16,24},{25,1},{1,9},{9,17},{17,25},{26,2},{2,... | collective-permute-start | bytes 1572872 | tf_op jit(solution)/shard_map/ppermute | solution.py:202
  68.3 24.8 %collective-permute-start.10 = (bf16[528,1024]{1,0:T(8,128)(2,1)}, bf16[528,1024]{1,0:T(8,128)(2,1)S(1)}, u32[]{:S(2)}, u32[]{:S(2)}) collective-permute-start(bf16[528,1024]{1,0:T(8,128)(2,1)} %collective-permute-done.8.refs_23_), channel_id=1, source_target_pairs={{3,0},{0,1},{1,2},{2,3},{7,4},{4,5},{5,6},{6,7},{11,8},{8,9},{9,10... | collective-permute-start | bytes 3244040 | tf_op jit(solution)/shard_map/ppermute | solution.py:202
  69.1 23.9 %collective-permute-start.6 = (bf16[528,1024]{1,0:T(8,128)(2,1)}, bf16[528,1024]{1,0:T(8,128)(2,1)S(1)}, u32[]{:S(2)}, u32[]{:S(2)}) collective-permute-start(bf16[528,1024]{1,0:T(8,128)(2,1)} %collective-permute-done.4.refs_17_), channel_id=1, source_target_pairs={{1,0},{2,1},{3,2},{0,3},{5,4},{6,5},{7,6},{4,7},{9,8},{10,9},{11,1... | collective-permute-start | bytes 3244040 | tf_op jit(solution)/shard_map/ppermute | solution.py:202
  78.7 14.4 %copy-start.15 = (bf16[256,1024]{1,0:T(8,128)(2,1)}, bf16[256,1024]{1,0:T(8,128)(2,1)S(1)}, u32[]{:S(2)}) copy-start(bf16[256,1024]{1,0:T(8,128)(2,1)S(1)} %collective-permute-done.13.refs_12_) | copy-start | bytes 1572868
  78.7 22.4 %collective-permute-start.14 = (bf16[528,1024]{1,0:T(8,128)(2,1)}, bf16[528,1024]{1,0:T(8,128)(2,1)S(1)}, u32[]{:S(2)}, u32[]{:S(2)}) collective-permute-start(bf16[528,1024]{1,0:T(8,128)(2,1)} %collective-permute-done.5.refs_21_), channel_id=1, source_target_pairs={{24,0},{0,8},{8,16},{16,24},{25,1},{1,9},{9,17},{17,25},{26,2},{2,... | collective-permute-start | bytes 3244040 | tf_op jit(solution)/shard_map/ppermute | solution.py:202
  78.7 14.3 %copy-start.12 = (bf16[272,1024]{1,0:T(8,128)(2,1)}, bf16[272,1024]{1,0:T(8,128)(2,1)S(1)}, u32[]{:S(2)}) copy-start(bf16[272,1024]{1,0:T(8,128)(2,1)S(1)} %collective-permute-done.12.refs_11_) | copy-start | bytes 1671172
  78.7 28.6 %collective-permute-start.15 = (bf16[528,1024]{1,0:T(8,128)(2,1)}, bf16[528,1024]{1,0:T(8,128)(2,1)S(1)}, u32[]{:S(2)}, u32[]{:S(2)}) collective-permute-start(bf16[528,1024]{1,0:T(8,128)(2,1)} %collective-permute-done.9.refs_19_), channel_id=1, source_target_pairs={{8,0},{16,8},{24,16},{0,24},{9,1},{17,9},{25,17},{1,25},{10,2},{18... | collective-permute-start | bytes 3244040 | tf_op jit(solution)/shard_map/ppermute | solution.py:202
  93.0 17.7 %copy-start.7 = (bf16[528,1024]{1,0:T(8,128)(2,1)}, bf16[528,1024]{1,0:T(8,128)(2,1)S(1)}, u32[]{:S(2)}) copy-start(bf16[528,1024]{1,0:T(8,128)(2,1)S(1)} %collective-permute-done.10.refs_22_) | copy-start | bytes 3244036
  93.0 17.7 %collective-permute-start.11 = (bf16[256,1024]{1,0:T(8,128)(2,1)S(1)}, bf16[256,1024]{1,0:T(8,128)(2,1)S(1)}, u32[]{:S(2)}, u32[]{:S(2)}) collective-permute-start(bf16[256,1024]{1,0:T(8,128)(2,1)S(1)} %slice.110), channel_id=1, source_target_pairs={{3,0},{0,1},{1,2},{2,3},{7,4},{4,5},{5,6},{6,7},{11,8},{8,9},{9,10... | collective-permute-start | bytes 1572872 | tf_op jit(solution)/shard_map/ppermute | solution.py:202
  93.1 18.5 %copy-start.8 = (bf16[528,1024]{1,0:T(8,128)(2,1)}, bf16[528,1024]{1,0:T(8,128)(2,1)S(1)}, u32[]{:S(2)}) copy-start(bf16[528,1024]{1,0:T(8,128)(2,1)S(1)} %collective-permute-done.6.refs_18_) | copy-start | bytes 3244036
  93.1 18.4 %collective-permute-start.7 = (bf16[272,1024]{1,0:T(8,128)(2,1)S(1)}, bf16[272,1024]{1,0:T(8,128)(2,1)S(1)}, u32[]{:S(2)}, u32[]{:S(2)}) collective-permute-start(bf16[272,1024]{1,0:T(8,128)(2,1)S(1)} %copy-done.13), channel_id=1, source_target_pairs={{1,0},{2,1},{3,2},{0,3},{5,4},{6,5},{7,6},{4,7},{9,8},{10,9},{11,1... | collective-permute-start | bytes 1671176 | tf_op jit(solution)/shard_map/ppermute | solution.py:202
  101.1 9.6 %copy-start.9 = (bf16[528,1024]{1,0:T(8,128)(2,1)}, bf16[528,1024]{1,0:T(8,128)(2,1)S(1)}, u32[]{:S(2)}) copy-start(bf16[528,1024]{1,0:T(8,128)(2,1)S(1)} %collective-permute-done.14.refs_13_) | copy-start | bytes 3244036
  101.1 21.2 %collective-permute-start.17 = (bf16[144,1024]{1,0:T(8,128)(2,1)S(1)}, bf16[144,1024]{1,0:T(8,128)(2,1)S(1)}, u32[]{:S(2)}, u32[]{:S(2)}) collective-permute-start(bf16[144,1024]{1,0:T(8,128)(2,1)S(1)} %slice.100), channel_id=1, source_target_pairs={{24,0},{0,8},{8,16},{16,24},{25,1},{1,9},{9,17},{17,25},{26,2},{2,... | collective-permute-start | bytes 884744 | tf_op jit(solution)/shard_map/ppermute | solution.py:202
  102.7 19.6 %collective-permute-start.19 = (bf16[128,1024]{1,0:T(8,128)(2,1)}, bf16[128,1024]{1,0:T(8,128)(2,1)}, u32[]{:S(2)}, u32[]{:S(2)}) collective-permute-start(bf16[128,1024]{1,0:T(8,128)(2,1)} %slice.115), channel_id=1, source_target_pairs={{1,0},{2,1},{3,2},{0,3},{5,4},{6,5},{7,6},{4,7},{9,8},{10,9},{11,1... | collective-permute-start | bytes 786440 | tf_op jit(solution)/shard_map/ppermute | solution.py:202
  107.4 3.5 %copy-start.10 = (bf16[528,1024]{1,0:T(8,128)(2,1)}, bf16[528,1024]{1,0:T(8,128)(2,1)S(1)}, u32[]{:S(2)}) copy-start(bf16[528,1024]{1,0:T(8,128)(2,1)S(1)} %collective-permute-done.15.refs_18_) | copy-start | bytes 3244036
  107.4 14.9 %collective-permute-start.16 = (bf16[128,1024]{1,0:T(8,128)(2,1)}, bf16[128,1024]{1,0:T(8,128)(2,1)}, u32[]{:S(2)}, u32[]{:S(2)}) collective-permute-start(bf16[128,1024]{1,0:T(8,128)(2,1)} %slice.101), channel_id=1, source_target_pairs={{8,0},{16,8},{24,16},{0,24},{9,1},{17,9},{25,17},{1,25},{10,2},{18... | collective-permute-start | bytes 786440 | tf_op jit(solution)/shard_map/ppermute | solution.py:202
  110.7 0.8 copy-start.14
  110.7 11.6 %collective-permute-start.18 = (bf16[128,1024]{1,0:T(8,128)(2,1)}, bf16[128,1024]{1,0:T(8,128)(2,1)S(1)}, u32[]{:S(2)}, u32[]{:S(2)}) collective-permute-start(bf16[128,1024]{1,0:T(8,128)(2,1)} %slice.114), channel_id=1, source_target_pairs={{3,0},{0,1},{1,2},{2,3},{7,4},{4,5},{5,6},{6,7},{11,8},{8,9},{9,10... | collective-permute-start | bytes 786440 | tf_op jit(solution)/shard_map/ppermute | solution.py:202
  111.5 0.8 copy-start.11
  122.3 0.7 copy-start.16
  122.3 0.8 copy-start.17
  129.4 17.5 %collective-permute-start.22 = (f32[16,128]{1,0:T(8,128)S(1)}, f32[16,128]{1,0:T(8,128)S(1)}, u32[]{:S(2)}, u32[]{:S(2)}) collective-permute-start(f32[16,128]{1,0:T(8,128)S(1)} %get-tuple-element.104), channel_id=1, source_target_pairs={{1,0},{2,1},{3,2},{0,3},{5,4},{6,5},{7,6},{4,7},{9,8},{10,9},{11,1... | collective-permute-start | bytes 24584 | tf_op jit(solution)/shard_map/ppermute | solution.py:202
  131.4 15.4 %collective-permute-start.21 = (f32[16,128]{1,0:T(8,128)S(1)}, f32[16,128]{1,0:T(8,128)S(1)}, u32[]{:S(2)}, u32[]{:S(2)}) collective-permute-start(f32[16,128]{1,0:T(8,128)S(1)} %get-tuple-element.103), channel_id=1, source_target_pairs={{2,0},{3,1},{0,2},{1,3},{6,4},{7,5},{4,6},{5,7},{10,8},{11,9},{8,1... | collective-permute-start | bytes 24584 | tf_op jit(solution)/shard_map/ppermute | solution.py:202
  131.4 15.4 %collective-permute-start.20 = (f32[16,128]{1,0:T(8,128)S(1)}, f32[16,128]{1,0:T(8,128)S(1)}, u32[]{:S(2)}, u32[]{:S(2)}) collective-permute-start(f32[16,128]{1,0:T(8,128)S(1)} %get-tuple-element.102), channel_id=1, source_target_pairs={{3,0},{0,1},{1,2},{2,3},{7,4},{4,5},{5,6},{6,7},{11,8},{8,9},{9,10... | collective-permute-start | bytes 24584 | tf_op jit(solution)/shard_map/ppermute | solution.py:202
  132.1 22.1 %all-to-all-start.1 = ((f32[16,4,128]{2,1,0:T(4,128)}), f32[16,4,128]{2,1,0:T(4,128)S(1)}, u32[]{:S(2)}, u32[]{:S(2)}) async-start(f32[16,4,128]{2,1,0:T(4,128)} %bitcast.5), calls=%async_computation.1 | async-start | bytes 65536 | tf_op jit(solution)/shard_map/all_to_all | solution.py:310
  146.9 7.4 %collective-permute-start.25 = (f32[4,128]{1,0:T(4,128)S(1)}, f32[4,128]{1,0:T(4,128)S(1)}, u32[]{:S(2)}, u32[]{:S(2)}) collective-permute-start(f32[4,128]{1,0:T(4,128)S(1)} %get-tuple-element.113), channel_id=1, source_target_pairs={{8,0},{16,8},{24,16},{0,24},{9,1},{17,9},{25,17},{1,25},{10,2},{18... | collective-permute-start | bytes 6152 | tf_op jit(solution)/shard_map/ppermute | solution.py:202
  147.6 6.7 %collective-permute-start.24 = (f32[4,128]{1,0:T(4,128)S(1)}, f32[4,128]{1,0:T(4,128)S(1)}, u32[]{:S(2)}, u32[]{:S(2)}) collective-permute-start(f32[4,128]{1,0:T(4,128)S(1)} %get-tuple-element.114), channel_id=1, source_target_pairs={{16,0},{24,8},{0,16},{8,24},{17,1},{25,9},{1,17},{9,25},{18,2},{26... | collective-permute-start | bytes 6152 | tf_op jit(solution)/shard_map/ppermute | solution.py:202
  148.9 5.3 %collective-permute-start.23 = (f32[4,128]{1,0:T(4,128)S(1)}, f32[4,128]{1,0:T(4,128)S(1)}, u32[]{:S(2)}, u32[]{:S(2)}) collective-permute-start(f32[4,128]{1,0:T(4,128)S(1)} %get-tuple-element.112), channel_id=1, source_target_pairs={{24,0},{0,8},{8,16},{16,24},{25,1},{1,9},{9,17},{17,25},{26,2},{2,... | collective-permute-start | bytes 6152 | tf_op jit(solution)/shard_map/ppermute | solution.py:202
  (1 other events, 0.7 us)
Sparse Core Ops, SparseCore 0:
  10.6 100.5 all-gather.1

commit v7 on v5

--- a/solution.py
+++ b/solution.py
@@ -17,17 +17,14 @@
 VMEM_LIMIT = 32 * 1024 * 1024
 
 
-def unit_kernel(emb_ref, unit_ref):
+def unit_kernel(emb_ref, unit_ref, full_ref):
     for block in range(BLOCKS):
         rows = emb_ref[block].astype(jnp.float32)
         scale = lax.rsqrt(jnp.sum(rows * rows, axis=-1, keepdims=True) + epsilon)
-        unit_ref[block * ROWS : (block + 1) * ROWS, :] = (rows * scale).astype(jnp.bfloat16)
-
-
-def message_kernel(unit_ref, meta_ref, full_ref):
-    full_ref[: 2 * ROWS, :] = unit_ref[: 2 * ROWS, :]
-    full_ref[2 * ROWS : HALF1, :] = meta_ref[...]
-    full_ref[HALF1:, :] = unit_ref[2 * ROWS :, :]
+        unit = (rows * scale).astype(jnp.bfloat16)
+        unit_ref[block * ROWS : (block + 1) * ROWS, :] = unit
+        at = block * ROWS + (META if block >= 2 else 0)
+        full_ref[at : at + ROWS, :] = unit
 
 
 def pair_kernel(right_at, meta_at, todo, block_of, used, place, left_tags, left_ref, *rest):
@@ -58,29 +55,21 @@
                 act(pltpu.make_async_copy(left_ref.at[pl.ds(row, ROWS), :], left_buf.at[slot, part, :], left_sems.at[slot * 2 + h]))
 
     count = used[16]
+    for j in range(2):
+        fetch_right(j)
+    for i in range(SLOTS):
+
+        @pl.when(i < count + 2)
+        def _(i=i):
+            each_left(jnp.int32(i), lambda copy: copy.start())
+
     for k in range(16):
         ref, row = meta_at[k]
         pltpu.make_async_copy(refs[ref].at[pl.ds(row, META), :], right_meta.at[k], right_sems.at[16]).start()
-    for j in range(2):
-        fetch_right(j)
-    for i in range(SLOTS):
-
-        @pl.when(i < count + 2)
-        def _(i=i):
-            each_left(jnp.int32(i), lambda copy: copy.start())
-
     for j in range(2, 16):
         fetch_right(j)
     left_best[...] = jnp.full(left_best.shape, -1.0, jnp.float32)
     right_best[...] = jnp.full(right_best.shape, -1.0, jnp.float32)
-    pltpu.make_async_copy(right_meta, right_meta, right_sems.at[16]).wait()
-    for k in range(16):
-        row = right_meta[k, 0:1, : 4 * ROWS].astype(jnp.float32)
-        row = jnp.where(row < 0.0, -2.0, row)
-        for b in range(4):
-            j = k // 4 * 4 + b
-            right_tags[j : j + 1, k % 4 * ROWS : (k % 4 + 1) * ROWS] = row[:, b * ROWS : (b + 1) * ROWS]
-
     off_diagonal = lax.broadcasted_iota(jnp.int32, (ROWS, ROWS), 0) != lax.broadcasted_iota(jnp.int32, (ROWS, ROWS), 1)
     me = place[0]
 
@@ -127,6 +116,13 @@
 
     arrive(jnp.int32(0))
     multiply(jnp.int32(0), even)
+    pltpu.make_async_copy(right_meta, right_meta, right_sems.at[16]).wait()
+    for k in range(16):
+        row = right_meta[k, 0:1, : 4 * ROWS].astype(jnp.float32)
+        row = jnp.where(row < 0.0, -2.0, row)
+        for b in range(4):
+            j = k // 4 * 4 + b
+            right_tags[j : j + 1, k % 4 * ROWS : (k % 4 + 1) * ROWS] = row[:, b * ROWS : (b + 1) * ROWS]
 
     def two(q, carry):
         i = 2 * q
@@ -180,10 +176,10 @@
 
 LINKS = {"x-": ("x", -1), "y-": ("y", -1), "x+": ("x", 1), "y+": ("y", 1)}
 CARRIED = {"c": {"x+": "y+", "x-": "y-", "y+": "x-", "y-": "x+"}, "d": {"y+": "x+", "y-": "x-", "x+": "y-", "x-": "y+"}}
-QUARTERS = {"x+": ("dy+", 0), "x-": ("dy-", ROWS), "y-": ("dx+", HALF1), "y+": ("dx-", HALF1 + ROWS)}
+LAST = {"x+": ("dy+", 0, ROWS), "x-": ("dy-", ROWS, HALF1 + ROWS), "y+": ("dx-", HALF1 + ROWS, FULL)}
 STEPS = (
     ("cx-", "cy-", "cx+", "cy+", "=", "dy-", "dy+", "bx-", "bx+"),
-    ("dx-", "dx+", "by-", "by+", "ey-", "ey+", "ex-", "ex+"),
+    ("dx-", "dx+", "by-", "by+", "ey+", "ex-", "ex+"),
 )
 AFTER = {"bx": "cx", "dx": "bx", "ex": "dx", "dy": "cy", "by": "dy"}
 
@@ -212,8 +208,8 @@
         elif kind == "b":
             send(step, cut[link])
         else:
-            name, at = QUARTERS[link]
-            send(step, cells[name][0][at : HALF1 if link == "x-" else at + ROWS])
+            name, low, high = LAST[link]
+            send(step, cells[name][0][low:high])
     whole = {(0, 0): [own]}
     names = ("ax+", "ax-", "ay+", "ay-", "cx+", "cx-", "cy+", "cy-", "dy+", "dy-", "dx+", "dx-")
     spots = [(1, 0), (3, 0), (0, 1), (0, 3), (1, 1), (3, 3), (3, 1), (1, 3), (1, 2), (3, 2), (2, 3), (2, 1)]
@@ -225,7 +221,7 @@
         h1, h2 = cells["b" + axis + "+"][0], cells["b" + axis + "-"][0]
         parts[key] = [(h1, 0), (h1, ROWS), (h2, 0), (h2, ROWS)]
         metas[key] = (h1, 2 * ROWS)
-    parts[2, 2] = [(cells[name][0], 0) for name in ("ex+", "ex-", "ey-", "ey+")]
+    parts[2, 2] = [(cells["ex+"][0], 0), (cells["ex-"][0], 0), (cells["ex-"][0], ROWS + META), (cells["ey+"][0], 0)]
     metas[2, 2] = (cells["ex-"][0], ROWS)
     return parts, metas, beside
 
@@ -257,17 +253,18 @@
 
 def local(embeddings, cluster_ids, valid, pair_left, pair_right):
     limit = pltpu.CompilerParams(vmem_limit_bytes=VMEM_LIMIT)
-    unit = pl.pallas_call(
-        unit_kernel, out_shape=jax.ShapeDtypeStruct((4 * ROWS, 1024), jnp.bfloat16), compiler_params=limit, name="unit_rows"
+    unit, full = pl.pallas_call(
+        unit_kernel,
+        out_shape=[jax.ShapeDtypeStruct((n, 1024), jnp.bfloat16) for n in (4 * ROWS, FULL)],
+        compiler_params=limit,
+        name="unit_rows",
     )(embeddings)
-    unit, cluster_ids, pair_left = lax.optimization_barrier((unit, cluster_ids, pair_left))
+    full, cluster_ids, pair_left = lax.optimization_barrier((full, cluster_ids, pair_left))
     left_rows = lax.all_gather(unit, ("z", "c"), axis=0, tiled=True)
     labels = jnp.where(valid > 0, cluster_ids, -1).reshape(1, -1)
     lists = jnp.concatenate([labels, (pair_left % BLOCKS)[None], pair_right[None]], axis=1)
-    meta = jnp.pad(lists.astype(jnp.bfloat16), ((0, META - 1), (0, 1024 - lists.shape[1])))
-    full = pl.pallas_call(
-        message_kernel, out_shape=jax.ShapeDtypeStruct((FULL, 1024), jnp.bfloat16), compiler_params=limit, name="message_rows"
-    )(unit, meta)
+    meta = jnp.pad(labels.astype(jnp.bfloat16), ((0, META - 1), (0, 1024 - labels.shape[1])))
+    full = lax.dynamic_update_slice(full, meta, (2 * ROWS, 0))
     full, lists = lax.optimization_barrier((full, lists))
     left_lists = lax.all_to_all(jnp.broadcast_to(lists, (16, lists.shape[1])), ("z", "c"), 0, 0, tiled=True)
     parts, metas, beside = gather_plane(full, left_lists, pair_lists)

time: 162 us -> 161 us (level)
  starting transfers between devices: 62.1 us -> 64 us
    ppermute x26 -> x25, starting transfers between devices: 33.4 us -> 38.4 us  [shift(): lax.ppermute(value, axis, [((i + by) % size, i) for i in range(size)])]
    all_to_all x1, starting transfers between devices: 19 us -> 15.9 us  [local(): lax.all_to_all(left_best.reshape(16, BLOCKS, ROWS), ('z', 'c'), 0, 0, til...]
    unnamed x43 -> x41, local copies, waits for them, and re-layouts: 4.2 us -> 2.64 us
    ppermute x26 -> x25, waiting for transfers between devices: 45 us -> 44.9 us  [shift(): lax.ppermute(value, axis, [((i + by) % size, i) for i in range(size)])]
  transfers between devices with their start and end apart: 29 -> 28, of which waited for: 13 -> 11; matrix products, arithmetic and copies ran while one was open for 4% -> 4% of each run, Pallas kernels for 1% -> 0%
where the time goes in v7:
time: 161 us; the launch traced here: 160 us
  starting transfers between devices  64 us (40%)
  waiting for transfers between devices  57.1 us (35%)
  Pallas kernels  14.7 us (9%)
  between operations  14.4 us (9%)
  local copies, waits for them, and re-layouts  7.55 us (5%)
  other arithmetic  2.71 us (2%)
    ppermute x25, waiting for transfers between devices, shift(): lax.ppermute(value, axis, [((i + by) % size, i) for i in range(size)])  44.9 us
    ppermute x25, starting transfers between devices, shift(): lax.ppermute(value, axis, [((i + by) % size, i) for i in range(size)])  38.4 us
    all_to_all x1, starting transfers between devices, local(): lax.all_to_all(left_best.reshape(16, BLOCKS, ROWS), ('z', 'c'), 0, 0, til...  15.9 us
    pallas_call x1, Pallas kernels, pair_maxima(): pl.pallas_call(kernel, out_shape=[jax.ShapeDtypeStruct((n, ROWS), jnp.flo...  13.3 us
    all_to_all x1, starting transfers between devices, local(): lax.all_to_all(jnp.broadcast_to(lists, (16, lists.shape[1])), ('z', 'c'),...  9.71 us
    all_to_all x1, waiting for transfers between devices, local(): lax.all_to_all(jnp.broadcast_to(lists, (16, lists.shape[1])), ('z', 'c'),...  7.88 us
    all_to_all x1, waiting for transfers between devices, local(): lax.all_to_all(left_best.reshape(16, BLOCKS, ROWS), ('z', 'c'), 0, 0, til...  4.26 us
  transfers between devices with their start and end apart: 28, of which 11 were waited for; matrix products, arithmetic and copies ran while one was open for 4% of the time, Pallas kernels for 0%

profile of v7, /device:TPU:1, one launch (start us, length us, event | category | flops | bytes accessed | tf_op | source)
XLA Modules:
  0.0 160.4 jit_solution(7802147128063871775)
XLA Ops:
  6.5 1.2 copy-done.1
  7.8 1.3 unit_rows.1
  9.3 3.6 %collective-permute-start.2 = (bf16[528,1024]{1,0:T(8,128)(2,1)S(1)}, bf16[528,1024]{1,0:T(8,128)(2,1)S(1)}, u32[]{:S(2)}, u32[]{:S(2)}) collective-permute-start(bf16[528,1024]{1,0:T(8,128)(2,1)S(1)} %pad_dynamic-update-slice_fusion.refs_6_), channel_id=1, source_target_pairs={{1,0},{2,1},{3,2},{0,3},{5,4},{6,5},{7,6},{4,7},{9,8},{10,9},{11,1... | collective-permute-start | bytes 3244040 | tf_op jit(solution)/shard_map/ppermute | solution.py:174
  12.9 2.5 %collective-permute-start = (bf16[528,1024]{1,0:T(8,128)(2,1)S(1)}, bf16[528,1024]{1,0:T(8,128)(2,1)S(1)}, u32[]{:S(2)}, u32[]{:S(2)}) collective-permute-start(bf16[528,1024]{1,0:T(8,128)(2,1)S(1)} %pad_dynamic-update-slice_fusion.refs_6_), channel_id=1, source_target_pairs={{8,0},{16,8},{24,16},{0,24},{9,1},{17,9},{25,17},{1,25},{10,2},{18... | collective-permute-start | bytes 3244040 | tf_op jit(solution)/shard_map/ppermute | solution.py:174
  15.4 0.6 broadcast_in_dim.73
  16.0 9.7 %all-to-all-start = ((s32[16,1,576]{2,1,0:T(1,128)}), s32[16,1,576]{2,1,0:T(1,128)S(1)}, u32[]{:S(2)}, u32[]{:S(2)}) async-start(s32[16,1,576]{2,1,0:T(1,128)} %broadcast_in_dim.73), calls=%async_computation | async-start | bytes 81920 | tf_op jit(solution)/shard_map/all_to_all | solution.py:269
  25.8 7.9 %all-to-all-done = s32[16,1,576]{2,1,0:T(1,128)S(1)} async-done(((s32[16,1,576]{2,1,0:T(1,128)}), s32[16,1,576]{2,1,0:T(1,128)S(1)}, u32[]{:S(2)}, u32[]{:S(2)}) %all-to-all-start) | async-done | bytes 36896 | tf_op jit(solution)/shard_map/all_to_all | solution.py:269
  33.7 1.8 %collective-permute-done.2.refs_7_ = bf16[528,1024]{1,0:T(8,128)(2,1)S(1)} collective-permute-done((bf16[528,1024]{1,0:T(8,128)(2,1)S(1)}, bf16[528,1024]{1,0:T(8,128)(2,1)S(1)}, u32[]{:S(2)}, u32[]{:S(2)}) %collective-permute-start.2) | collective-permute-done | bytes 1081376 | tf_op jit(solution)/shard_map/ppermute | solution.py:174
  35.4 0.1 fusion.8
  35.6 0.3 select_reduce_fusion
  36.0 0.4 convert_reduce_fusion
  36.4 2.5 %collective-permute-start.4 = (bf16[528,1024]{1,0:T(8,128)(2,1)S(1)}, bf16[528,1024]{1,0:T(8,128)(2,1)}, u32[]{:S(2)}, u32[]{:S(2)}) collective-permute-start(bf16[528,1024]{1,0:T(8,128)(2,1)S(1)} %collective-permute-done.2.refs_7_), channel_id=1, source_target_pairs={{8,0},{16,8},{24,16},{0,24},{9,1},{17,9},{25,17},{1,25},{10,2},{18... | collective-permute-start | bytes 3244040 | tf_op jit(solution)/shard_map/ppermute | solution.py:174
  38.9 0.9 collective-permute-start.8
  40.0 0.6 slice.60
  41.3 0.9 slice.54
  42.5 1.1 slice.71
  43.6 1.1 slice.70
  44.8 2.7 %collective-permute-start.5 = (bf16[528,1024]{1,0:T(8,128)(2,1)}, bf16[528,1024]{1,0:T(8,128)(2,1)S(1)}, u32[]{:S(2)}, u32[]{:S(2)}) collective-permute-start(bf16[528,1024]{1,0:T(8,128)(2,1)} %collective-permute-done.1.refs_22_), channel_id=1, source_target_pairs={{1,0},{2,1},{3,2},{0,3},{5,4},{6,5},{7,6},{4,7},{9,8},{10,9},{11,1... | collective-permute-start | bytes 3244040 | tf_op jit(solution)/shard_map/ppermute | solution.py:174
  47.7 0.1 select_reduce_fusion.1
  47.8 0.8 pad_add_fusion.1.refs_2_
  48.6 12.0 %collective-permute-done.4.refs_12_ = bf16[528,1024]{1,0:T(8,128)(2,1)} collective-permute-done((bf16[528,1024]{1,0:T(8,128)(2,1)S(1)}, bf16[528,1024]{1,0:T(8,128)(2,1)}, u32[]{:S(2)}, u32[]{:S(2)}) %collective-permute-start.4) | collective-permute-done | bytes 1081376 | tf_op jit(solution)/shard_map/ppermute | solution.py:174
  60.5 3.5 %collective-permute-done.8.refs_25_ = bf16[528,1024]{1,0:T(8,128)(2,1)} collective-permute-done((bf16[528,1024]{1,0:T(8,128)(2,1)}, bf16[528,1024]{1,0:T(8,128)(2,1)}, u32[]{:S(2)}, u32[]{:S(2)}) %collective-permute-start.8) | collective-permute-done | bytes 1081376 | tf_op jit(solution)/shard_map/ppermute | solution.py:174
  64.0 2.7 %collective-permute-start.12 = (bf16[272,1024]{1,0:T(8,128)(2,1)S(1)}, bf16[272,1024]{1,0:T(8,128)(2,1)}, u32[]{:S(2)}, u32[]{:S(2)}) collective-permute-start(bf16[272,1024]{1,0:T(8,128)(2,1)S(1)} %slice.69), channel_id=1, source_target_pairs={{8,0},{16,8},{24,16},{0,24},{9,1},{17,9},{25,17},{1,25},{10,2},{18... | collective-permute-start | bytes 1671176 | tf_op jit(solution)/shard_map/ppermute | solution.py:174
  66.7 2.5 %collective-permute-done.5.refs_23_ = bf16[528,1024]{1,0:T(8,128)(2,1)S(1)} collective-permute-done((bf16[528,1024]{1,0:T(8,128)(2,1)}, bf16[528,1024]{1,0:T(8,128)(2,1)S(1)}, u32[]{:S(2)}, u32[]{:S(2)}) %collective-permute-start.5) | collective-permute-done | bytes 1081376 | tf_op jit(solution)/shard_map/ppermute | solution.py:174
  69.2 3.4 %collective-permute-start.6 = (bf16[528,1024]{1,0:T(8,128)(2,1)}, bf16[528,1024]{1,0:T(8,128)(2,1)S(1)}, u32[]{:S(2)}, u32[]{:S(2)}) collective-permute-start(bf16[528,1024]{1,0:T(8,128)(2,1)} %collective-permute-done.4.refs_12_), channel_id=1, source_target_pairs={{1,0},{2,1},{3,2},{0,3},{5,4},{6,5},{7,6},{4,7},{9,8},{10,9},{11,1... | collective-permute-start | bytes 3244040 | tf_op jit(solution)/shard_map/ppermute | solution.py:174
  72.6 3.4 %collective-permute-done.13.refs_16_ = bf16[256,1024]{1,0:T(8,128)(2,1)} collective-permute-done((bf16[256,1024]{1,0:T(8,128)(2,1)S(1)}, bf16[256,1024]{1,0:T(8,128)(2,1)}, u32[]{:S(2)}, u32[]{:S(2)}) %collective-permute-start.13) | collective-permute-done | bytes 524320 | tf_op jit(solution)/shard_map/ppermute | solution.py:174
  76.0 3.1 %collective-permute-start.15 = (bf16[528,1024]{1,0:T(8,128)(2,1)S(1)}, bf16[528,1024]{1,0:T(8,128)(2,1)S(1)}, u32[]{:S(2)}, u32[]{:S(2)}) collective-permute-start(bf16[528,1024]{1,0:T(8,128)(2,1)S(1)} %collective-permute-done.9.refs_14_), channel_id=1, source_target_pairs={{8,0},{16,8},{24,16},{0,24},{9,1},{17,9},{25,17},{1,25},{10,2},{18... | collective-permute-start | bytes 3244040 | tf_op jit(solution)/shard_map/ppermute | solution.py:174
  79.1 14.5 %collective-permute-done.6.refs_13_ = bf16[528,1024]{1,0:T(8,128)(2,1)S(1)} collective-permute-done((bf16[528,1024]{1,0:T(8,128)(2,1)}, bf16[528,1024]{1,0:T(8,128)(2,1)S(1)}, u32[]{:S(2)}, u32[]{:S(2)}) %collective-permute-start.6) | collective-permute-done | bytes 1081376 | tf_op jit(solution)/shard_map/ppermute | solution.py:174
  93.5 3.4 %collective-permute-start.7 = (bf16[272,1024]{1,0:T(8,128)(2,1)S(1)}, bf16[272,1024]{1,0:T(8,128)(2,1)S(1)}, u32[]{:S(2)}, u32[]{:S(2)}) collective-permute-start(bf16[272,1024]{1,0:T(8,128)(2,1)S(1)} %copy-done.10), channel_id=1, source_target_pairs={{1,0},{2,1},{3,2},{0,3},{5,4},{6,5},{7,6},{4,7},{9,8},{10,9},{11,1... | collective-permute-start | bytes 1671176 | tf_op jit(solution)/shard_map/ppermute | solution.py:174
  97.0 2.0 %collective-permute-done.14.refs_17_ = bf16[528,1024]{1,0:T(8,128)(2,1)S(1)} collective-permute-done((bf16[528,1024]{1,0:T(8,128)(2,1)S(1)}, bf16[528,1024]{1,0:T(8,128)(2,1)S(1)}, u32[]{:S(2)}, u32[]{:S(2)}) %collective-permute-start.14) | collective-permute-done | bytes 1081376 | tf_op jit(solution)/shard_map/ppermute | solution.py:174
  99.0 1.2 collective-permute-start.11
  100.2 2.7 %collective-permute-start.18 = (bf16[128,1024]{1,0:T(8,128)(2,1)S(1)}, bf16[128,1024]{1,0:T(8,128)(2,1)S(1)}, u32[]{:S(2)}, u32[]{:S(2)}) collective-permute-start(bf16[128,1024]{1,0:T(8,128)(2,1)S(1)} %slice.72), channel_id=1, source_target_pairs={{1,0},{2,1},{3,2},{0,3},{5,4},{6,5},{7,6},{4,7},{9,8},{10,9},{11,1... | collective-permute-start | bytes 786440 | tf_op jit(solution)/shard_map/ppermute | solution.py:174
  103.0 2.7 %collective-permute-start.16 = (bf16[128,1024]{1,0:T(8,128)(2,1)S(1)}, bf16[128,1024]{1,0:T(8,128)(2,1)S(1)}, u32[]{:S(2)}, u32[]{:S(2)}) collective-permute-start(bf16[128,1024]{1,0:T(8,128)(2,1)S(1)} %slice.63), channel_id=1, source_target_pairs={{8,0},{16,8},{24,16},{0,24},{9,1},{17,9},{25,17},{1,25},{10,2},{18... | collective-permute-start | bytes 786440 | tf_op jit(solution)/shard_map/ppermute | solution.py:174
  105.7 4.9 %collective-permute-done.11.refs_9_ = bf16[256,1024]{1,0:T(8,128)(2,1)S(1)} collective-permute-done((bf16[256,1024]{1,0:T(8,128)(2,1)S(1)}, bf16[256,1024]{1,0:T(8,128)(2,1)S(1)}, u32[]{:S(2)}, u32[]{:S(2)}) %collective-permute-start.11) | collective-permute-done | bytes 524320 | tf_op jit(solution)/shard_map/ppermute | solution.py:174
  110.7 0.4 collective-permute-done.18.refs_20_
  111.1 0.4 copy-done.11
  111.6 0.1 copy-done.13
  111.7 0.5 copy-done.14
  112.2 0.1 copy-done.15
  112.3 0.2 copy-done.12
  112.5 13.3 %pair_maxima.1 = (f32[64,128]{1,0:T(8,128)}, f32[16,128]{1,0:T(8,128)S(1)}, f32[16,128]{1,0:T(8,128)S(1)}, f32[16,128]{1,0:T(8,128)S(1)}, f32[16,128]{1,0:T(8,128)S(1)}) custom-call(s32[88]{0:T(128)S(1)} %compare_select_fusion.2.refs_0_, s32[44]{0:T(128)S(1)} %broadcast_minimum_fusion.refs_1_, s32[18]{0:T(128)S(1)} %pad_add_fusion.1.refs_2_, ...), custom_call_target="tpu_custom_call" | custom-call | tf_op jit(solution)/shard_map/pair_maxima/pallas_call | solution.py:151
  125.9 3.1 %collective-permute-start.21 = (f32[16,128]{1,0:T(8,128)S(1)}, f32[16,128]{1,0:T(8,128)S(1)}, u32[]{:S(2)}, u32[]{:S(2)}) collective-permute-start(f32[16,128]{1,0:T(8,128)S(1)} %get-tuple-element.92), channel_id=1, source_target_pairs={{1,0},{2,1},{3,2},{0,3},{5,4},{6,5},{7,6},{4,7},{9,8},{10,9},{11,1... | collective-permute-start | bytes 24584 | tf_op jit(solution)/shard_map/ppermute | solution.py:174
  129.0 0.7 collective-permute-start.19
  129.7 15.9 %all-to-all-start.1 = ((f32[16,4,128]{2,1,0:T(4,128)}), f32[16,4,128]{2,1,0:T(4,128)S(1)}, u32[]{:S(2)}, u32[]{:S(2)}) async-start(f32[16,4,128]{2,1,0:T(4,128)} %bitcast.5), calls=%async_computation.1 | async-start | bytes 65536 | tf_op jit(solution)/shard_map/all_to_all | solution.py:284
  145.6 2.2 %collective-permute-start.24 = (f32[4,128]{1,0:T(4,128)S(1)}, f32[4,128]{1,0:T(4,128)S(1)}, u32[]{:S(2)}, u32[]{:S(2)}) collective-permute-start(f32[4,128]{1,0:T(4,128)S(1)} %get-tuple-element.98), channel_id=1, source_target_pairs={{8,0},{16,8},{24,16},{0,24},{9,1},{17,9},{25,17},{1,25},{10,2},{18... | collective-permute-start | bytes 6152 | tf_op jit(solution)/shard_map/ppermute | solution.py:174
  147.8 0.9 collective-permute-start.23
  148.7 4.3 %all-to-all-done.1 = f32[16,4,128]{2,1,0:T(4,128)S(1)} async-done(((f32[16,4,128]{2,1,0:T(4,128)}), f32[16,4,128]{2,1,0:T(4,128)S(1)}, u32[]{:S(2)}, u32[]{:S(2)}) %all-to-all-start.1) | async-done | bytes 32800 | tf_op jit(solution)/shard_map/all_to_all | solution.py:284
  153.0 0.6 fusion.15
  (95 shorter events, 1.3 us)
Async XLA Ops:
  6.5 105.0 %all-gather.2.cloned.1.call-start = ((), (), s32[]{:S(2)}) async-start(), calls=%async_computation.2 | async-start | bytes 17825792 | tf_op jit(solution)/shard_map/all_gather | solution.py:263
  6.5 1.2 copy-start.1
  7.8 1.3 copy-start.16
  7.8 1.4 copy-start.17
  7.8 1.4 copy-start.19
  7.8 1.4 copy-start.18
  9.3 34.3 %copy-start = (bf16[528,1024]{1,0:T(8,128)(2,1)}, bf16[528,1024]{1,0:T(8,128)(2,1)S(1)}, u32[]{:S(2)}) copy-start(bf16[528,1024]{1,0:T(8,128)(2,1)S(1)} %pad_dynamic-update-slice_fusion.refs_6_) | copy-start | bytes 3244036
  9.3 26.2 %collective-permute-start.2 = (bf16[528,1024]{1,0:T(8,128)(2,1)S(1)}, bf16[528,1024]{1,0:T(8,128)(2,1)S(1)}, u32[]{:S(2)}, u32[]{:S(2)}) collective-permute-start(bf16[528,1024]{1,0:T(8,128)(2,1)S(1)} %pad_dynamic-update-slice_fusion.refs_6_), channel_id=1, source_target_pairs={{1,0},{2,1},{3,2},{0,3},{5,4},{6,5},{7,6},{4,7},{9,8},{10,9},{11,1... | collective-permute-start | bytes 3244040 | tf_op jit(solution)/shard_map/ppermute | solution.py:174
  12.9 26.0 %collective-permute-start.3 = (bf16[528,1024]{1,0:T(8,128)(2,1)S(1)}, bf16[528,1024]{1,0:T(8,128)(2,1)}, u32[]{:S(2)}, u32[]{:S(2)}) collective-permute-start(bf16[528,1024]{1,0:T(8,128)(2,1)S(1)} %pad_dynamic-update-slice_fusion.refs_6_), channel_id=1, source_target_pairs={{3,0},{0,1},{1,2},{2,3},{7,4},{4,5},{5,6},{6,7},{11,8},{8,9},{9,10... | collective-permute-start | bytes 3244040 | tf_op jit(solution)/shard_map/ppermute | solution.py:174
  12.9 34.6 %collective-permute-start = (bf16[528,1024]{1,0:T(8,128)(2,1)S(1)}, bf16[528,1024]{1,0:T(8,128)(2,1)S(1)}, u32[]{:S(2)}, u32[]{:S(2)}) collective-permute-start(bf16[528,1024]{1,0:T(8,128)(2,1)S(1)} %pad_dynamic-update-slice_fusion.refs_6_), channel_id=1, source_target_pairs={{8,0},{16,8},{24,16},{0,24},{9,1},{17,9},{25,17},{1,25},{10,2},{18... | collective-permute-start | bytes 3244040 | tf_op jit(solution)/shard_map/ppermute | solution.py:174
  15.4 28.2 %collective-permute-start.1 = (bf16[528,1024]{1,0:T(8,128)(2,1)S(1)}, bf16[528,1024]{1,0:T(8,128)(2,1)}, u32[]{:S(2)}, u32[]{:S(2)}) collective-permute-start(bf16[528,1024]{1,0:T(8,128)(2,1)S(1)} %pad_dynamic-update-slice_fusion.refs_6_), channel_id=1, source_target_pairs={{24,0},{0,8},{8,16},{16,24},{25,1},{1,9},{9,17},{17,25},{26,2},{2,... | collective-permute-start | bytes 3244040 | tf_op jit(solution)/shard_map/ppermute | solution.py:174
  16.0 17.6 %all-to-all-start = ((s32[16,1,576]{2,1,0:T(1,128)}), s32[16,1,576]{2,1,0:T(1,128)S(1)}, u32[]{:S(2)}, u32[]{:S(2)}) async-start(s32[16,1,576]{2,1,0:T(1,128)} %broadcast_in_dim.73), calls=%async_computation | async-start | bytes 81920 | tf_op jit(solution)/shard_map/all_to_all | solution.py:269
  35.4 8.2 %copy-start.2 = (bf16[528,1024]{1,0:T(8,128)(2,1)}, bf16[528,1024]{1,0:T(8,128)(2,1)S(1)}, u32[]{:S(2)}) copy-start(bf16[528,1024]{1,0:T(8,128)(2,1)S(1)} %collective-permute-done.2.refs_7_) | copy-start | bytes 3244036
  36.4 24.1 %collective-permute-start.4 = (bf16[528,1024]{1,0:T(8,128)(2,1)S(1)}, bf16[528,1024]{1,0:T(8,128)(2,1)}, u32[]{:S(2)}, u32[]{:S(2)}) collective-permute-start(bf16[528,1024]{1,0:T(8,128)(2,1)S(1)} %collective-permute-done.2.refs_7_), channel_id=1, source_target_pairs={{8,0},{16,8},{24,16},{0,24},{9,1},{17,9},{25,17},{1,25},{10,2},{18... | collective-permute-start | bytes 3244040 | tf_op jit(solution)/shard_map/ppermute | solution.py:174
  38.9 25.1 %collective-permute-start.8 = (bf16[528,1024]{1,0:T(8,128)(2,1)}, bf16[528,1024]{1,0:T(8,128)(2,1)}, u32[]{:S(2)}, u32[]{:S(2)}) collective-permute-start(bf16[528,1024]{1,0:T(8,128)(2,1)} %collective-permute-done.3.refs_10_), channel_id=1, source_target_pairs={{24,0},{0,8},{8,16},{16,24},{25,1},{1,9},{9,17},{17,25},{26,2},{2,... | collective-permute-start | bytes 3244040 | tf_op jit(solution)/shard_map/ppermute | solution.py:174
  43.6 49.9 %copy-start.10 = (bf16[272,1024]{1,0:T(8,128)(2,1)S(1)}, bf16[272,1024]{1,0:T(8,128)(2,1)}, u32[]{:S(2)}) copy-start(bf16[272,1024]{1,0:T(8,128)(2,1)} %slice.54) | copy-start | bytes 1671172
  44.8 24.4 %collective-permute-start.5 = (bf16[528,1024]{1,0:T(8,128)(2,1)}, bf16[528,1024]{1,0:T(8,128)(2,1)S(1)}, u32[]{:S(2)}, u32[]{:S(2)}) collective-permute-start(bf16[528,1024]{1,0:T(8,128)(2,1)} %collective-permute-done.1.refs_22_), channel_id=1, source_target_pairs={{1,0},{2,1},{3,2},{0,3},{5,4},{6,5},{7,6},{4,7},{9,8},{10,9},{11,1... | collective-permute-start | bytes 3244040 | tf_op jit(solution)/shard_map/ppermute | solution.py:174
  47.5 49.5 %copy-start.3 = (bf16[528,1024]{1,0:T(8,128)(2,1)}, bf16[528,1024]{1,0:T(8,128)(2,1)S(1)}, u32[]{:S(2)}) copy-start(bf16[528,1024]{1,0:T(8,128)(2,1)S(1)} %collective-permute-done.refs_11_) | copy-start | bytes 3244036
  47.5 25.1 %collective-permute-start.9 = (bf16[528,1024]{1,0:T(8,128)(2,1)S(1)}, bf16[528,1024]{1,0:T(8,128)(2,1)S(1)}, u32[]{:S(2)}, u32[]{:S(2)}) collective-permute-start(bf16[528,1024]{1,0:T(8,128)(2,1)S(1)} %collective-permute-done.refs_11_), channel_id=1, source_target_pairs={{3,0},{0,1},{1,2},{2,3},{7,4},{4,5},{5,6},{6,7},{11,8},{8,9},{9,10... | collective-permute-start | bytes 3244040 | tf_op jit(solution)/shard_map/ppermute | solution.py:174
  64.0 12.0 %collective-permute-start.13 = (bf16[256,1024]{1,0:T(8,128)(2,1)S(1)}, bf16[256,1024]{1,0:T(8,128)(2,1)}, u32[]{:S(2)}, u32[]{:S(2)}) collective-permute-start(bf16[256,1024]{1,0:T(8,128)(2,1)S(1)} %slice.70), channel_id=1, source_target_pairs={{24,0},{0,8},{8,16},{16,24},{25,1},{1,9},{9,17},{17,25},{26,2},{2,... | collective-permute-start | bytes 1572872 | tf_op jit(solution)/shard_map/ppermute | solution.py:174
  64.0 12.0 %collective-permute-start.12 = (bf16[272,1024]{1,0:T(8,128)(2,1)S(1)}, bf16[272,1024]{1,0:T(8,128)(2,1)}, u32[]{:S(2)}, u32[]{:S(2)}) collective-permute-start(bf16[272,1024]{1,0:T(8,128)(2,1)S(1)} %slice.69), channel_id=1, source_target_pairs={{8,0},{16,8},{24,16},{0,24},{9,1},{17,9},{25,17},{1,25},{10,2},{18... | collective-permute-start | bytes 1671176 | tf_op jit(solution)/shard_map/ppermute | solution.py:174
  69.2 36.5 %copy-start.7 = (bf16[528,1024]{1,0:T(8,128)(2,1)}, bf16[528,1024]{1,0:T(8,128)(2,1)S(1)}, u32[]{:S(2)}) copy-start(bf16[528,1024]{1,0:T(8,128)(2,1)S(1)} %collective-permute-done.5.refs_23_) | copy-start | bytes 3244036
  69.2 24.3 %collective-permute-start.6 = (bf16[528,1024]{1,0:T(8,128)(2,1)}, bf16[528,1024]{1,0:T(8,128)(2,1)S(1)}, u32[]{:S(2)}, u32[]{:S(2)}) collective-permute-start(bf16[528,1024]{1,0:T(8,128)(2,1)} %collective-permute-done.4.refs_12_), channel_id=1, source_target_pairs={{1,0},{2,1},{3,2},{0,3},{5,4},{6,5},{7,6},{4,7},{9,8},{10,9},{11,1... | collective-permute-start | bytes 3244040 | tf_op jit(solution)/shard_map/ppermute | solution.py:174
  72.6 38.0 %copy-start.8 = (bf16[528,1024]{1,0:T(8,128)(2,1)}, bf16[528,1024]{1,0:T(8,128)(2,1)S(1)}, u32[]{:S(2)}) copy-start(bf16[528,1024]{1,0:T(8,128)(2,1)S(1)} %collective-permute-done.9.refs_14_) | copy-start | bytes 3244036
  72.6 24.3 %collective-permute-start.10 = (bf16[528,1024]{1,0:T(8,128)(2,1)}, bf16[528,1024]{1,0:T(8,128)(2,1)S(1)}, u32[]{:S(2)}, u32[]{:S(2)}) collective-permute-start(bf16[528,1024]{1,0:T(8,128)(2,1)} %collective-permute-done.8.refs_25_), channel_id=1, source_target_pairs={{3,0},{0,1},{1,2},{2,3},{7,4},{4,5},{5,6},{6,7},{11,8},{8,9},{9,10... | collective-permute-start | bytes 3244040 | tf_op jit(solution)/shard_map/ppermute | solution.py:174
  76.0 23.0 %collective-permute-start.14 = (bf16[528,1024]{1,0:T(8,128)(2,1)S(1)}, bf16[528,1024]{1,0:T(8,128)(2,1)S(1)}, u32[]{:S(2)}, u32[]{:S(2)}) collective-permute-start(bf16[528,1024]{1,0:T(8,128)(2,1)S(1)} %collective-permute-done.5.refs_23_), channel_id=1, source_target_pairs={{24,0},{0,8},{8,16},{16,24},{25,1},{1,9},{9,17},{17,25},{26,2},{2,... | collective-permute-start | bytes 3244040 | tf_op jit(solution)/shard_map/ppermute | solution.py:174
  76.0 27.0 %collective-permute-start.15 = (bf16[528,1024]{1,0:T(8,128)(2,1)S(1)}, bf16[528,1024]{1,0:T(8,128)(2,1)S(1)}, u32[]{:S(2)}, u32[]{:S(2)}) collective-permute-start(bf16[528,1024]{1,0:T(8,128)(2,1)S(1)} %collective-permute-done.9.refs_14_), channel_id=1, source_target_pairs={{8,0},{16,8},{24,16},{0,24},{9,1},{17,9},{25,17},{1,25},{10,2},{18... | collective-permute-start | bytes 3244040 | tf_op jit(solution)/shard_map/ppermute | solution.py:174
  93.5 9.4 %copy-start.5 = (bf16[528,1024]{1,0:T(8,128)(2,1)}, bf16[528,1024]{1,0:T(8,128)(2,1)S(1)}, u32[]{:S(2)}) copy-start(bf16[528,1024]{1,0:T(8,128)(2,1)S(1)} %collective-permute-done.6.refs_13_) | copy-start | bytes 3244036
  93.5 17.1 %collective-permute-start.7 = (bf16[272,1024]{1,0:T(8,128)(2,1)S(1)}, bf16[272,1024]{1,0:T(8,128)(2,1)S(1)}, u32[]{:S(2)}, u32[]{:S(2)}) collective-permute-start(bf16[272,1024]{1,0:T(8,128)(2,1)S(1)} %copy-done.10), channel_id=1, source_target_pairs={{1,0},{2,1},{3,2},{0,3},{5,4},{6,5},{7,6},{4,7},{9,8},{10,9},{11,1... | collective-permute-start | bytes 1671176 | tf_op jit(solution)/shard_map/ppermute | solution.py:174
  97.0 3.3 %copy-start.4 = (bf16[528,1024]{1,0:T(8,128)(2,1)}, bf16[528,1024]{1,0:T(8,128)(2,1)S(1)}, u32[]{:S(2)}) copy-start(bf16[528,1024]{1,0:T(8,128)(2,1)S(1)} %collective-permute-done.10.refs_24_) | copy-start | bytes 3244036
  99.0 4.0 %copy-start.6 = (bf16[528,1024]{1,0:T(8,128)(2,1)}, bf16[528,1024]{1,0:T(8,128)(2,1)S(1)}, u32[]{:S(2)}) copy-start(bf16[528,1024]{1,0:T(8,128)(2,1)S(1)} %collective-permute-done.14.refs_17_) | copy-start | bytes 3244036
  99.0 12.6 %collective-permute-start.17 = (bf16[272,1024]{1,0:T(8,128)(2,1)S(1)}, bf16[272,1024]{1,0:T(8,128)(2,1)S(1)}, u32[]{:S(2)}, u32[]{:S(2)}) collective-permute-start(bf16[272,1024]{1,0:T(8,128)(2,1)S(1)} %slice.62), channel_id=1, source_target_pairs={{24,0},{0,8},{8,16},{16,24},{25,1},{1,9},{9,17},{17,25},{26,2},{2,... | collective-permute-start | bytes 1671176 | tf_op jit(solution)/shard_map/ppermute | solution.py:174
  99.0 11.7 %collective-permute-start.11 = (bf16[256,1024]{1,0:T(8,128)(2,1)S(1)}, bf16[256,1024]{1,0:T(8,128)(2,1)S(1)}, u32[]{:S(2)}, u32[]{:S(2)}) collective-permute-start(bf16[256,1024]{1,0:T(8,128)(2,1)S(1)} %slice.71), channel_id=1, source_target_pairs={{3,0},{0,1},{1,2},{2,3},{7,4},{4,5},{5,6},{6,7},{11,8},{8,9},{9,10... | collective-permute-start | bytes 1572872 | tf_op jit(solution)/shard_map/ppermute | solution.py:174
  100.2 10.9 %collective-permute-start.18 = (bf16[128,1024]{1,0:T(8,128)(2,1)S(1)}, bf16[128,1024]{1,0:T(8,128)(2,1)S(1)}, u32[]{:S(2)}, u32[]{:S(2)}) collective-permute-start(bf16[128,1024]{1,0:T(8,128)(2,1)S(1)} %slice.72), channel_id=1, source_target_pairs={{1,0},{2,1},{3,2},{0,3},{5,4},{6,5},{7,6},{4,7},{9,8},{10,9},{11,1... | collective-permute-start | bytes 786440 | tf_op jit(solution)/shard_map/ppermute | solution.py:174
  103.0 7.7 %copy-start.9 = (bf16[528,1024]{1,0:T(8,128)(2,1)}, bf16[528,1024]{1,0:T(8,128)(2,1)S(1)}, u32[]{:S(2)}) copy-start(bf16[528,1024]{1,0:T(8,128)(2,1)S(1)} %collective-permute-done.15.refs_21_) | copy-start | bytes 3244036
  103.0 8.5 %collective-permute-start.16 = (bf16[128,1024]{1,0:T(8,128)(2,1)S(1)}, bf16[128,1024]{1,0:T(8,128)(2,1)S(1)}, u32[]{:S(2)}, u32[]{:S(2)}) collective-permute-start(bf16[128,1024]{1,0:T(8,128)(2,1)S(1)} %slice.63), channel_id=1, source_target_pairs={{8,0},{16,8},{24,16},{0,24},{9,1},{17,9},{25,17},{1,25},{10,2},{18... | collective-permute-start | bytes 786440 | tf_op jit(solution)/shard_map/ppermute | solution.py:174
  110.7 1.0 copy-start.13
  110.7 0.8 copy-start.11
  111.5 0.7 copy-start.14
  111.5 0.8 copy-start.15
  111.5 1.0 copy-start.12
  125.9 19.6 %collective-permute-start.21 = (f32[16,128]{1,0:T(8,128)S(1)}, f32[16,128]{1,0:T(8,128)S(1)}, u32[]{:S(2)}, u32[]{:S(2)}) collective-permute-start(f32[16,128]{1,0:T(8,128)S(1)} %get-tuple-element.92), channel_id=1, source_target_pairs={{1,0},{2,1},{3,2},{0,3},{5,4},{6,5},{7,6},{4,7},{9,8},{10,9},{11,1... | collective-permute-start | bytes 24584 | tf_op jit(solution)/shard_map/ppermute | solution.py:174
  129.0 16.6 %collective-permute-start.20 = (f32[16,128]{1,0:T(8,128)S(1)}, f32[16,128]{1,0:T(8,128)S(1)}, u32[]{:S(2)}, u32[]{:S(2)}) collective-permute-start(f32[16,128]{1,0:T(8,128)S(1)} %get-tuple-element.91), channel_id=1, source_target_pairs={{2,0},{3,1},{0,2},{1,3},{6,4},{7,5},{4,6},{5,7},{10,8},{11,9},{8,1... | collective-permute-start | bytes 24584 | tf_op jit(solution)/shard_map/ppermute | solution.py:174
  129.0 16.6 %collective-permute-start.19 = (f32[16,128]{1,0:T(8,128)S(1)}, f32[16,128]{1,0:T(8,128)S(1)}, u32[]{:S(2)}, u32[]{:S(2)}) collective-permute-start(f32[16,128]{1,0:T(8,128)S(1)} %get-tuple-element.90), channel_id=1, source_target_pairs={{3,0},{0,1},{1,2},{2,3},{7,4},{4,5},{5,6},{6,7},{11,8},{8,9},{9,10... | collective-permute-start | bytes 24584 | tf_op jit(solution)/shard_map/ppermute | solution.py:174
  129.7 23.3 %all-to-all-start.1 = ((f32[16,4,128]{2,1,0:T(4,128)}), f32[16,4,128]{2,1,0:T(4,128)S(1)}, u32[]{:S(2)}, u32[]{:S(2)}) async-start(f32[16,4,128]{2,1,0:T(4,128)} %bitcast.5), calls=%async_computation.1 | async-start | bytes 65536 | tf_op jit(solution)/shard_map/all_to_all | solution.py:284
  145.6 7.4 %collective-permute-start.24 = (f32[4,128]{1,0:T(4,128)S(1)}, f32[4,128]{1,0:T(4,128)S(1)}, u32[]{:S(2)}, u32[]{:S(2)}) collective-permute-start(f32[4,128]{1,0:T(4,128)S(1)} %get-tuple-element.98), channel_id=1, source_target_pairs={{8,0},{16,8},{24,16},{0,24},{9,1},{17,9},{25,17},{1,25},{10,2},{18... | collective-permute-start | bytes 6152 | tf_op jit(solution)/shard_map/ppermute | solution.py:174
  147.8 5.2 %collective-permute-start.23 = (f32[4,128]{1,0:T(4,128)S(1)}, f32[4,128]{1,0:T(4,128)S(1)}, u32[]{:S(2)}, u32[]{:S(2)}) collective-permute-start(f32[4,128]{1,0:T(4,128)S(1)} %get-tuple-element.99), channel_id=1, source_target_pairs={{16,0},{24,8},{0,16},{8,24},{17,1},{25,9},{1,17},{9,25},{18,2},{26... | collective-permute-start | bytes 6152 | tf_op jit(solution)/shard_map/ppermute | solution.py:174
  148.7 4.3 %collective-permute-start.22 = (f32[4,128]{1,0:T(4,128)S(1)}, f32[4,128]{1,0:T(4,128)S(1)}, u32[]{:S(2)}, u32[]{:S(2)}) collective-permute-start(f32[4,128]{1,0:T(4,128)S(1)} %get-tuple-element.97), channel_id=1, source_target_pairs={{24,0},{0,8},{8,16},{16,24},{25,1},{1,9},{9,17},{17,25},{26,2},{2,... | collective-permute-start | bytes 6152 | tf_op jit(solution)/shard_map/ppermute | solution.py:174
Sparse Core Ops, SparseCore 0:
  9.2 100.5 all-gather.1

commit v8 on v7

--- a/solution.py
+++ b/solution.py
@@ -114,8 +114,9 @@
         def _():
             each_left(i + SLOTS, lambda copy: copy.start())
 
-    arrive(jnp.int32(0))
-    multiply(jnp.int32(0), even)
+    for i, into in ((0, even), (1, odd)):
+        arrive(jnp.int32(i))
+        multiply(jnp.int32(i), into)
     pltpu.make_async_copy(right_meta, right_meta, right_sems.at[16]).wait()
     for k in range(16):
         row = right_meta[k, 0:1, : 4 * ROWS].astype(jnp.float32)
@@ -126,18 +127,17 @@
 
     def two(q, carry):
         i = 2 * q
-        arrive(i + 1)
-        multiply(i + 1, odd)
+        arrive(i + 2)
+        arrive(i + 3)
         maxima(i, even)
+        maxima(i + 1, odd)
+        multiply(i + 2, even)
+        multiply(i + 3, odd)
         refill(i)
-        arrive(i + 2)
-        multiply(i + 2, even)
-        maxima(i + 1, odd)
         refill(i + 1)
         return carry
 
     lax.fori_loop(0, count // 2, two, 0)
-    each_left(count + 1, lambda copy: copy.wait())
     left_out[...] = left_best[0:64, :]
     for dy in range(4):
         right_out[dy][...] = right_best[:, dy * ROWS : (dy + 1) * ROWS]

time: 161 us -> 160 us (level)
  starting transfers between devices: 64 us -> 62.3 us
    all_to_all x1, starting transfers between devices: 15.9 us -> 13.7 us  [local(): lax.all_to_all(left_best.reshape(16, BLOCKS, ROWS), ('z', 'c'), 0, 0, til...]
where the time goes in v8:
time: 160 us; the launch traced here: 159 us
  starting transfers between devices  62.3 us (39%)
  waiting for transfers between devices  56.6 us (35%)
  Pallas kernels  15.3 us (10%)
  between operations  14.4 us (9%)
  local copies, waits for them, and re-layouts  7.55 us (5%)
  other arithmetic  2.71 us (2%)
    ppermute x25, waiting for transfers between devices, shift(): lax.ppermute(value, axis, [((i + by) % size, i) for i in range(size)])  44.9 us
    ppermute x25, starting transfers between devices, shift(): lax.ppermute(value, axis, [((i + by) % size, i) for i in range(size)])  38.9 us
    pallas_call x1, Pallas kernels, pair_maxima(): pl.pallas_call(kernel, out_shape=[jax.ShapeDtypeStruct((n, ROWS), jnp.flo...  14 us
    all_to_all x1, starting transfers between devices, local(): lax.all_to_all(left_best.reshape(16, BLOCKS, ROWS), ('z', 'c'), 0, 0, til...  13.7 us
    all_to_all x1, starting transfers between devices, local(): lax.all_to_all(jnp.broadcast_to(lists, (16, lists.shape[1])), ('z', 'c'),...  9.71 us
    all_to_all x1, waiting for transfers between devices, local(): lax.all_to_all(jnp.broadcast_to(lists, (16, lists.shape[1])), ('z', 'c'),...  7.88 us
    all_to_all x1, waiting for transfers between devices, local(): lax.all_to_all(left_best.reshape(16, BLOCKS, ROWS), ('z', 'c'), 0, 0, til...  3.74 us
  transfers between devices with their start and end apart: 28, of which 11 were waited for; matrix products, arithmetic and copies ran while one was open for 4% of the time, Pallas kernels for 0%

profile of v8, /device:TPU:1, one launch (start us, length us, event | category | flops | bytes accessed | tf_op | source)
XLA Modules:
  0.0 158.9 jit_solution(7624830696945670805)
XLA Ops:
  6.5 1.2 copy-done.1
  7.8 1.3 unit_rows.1
  9.3 3.6 %collective-permute-start.2 = (bf16[528,1024]{1,0:T(8,128)(2,1)S(1)}, bf16[528,1024]{1,0:T(8,128)(2,1)S(1)}, u32[]{:S(2)}, u32[]{:S(2)}) collective-permute-start(bf16[528,1024]{1,0:T(8,128)(2,1)S(1)} %pad_dynamic-update-slice_fusion.refs_6_), channel_id=1, source_target_pairs={{1,0},{2,1},{3,2},{0,3},{5,4},{6,5},{7,6},{4,7},{9,8},{10,9},{11,1... | collective-permute-start | bytes 3244040 | tf_op jit(solution)/shard_map/ppermute | solution.py:174
  12.9 2.5 %collective-permute-start = (bf16[528,1024]{1,0:T(8,128)(2,1)S(1)}, bf16[528,1024]{1,0:T(8,128)(2,1)S(1)}, u32[]{:S(2)}, u32[]{:S(2)}) collective-permute-start(bf16[528,1024]{1,0:T(8,128)(2,1)S(1)} %pad_dynamic-update-slice_fusion.refs_6_), channel_id=1, source_target_pairs={{8,0},{16,8},{24,16},{0,24},{9,1},{17,9},{25,17},{1,25},{10,2},{18... | collective-permute-start | bytes 3244040 | tf_op jit(solution)/shard_map/ppermute | solution.py:174
  15.4 0.6 broadcast_in_dim.73
  16.0 9.7 %all-to-all-start = ((s32[16,1,576]{2,1,0:T(1,128)}), s32[16,1,576]{2,1,0:T(1,128)S(1)}, u32[]{:S(2)}, u32[]{:S(2)}) async-start(s32[16,1,576]{2,1,0:T(1,128)} %broadcast_in_dim.73), calls=%async_computation | async-start | bytes 81920 | tf_op jit(solution)/shard_map/all_to_all | solution.py:269
  25.8 7.9 %all-to-all-done = s32[16,1,576]{2,1,0:T(1,128)S(1)} async-done(((s32[16,1,576]{2,1,0:T(1,128)}), s32[16,1,576]{2,1,0:T(1,128)S(1)}, u32[]{:S(2)}, u32[]{:S(2)}) %all-to-all-start) | async-done | bytes 36896 | tf_op jit(solution)/shard_map/all_to_all | solution.py:269
  33.7 1.8 %collective-permute-done.2.refs_7_ = bf16[528,1024]{1,0:T(8,128)(2,1)S(1)} collective-permute-done((bf16[528,1024]{1,0:T(8,128)(2,1)S(1)}, bf16[528,1024]{1,0:T(8,128)(2,1)S(1)}, u32[]{:S(2)}, u32[]{:S(2)}) %collective-permute-start.2) | collective-permute-done | bytes 1081376 | tf_op jit(solution)/shard_map/ppermute | solution.py:174
  35.4 0.1 fusion.8
  35.6 0.3 select_reduce_fusion
  36.0 0.4 convert_reduce_fusion
  36.4 2.5 %collective-permute-start.4 = (bf16[528,1024]{1,0:T(8,128)(2,1)S(1)}, bf16[528,1024]{1,0:T(8,128)(2,1)}, u32[]{:S(2)}, u32[]{:S(2)}) collective-permute-start(bf16[528,1024]{1,0:T(8,128)(2,1)S(1)} %collective-permute-done.2.refs_7_), channel_id=1, source_target_pairs={{8,0},{16,8},{24,16},{0,24},{9,1},{17,9},{25,17},{1,25},{10,2},{18... | collective-permute-start | bytes 3244040 | tf_op jit(solution)/shard_map/ppermute | solution.py:174
  38.9 0.9 collective-permute-start.8
  40.0 0.6 slice.60
  41.3 0.9 slice.54
  42.5 1.1 slice.71
  43.6 1.1 slice.70
  44.8 2.7 %collective-permute-start.5 = (bf16[528,1024]{1,0:T(8,128)(2,1)}, bf16[528,1024]{1,0:T(8,128)(2,1)S(1)}, u32[]{:S(2)}, u32[]{:S(2)}) collective-permute-start(bf16[528,1024]{1,0:T(8,128)(2,1)} %collective-permute-done.1.refs_22_), channel_id=1, source_target_pairs={{1,0},{2,1},{3,2},{0,3},{5,4},{6,5},{7,6},{4,7},{9,8},{10,9},{11,1... | collective-permute-start | bytes 3244040 | tf_op jit(solution)/shard_map/ppermute | solution.py:174
  47.7 0.1 select_reduce_fusion.1
  47.8 0.8 pad_add_fusion.1.refs_2_
  48.6 12.0 %collective-permute-done.4.refs_12_ = bf16[528,1024]{1,0:T(8,128)(2,1)} collective-permute-done((bf16[528,1024]{1,0:T(8,128)(2,1)S(1)}, bf16[528,1024]{1,0:T(8,128)(2,1)}, u32[]{:S(2)}, u32[]{:S(2)}) %collective-permute-start.4) | collective-permute-done | bytes 1081376 | tf_op jit(solution)/shard_map/ppermute | solution.py:174
  60.5 3.5 %collective-permute-done.8.refs_25_ = bf16[528,1024]{1,0:T(8,128)(2,1)} collective-permute-done((bf16[528,1024]{1,0:T(8,128)(2,1)}, bf16[528,1024]{1,0:T(8,128)(2,1)}, u32[]{:S(2)}, u32[]{:S(2)}) %collective-permute-start.8) | collective-permute-done | bytes 1081376 | tf_op jit(solution)/shard_map/ppermute | solution.py:174
  64.0 2.7 %collective-permute-start.12 = (bf16[272,1024]{1,0:T(8,128)(2,1)S(1)}, bf16[272,1024]{1,0:T(8,128)(2,1)}, u32[]{:S(2)}, u32[]{:S(2)}) collective-permute-start(bf16[272,1024]{1,0:T(8,128)(2,1)S(1)} %slice.69), channel_id=1, source_target_pairs={{8,0},{16,8},{24,16},{0,24},{9,1},{17,9},{25,17},{1,25},{10,2},{18... | collective-permute-start | bytes 1671176 | tf_op jit(solution)/shard_map/ppermute | solution.py:174
  66.7 2.5 %collective-permute-done.5.refs_23_ = bf16[528,1024]{1,0:T(8,128)(2,1)S(1)} collective-permute-done((bf16[528,1024]{1,0:T(8,128)(2,1)}, bf16[528,1024]{1,0:T(8,128)(2,1)S(1)}, u32[]{:S(2)}, u32[]{:S(2)}) %collective-permute-start.5) | collective-permute-done | bytes 1081376 | tf_op jit(solution)/shard_map/ppermute | solution.py:174
  69.2 3.4 %collective-permute-start.6 = (bf16[528,1024]{1,0:T(8,128)(2,1)}, bf16[528,1024]{1,0:T(8,128)(2,1)S(1)}, u32[]{:S(2)}, u32[]{:S(2)}) collective-permute-start(bf16[528,1024]{1,0:T(8,128)(2,1)} %collective-permute-done.4.refs_12_), channel_id=1, source_target_pairs={{1,0},{2,1},{3,2},{0,3},{5,4},{6,5},{7,6},{4,7},{9,8},{10,9},{11,1... | collective-permute-start | bytes 3244040 | tf_op jit(solution)/shard_map/ppermute | solution.py:174
  72.6 3.4 %collective-permute-done.13.refs_16_ = bf16[256,1024]{1,0:T(8,128)(2,1)} collective-permute-done((bf16[256,1024]{1,0:T(8,128)(2,1)S(1)}, bf16[256,1024]{1,0:T(8,128)(2,1)}, u32[]{:S(2)}, u32[]{:S(2)}) %collective-permute-start.13) | collective-permute-done | bytes 524320 | tf_op jit(solution)/shard_map/ppermute | solution.py:174
  76.0 3.1 %collective-permute-start.15 = (bf16[528,1024]{1,0:T(8,128)(2,1)S(1)}, bf16[528,1024]{1,0:T(8,128)(2,1)S(1)}, u32[]{:S(2)}, u32[]{:S(2)}) collective-permute-start(bf16[528,1024]{1,0:T(8,128)(2,1)S(1)} %collective-permute-done.9.refs_14_), channel_id=1, source_target_pairs={{8,0},{16,8},{24,16},{0,24},{9,1},{17,9},{25,17},{1,25},{10,2},{18... | collective-permute-start | bytes 3244040 | tf_op jit(solution)/shard_map/ppermute | solution.py:174
  79.1 14.5 %collective-permute-done.6.refs_13_ = bf16[528,1024]{1,0:T(8,128)(2,1)S(1)} collective-permute-done((bf16[528,1024]{1,0:T(8,128)(2,1)}, bf16[528,1024]{1,0:T(8,128)(2,1)S(1)}, u32[]{:S(2)}, u32[]{:S(2)}) %collective-permute-start.6) | collective-permute-done | bytes 1081376 | tf_op jit(solution)/shard_map/ppermute | solution.py:174
  93.5 3.4 %collective-permute-start.7 = (bf16[272,1024]{1,0:T(8,128)(2,1)S(1)}, bf16[272,1024]{1,0:T(8,128)(2,1)S(1)}, u32[]{:S(2)}, u32[]{:S(2)}) collective-permute-start(bf16[272,1024]{1,0:T(8,128)(2,1)S(1)} %copy-done.10), channel_id=1, source_target_pairs={{1,0},{2,1},{3,2},{0,3},{5,4},{6,5},{7,6},{4,7},{9,8},{10,9},{11,1... | collective-permute-start | bytes 1671176 | tf_op jit(solution)/shard_map/ppermute | solution.py:174
  97.0 2.0 %collective-permute-done.14.refs_17_ = bf16[528,1024]{1,0:T(8,128)(2,1)S(1)} collective-permute-done((bf16[528,1024]{1,0:T(8,128)(2,1)S(1)}, bf16[528,1024]{1,0:T(8,128)(2,1)S(1)}, u32[]{:S(2)}, u32[]{:S(2)}) %collective-permute-start.14) | collective-permute-done | bytes 1081376 | tf_op jit(solution)/shard_map/ppermute | solution.py:174
  99.0 1.2 collective-permute-start.11
  100.2 2.7 %collective-permute-start.18 = (bf16[128,1024]{1,0:T(8,128)(2,1)S(1)}, bf16[128,1024]{1,0:T(8,128)(2,1)S(1)}, u32[]{:S(2)}, u32[]{:S(2)}) collective-permute-start(bf16[128,1024]{1,0:T(8,128)(2,1)S(1)} %slice.72), channel_id=1, source_target_pairs={{1,0},{2,1},{3,2},{0,3},{5,4},{6,5},{7,6},{4,7},{9,8},{10,9},{11,1... | collective-permute-start | bytes 786440 | tf_op jit(solution)/shard_map/ppermute | solution.py:174
  103.0 2.7 %collective-permute-start.16 = (bf16[128,1024]{1,0:T(8,128)(2,1)S(1)}, bf16[128,1024]{1,0:T(8,128)(2,1)S(1)}, u32[]{:S(2)}, u32[]{:S(2)}) collective-permute-start(bf16[128,1024]{1,0:T(8,128)(2,1)S(1)} %slice.63), channel_id=1, source_target_pairs={{8,0},{16,8},{24,16},{0,24},{9,1},{17,9},{25,17},{1,25},{10,2},{18... | collective-permute-start | bytes 786440 | tf_op jit(solution)/shard_map/ppermute | solution.py:174
  105.7 4.9 %collective-permute-done.11.refs_9_ = bf16[256,1024]{1,0:T(8,128)(2,1)S(1)} collective-permute-done((bf16[256,1024]{1,0:T(8,128)(2,1)S(1)}, bf16[256,1024]{1,0:T(8,128)(2,1)S(1)}, u32[]{:S(2)}, u32[]{:S(2)}) %collective-permute-start.11) | collective-permute-done | bytes 524320 | tf_op jit(solution)/shard_map/ppermute | solution.py:174
  110.7 0.4 collective-permute-done.18.refs_20_
  111.1 0.4 copy-done.11
  111.6 0.1 copy-done.13
  111.7 0.5 copy-done.14
  112.2 0.1 copy-done.15
  112.3 0.2 copy-done.12
  112.5 14.0 %pair_maxima.1 = (f32[64,128]{1,0:T(8,128)}, f32[16,128]{1,0:T(8,128)S(1)}, f32[16,128]{1,0:T(8,128)S(1)}, f32[16,128]{1,0:T(8,128)S(1)}, f32[16,128]{1,0:T(8,128)S(1)}) custom-call(s32[88]{0:T(128)S(1)} %compare_select_fusion.2.refs_0_, s32[44]{0:T(128)S(1)} %broadcast_minimum_fusion.refs_1_, s32[18]{0:T(128)S(1)} %pad_add_fusion.1.refs_2_, ...), custom_call_target="tpu_custom_call" | custom-call | tf_op jit(solution)/shard_map/pair_maxima/pallas_call | solution.py:151
  126.5 3.1 %collective-permute-start.21 = (f32[16,128]{1,0:T(8,128)S(1)}, f32[16,128]{1,0:T(8,128)S(1)}, u32[]{:S(2)}, u32[]{:S(2)}) collective-permute-start(f32[16,128]{1,0:T(8,128)S(1)} %get-tuple-element.92), channel_id=1, source_target_pairs={{1,0},{2,1},{3,2},{0,3},{5,4},{6,5},{7,6},{4,7},{9,8},{10,9},{11,1... | collective-permute-start | bytes 24584 | tf_op jit(solution)/shard_map/ppermute | solution.py:174
  129.6 0.7 collective-permute-start.19
  130.3 13.7 %all-to-all-start.1 = ((f32[16,4,128]{2,1,0:T(4,128)}), f32[16,4,128]{2,1,0:T(4,128)S(1)}, u32[]{:S(2)}, u32[]{:S(2)}) async-start(f32[16,4,128]{2,1,0:T(4,128)} %bitcast.5), calls=%async_computation.1 | async-start | bytes 65536 | tf_op jit(solution)/shard_map/all_to_all | solution.py:284
  144.0 2.9 %collective-permute-start.24 = (f32[4,128]{1,0:T(4,128)S(1)}, f32[4,128]{1,0:T(4,128)S(1)}, u32[]{:S(2)}, u32[]{:S(2)}) collective-permute-start(f32[4,128]{1,0:T(4,128)S(1)} %get-tuple-element.98), channel_id=1, source_target_pairs={{8,0},{16,8},{24,16},{0,24},{9,1},{17,9},{25,17},{1,25},{10,2},{18... | collective-permute-start | bytes 6152 | tf_op jit(solution)/shard_map/ppermute | solution.py:174
  147.0 0.7 collective-permute-start.22
  147.6 3.7 %all-to-all-done.1 = f32[16,4,128]{2,1,0:T(4,128)S(1)} async-done(((f32[16,4,128]{2,1,0:T(4,128)}), f32[16,4,128]{2,1,0:T(4,128)S(1)}, u32[]{:S(2)}, u32[]{:S(2)}) %all-to-all-start.1) | async-done | bytes 32800 | tf_op jit(solution)/shard_map/all_to_all | solution.py:284
  151.4 0.6 fusion.15
  (95 shorter events, 1.3 us)
Async XLA Ops:
  6.5 105.0 %all-gather.2.cloned.1.call-start = ((), (), s32[]{:S(2)}) async-start(), calls=%async_computation.2 | async-start | bytes 17825792 | tf_op jit(solution)/shard_map/all_gather | solution.py:263
  6.5 1.2 copy-start.1
  7.8 1.3 copy-start.16
  7.8 1.4 copy-start.17
  7.8 1.4 copy-start.19
  7.8 1.4 copy-start.18
  9.3 34.3 %copy-start = (bf16[528,1024]{1,0:T(8,128)(2,1)}, bf16[528,1024]{1,0:T(8,128)(2,1)S(1)}, u32[]{:S(2)}) copy-start(bf16[528,1024]{1,0:T(8,128)(2,1)S(1)} %pad_dynamic-update-slice_fusion.refs_6_) | copy-start | bytes 3244036
  9.3 26.2 %collective-permute-start.2 = (bf16[528,1024]{1,0:T(8,128)(2,1)S(1)}, bf16[528,1024]{1,0:T(8,128)(2,1)S(1)}, u32[]{:S(2)}, u32[]{:S(2)}) collective-permute-start(bf16[528,1024]{1,0:T(8,128)(2,1)S(1)} %pad_dynamic-update-slice_fusion.refs_6_), channel_id=1, source_target_pairs={{1,0},{2,1},{3,2},{0,3},{5,4},{6,5},{7,6},{4,7},{9,8},{10,9},{11,1... | collective-permute-start | bytes 3244040 | tf_op jit(solution)/shard_map/ppermute | solution.py:174
  12.9 26.0 %collective-permute-start.3 = (bf16[528,1024]{1,0:T(8,128)(2,1)S(1)}, bf16[528,1024]{1,0:T(8,128)(2,1)}, u32[]{:S(2)}, u32[]{:S(2)}) collective-permute-start(bf16[528,1024]{1,0:T(8,128)(2,1)S(1)} %pad_dynamic-update-slice_fusion.refs_6_), channel_id=1, source_target_pairs={{3,0},{0,1},{1,2},{2,3},{7,4},{4,5},{5,6},{6,7},{11,8},{8,9},{9,10... | collective-permute-start | bytes 3244040 | tf_op jit(solution)/shard_map/ppermute | solution.py:174
  12.9 34.6 %collective-permute-start = (bf16[528,1024]{1,0:T(8,128)(2,1)S(1)}, bf16[528,1024]{1,0:T(8,128)(2,1)S(1)}, u32[]{:S(2)}, u32[]{:S(2)}) collective-permute-start(bf16[528,1024]{1,0:T(8,128)(2,1)S(1)} %pad_dynamic-update-slice_fusion.refs_6_), channel_id=1, source_target_pairs={{8,0},{16,8},{24,16},{0,24},{9,1},{17,9},{25,17},{1,25},{10,2},{18... | collective-permute-start | bytes 3244040 | tf_op jit(solution)/shard_map/ppermute | solution.py:174
  15.4 28.2 %collective-permute-start.1 = (bf16[528,1024]{1,0:T(8,128)(2,1)S(1)}, bf16[528,1024]{1,0:T(8,128)(2,1)}, u32[]{:S(2)}, u32[]{:S(2)}) collective-permute-start(bf16[528,1024]{1,0:T(8,128)(2,1)S(1)} %pad_dynamic-update-slice_fusion.refs_6_), channel_id=1, source_target_pairs={{24,0},{0,8},{8,16},{16,24},{25,1},{1,9},{9,17},{17,25},{26,2},{2,... | collective-permute-start | bytes 3244040 | tf_op jit(solution)/shard_map/ppermute | solution.py:174
  16.0 17.6 %all-to-all-start = ((s32[16,1,576]{2,1,0:T(1,128)}), s32[16,1,576]{2,1,0:T(1,128)S(1)}, u32[]{:S(2)}, u32[]{:S(2)}) async-start(s32[16,1,576]{2,1,0:T(1,128)} %broadcast_in_dim.73), calls=%async_computation | async-start | bytes 81920 | tf_op jit(solution)/shard_map/all_to_all | solution.py:269
  35.4 8.2 %copy-start.2 = (bf16[528,1024]{1,0:T(8,128)(2,1)}, bf16[528,1024]{1,0:T(8,128)(2,1)S(1)}, u32[]{:S(2)}) copy-start(bf16[528,1024]{1,0:T(8,128)(2,1)S(1)} %collective-permute-done.2.refs_7_) | copy-start | bytes 3244036
  36.4 24.1 %collective-permute-start.4 = (bf16[528,1024]{1,0:T(8,128)(2,1)S(1)}, bf16[528,1024]{1,0:T(8,128)(2,1)}, u32[]{:S(2)}, u32[]{:S(2)}) collective-permute-start(bf16[528,1024]{1,0:T(8,128)(2,1)S(1)} %collective-permute-done.2.refs_7_), channel_id=1, source_target_pairs={{8,0},{16,8},{24,16},{0,24},{9,1},{17,9},{25,17},{1,25},{10,2},{18... | collective-permute-start | bytes 3244040 | tf_op jit(solution)/shard_map/ppermute | solution.py:174
  38.9 25.1 %collective-permute-start.8 = (bf16[528,1024]{1,0:T(8,128)(2,1)}, bf16[528,1024]{1,0:T(8,128)(2,1)}, u32[]{:S(2)}, u32[]{:S(2)}) collective-permute-start(bf16[528,1024]{1,0:T(8,128)(2,1)} %collective-permute-done.3.refs_10_), channel_id=1, source_target_pairs={{24,0},{0,8},{8,16},{16,24},{25,1},{1,9},{9,17},{17,25},{26,2},{2,... | collective-permute-start | bytes 3244040 | tf_op jit(solution)/shard_map/ppermute | solution.py:174
  43.6 49.9 %copy-start.10 = (bf16[272,1024]{1,0:T(8,128)(2,1)S(1)}, bf16[272,1024]{1,0:T(8,128)(2,1)}, u32[]{:S(2)}) copy-start(bf16[272,1024]{1,0:T(8,128)(2,1)} %slice.54) | copy-start | bytes 1671172
  44.8 24.4 %collective-permute-start.5 = (bf16[528,1024]{1,0:T(8,128)(2,1)}, bf16[528,1024]{1,0:T(8,128)(2,1)S(1)}, u32[]{:S(2)}, u32[]{:S(2)}) collective-permute-start(bf16[528,1024]{1,0:T(8,128)(2,1)} %collective-permute-done.1.refs_22_), channel_id=1, source_target_pairs={{1,0},{2,1},{3,2},{0,3},{5,4},{6,5},{7,6},{4,7},{9,8},{10,9},{11,1... | collective-permute-start | bytes 3244040 | tf_op jit(solution)/shard_map/ppermute | solution.py:174
  47.5 49.5 %copy-start.3 = (bf16[528,1024]{1,0:T(8,128)(2,1)}, bf16[528,1024]{1,0:T(8,128)(2,1)S(1)}, u32[]{:S(2)}) copy-start(bf16[528,1024]{1,0:T(8,128)(2,1)S(1)} %collective-permute-done.refs_11_) | copy-start | bytes 3244036
  47.5 25.1 %collective-permute-start.9 = (bf16[528,1024]{1,0:T(8,128)(2,1)S(1)}, bf16[528,1024]{1,0:T(8,128)(2,1)S(1)}, u32[]{:S(2)}, u32[]{:S(2)}) collective-permute-start(bf16[528,1024]{1,0:T(8,128)(2,1)S(1)} %collective-permute-done.refs_11_), channel_id=1, source_target_pairs={{3,0},{0,1},{1,2},{2,3},{7,4},{4,5},{5,6},{6,7},{11,8},{8,9},{9,10... | collective-permute-start | bytes 3244040 | tf_op jit(solution)/shard_map/ppermute | solution.py:174
  64.0 12.0 %collective-permute-start.13 = (bf16[256,1024]{1,0:T(8,128)(2,1)S(1)}, bf16[256,1024]{1,0:T(8,128)(2,1)}, u32[]{:S(2)}, u32[]{:S(2)}) collective-permute-start(bf16[256,1024]{1,0:T(8,128)(2,1)S(1)} %slice.70), channel_id=1, source_target_pairs={{24,0},{0,8},{8,16},{16,24},{25,1},{1,9},{9,17},{17,25},{26,2},{2,... | collective-permute-start | bytes 1572872 | tf_op jit(solution)/shard_map/ppermute | solution.py:174
  64.0 12.0 %collective-permute-start.12 = (bf16[272,1024]{1,0:T(8,128)(2,1)S(1)}, bf16[272,1024]{1,0:T(8,128)(2,1)}, u32[]{:S(2)}, u32[]{:S(2)}) collective-permute-start(bf16[272,1024]{1,0:T(8,128)(2,1)S(1)} %slice.69), channel_id=1, source_target_pairs={{8,0},{16,8},{24,16},{0,24},{9,1},{17,9},{25,17},{1,25},{10,2},{18... | collective-permute-start | bytes 1671176 | tf_op jit(solution)/shard_map/ppermute | solution.py:174
  69.2 36.5 %copy-start.7 = (bf16[528,1024]{1,0:T(8,128)(2,1)}, bf16[528,1024]{1,0:T(8,128)(2,1)S(1)}, u32[]{:S(2)}) copy-start(bf16[528,1024]{1,0:T(8,128)(2,1)S(1)} %collective-permute-done.5.refs_23_) | copy-start | bytes 3244036
  69.2 24.3 %collective-permute-start.6 = (bf16[528,1024]{1,0:T(8,128)(2,1)}, bf16[528,1024]{1,0:T(8,128)(2,1)S(1)}, u32[]{:S(2)}, u32[]{:S(2)}) collective-permute-start(bf16[528,1024]{1,0:T(8,128)(2,1)} %collective-permute-done.4.refs_12_), channel_id=1, source_target_pairs={{1,0},{2,1},{3,2},{0,3},{5,4},{6,5},{7,6},{4,7},{9,8},{10,9},{11,1... | collective-permute-start | bytes 3244040 | tf_op jit(solution)/shard_map/ppermute | solution.py:174
  72.6 38.0 %copy-start.8 = (bf16[528,1024]{1,0:T(8,128)(2,1)}, bf16[528,1024]{1,0:T(8,128)(2,1)S(1)}, u32[]{:S(2)}) copy-start(bf16[528,1024]{1,0:T(8,128)(2,1)S(1)} %collective-permute-done.9.refs_14_) | copy-start | bytes 3244036
  72.6 24.3 %collective-permute-start.10 = (bf16[528,1024]{1,0:T(8,128)(2,1)}, bf16[528,1024]{1,0:T(8,128)(2,1)S(1)}, u32[]{:S(2)}, u32[]{:S(2)}) collective-permute-start(bf16[528,1024]{1,0:T(8,128)(2,1)} %collective-permute-done.8.refs_25_), channel_id=1, source_target_pairs={{3,0},{0,1},{1,2},{2,3},{7,4},{4,5},{5,6},{6,7},{11,8},{8,9},{9,10... | collective-permute-start | bytes 3244040 | tf_op jit(solution)/shard_map/ppermute | solution.py:174
  76.0 23.0 %collective-permute-start.14 = (bf16[528,1024]{1,0:T(8,128)(2,1)S(1)}, bf16[528,1024]{1,0:T(8,128)(2,1)S(1)}, u32[]{:S(2)}, u32[]{:S(2)}) collective-permute-start(bf16[528,1024]{1,0:T(8,128)(2,1)S(1)} %collective-permute-done.5.refs_23_), channel_id=1, source_target_pairs={{24,0},{0,8},{8,16},{16,24},{25,1},{1,9},{9,17},{17,25},{26,2},{2,... | collective-permute-start | bytes 3244040 | tf_op jit(solution)/shard_map/ppermute | solution.py:174
  76.0 27.0 %collective-permute-start.15 = (bf16[528,1024]{1,0:T(8,128)(2,1)S(1)}, bf16[528,1024]{1,0:T(8,128)(2,1)S(1)}, u32[]{:S(2)}, u32[]{:S(2)}) collective-permute-start(bf16[528,1024]{1,0:T(8,128)(2,1)S(1)} %collective-permute-done.9.refs_14_), channel_id=1, source_target_pairs={{8,0},{16,8},{24,16},{0,24},{9,1},{17,9},{25,17},{1,25},{10,2},{18... | collective-permute-start | bytes 3244040 | tf_op jit(solution)/shard_map/ppermute | solution.py:174
  93.5 9.4 %copy-start.5 = (bf16[528,1024]{1,0:T(8,128)(2,1)}, bf16[528,1024]{1,0:T(8,128)(2,1)S(1)}, u32[]{:S(2)}) copy-start(bf16[528,1024]{1,0:T(8,128)(2,1)S(1)} %collective-permute-done.6.refs_13_) | copy-start | bytes 3244036
  93.5 17.1 %collective-permute-start.7 = (bf16[272,1024]{1,0:T(8,128)(2,1)S(1)}, bf16[272,1024]{1,0:T(8,128)(2,1)S(1)}, u32[]{:S(2)}, u32[]{:S(2)}) collective-permute-start(bf16[272,1024]{1,0:T(8,128)(2,1)S(1)} %copy-done.10), channel_id=1, source_target_pairs={{1,0},{2,1},{3,2},{0,3},{5,4},{6,5},{7,6},{4,7},{9,8},{10,9},{11,1... | collective-permute-start | bytes 1671176 | tf_op jit(solution)/shard_map/ppermute | solution.py:174
  97.0 3.3 %copy-start.4 = (bf16[528,1024]{1,0:T(8,128)(2,1)}, bf16[528,1024]{1,0:T(8,128)(2,1)S(1)}, u32[]{:S(2)}) copy-start(bf16[528,1024]{1,0:T(8,128)(2,1)S(1)} %collective-permute-done.10.refs_24_) | copy-start | bytes 3244036
  99.0 4.0 %copy-start.6 = (bf16[528,1024]{1,0:T(8,128)(2,1)}, bf16[528,1024]{1,0:T(8,128)(2,1)S(1)}, u32[]{:S(2)}) copy-start(bf16[528,1024]{1,0:T(8,128)(2,1)S(1)} %collective-permute-done.14.refs_17_) | copy-start | bytes 3244036
  99.0 12.6 %collective-permute-start.17 = (bf16[272,1024]{1,0:T(8,128)(2,1)S(1)}, bf16[272,1024]{1,0:T(8,128)(2,1)S(1)}, u32[]{:S(2)}, u32[]{:S(2)}) collective-permute-start(bf16[272,1024]{1,0:T(8,128)(2,1)S(1)} %slice.62), channel_id=1, source_target_pairs={{24,0},{0,8},{8,16},{16,24},{25,1},{1,9},{9,17},{17,25},{26,2},{2,... | collective-permute-start | bytes 1671176 | tf_op jit(solution)/shard_map/ppermute | solution.py:174
  99.0 11.7 %collective-permute-start.11 = (bf16[256,1024]{1,0:T(8,128)(2,1)S(1)}, bf16[256,1024]{1,0:T(8,128)(2,1)S(1)}, u32[]{:S(2)}, u32[]{:S(2)}) collective-permute-start(bf16[256,1024]{1,0:T(8,128)(2,1)S(1)} %slice.71), channel_id=1, source_target_pairs={{3,0},{0,1},{1,2},{2,3},{7,4},{4,5},{5,6},{6,7},{11,8},{8,9},{9,10... | collective-permute-start | bytes 1572872 | tf_op jit(solution)/shard_map/ppermute | solution.py:174
  100.2 10.9 %collective-permute-start.18 = (bf16[128,1024]{1,0:T(8,128)(2,1)S(1)}, bf16[128,1024]{1,0:T(8,128)(2,1)S(1)}, u32[]{:S(2)}, u32[]{:S(2)}) collective-permute-start(bf16[128,1024]{1,0:T(8,128)(2,1)S(1)} %slice.72), channel_id=1, source_target_pairs={{1,0},{2,1},{3,2},{0,3},{5,4},{6,5},{7,6},{4,7},{9,8},{10,9},{11,1... | collective-permute-start | bytes 786440 | tf_op jit(solution)/shard_map/ppermute | solution.py:174
  103.0 7.7 %copy-start.9 = (bf16[528,1024]{1,0:T(8,128)(2,1)}, bf16[528,1024]{1,0:T(8,128)(2,1)S(1)}, u32[]{:S(2)}) copy-start(bf16[528,1024]{1,0:T(8,128)(2,1)S(1)} %collective-permute-done.15.refs_21_) | copy-start | bytes 3244036
  103.0 8.5 %collective-permute-start.16 = (bf16[128,1024]{1,0:T(8,128)(2,1)S(1)}, bf16[128,1024]{1,0:T(8,128)(2,1)S(1)}, u32[]{:S(2)}, u32[]{:S(2)}) collective-permute-start(bf16[128,1024]{1,0:T(8,128)(2,1)S(1)} %slice.63), channel_id=1, source_target_pairs={{8,0},{16,8},{24,16},{0,24},{9,1},{17,9},{25,17},{1,25},{10,2},{18... | collective-permute-start | bytes 786440 | tf_op jit(solution)/shard_map/ppermute | solution.py:174
  110.7 1.0 copy-start.13
  110.7 0.8 copy-start.11
  111.5 0.7 copy-start.14
  111.5 0.8 copy-start.15
  111.5 1.0 copy-start.12
  126.5 17.5 %collective-permute-start.21 = (f32[16,128]{1,0:T(8,128)S(1)}, f32[16,128]{1,0:T(8,128)S(1)}, u32[]{:S(2)}, u32[]{:S(2)}) collective-permute-start(f32[16,128]{1,0:T(8,128)S(1)} %get-tuple-element.92), channel_id=1, source_target_pairs={{1,0},{2,1},{3,2},{0,3},{5,4},{6,5},{7,6},{4,7},{9,8},{10,9},{11,1... | collective-permute-start | bytes 24584 | tf_op jit(solution)/shard_map/ppermute | solution.py:174
  129.6 14.4 %collective-permute-start.20 = (f32[16,128]{1,0:T(8,128)S(1)}, f32[16,128]{1,0:T(8,128)S(1)}, u32[]{:S(2)}, u32[]{:S(2)}) collective-permute-start(f32[16,128]{1,0:T(8,128)S(1)} %get-tuple-element.91), channel_id=1, source_target_pairs={{2,0},{3,1},{0,2},{1,3},{6,4},{7,5},{4,6},{5,7},{10,8},{11,9},{8,1... | collective-permute-start | bytes 24584 | tf_op jit(solution)/shard_map/ppermute | solution.py:174
  129.6 14.4 %collective-permute-start.19 = (f32[16,128]{1,0:T(8,128)S(1)}, f32[16,128]{1,0:T(8,128)S(1)}, u32[]{:S(2)}, u32[]{:S(2)}) collective-permute-start(f32[16,128]{1,0:T(8,128)S(1)} %get-tuple-element.90), channel_id=1, source_target_pairs={{3,0},{0,1},{1,2},{2,3},{7,4},{4,5},{5,6},{6,7},{11,8},{8,9},{9,10... | collective-permute-start | bytes 24584 | tf_op jit(solution)/shard_map/ppermute | solution.py:174
  130.3 21.1 %all-to-all-start.1 = ((f32[16,4,128]{2,1,0:T(4,128)}), f32[16,4,128]{2,1,0:T(4,128)S(1)}, u32[]{:S(2)}, u32[]{:S(2)}) async-start(f32[16,4,128]{2,1,0:T(4,128)} %bitcast.5), calls=%async_computation.1 | async-start | bytes 65536 | tf_op jit(solution)/shard_map/all_to_all | solution.py:284
  144.0 7.4 %collective-permute-start.24 = (f32[4,128]{1,0:T(4,128)S(1)}, f32[4,128]{1,0:T(4,128)S(1)}, u32[]{:S(2)}, u32[]{:S(2)}) collective-permute-start(f32[4,128]{1,0:T(4,128)S(1)} %get-tuple-element.98), channel_id=1, source_target_pairs={{8,0},{16,8},{24,16},{0,24},{9,1},{17,9},{25,17},{1,25},{10,2},{18... | collective-permute-start | bytes 6152 | tf_op jit(solution)/shard_map/ppermute | solution.py:174
  147.0 4.5 %collective-permute-start.23 = (f32[4,128]{1,0:T(4,128)S(1)}, f32[4,128]{1,0:T(4,128)S(1)}, u32[]{:S(2)}, u32[]{:S(2)}) collective-permute-start(f32[4,128]{1,0:T(4,128)S(1)} %get-tuple-element.99), channel_id=1, source_target_pairs={{16,0},{24,8},{0,16},{8,24},{17,1},{25,9},{1,17},{9,25},{18,2},{26... | collective-permute-start | bytes 6152 | tf_op jit(solution)/shard_map/ppermute | solution.py:174
  147.0 4.5 %collective-permute-start.22 = (f32[4,128]{1,0:T(4,128)S(1)}, f32[4,128]{1,0:T(4,128)S(1)}, u32[]{:S(2)}, u32[]{:S(2)}) collective-permute-start(f32[4,128]{1,0:T(4,128)S(1)} %get-tuple-element.97), channel_id=1, source_target_pairs={{24,0},{0,8},{8,16},{16,24},{25,1},{1,9},{9,17},{17,25},{26,2},{2,... | collective-permute-start | bytes 6152 | tf_op jit(solution)/shard_map/ppermute | solution.py:174
Sparse Core Ops, SparseCore 0:
  9.2 100.5 all-gather.1

commit v9 on v8

--- a/solution.py
+++ b/solution.py
@@ -176,53 +176,45 @@
 
 LINKS = {"x-": ("x", -1), "y-": ("y", -1), "x+": ("x", 1), "y+": ("y", 1)}
 CARRIED = {"c": {"x+": "y+", "x-": "y-", "y+": "x-", "y-": "x+"}, "d": {"y+": "x+", "y-": "x-", "x+": "y-", "x-": "y+"}}
-LAST = {"x+": ("dy+", 0, ROWS), "x-": ("dy-", ROWS, HALF1 + ROWS), "y+": ("dx-", HALF1 + ROWS, FULL)}
-STEPS = (
-    ("cx-", "cy-", "cx+", "cy+", "=", "dy-", "dy+", "bx-", "bx+"),
-    ("dx-", "dx+", "by-", "by+", "ey+", "ex-", "ex+"),
-)
-AFTER = {"bx": "cx", "dx": "bx", "ex": "dx", "dy": "cy", "by": "dy"}
+LAST = {"x-": ("dy-", 0, HALF1), "y-": ("dx+", HALF1, FULL)}
+STEPS = ("cx-", "cy-", "cx+", "cy+", "=", "dy-", "dx-", "dx+", "dy+", "bx+", "by+", "ex-", "ey-")
+AFTER = {"bx+": "dx+", "by+": "dy+"}
 
 
 def gather_plane(own, extra, make_beside):
-    cells, cut = {}, {}
+    cells = {}
 
     def send(name, value):
-        before = AFTER.get(name[:2])
+        before = AFTER.get(name)
         if before:
-            other = cells[before + name[2]]
+            other = cells[before]
             value, other[0] = lax.optimization_barrier((value, other[0]))
         cells[name] = [shift(value, *LINKS[name[1:]])]
 
     for link in LINKS:
         send("a" + link, own)
-    for step in STEPS[0] + STEPS[1]:
+    for step in STEPS:
         kind, link = step[0], step[1:]
         if kind == "=":
             extra, cells["ay+"][0] = lax.optimization_barrier((extra, cells["ay+"][0]))
-            for other in LINKS:
-                cut[other] = cells["a" + other][0][:HALF1] if other[1] == "+" else cells["a" + other][0][HALF1:]
-            cut, cells["cx+"][0], beside = lax.optimization_barrier((cut, cells["cx+"][0], make_beside(extra)))
+            beside, cells["cx+"][0] = lax.optimization_barrier((make_beside(extra), cells["cx+"][0]))
         elif kind in CARRIED:
             send(step, cells[{"c": "a", "d": "c"}[kind] + CARRIED[kind][link]][0])
         elif kind == "b":
-            send(step, cut[link])
+            send(step, cells["a" + link][0])
         else:
             name, low, high = LAST[link]
             send(step, cells[name][0][low:high])
     whole = {(0, 0): [own]}
-    names = ("ax+", "ax-", "ay+", "ay-", "cx+", "cx-", "cy+", "cy-", "dy+", "dy-", "dx+", "dx-")
-    spots = [(1, 0), (3, 0), (0, 1), (0, 3), (1, 1), (3, 3), (3, 1), (1, 3), (1, 2), (3, 2), (2, 3), (2, 1)]
+    names = ("ax+", "ax-", "ay+", "ay-", "cx+", "cx-", "cy+", "cy-", "dy+", "dy-", "dx+", "dx-", "bx+", "by+")
+    spots = [(1, 0), (3, 0), (0, 1), (0, 3), (1, 1), (3, 3), (3, 1), (1, 3), (1, 2), (3, 2), (2, 3), (2, 1), (2, 0), (0, 2)]
     whole.update((spot, cells[name]) for spot, name in zip(spots, names))
     starts = (0, ROWS, HALF1, HALF1 + ROWS)
     parts = {key: [(v[0], at) for at in starts] for key, v in whole.items()}
     metas = {key: (v[0], 2 * ROWS) for key, v in whole.items()}
-    for key, axis in (((2, 0), "x"), ((0, 2), "y")):
-        h1, h2 = cells["b" + axis + "+"][0], cells["b" + axis + "-"][0]
-        parts[key] = [(h1, 0), (h1, ROWS), (h2, 0), (h2, ROWS)]
-        metas[key] = (h1, 2 * ROWS)
-    parts[2, 2] = [(cells["ex+"][0], 0), (cells["ex-"][0], 0), (cells["ex-"][0], ROWS + META), (cells["ey+"][0], 0)]
-    metas[2, 2] = (cells["ex-"][0], ROWS)
+    h1, h2 = cells["ex-"][0], cells["ey-"][0]
+    parts[2, 2] = [(h1, 0), (h1, ROWS), (h2, 0), (h2, ROWS)]
+    metas[2, 2] = (h1, 2 * ROWS)
     return parts, metas, beside
 
 

time: 160 us -> 160 us (level)
  waiting for transfers between devices: 56.6 us -> 72.6 us
  starting transfers between devices: 62.3 us -> 48.9 us
  local copies, waits for them, and re-layouts: 7.55 us -> 4.9 us
    ppermute x25 -> x22, waiting for transfers between devices: 44.9 us -> 61.6 us  [shift(): lax.ppermute(value, axis, [((i + by) % size, i) for i in range(size)])]
    ppermute x25 -> x22, starting transfers between devices: 38.9 us -> 27.5 us  [shift(): lax.ppermute(value, axis, [((i + by) % size, i) for i in range(size)])]
    slice x4 -> x0, local copies, waits for them, and re-layouts: 3.14 us -> none  [the longest x2 2.22 us: gather_plane(): cells['a' + other][0][HALF1:]]
    all_to_all x1, starting transfers between devices: 13.7 us -> 11.4 us  [local(): lax.all_to_all(left_best.reshape(16, BLOCKS, ROWS), ('z', 'c'), 0, 0, til...]
  transfers between devices with their start and end apart: 28 -> 25, of which waited for: 11 -> 11; matrix products, arithmetic and copies ran while one was open for 4% -> 2% of each run, Pallas kernels for 0% -> 0%
where the time goes in v9:
time: 160 us
  waiting for transfers between devices  72.6 us (45%)
  starting transfers between devices  48.9 us (31%)
  Pallas kernels  16.1 us (10%)
  between operations  14.4 us (9%)
  local copies, waits for them, and re-layouts  4.9 us (3%)
  other arithmetic  2.68 us (2%)
    ppermute x22, waiting for transfers between devices, shift(): lax.ppermute(value, axis, [((i + by) % size, i) for i in range(size)])  61.6 us
    ppermute x22, starting transfers between devices, shift(): lax.ppermute(value, axis, [((i + by) % size, i) for i in range(size)])  27.5 us
    pallas_call x1, Pallas kernels, pair_maxima(): pl.pallas_call(kernel, out_shape=[jax.ShapeDtypeStruct((n, ROWS), jnp.flo...  14.8 us
    all_to_all x1, starting transfers between devices, local(): lax.all_to_all(left_best.reshape(16, BLOCKS, ROWS), ('z', 'c'), 0, 0, til...  11.4 us
    all_to_all x1, starting transfers between devices, local(): lax.all_to_all(jnp.broadcast_to(lists, (16, lists.shape[1])), ('z', 'c'),...  9.99 us
    all_to_all x1, waiting for transfers between devices, local(): lax.all_to_all(jnp.broadcast_to(lists, (16, lists.shape[1])), ('z', 'c'),...  7.9 us
  transfers between devices with their start and end apart: 25, of which 11 were waited for; matrix products, arithmetic and copies ran while one was open for 2% of the time, Pallas kernels for 0%

profile of v9, /device:TPU:1, one launch (start us, length us, event | category | flops | bytes accessed | tf_op | source)
XLA Modules:
  0.0 159.5 jit_solution(26944189077834959)
XLA Ops:
  6.5 1.2 copy-done.1
  7.8 1.3 unit_rows.1
  9.3 3.6 %collective-permute-start = (bf16[528,1024]{1,0:T(8,128)(2,1)S(1)}, bf16[528,1024]{1,0:T(8,128)(2,1)S(1)}, u32[]{:S(2)}, u32[]{:S(2)}) collective-permute-start(bf16[528,1024]{1,0:T(8,128)(2,1)S(1)} %pad_dynamic-update-slice_fusion.refs_6_), channel_id=1, source_target_pairs={{1,0},{2,1},{3,2},{0,3},{5,4},{6,5},{7,6},{4,7},{9,8},{10,9},{11,1... | collective-permute-start | bytes 3244040 | tf_op jit(solution)/shard_map/ppermute | solution.py:174
  12.9 1.2 collective-permute-start.9
  14.1 1.5 collective-permute-start.5
  15.6 0.6 broadcast_in_dim.73
  16.2 10.0 %all-to-all-start = ((s32[16,1,576]{2,1,0:T(1,128)}), s32[16,1,576]{2,1,0:T(1,128)S(1)}, u32[]{:S(2)}, u32[]{:S(2)}) async-start(s32[16,1,576]{2,1,0:T(1,128)} %broadcast_in_dim.73), calls=%async_computation | async-start | bytes 81920 | tf_op jit(solution)/shard_map/all_to_all | solution.py:261
  26.3 7.9 %all-to-all-done = s32[16,1,576]{2,1,0:T(1,128)S(1)} async-done(((s32[16,1,576]{2,1,0:T(1,128)}), s32[16,1,576]{2,1,0:T(1,128)S(1)}, u32[]{:S(2)}, u32[]{:S(2)}) %all-to-all-start) | async-done | bytes 36896 | tf_op jit(solution)/shard_map/all_to_all | solution.py:261
  34.2 1.3 collective-permute-done.refs_7_
  35.4 0.1 fusion.8
  35.5 0.3 select_reduce_fusion
  35.9 0.1 select_reduce_fusion.2
  36.0 0.6 slice.41
  37.3 0.1 copy.7
  37.4 2.5 %collective-permute-start.1 = (bf16[528,1024]{1,0:T(8,128)(2,1)S(1)}, bf16[528,1024]{1,0:T(8,128)(2,1)}, u32[]{:S(2)}, u32[]{:S(2)}) collective-permute-start(bf16[528,1024]{1,0:T(8,128)(2,1)S(1)} %collective-permute-done.refs_7_), channel_id=1, source_target_pairs={{8,0},{16,8},{24,16},{0,24},{9,1},{17,9},{25,17},{1,25},{10,2},{18... | collective-permute-start | bytes 3244040 | tf_op jit(solution)/shard_map/ppermute | solution.py:174
  39.9 0.9 collective-permute-start.6
  40.8 0.3 convert_reduce_fusion
  41.6 2.7 %collective-permute-start.10 = (bf16[528,1024]{1,0:T(8,128)(2,1)}, bf16[528,1024]{1,0:T(8,128)(2,1)S(1)}, u32[]{:S(2)}, u32[]{:S(2)}) collective-permute-start(bf16[528,1024]{1,0:T(8,128)(2,1)} %collective-permute-done.9.refs_19_), channel_id=1, source_target_pairs={{1,0},{2,1},{3,2},{0,3},{5,4},{6,5},{7,6},{4,7},{9,8},{10,9},{11,1... | collective-permute-start | bytes 3244040 | tf_op jit(solution)/shard_map/ppermute | solution.py:174
  44.4 0.1 convert_reduce_fusion.1
  44.4 0.1 select_reduce_fusion.1
  44.6 0.7 pad_add_fusion.1.refs_2_
  45.3 20.7 %collective-permute-done.6.refs_13_ = bf16[528,1024]{1,0:T(8,128)(2,1)} collective-permute-done((bf16[528,1024]{1,0:T(8,128)(2,1)S(1)}, bf16[528,1024]{1,0:T(8,128)(2,1)}, u32[]{:S(2)}, u32[]{:S(2)}) %collective-permute-start.6) | collective-permute-done | bytes 1081376 | tf_op jit(solution)/shard_map/ppermute | solution.py:174
  66.0 0.2 collective-permute-start.7
  66.2 1.5 collective-permute-start.2
  67.7 1.5 collective-permute-done.12.refs_22_
  69.3 0.1 collective-permute-start.11
  69.4 20.0 %collective-permute-done.7.refs_18_ = bf16[528,1024]{1,0:T(8,128)(2,1)S(1)} collective-permute-done((bf16[528,1024]{1,0:T(8,128)(2,1)}, bf16[528,1024]{1,0:T(8,128)(2,1)S(1)}, u32[]{:S(2)}, u32[]{:S(2)}) %collective-permute-start.7) | collective-permute-done | bytes 1081376 | tf_op jit(solution)/shard_map/ppermute | solution.py:174
  89.3 1.1 collective-permute-start.8
  90.4 1.8 %collective-permute-start.3 = (bf16[528,1024]{1,0:T(8,128)(2,1)}, bf16[528,1024]{1,0:T(8,128)(2,1)}, u32[]{:S(2)}, u32[]{:S(2)}) collective-permute-start(bf16[528,1024]{1,0:T(8,128)(2,1)} %copy-done.4), channel_id=1, source_target_pairs={{1,0},{2,1},{3,2},{0,3},{5,4},{6,5},{7,6},{4,7},{9,8},{10,9},{11,1... | collective-permute-start | bytes 3244040 | tf_op jit(solution)/shard_map/ppermute | solution.py:174
  92.2 0.9 collective-permute-done.13.refs_21_
  93.1 0.1 collective-permute-start.14
  93.3 0.1 collective-permute-start.15
  93.4 1.0 copy-done.9
  94.5 9.9 %collective-permute-done.15.refs_17_ = bf16[256,1024]{1,0:T(8,128)(2,1)S(1)} collective-permute-done((bf16[256,1024]{1,0:T(8,128)(2,1)S(1)}, bf16[256,1024]{1,0:T(8,128)(2,1)S(1)}, u32[]{:S(2)}, u32[]{:S(2)}) %collective-permute-start.15) | collective-permute-done | bytes 524320 | tf_op jit(solution)/shard_map/ppermute | solution.py:174
  104.3 0.7 collective-permute-done.14.refs_16_
  105.0 0.8 copy-done.10
  105.8 6.0 %collective-permute-done.8.refs_14_ = bf16[528,1024]{1,0:T(8,128)(2,1)} collective-permute-done((bf16[528,1024]{1,0:T(8,128)(2,1)}, bf16[528,1024]{1,0:T(8,128)(2,1)}, u32[]{:S(2)}, u32[]{:S(2)}) %collective-permute-start.8) | collective-permute-done | bytes 1081376 | tf_op jit(solution)/shard_map/ppermute | solution.py:174
  111.8 0.7 collective-permute-done.3.refs_8_
  112.5 14.8 %pair_maxima.1 = (f32[64,128]{1,0:T(8,128)}, f32[16,128]{1,0:T(8,128)S(1)}, f32[16,128]{1,0:T(8,128)S(1)}, f32[16,128]{1,0:T(8,128)S(1)}, f32[16,128]{1,0:T(8,128)S(1)}) custom-call(s32[88]{0:T(128)S(1)} %compare_select_fusion.2.refs_0_, s32[44]{0:T(128)S(1)} %broadcast_minimum_fusion.refs_1_, s32[18]{0:T(128)S(1)} %pad_add_fusion.1.refs_2_, ...), custom_call_target="tpu_custom_call" | custom-call | tf_op jit(solution)/shard_map/pair_maxima/pallas_call | solution.py:151
  127.3 2.5 %collective-permute-start.16 = (f32[16,128]{1,0:T(8,128)S(1)}, f32[16,128]{1,0:T(8,128)S(1)}, u32[]{:S(2)}, u32[]{:S(2)}) collective-permute-start(f32[16,128]{1,0:T(8,128)S(1)} %get-tuple-element.50), channel_id=1, source_target_pairs={{3,0},{0,1},{1,2},{2,3},{7,4},{4,5},{5,6},{6,7},{11,8},{8,9},{9,10... | collective-permute-start | bytes 24584 | tf_op jit(solution)/shard_map/ppermute | solution.py:174
  129.8 1.6 %collective-permute-start.17 = (f32[16,128]{1,0:T(8,128)S(1)}, f32[16,128]{1,0:T(8,128)S(1)}, u32[]{:S(2)}, u32[]{:S(2)}) collective-permute-start(f32[16,128]{1,0:T(8,128)S(1)} %get-tuple-element.51), channel_id=1, source_target_pairs={{2,0},{3,1},{0,2},{1,3},{6,4},{7,5},{4,6},{5,7},{10,8},{11,9},{8,1... | collective-permute-start | bytes 24584 | tf_op jit(solution)/shard_map/ppermute | solution.py:174
  131.4 1.8 %collective-permute-start.18 = (f32[16,128]{1,0:T(8,128)S(1)}, f32[16,128]{1,0:T(8,128)S(1)}, u32[]{:S(2)}, u32[]{:S(2)}) collective-permute-start(f32[16,128]{1,0:T(8,128)S(1)} %get-tuple-element.52), channel_id=1, source_target_pairs={{1,0},{2,1},{3,2},{0,3},{5,4},{6,5},{7,6},{4,7},{9,8},{10,9},{11,1... | collective-permute-start | bytes 24584 | tf_op jit(solution)/shard_map/ppermute | solution.py:174
  133.2 11.4 %all-to-all-start.1 = ((f32[16,4,128]{2,1,0:T(4,128)}), f32[16,4,128]{2,1,0:T(4,128)S(1)}, u32[]{:S(2)}, u32[]{:S(2)}) async-start(f32[16,4,128]{2,1,0:T(4,128)} %bitcast.5), calls=%async_computation.1 | async-start | bytes 65536 | tf_op jit(solution)/shard_map/all_to_all | solution.py:276
  144.7 0.1 collective-permute-start.19
  144.8 3.1 %collective-permute-start.21 = (f32[4,128]{1,0:T(4,128)S(1)}, f32[4,128]{1,0:T(4,128)S(1)}, u32[]{:S(2)}, u32[]{:S(2)}) collective-permute-start(f32[4,128]{1,0:T(4,128)S(1)} %get-tuple-element.58), channel_id=1, source_target_pairs={{8,0},{16,8},{24,16},{0,24},{9,1},{17,9},{25,17},{1,25},{10,2},{18... | collective-permute-start | bytes 6152 | tf_op jit(solution)/shard_map/ppermute | solution.py:174
  147.9 1.1 collective-permute-start.20
  149.0 3.0 %all-to-all-done.1 = f32[16,4,128]{2,1,0:T(4,128)S(1)} async-done(((f32[16,4,128]{2,1,0:T(4,128)}), f32[16,4,128]{2,1,0:T(4,128)S(1)}, u32[]{:S(2)}, u32[]{:S(2)}) %all-to-all-start.1) | async-done | bytes 32800 | tf_op jit(solution)/shard_map/all_to_all | solution.py:276
  152.1 0.6 fusion.15
  (76 shorter events, 0.9 us)
Async XLA Ops:
  6.5 106.0 %all-gather.2.cloned.1.call-start = ((), (), s32[]{:S(2)}) async-start(), calls=%async_computation.2 | async-start | bytes 17825792 | tf_op jit(solution)/shard_map/all_gather | solution.py:255
  6.5 1.2 copy-start.1
  7.8 1.3 copy-start.12
  7.8 1.4 copy-start.13
  7.8 1.4 copy-start.15
  7.8 1.4 copy-start.14
  9.3 84.0 %copy-start = (bf16[528,1024]{1,0:T(8,128)(2,1)}, bf16[528,1024]{1,0:T(8,128)(2,1)S(1)}, u32[]{:S(2)}) copy-start(bf16[528,1024]{1,0:T(8,128)(2,1)S(1)} %pad_dynamic-update-slice_fusion.refs_6_) | copy-start | bytes 3244036
  9.3 26.2 %collective-permute-start = (bf16[528,1024]{1,0:T(8,128)(2,1)S(1)}, bf16[528,1024]{1,0:T(8,128)(2,1)S(1)}, u32[]{:S(2)}, u32[]{:S(2)}) collective-permute-start(bf16[528,1024]{1,0:T(8,128)(2,1)S(1)} %pad_dynamic-update-slice_fusion.refs_6_), channel_id=1, source_target_pairs={{1,0},{2,1},{3,2},{0,3},{5,4},{6,5},{7,6},{4,7},{9,8},{10,9},{11,1... | collective-permute-start | bytes 3244040 | tf_op jit(solution)/shard_map/ppermute | solution.py:174
  12.9 28.7 %collective-permute-start.9 = (bf16[528,1024]{1,0:T(8,128)(2,1)S(1)}, bf16[528,1024]{1,0:T(8,128)(2,1)}, u32[]{:S(2)}, u32[]{:S(2)}) collective-permute-start(bf16[528,1024]{1,0:T(8,128)(2,1)S(1)} %pad_dynamic-update-slice_fusion.refs_6_), channel_id=1, source_target_pairs={{24,0},{0,8},{8,16},{16,24},{25,1},{1,9},{9,17},{17,25},{26,2},{2,... | collective-permute-start | bytes 3244040 | tf_op jit(solution)/shard_map/ppermute | solution.py:174
  14.1 25.8 %collective-permute-start.5 = (bf16[528,1024]{1,0:T(8,128)(2,1)S(1)}, bf16[528,1024]{1,0:T(8,128)(2,1)S(1)}, u32[]{:S(2)}, u32[]{:S(2)}) collective-permute-start(bf16[528,1024]{1,0:T(8,128)(2,1)S(1)} %pad_dynamic-update-slice_fusion.refs_6_), channel_id=1, source_target_pairs={{8,0},{16,8},{24,16},{0,24},{9,1},{17,9},{25,17},{1,25},{10,2},{18... | collective-permute-start | bytes 3244040 | tf_op jit(solution)/shard_map/ppermute | solution.py:174
  15.6 28.8 %collective-permute-start.4 = (bf16[528,1024]{1,0:T(8,128)(2,1)S(1)}, bf16[528,1024]{1,0:T(8,128)(2,1)}, u32[]{:S(2)}, u32[]{:S(2)}) collective-permute-start(bf16[528,1024]{1,0:T(8,128)(2,1)S(1)} %pad_dynamic-update-slice_fusion.refs_6_), channel_id=1, source_target_pairs={{3,0},{0,1},{1,2},{2,3},{7,4},{4,5},{5,6},{6,7},{11,8},{8,9},{9,10... | collective-permute-start | bytes 3244040 | tf_op jit(solution)/shard_map/ppermute | solution.py:174
  16.2 17.9 %all-to-all-start = ((s32[16,1,576]{2,1,0:T(1,128)}), s32[16,1,576]{2,1,0:T(1,128)S(1)}, u32[]{:S(2)}, u32[]{:S(2)}) async-start(s32[16,1,576]{2,1,0:T(1,128)} %broadcast_in_dim.73), calls=%async_computation | async-start | bytes 81920 | tf_op jit(solution)/shard_map/all_to_all | solution.py:261
  35.4 32.3 %copy-start.4 = (bf16[528,1024]{1,0:T(8,128)(2,1)}, bf16[528,1024]{1,0:T(8,128)(2,1)S(1)}, u32[]{:S(2)}) copy-start(bf16[528,1024]{1,0:T(8,128)(2,1)S(1)} %collective-permute-done.refs_7_) | copy-start | bytes 3244036
  37.4 28.8 %collective-permute-start.1 = (bf16[528,1024]{1,0:T(8,128)(2,1)S(1)}, bf16[528,1024]{1,0:T(8,128)(2,1)}, u32[]{:S(2)}, u32[]{:S(2)}) collective-permute-start(bf16[528,1024]{1,0:T(8,128)(2,1)S(1)} %collective-permute-done.refs_7_), channel_id=1, source_target_pairs={{8,0},{16,8},{24,16},{0,24},{9,1},{17,9},{25,17},{1,25},{10,2},{18... | collective-permute-start | bytes 3244040 | tf_op jit(solution)/shard_map/ppermute | solution.py:174
  39.9 5.4 %copy-start.5 = (bf16[528,1024]{1,0:T(8,128)(2,1)}, bf16[528,1024]{1,0:T(8,128)(2,1)S(1)}, u32[]{:S(2)}) copy-start(bf16[528,1024]{1,0:T(8,128)(2,1)S(1)} %collective-permute-done.5.refs_10_) | copy-start | bytes 3244036
  39.9 26.1 %collective-permute-start.6 = (bf16[528,1024]{1,0:T(8,128)(2,1)S(1)}, bf16[528,1024]{1,0:T(8,128)(2,1)}, u32[]{:S(2)}, u32[]{:S(2)}) collective-permute-start(bf16[528,1024]{1,0:T(8,128)(2,1)S(1)} %collective-permute-done.5.refs_10_), channel_id=1, source_target_pairs={{3,0},{0,1},{1,2},{2,3},{7,4},{4,5},{5,6},{6,7},{11,8},{8,9},{9,10... | collective-permute-start | bytes 3244040 | tf_op jit(solution)/shard_map/ppermute | solution.py:174
  41.6 27.6 %collective-permute-start.10 = (bf16[528,1024]{1,0:T(8,128)(2,1)}, bf16[528,1024]{1,0:T(8,128)(2,1)S(1)}, u32[]{:S(2)}, u32[]{:S(2)}) collective-permute-start(bf16[528,1024]{1,0:T(8,128)(2,1)} %collective-permute-done.9.refs_19_), channel_id=1, source_target_pairs={{1,0},{2,1},{3,2},{0,3},{5,4},{6,5},{7,6},{4,7},{9,8},{10,9},{11,1... | collective-permute-start | bytes 3244040 | tf_op jit(solution)/shard_map/ppermute | solution.py:174
  44.4 24.9 %collective-permute-start.12 = (bf16[528,1024]{1,0:T(8,128)(2,1)}, bf16[528,1024]{1,0:T(8,128)(2,1)S(1)}, u32[]{:S(2)}, u32[]{:S(2)}) collective-permute-start(bf16[528,1024]{1,0:T(8,128)(2,1)} %collective-permute-done.4.refs_9_), channel_id=1, source_target_pairs={{24,0},{0,8},{8,16},{16,24},{25,1},{1,9},{9,17},{17,25},{26,2},{2,... | collective-permute-start | bytes 3244040 | tf_op jit(solution)/shard_map/ppermute | solution.py:174
  66.0 23.3 %collective-permute-start.7 = (bf16[528,1024]{1,0:T(8,128)(2,1)}, bf16[528,1024]{1,0:T(8,128)(2,1)S(1)}, u32[]{:S(2)}, u32[]{:S(2)}) collective-permute-start(bf16[528,1024]{1,0:T(8,128)(2,1)} %collective-permute-done.6.refs_13_), channel_id=1, source_target_pairs={{8,0},{16,8},{24,16},{0,24},{9,1},{17,9},{25,17},{1,25},{10,2},{18... | collective-permute-start | bytes 3244040 | tf_op jit(solution)/shard_map/ppermute | solution.py:174
  66.2 24.2 %collective-permute-start.2 = (bf16[528,1024]{1,0:T(8,128)(2,1)}, bf16[528,1024]{1,0:T(8,128)(2,1)S(1)}, u32[]{:S(2)}, u32[]{:S(2)}) collective-permute-start(bf16[528,1024]{1,0:T(8,128)(2,1)} %collective-permute-done.1.refs_11_), channel_id=1, source_target_pairs={{1,0},{2,1},{3,2},{0,3},{5,4},{6,5},{7,6},{4,7},{9,8},{10,9},{11,1... | collective-permute-start | bytes 3244040 | tf_op jit(solution)/shard_map/ppermute | solution.py:174
  69.2 21.1 %copy-start.7 = (bf16[528,1024]{1,0:T(8,128)(2,1)}, bf16[528,1024]{1,0:T(8,128)(2,1)S(1)}, u32[]{:S(2)}) copy-start(bf16[528,1024]{1,0:T(8,128)(2,1)S(1)} %collective-permute-done.12.refs_22_) | copy-start | bytes 3244036
  69.2 23.9 %collective-permute-start.13 = (bf16[528,1024]{1,0:T(8,128)(2,1)S(1)}, bf16[528,1024]{1,0:T(8,128)(2,1)S(1)}, u32[]{:S(2)}, u32[]{:S(2)}) collective-permute-start(bf16[528,1024]{1,0:T(8,128)(2,1)S(1)} %collective-permute-done.12.refs_22_), channel_id=1, source_target_pairs={{3,0},{0,1},{1,2},{2,3},{7,4},{4,5},{5,6},{6,7},{11,8},{8,9},{9,10... | collective-permute-start | bytes 3244040 | tf_op jit(solution)/shard_map/ppermute | solution.py:174
  69.3 24.1 %copy-start.6 = (bf16[528,1024]{1,0:T(8,128)(2,1)}, bf16[528,1024]{1,0:T(8,128)(2,1)S(1)}, u32[]{:S(2)}) copy-start(bf16[528,1024]{1,0:T(8,128)(2,1)S(1)} %collective-permute-done.10.refs_20_) | copy-start | bytes 3244036
  69.3 24.1 %collective-permute-start.11 = (bf16[528,1024]{1,0:T(8,128)(2,1)S(1)}, bf16[528,1024]{1,0:T(8,128)(2,1)S(1)}, u32[]{:S(2)}, u32[]{:S(2)}) collective-permute-start(bf16[528,1024]{1,0:T(8,128)(2,1)S(1)} %collective-permute-done.10.refs_20_), channel_id=1, source_target_pairs={{24,0},{0,8},{8,16},{16,24},{25,1},{1,9},{9,17},{17,25},{26,2},{2,... | collective-permute-start | bytes 3244040 | tf_op jit(solution)/shard_map/ppermute | solution.py:174
  89.3 23.2 %copy-start.3 = (bf16[528,1024]{1,0:T(8,128)(2,1)}, bf16[528,1024]{1,0:T(8,128)(2,1)S(1)}, u32[]{:S(2)}) copy-start(bf16[528,1024]{1,0:T(8,128)(2,1)S(1)} %collective-permute-done.7.refs_18_) | copy-start | bytes 3244036
  89.3 22.5 %collective-permute-start.8 = (bf16[528,1024]{1,0:T(8,128)(2,1)}, bf16[528,1024]{1,0:T(8,128)(2,1)}, u32[]{:S(2)}, u32[]{:S(2)}) collective-permute-start(bf16[528,1024]{1,0:T(8,128)(2,1)} %copy-done.5), channel_id=1, source_target_pairs={{8,0},{16,8},{24,16},{0,24},{9,1},{17,9},{25,17},{1,25},{10,2},{18... | collective-permute-start | bytes 3244040 | tf_op jit(solution)/shard_map/ppermute | solution.py:174
  90.4 1.9 %copy-start.8 = (bf16[528,1024]{1,0:T(8,128)(2,1)}, bf16[528,1024]{1,0:T(8,128)(2,1)S(1)}, u32[]{:S(2)}) copy-start(bf16[528,1024]{1,0:T(8,128)(2,1)S(1)} %collective-permute-done.2.refs_12_) | copy-start | bytes 3244036
  90.4 22.1 %collective-permute-start.3 = (bf16[528,1024]{1,0:T(8,128)(2,1)}, bf16[528,1024]{1,0:T(8,128)(2,1)}, u32[]{:S(2)}, u32[]{:S(2)}) collective-permute-start(bf16[528,1024]{1,0:T(8,128)(2,1)} %copy-done.4), channel_id=1, source_target_pairs={{1,0},{2,1},{3,2},{0,3},{5,4},{6,5},{7,6},{4,7},{9,8},{10,9},{11,1... | collective-permute-start | bytes 3244040 | tf_op jit(solution)/shard_map/ppermute | solution.py:174
  93.1 19.4 %copy-start.2 = (bf16[528,1024]{1,0:T(8,128)(2,1)}, bf16[528,1024]{1,0:T(8,128)(2,1)S(1)}, u32[]{:S(2)}) copy-start(bf16[528,1024]{1,0:T(8,128)(2,1)S(1)} %collective-permute-done.13.refs_21_) | copy-start | bytes 3244036
  93.1 11.9 %collective-permute-start.14 = (bf16[272,1024]{1,0:T(8,128)(2,1)S(1)}, bf16[272,1024]{1,0:T(8,128)(2,1)S(1)}, u32[]{:S(2)}, u32[]{:S(2)}) collective-permute-start(bf16[272,1024]{1,0:T(8,128)(2,1)S(1)} %slice.49), channel_id=1, source_target_pairs={{24,0},{0,8},{8,16},{16,24},{25,1},{1,9},{9,17},{17,25},{26,2},{2,... | collective-permute-start | bytes 1671176 | tf_op jit(solution)/shard_map/ppermute | solution.py:174
  93.3 11.0 %collective-permute-start.15 = (bf16[256,1024]{1,0:T(8,128)(2,1)S(1)}, bf16[256,1024]{1,0:T(8,128)(2,1)S(1)}, u32[]{:S(2)}, u32[]{:S(2)}) collective-permute-start(bf16[256,1024]{1,0:T(8,128)(2,1)S(1)} %slice.44), channel_id=1, source_target_pairs={{3,0},{0,1},{1,2},{2,3},{7,4},{4,5},{5,6},{6,7},{11,8},{8,9},{9,10... | collective-permute-start | bytes 1572872 | tf_op jit(solution)/shard_map/ppermute | solution.py:174
  93.4 1.1 copy-start.9
  104.3 7.5 %copy-start.11 = (bf16[256,1024]{1,0:T(8,128)(2,1)}, bf16[256,1024]{1,0:T(8,128)(2,1)S(1)}, u32[]{:S(2)}) copy-start(bf16[256,1024]{1,0:T(8,128)(2,1)S(1)} %collective-permute-done.15.refs_17_) | copy-start | bytes 1572868
  105.0 0.8 copy-start.10
  127.3 17.3 %collective-permute-start.16 = (f32[16,128]{1,0:T(8,128)S(1)}, f32[16,128]{1,0:T(8,128)S(1)}, u32[]{:S(2)}, u32[]{:S(2)}) collective-permute-start(f32[16,128]{1,0:T(8,128)S(1)} %get-tuple-element.50), channel_id=1, source_target_pairs={{3,0},{0,1},{1,2},{2,3},{7,4},{4,5},{5,6},{6,7},{11,8},{8,9},{9,10... | collective-permute-start | bytes 24584 | tf_op jit(solution)/shard_map/ppermute | solution.py:174
  129.8 14.8 %collective-permute-start.17 = (f32[16,128]{1,0:T(8,128)S(1)}, f32[16,128]{1,0:T(8,128)S(1)}, u32[]{:S(2)}, u32[]{:S(2)}) collective-permute-start(f32[16,128]{1,0:T(8,128)S(1)} %get-tuple-element.51), channel_id=1, source_target_pairs={{2,0},{3,1},{0,2},{1,3},{6,4},{7,5},{4,6},{5,7},{10,8},{11,9},{8,1... | collective-permute-start | bytes 24584 | tf_op jit(solution)/shard_map/ppermute | solution.py:174
  131.4 13.2 %collective-permute-start.18 = (f32[16,128]{1,0:T(8,128)S(1)}, f32[16,128]{1,0:T(8,128)S(1)}, u32[]{:S(2)}, u32[]{:S(2)}) collective-permute-start(f32[16,128]{1,0:T(8,128)S(1)} %get-tuple-element.52), channel_id=1, source_target_pairs={{1,0},{2,1},{3,2},{0,3},{5,4},{6,5},{7,6},{4,7},{9,8},{10,9},{11,1... | collective-permute-start | bytes 24584 | tf_op jit(solution)/shard_map/ppermute | solution.py:174
  133.2 18.8 %all-to-all-start.1 = ((f32[16,4,128]{2,1,0:T(4,128)}), f32[16,4,128]{2,1,0:T(4,128)S(1)}, u32[]{:S(2)}, u32[]{:S(2)}) async-start(f32[16,4,128]{2,1,0:T(4,128)} %bitcast.5), calls=%async_computation.1 | async-start | bytes 65536 | tf_op jit(solution)/shard_map/all_to_all | solution.py:276
  144.7 7.4 %collective-permute-start.19 = (f32[4,128]{1,0:T(4,128)S(1)}, f32[4,128]{1,0:T(4,128)S(1)}, u32[]{:S(2)}, u32[]{:S(2)}) collective-permute-start(f32[4,128]{1,0:T(4,128)S(1)} %get-tuple-element.57), channel_id=1, source_target_pairs={{24,0},{0,8},{8,16},{16,24},{25,1},{1,9},{9,17},{17,25},{26,2},{2,... | collective-permute-start | bytes 6152 | tf_op jit(solution)/shard_map/ppermute | solution.py:174
  144.8 7.3 %collective-permute-start.21 = (f32[4,128]{1,0:T(4,128)S(1)}, f32[4,128]{1,0:T(4,128)S(1)}, u32[]{:S(2)}, u32[]{:S(2)}) collective-permute-start(f32[4,128]{1,0:T(4,128)S(1)} %get-tuple-element.58), channel_id=1, source_target_pairs={{8,0},{16,8},{24,16},{0,24},{9,1},{17,9},{25,17},{1,25},{10,2},{18... | collective-permute-start | bytes 6152 | tf_op jit(solution)/shard_map/ppermute | solution.py:174
  147.9 4.2 %collective-permute-start.20 = (f32[4,128]{1,0:T(4,128)S(1)}, f32[4,128]{1,0:T(4,128)S(1)}, u32[]{:S(2)}, u32[]{:S(2)}) collective-permute-start(f32[4,128]{1,0:T(4,128)S(1)} %get-tuple-element.59), channel_id=1, source_target_pairs={{16,0},{24,8},{0,16},{8,24},{17,1},{25,9},{1,17},{9,25},{18,2},{26... | collective-permute-start | bytes 6152 | tf_op jit(solution)/shard_map/ppermute | solution.py:174
Sparse Core Ops, SparseCore 0:
  9.2 100.5 all-gather.1

commit v10 on v9

--- a/solution.py
+++ b/solution.py
@@ -12,7 +12,7 @@
 HALF1 = 2 * ROWS + META
 HALF2 = 2 * ROWS
 FULL = HALF1 + HALF2
-SLOTS = 8
+SLOTS = 12
 DEPTH = 5
 VMEM_LIMIT = 32 * 1024 * 1024
 

time: 160 us -> 161 us (level)
    all_to_all x1, starting transfers between devices: 11.4 us -> 13.3 us  [local(): lax.all_to_all(left_best.reshape(16, BLOCKS, ROWS), ('z', 'c'), 0, 0, til...]
where the time goes in v10:
time: 161 us; the launch traced here: 160 us
  waiting for transfers between devices  74.1 us (46%)
  starting transfers between devices  49.3 us (31%)
  Pallas kernels  15 us (9%)
  between operations  14.4 us (9%)
  local copies, waits for them, and re-layouts  4.9 us (3%)
  other arithmetic  2.68 us (2%)
    ppermute x22, waiting for transfers between devices, shift(): lax.ppermute(value, axis, [((i + by) % size, i) for i in range(size)])  61.6 us
    ppermute x22, starting transfers between devices, shift(): lax.ppermute(value, axis, [((i + by) % size, i) for i in range(size)])  26 us
    pallas_call x1, Pallas kernels, pair_maxima(): pl.pallas_call(kernel, out_shape=[jax.ShapeDtypeStruct((n, ROWS), jnp.flo...  13.7 us
    all_to_all x1, starting transfers between devices, local(): lax.all_to_all(left_best.reshape(16, BLOCKS, ROWS), ('z', 'c'), 0, 0, til...  13.3 us
    all_to_all x1, starting transfers between devices, local(): lax.all_to_all(jnp.broadcast_to(lists, (16, lists.shape[1])), ('z', 'c'),...  9.99 us
    all_to_all x1, waiting for transfers between devices, local(): lax.all_to_all(jnp.broadcast_to(lists, (16, lists.shape[1])), ('z', 'c'),...  7.9 us
    all_to_all x1, waiting for transfers between devices, local(): lax.all_to_all(left_best.reshape(16, BLOCKS, ROWS), ('z', 'c'), 0, 0, til...  4.56 us
  transfers between devices with their start and end apart: 25, of which 11 were waited for; matrix products, arithmetic and copies ran while one was open for 2% of the time, Pallas kernels for 0%

profile of v10, /device:TPU:1, one launch (start us, length us, event | category | flops | bytes accessed | tf_op | source)
XLA Modules:
  0.0 160.3 jit_solution(4873459353207592876)
XLA Ops:
  6.5 1.2 copy-done.1
  7.8 1.3 unit_rows.1
  9.3 3.6 %collective-permute-start = (bf16[528,1024]{1,0:T(8,128)(2,1)S(1)}, bf16[528,1024]{1,0:T(8,128)(2,1)S(1)}, u32[]{:S(2)}, u32[]{:S(2)}) collective-permute-start(bf16[528,1024]{1,0:T(8,128)(2,1)S(1)} %pad_dynamic-update-slice_fusion.refs_6_), channel_id=1, source_target_pairs={{1,0},{2,1},{3,2},{0,3},{5,4},{6,5},{7,6},{4,7},{9,8},{10,9},{11,1... | collective-permute-start | bytes 3244040 | tf_op jit(solution)/shard_map/ppermute | solution.py:174
  12.9 1.2 collective-permute-start.9
  14.1 1.5 collective-permute-start.5
  15.6 0.6 broadcast_in_dim.73
  16.2 10.0 %all-to-all-start = ((s32[16,1,576]{2,1,0:T(1,128)}), s32[16,1,576]{2,1,0:T(1,128)S(1)}, u32[]{:S(2)}, u32[]{:S(2)}) async-start(s32[16,1,576]{2,1,0:T(1,128)} %broadcast_in_dim.73), calls=%async_computation | async-start | bytes 81920 | tf_op jit(solution)/shard_map/all_to_all | solution.py:261
  26.3 7.9 %all-to-all-done = s32[16,1,576]{2,1,0:T(1,128)S(1)} async-done(((s32[16,1,576]{2,1,0:T(1,128)}), s32[16,1,576]{2,1,0:T(1,128)S(1)}, u32[]{:S(2)}, u32[]{:S(2)}) %all-to-all-start) | async-done | bytes 36896 | tf_op jit(solution)/shard_map/all_to_all | solution.py:261
  34.2 1.3 collective-permute-done.refs_7_
  35.4 0.1 fusion.8
  35.5 0.3 select_reduce_fusion
  35.9 0.1 select_reduce_fusion.2
  36.0 0.6 slice.41
  37.3 0.1 copy.7
  37.4 2.5 %collective-permute-start.1 = (bf16[528,1024]{1,0:T(8,128)(2,1)S(1)}, bf16[528,1024]{1,0:T(8,128)(2,1)}, u32[]{:S(2)}, u32[]{:S(2)}) collective-permute-start(bf16[528,1024]{1,0:T(8,128)(2,1)S(1)} %collective-permute-done.refs_7_), channel_id=1, source_target_pairs={{8,0},{16,8},{24,16},{0,24},{9,1},{17,9},{25,17},{1,25},{10,2},{18... | collective-permute-start | bytes 3244040 | tf_op jit(solution)/shard_map/ppermute | solution.py:174
  39.9 0.9 collective-permute-start.6
  40.8 0.3 convert_reduce_fusion
  41.3 0.1 eq.54
  41.6 2.7 %collective-permute-start.10 = (bf16[528,1024]{1,0:T(8,128)(2,1)}, bf16[528,1024]{1,0:T(8,128)(2,1)S(1)}, u32[]{:S(2)}, u32[]{:S(2)}) collective-permute-start(bf16[528,1024]{1,0:T(8,128)(2,1)} %collective-permute-done.9.refs_19_), channel_id=1, source_target_pairs={{1,0},{2,1},{3,2},{0,3},{5,4},{6,5},{7,6},{4,7},{9,8},{10,9},{11,1... | collective-permute-start | bytes 3244040 | tf_op jit(solution)/shard_map/ppermute | solution.py:174
  44.4 0.1 convert_reduce_fusion.1
  44.4 0.1 select_reduce_fusion.1
  44.6 0.7 pad_add_fusion.1.refs_2_
  45.3 20.7 %collective-permute-done.6.refs_13_ = bf16[528,1024]{1,0:T(8,128)(2,1)} collective-permute-done((bf16[528,1024]{1,0:T(8,128)(2,1)S(1)}, bf16[528,1024]{1,0:T(8,128)(2,1)}, u32[]{:S(2)}, u32[]{:S(2)}) %collective-permute-start.6) | collective-permute-done | bytes 1081376 | tf_op jit(solution)/shard_map/ppermute | solution.py:174
  66.0 0.2 collective-permute-start.7
  66.2 1.5 collective-permute-start.2
  67.7 1.5 collective-permute-done.12.refs_22_
  69.3 0.1 collective-permute-start.11
  69.4 20.0 %collective-permute-done.7.refs_18_ = bf16[528,1024]{1,0:T(8,128)(2,1)S(1)} collective-permute-done((bf16[528,1024]{1,0:T(8,128)(2,1)}, bf16[528,1024]{1,0:T(8,128)(2,1)S(1)}, u32[]{:S(2)}, u32[]{:S(2)}) %collective-permute-start.7) | collective-permute-done | bytes 1081376 | tf_op jit(solution)/shard_map/ppermute | solution.py:174
  89.3 1.1 collective-permute-start.8
  90.4 1.8 %collective-permute-start.3 = (bf16[528,1024]{1,0:T(8,128)(2,1)}, bf16[528,1024]{1,0:T(8,128)(2,1)}, u32[]{:S(2)}, u32[]{:S(2)}) collective-permute-start(bf16[528,1024]{1,0:T(8,128)(2,1)} %copy-done.4), channel_id=1, source_target_pairs={{1,0},{2,1},{3,2},{0,3},{5,4},{6,5},{7,6},{4,7},{9,8},{10,9},{11,1... | collective-permute-start | bytes 3244040 | tf_op jit(solution)/shard_map/ppermute | solution.py:174
  92.2 0.9 collective-permute-done.13.refs_21_
  93.1 0.1 collective-permute-start.14
  93.3 0.1 collective-permute-start.15
  93.4 1.0 copy-done.9
  94.5 9.9 %collective-permute-done.15.refs_17_ = bf16[256,1024]{1,0:T(8,128)(2,1)S(1)} collective-permute-done((bf16[256,1024]{1,0:T(8,128)(2,1)S(1)}, bf16[256,1024]{1,0:T(8,128)(2,1)S(1)}, u32[]{:S(2)}, u32[]{:S(2)}) %collective-permute-start.15) | collective-permute-done | bytes 524320 | tf_op jit(solution)/shard_map/ppermute | solution.py:174
  104.3 0.7 collective-permute-done.14.refs_16_
  105.0 0.8 copy-done.10
  105.8 6.0 %collective-permute-done.8.refs_14_ = bf16[528,1024]{1,0:T(8,128)(2,1)} collective-permute-done((bf16[528,1024]{1,0:T(8,128)(2,1)}, bf16[528,1024]{1,0:T(8,128)(2,1)}, u32[]{:S(2)}, u32[]{:S(2)}) %collective-permute-start.8) | collective-permute-done | bytes 1081376 | tf_op jit(solution)/shard_map/ppermute | solution.py:174
  111.8 0.7 collective-permute-done.3.refs_8_
  112.5 13.7 %pair_maxima.1 = (f32[64,128]{1,0:T(8,128)}, f32[16,128]{1,0:T(8,128)S(1)}, f32[16,128]{1,0:T(8,128)S(1)}, f32[16,128]{1,0:T(8,128)S(1)}, f32[16,128]{1,0:T(8,128)S(1)}) custom-call(s32[88]{0:T(128)S(1)} %compare_select_fusion.2.refs_0_, s32[44]{0:T(128)S(1)} %broadcast_minimum_fusion.refs_1_, s32[18]{0:T(128)S(1)} %pad_add_fusion.1.refs_2_, ...), custom_call_target="tpu_custom_call" | custom-call | tf_op jit(solution)/shard_map/pair_maxima/pallas_call | solution.py:151
  126.2 2.5 %collective-permute-start.16 = (f32[16,128]{1,0:T(8,128)S(1)}, f32[16,128]{1,0:T(8,128)S(1)}, u32[]{:S(2)}, u32[]{:S(2)}) collective-permute-start(f32[16,128]{1,0:T(8,128)S(1)} %get-tuple-element.50), channel_id=1, source_target_pairs={{3,0},{0,1},{1,2},{2,3},{7,4},{4,5},{5,6},{6,7},{11,8},{8,9},{9,10... | collective-permute-start | bytes 24584 | tf_op jit(solution)/shard_map/ppermute | solution.py:174
  128.7 1.6 %collective-permute-start.17 = (f32[16,128]{1,0:T(8,128)S(1)}, f32[16,128]{1,0:T(8,128)S(1)}, u32[]{:S(2)}, u32[]{:S(2)}) collective-permute-start(f32[16,128]{1,0:T(8,128)S(1)} %get-tuple-element.51), channel_id=1, source_target_pairs={{2,0},{3,1},{0,2},{1,3},{6,4},{7,5},{4,6},{5,7},{10,8},{11,9},{8,1... | collective-permute-start | bytes 24584 | tf_op jit(solution)/shard_map/ppermute | solution.py:174
  130.4 1.8 %collective-permute-start.18 = (f32[16,128]{1,0:T(8,128)S(1)}, f32[16,128]{1,0:T(8,128)S(1)}, u32[]{:S(2)}, u32[]{:S(2)}) collective-permute-start(f32[16,128]{1,0:T(8,128)S(1)} %get-tuple-element.52), channel_id=1, source_target_pairs={{1,0},{2,1},{3,2},{0,3},{5,4},{6,5},{7,6},{4,7},{9,8},{10,9},{11,1... | collective-permute-start | bytes 24584 | tf_op jit(solution)/shard_map/ppermute | solution.py:174
  132.2 13.3 %all-to-all-start.1 = ((f32[16,4,128]{2,1,0:T(4,128)}), f32[16,4,128]{2,1,0:T(4,128)S(1)}, u32[]{:S(2)}, u32[]{:S(2)}) async-start(f32[16,4,128]{2,1,0:T(4,128)} %bitcast.5), calls=%async_computation.1 | async-start | bytes 65536 | tf_op jit(solution)/shard_map/all_to_all | solution.py:276
  145.5 0.1 collective-permute-start.19
  145.6 2.7 %collective-permute-start.21 = (f32[4,128]{1,0:T(4,128)S(1)}, f32[4,128]{1,0:T(4,128)S(1)}, u32[]{:S(2)}, u32[]{:S(2)}) collective-permute-start(f32[4,128]{1,0:T(4,128)S(1)} %get-tuple-element.58), channel_id=1, source_target_pairs={{8,0},{16,8},{24,16},{0,24},{9,1},{17,9},{25,17},{1,25},{10,2},{18... | collective-permute-start | bytes 6152 | tf_op jit(solution)/shard_map/ppermute | solution.py:174
  148.3 4.6 %all-to-all-done.1 = f32[16,4,128]{2,1,0:T(4,128)S(1)} async-done(((f32[16,4,128]{2,1,0:T(4,128)}), f32[16,4,128]{2,1,0:T(4,128)S(1)}, u32[]{:S(2)}, u32[]{:S(2)}) %all-to-all-start.1) | async-done | bytes 32800 | tf_op jit(solution)/shard_map/all_to_all | solution.py:276
  152.9 0.6 fusion.15
  (76 shorter events, 0.8 us)
Async XLA Ops:
  6.5 106.0 %all-gather.2.cloned.1.call-start = ((), (), s32[]{:S(2)}) async-start(), calls=%async_computation.2 | async-start | bytes 17825792 | tf_op jit(solution)/shard_map/all_gather | solution.py:255
  6.5 1.2 copy-start.1
  7.8 1.3 copy-start.12
  7.8 1.4 copy-start.13
  7.8 1.4 copy-start.15
  7.8 1.4 copy-start.14
  9.3 84.0 %copy-start = (bf16[528,1024]{1,0:T(8,128)(2,1)}, bf16[528,1024]{1,0:T(8,128)(2,1)S(1)}, u32[]{:S(2)}) copy-start(bf16[528,1024]{1,0:T(8,128)(2,1)S(1)} %pad_dynamic-update-slice_fusion.refs_6_) | copy-start | bytes 3244036
  9.3 26.2 %collective-permute-start = (bf16[528,1024]{1,0:T(8,128)(2,1)S(1)}, bf16[528,1024]{1,0:T(8,128)(2,1)S(1)}, u32[]{:S(2)}, u32[]{:S(2)}) collective-permute-start(bf16[528,1024]{1,0:T(8,128)(2,1)S(1)} %pad_dynamic-update-slice_fusion.refs_6_), channel_id=1, source_target_pairs={{1,0},{2,1},{3,2},{0,3},{5,4},{6,5},{7,6},{4,7},{9,8},{10,9},{11,1... | collective-permute-start | bytes 3244040 | tf_op jit(solution)/shard_map/ppermute | solution.py:174
  12.9 28.7 %collective-permute-start.9 = (bf16[528,1024]{1,0:T(8,128)(2,1)S(1)}, bf16[528,1024]{1,0:T(8,128)(2,1)}, u32[]{:S(2)}, u32[]{:S(2)}) collective-permute-start(bf16[528,1024]{1,0:T(8,128)(2,1)S(1)} %pad_dynamic-update-slice_fusion.refs_6_), channel_id=1, source_target_pairs={{24,0},{0,8},{8,16},{16,24},{25,1},{1,9},{9,17},{17,25},{26,2},{2,... | collective-permute-start | bytes 3244040 | tf_op jit(solution)/shard_map/ppermute | solution.py:174
  14.1 25.8 %collective-permute-start.5 = (bf16[528,1024]{1,0:T(8,128)(2,1)S(1)}, bf16[528,1024]{1,0:T(8,128)(2,1)S(1)}, u32[]{:S(2)}, u32[]{:S(2)}) collective-permute-start(bf16[528,1024]{1,0:T(8,128)(2,1)S(1)} %pad_dynamic-update-slice_fusion.refs_6_), channel_id=1, source_target_pairs={{8,0},{16,8},{24,16},{0,24},{9,1},{17,9},{25,17},{1,25},{10,2},{18... | collective-permute-start | bytes 3244040 | tf_op jit(solution)/shard_map/ppermute | solution.py:174
  15.6 28.8 %collective-permute-start.4 = (bf16[528,1024]{1,0:T(8,128)(2,1)S(1)}, bf16[528,1024]{1,0:T(8,128)(2,1)}, u32[]{:S(2)}, u32[]{:S(2)}) collective-permute-start(bf16[528,1024]{1,0:T(8,128)(2,1)S(1)} %pad_dynamic-update-slice_fusion.refs_6_), channel_id=1, source_target_pairs={{3,0},{0,1},{1,2},{2,3},{7,4},{4,5},{5,6},{6,7},{11,8},{8,9},{9,10... | collective-permute-start | bytes 3244040 | tf_op jit(solution)/shard_map/ppermute | solution.py:174
  16.2 17.9 %all-to-all-start = ((s32[16,1,576]{2,1,0:T(1,128)}), s32[16,1,576]{2,1,0:T(1,128)S(1)}, u32[]{:S(2)}, u32[]{:S(2)}) async-start(s32[16,1,576]{2,1,0:T(1,128)} %broadcast_in_dim.73), calls=%async_computation | async-start | bytes 81920 | tf_op jit(solution)/shard_map/all_to_all | solution.py:261
  35.4 32.3 %copy-start.4 = (bf16[528,1024]{1,0:T(8,128)(2,1)}, bf16[528,1024]{1,0:T(8,128)(2,1)S(1)}, u32[]{:S(2)}) copy-start(bf16[528,1024]{1,0:T(8,128)(2,1)S(1)} %collective-permute-done.refs_7_) | copy-start | bytes 3244036
  37.4 28.8 %collective-permute-start.1 = (bf16[528,1024]{1,0:T(8,128)(2,1)S(1)}, bf16[528,1024]{1,0:T(8,128)(2,1)}, u32[]{:S(2)}, u32[]{:S(2)}) collective-permute-start(bf16[528,1024]{1,0:T(8,128)(2,1)S(1)} %collective-permute-done.refs_7_), channel_id=1, source_target_pairs={{8,0},{16,8},{24,16},{0,24},{9,1},{17,9},{25,17},{1,25},{10,2},{18... | collective-permute-start | bytes 3244040 | tf_op jit(solution)/shard_map/ppermute | solution.py:174
  39.9 5.4 %copy-start.5 = (bf16[528,1024]{1,0:T(8,128)(2,1)}, bf16[528,1024]{1,0:T(8,128)(2,1)S(1)}, u32[]{:S(2)}) copy-start(bf16[528,1024]{1,0:T(8,128)(2,1)S(1)} %collective-permute-done.5.refs_10_) | copy-start | bytes 3244036
  39.9 26.1 %collective-permute-start.6 = (bf16[528,1024]{1,0:T(8,128)(2,1)S(1)}, bf16[528,1024]{1,0:T(8,128)(2,1)}, u32[]{:S(2)}, u32[]{:S(2)}) collective-permute-start(bf16[528,1024]{1,0:T(8,128)(2,1)S(1)} %collective-permute-done.5.refs_10_), channel_id=1, source_target_pairs={{3,0},{0,1},{1,2},{2,3},{7,4},{4,5},{5,6},{6,7},{11,8},{8,9},{9,10... | collective-permute-start | bytes 3244040 | tf_op jit(solution)/shard_map/ppermute | solution.py:174
  41.6 27.6 %collective-permute-start.10 = (bf16[528,1024]{1,0:T(8,128)(2,1)}, bf16[528,1024]{1,0:T(8,128)(2,1)S(1)}, u32[]{:S(2)}, u32[]{:S(2)}) collective-permute-start(bf16[528,1024]{1,0:T(8,128)(2,1)} %collective-permute-done.9.refs_19_), channel_id=1, source_target_pairs={{1,0},{2,1},{3,2},{0,3},{5,4},{6,5},{7,6},{4,7},{9,8},{10,9},{11,1... | collective-permute-start | bytes 3244040 | tf_op jit(solution)/shard_map/ppermute | solution.py:174
  44.4 24.9 %collective-permute-start.12 = (bf16[528,1024]{1,0:T(8,128)(2,1)}, bf16[528,1024]{1,0:T(8,128)(2,1)S(1)}, u32[]{:S(2)}, u32[]{:S(2)}) collective-permute-start(bf16[528,1024]{1,0:T(8,128)(2,1)} %collective-permute-done.4.refs_9_), channel_id=1, source_target_pairs={{24,0},{0,8},{8,16},{16,24},{25,1},{1,9},{9,17},{17,25},{26,2},{2,... | collective-permute-start | bytes 3244040 | tf_op jit(solution)/shard_map/ppermute | solution.py:174
  66.0 23.3 %collective-permute-start.7 = (bf16[528,1024]{1,0:T(8,128)(2,1)}, bf16[528,1024]{1,0:T(8,128)(2,1)S(1)}, u32[]{:S(2)}, u32[]{:S(2)}) collective-permute-start(bf16[528,1024]{1,0:T(8,128)(2,1)} %collective-permute-done.6.refs_13_), channel_id=1, source_target_pairs={{8,0},{16,8},{24,16},{0,24},{9,1},{17,9},{25,17},{1,25},{10,2},{18... | collective-permute-start | bytes 3244040 | tf_op jit(solution)/shard_map/ppermute | solution.py:174
  66.2 24.2 %collective-permute-start.2 = (bf16[528,1024]{1,0:T(8,128)(2,1)}, bf16[528,1024]{1,0:T(8,128)(2,1)S(1)}, u32[]{:S(2)}, u32[]{:S(2)}) collective-permute-start(bf16[528,1024]{1,0:T(8,128)(2,1)} %collective-permute-done.1.refs_11_), channel_id=1, source_target_pairs={{1,0},{2,1},{3,2},{0,3},{5,4},{6,5},{7,6},{4,7},{9,8},{10,9},{11,1... | collective-permute-start | bytes 3244040 | tf_op jit(solution)/shard_map/ppermute | solution.py:174
  69.2 21.1 %copy-start.7 = (bf16[528,1024]{1,0:T(8,128)(2,1)}, bf16[528,1024]{1,0:T(8,128)(2,1)S(1)}, u32[]{:S(2)}) copy-start(bf16[528,1024]{1,0:T(8,128)(2,1)S(1)} %collective-permute-done.12.refs_22_) | copy-start | bytes 3244036
  69.2 23.9 %collective-permute-start.13 = (bf16[528,1024]{1,0:T(8,128)(2,1)S(1)}, bf16[528,1024]{1,0:T(8,128)(2,1)S(1)}, u32[]{:S(2)}, u32[]{:S(2)}) collective-permute-start(bf16[528,1024]{1,0:T(8,128)(2,1)S(1)} %collective-permute-done.12.refs_22_), channel_id=1, source_target_pairs={{3,0},{0,1},{1,2},{2,3},{7,4},{4,5},{5,6},{6,7},{11,8},{8,9},{9,10... | collective-permute-start | bytes 3244040 | tf_op jit(solution)/shard_map/ppermute | solution.py:174
  69.3 24.1 %copy-start.6 = (bf16[528,1024]{1,0:T(8,128)(2,1)}, bf16[528,1024]{1,0:T(8,128)(2,1)S(1)}, u32[]{:S(2)}) copy-start(bf16[528,1024]{1,0:T(8,128)(2,1)S(1)} %collective-permute-done.10.refs_20_) | copy-start | bytes 3244036
  69.3 24.1 %collective-permute-start.11 = (bf16[528,1024]{1,0:T(8,128)(2,1)S(1)}, bf16[528,1024]{1,0:T(8,128)(2,1)S(1)}, u32[]{:S(2)}, u32[]{:S(2)}) collective-permute-start(bf16[528,1024]{1,0:T(8,128)(2,1)S(1)} %collective-permute-done.10.refs_20_), channel_id=1, source_target_pairs={{24,0},{0,8},{8,16},{16,24},{25,1},{1,9},{9,17},{17,25},{26,2},{2,... | collective-permute-start | bytes 3244040 | tf_op jit(solution)/shard_map/ppermute | solution.py:174
  89.3 23.2 %copy-start.3 = (bf16[528,1024]{1,0:T(8,128)(2,1)}, bf16[528,1024]{1,0:T(8,128)(2,1)S(1)}, u32[]{:S(2)}) copy-start(bf16[528,1024]{1,0:T(8,128)(2,1)S(1)} %collective-permute-done.7.refs_18_) | copy-start | bytes 3244036
  89.3 22.5 %collective-permute-start.8 = (bf16[528,1024]{1,0:T(8,128)(2,1)}, bf16[528,1024]{1,0:T(8,128)(2,1)}, u32[]{:S(2)}, u32[]{:S(2)}) collective-permute-start(bf16[528,1024]{1,0:T(8,128)(2,1)} %copy-done.5), channel_id=1, source_target_pairs={{8,0},{16,8},{24,16},{0,24},{9,1},{17,9},{25,17},{1,25},{10,2},{18... | collective-permute-start | bytes 3244040 | tf_op jit(solution)/shard_map/ppermute | solution.py:174
  90.4 1.9 %copy-start.8 = (bf16[528,1024]{1,0:T(8,128)(2,1)}, bf16[528,1024]{1,0:T(8,128)(2,1)S(1)}, u32[]{:S(2)}) copy-start(bf16[528,1024]{1,0:T(8,128)(2,1)S(1)} %collective-permute-done.2.refs_12_) | copy-start | bytes 3244036
  90.4 22.1 %collective-permute-start.3 = (bf16[528,1024]{1,0:T(8,128)(2,1)}, bf16[528,1024]{1,0:T(8,128)(2,1)}, u32[]{:S(2)}, u32[]{:S(2)}) collective-permute-start(bf16[528,1024]{1,0:T(8,128)(2,1)} %copy-done.4), channel_id=1, source_target_pairs={{1,0},{2,1},{3,2},{0,3},{5,4},{6,5},{7,6},{4,7},{9,8},{10,9},{11,1... | collective-permute-start | bytes 3244040 | tf_op jit(solution)/shard_map/ppermute | solution.py:174
  93.1 19.4 %copy-start.2 = (bf16[528,1024]{1,0:T(8,128)(2,1)}, bf16[528,1024]{1,0:T(8,128)(2,1)S(1)}, u32[]{:S(2)}) copy-start(bf16[528,1024]{1,0:T(8,128)(2,1)S(1)} %collective-permute-done.13.refs_21_) | copy-start | bytes 3244036
  93.1 11.9 %collective-permute-start.14 = (bf16[272,1024]{1,0:T(8,128)(2,1)S(1)}, bf16[272,1024]{1,0:T(8,128)(2,1)S(1)}, u32[]{:S(2)}, u32[]{:S(2)}) collective-permute-start(bf16[272,1024]{1,0:T(8,128)(2,1)S(1)} %slice.49), channel_id=1, source_target_pairs={{24,0},{0,8},{8,16},{16,24},{25,1},{1,9},{9,17},{17,25},{26,2},{2,... | collective-permute-start | bytes 1671176 | tf_op jit(solution)/shard_map/ppermute | solution.py:174
  93.3 11.0 %collective-permute-start.15 = (bf16[256,1024]{1,0:T(8,128)(2,1)S(1)}, bf16[256,1024]{1,0:T(8,128)(2,1)S(1)}, u32[]{:S(2)}, u32[]{:S(2)}) collective-permute-start(bf16[256,1024]{1,0:T(8,128)(2,1)S(1)} %slice.44), channel_id=1, source_target_pairs={{3,0},{0,1},{1,2},{2,3},{7,4},{4,5},{5,6},{6,7},{11,8},{8,9},{9,10... | collective-permute-start | bytes 1572872 | tf_op jit(solution)/shard_map/ppermute | solution.py:174
  93.4 1.1 copy-start.9
  104.3 7.5 %copy-start.11 = (bf16[256,1024]{1,0:T(8,128)(2,1)}, bf16[256,1024]{1,0:T(8,128)(2,1)S(1)}, u32[]{:S(2)}) copy-start(bf16[256,1024]{1,0:T(8,128)(2,1)S(1)} %collective-permute-done.15.refs_17_) | copy-start | bytes 1572868
  105.0 0.8 copy-start.10
  126.2 19.2 %collective-permute-start.16 = (f32[16,128]{1,0:T(8,128)S(1)}, f32[16,128]{1,0:T(8,128)S(1)}, u32[]{:S(2)}, u32[]{:S(2)}) collective-permute-start(f32[16,128]{1,0:T(8,128)S(1)} %get-tuple-element.50), channel_id=1, source_target_pairs={{3,0},{0,1},{1,2},{2,3},{7,4},{4,5},{5,6},{6,7},{11,8},{8,9},{9,10... | collective-permute-start | bytes 24584 | tf_op jit(solution)/shard_map/ppermute | solution.py:174
  128.7 16.7 %collective-permute-start.17 = (f32[16,128]{1,0:T(8,128)S(1)}, f32[16,128]{1,0:T(8,128)S(1)}, u32[]{:S(2)}, u32[]{:S(2)}) collective-permute-start(f32[16,128]{1,0:T(8,128)S(1)} %get-tuple-element.51), channel_id=1, source_target_pairs={{2,0},{3,1},{0,2},{1,3},{6,4},{7,5},{4,6},{5,7},{10,8},{11,9},{8,1... | collective-permute-start | bytes 24584 | tf_op jit(solution)/shard_map/ppermute | solution.py:174
  130.4 15.1 %collective-permute-start.18 = (f32[16,128]{1,0:T(8,128)S(1)}, f32[16,128]{1,0:T(8,128)S(1)}, u32[]{:S(2)}, u32[]{:S(2)}) collective-permute-start(f32[16,128]{1,0:T(8,128)S(1)} %get-tuple-element.52), channel_id=1, source_target_pairs={{1,0},{2,1},{3,2},{0,3},{5,4},{6,5},{7,6},{4,7},{9,8},{10,9},{11,1... | collective-permute-start | bytes 24584 | tf_op jit(solution)/shard_map/ppermute | solution.py:174
  132.2 20.7 %all-to-all-start.1 = ((f32[16,4,128]{2,1,0:T(4,128)}), f32[16,4,128]{2,1,0:T(4,128)S(1)}, u32[]{:S(2)}, u32[]{:S(2)}) async-start(f32[16,4,128]{2,1,0:T(4,128)} %bitcast.5), calls=%async_computation.1 | async-start | bytes 65536 | tf_op jit(solution)/shard_map/all_to_all | solution.py:276
  145.5 7.4 %collective-permute-start.19 = (f32[4,128]{1,0:T(4,128)S(1)}, f32[4,128]{1,0:T(4,128)S(1)}, u32[]{:S(2)}, u32[]{:S(2)}) collective-permute-start(f32[4,128]{1,0:T(4,128)S(1)} %get-tuple-element.57), channel_id=1, source_target_pairs={{24,0},{0,8},{8,16},{16,24},{25,1},{1,9},{9,17},{17,25},{26,2},{2,... | collective-permute-start | bytes 6152 | tf_op jit(solution)/shard_map/ppermute | solution.py:174
  145.6 7.3 %collective-permute-start.21 = (f32[4,128]{1,0:T(4,128)S(1)}, f32[4,128]{1,0:T(4,128)S(1)}, u32[]{:S(2)}, u32[]{:S(2)}) collective-permute-start(f32[4,128]{1,0:T(4,128)S(1)} %get-tuple-element.58), channel_id=1, source_target_pairs={{8,0},{16,8},{24,16},{0,24},{9,1},{17,9},{25,17},{1,25},{10,2},{18... | collective-permute-start | bytes 6152 | tf_op jit(solution)/shard_map/ppermute | solution.py:174
  148.3 4.6 %collective-permute-start.20 = (f32[4,128]{1,0:T(4,128)S(1)}, f32[4,128]{1,0:T(4,128)S(1)}, u32[]{:S(2)}, u32[]{:S(2)}) collective-permute-start(f32[4,128]{1,0:T(4,128)S(1)} %get-tuple-element.59), channel_id=1, source_target_pairs={{16,0},{24,8},{0,16},{8,24},{17,1},{25,9},{1,17},{9,25},{18,2},{26... | collective-permute-start | bytes 6152 | tf_op jit(solution)/shard_map/ppermute | solution.py:174
Sparse Core Ops, SparseCore 0:
  9.2 100.5 all-gather.1
